TPU v7x, 32 devices: a whole 2x2x4 slice. The times are simulated.
32 devices in a mesh: dp: 8 (over y, x, core), fsdp: 4 (over z).
Axes of the slice: x: 2, y: 2, z: 4, core: 2. Of those that a mesh axis runs over, the one named last changes fastest.
Arguments:
- acts: bfloat16 [4096, 5120], P(('dp', 'fsdp')), may hold values from -6 to 6
- grad_out: bfloat16 [4096, 6912], P('dp', 'fsdp'), may hold values from -0.125 to 0.125
- projection: bfloat16 [5120, 256], replicated, may hold values from -0.375 to 0.375
- moment_one: float32 [256, 6912], P('dp', 'fsdp'), may hold values from -6 to 6
- moment_two: float32 [256, 6912], P('dp', 'fsdp'), may hold values from 0.5 to 4
- master: float32 [5120, 6912], P('dp', 'fsdp'), may hold values from -6 to 6
Outputs:
- moment_one_new: float32 [256, 6912], P('dp', 'fsdp')
- moment_two_new: float32 [256, 6912], P('dp', 'fsdp')
- master_new: float32 [5120, 6912], P('dp', 'fsdp')
- weight_cols: bfloat16 [5120, 6912], P(None, 'fsdp')
All inputs are finite; a program needn't handle non-finite values.
Results may differ from a plain program's by a relative error of at most 0.001.
The roundings to bfloat16 on the way count: a program that leaves them out, or rounds other values in their place, can miss the bound.
Values may be sent and summed in bfloat16 or wider, within the bound.
No kernel may reach another device: no remote copies, remote signals or barrier semaphores. Data moves between devices by JAX's collectives and lax.ppermute only.
A program may use at most 128 MiB of HBM per device.

v0:
```python
import jax
import jax.numpy as jnp
from jax import lax
from jax.sharding import PartitionSpec as P

STEP = 1000


BETA_ONE = 0.9
BETA_TWO = 0.999
ADAM_EPS = 1e-08
LEARN_RATE = 0.01


def body(acts, grad_out, projection, moment_one, moment_two, master):
    col_width = grad_out.shape[1]
    projected = jnp.dot(acts, projection, preferred_element_type=jnp.float32).astype(jnp.bfloat16)
    group_proj = lax.all_gather(projected, "fsdp", axis=0, tiled=True)
    partial_value = jnp.einsum(
        "tr,tc->rc", group_proj, grad_out, preferred_element_type=jnp.float32
    )
    partial_value = lax.optimization_barrier(partial_value.astype(jnp.bfloat16))
    grad = lax.psum_scatter(
        partial_value.astype(jnp.float32), "dp", scatter_dimension=0, tiled=True
    )
    moment_one_new = BETA_ONE * moment_one + (1.0 - BETA_ONE) * grad
    moment_two_new = BETA_TWO * moment_two + (1.0 - BETA_TWO) * grad * grad
    correct_one = 1.0 - BETA_ONE**STEP
    correct_two = 1.0 - BETA_TWO**STEP
    update = (
        moment_one_new / correct_one / (jnp.sqrt(moment_two_new / correct_two) + ADAM_EPS)
    ).astype(jnp.bfloat16)
    slab_rows = master.shape[0]
    proj_slab = lax.dynamic_slice_in_dim(projection, lax.axis_index("dp") * slab_rows, slab_rows, 0)
    piece = lax.all_gather(update, "dp", axis=0, tiled=True)
    left_cols = lax.slice_in_dim(proj_slab, 0, piece.shape[0], axis=1)
    expanded = jnp.zeros((slab_rows, col_width), jnp.float32) + jnp.dot(
        left_cols, piece, preferred_element_type=jnp.float32
    )
    master_new = master - LEARN_RATE * expanded
    weight_cols = lax.all_gather(master_new.astype(jnp.bfloat16), "dp", axis=0, tiled=True)
    return (moment_one_new, moment_two_new, master_new, weight_cols)


def solution(mesh):
    in_specs = (
        P(("dp", "fsdp"), None),
        P("dp", "fsdp"),
        P(),
        P("dp", "fsdp"),
        P("dp", "fsdp"),
        P("dp", "fsdp"),
    )
    out_specs = (P("dp", "fsdp"), P("dp", "fsdp"), P("dp", "fsdp"), P(None, "fsdp"))
    return jax.shard_map(body, mesh=mesh, in_specs=in_specs, out_specs=out_specs, check_vma=False)
```

profile of v0, /device:TPU:0, one launch (start us, length us, event | category | flops | bytes accessed | tf_op | source)
XLA Modules:
  0.0 205.1 jit_solution(15800413369955223752)
XLA Ops:
  7.2 0.0 copy-start
  7.2 0.0 reduce-scatter.4.cloned.1.call-start
  7.2 1.7 copy-done
  8.9 0.0 copy-start.1
  8.9 2.0 convolution_convert_fusion.1
  10.9 15.6 %all_gather.9 = bf16[512,256]{1,0:T(8,128)(2,1)S(1)} all-gather(bf16[128,256]{1,0:T(8,128)(2,1)S(1)} %convolution_convert_fusion.1), channel_id=1, replica_groups=mesh['dp'=8,'fsdp'=4] {'fsdp'}, dimensions={0}, use_global_device_ids=true | all-gather | bytes 327680 | tf_op jit(solution)/shard_map/all_gather | solution.py:18
  26.5 0.0 copy-done.1
  26.5 0.6 convolution_convert_fusion
  27.1 1.6 copy.22
  28.7 0.0 reduce-scatter.4.cloned.1.call-update
  28.8 0.0 all-gather.2.cloned.1.call-start
  28.8 41.3 %reduce-scatter.4.cloned.1.call-done = f32[32,1728]{1,0:T(8,128)} async-done(((f32[256,1728]{1,0:T(8,128)}), f32[32,1728]{1,0:T(8,128)}) %reduce-scatter.4.cloned.1.call-update) | async-done | bytes 221200 | tf_op jit(solution)/shard_map/reduce_scatter | solution.py:23
  70.2 2.1 divide_convert_fusion
  72.2 10.6 %all_gather.10 = bf16[256,1728]{1,0:T(8,128)(2,1)S(1)} all-gather(bf16[32,1728]{1,0:T(8,128)(2,1)S(1)} %get-tuple-element.12), channel_id=1, replica_groups=mesh['dp'=8,'fsdp'=4] {'dp'}, dimensions={0}, use_global_device_ids=true | all-gather | bytes 995328 | tf_op jit(solution)/shard_map/all_gather | solution.py:35
  82.8 6.0 %fusion.4 = (bf16[640,1728]{0,1:T(8,128)(2,1)}, f32[640,1728]{0,1:T(8,128)}) fusion(f32[640,1728]{0,1:T(8,128)} %param.11, bf16[256,1728]{1,0:T(8,128)(2,1)S(1)} %all_gather.10, bf16[5120,256]{1,0:T(8,128)(2,1)S(1)} %copy-done, s32[]{:T(128)S(6)} %select_n.3), kind=kOutput, calls=%fused_computation.9 | convolution fusion | flops 569548800 | bytes 12304388 | tf_op jit(solution)/shard_map/dot_general | solution.py:37
  88.8 0.0 all-gather.2.cloned.1.call-update
  88.8 93.7 %all-gather.2.cloned.1.call-done = bf16[5120,1728]{0,1:T(8,128)(2,1)} async-done(((bf16[640,1728]{0,1:T(8,128)(2,1)}), bf16[5120,1728]{0,1:T(8,128)(2,1)}) %all-gather.2.cloned.1.call-update) | async-done | bytes 17694736 | tf_op jit(solution)/shard_map/all_gather | solution.py:41
  182.5 15.7 %copy.25 = bf16[5120,1728]{0,1:T(8,128)(2,1)} copy(bf16[5120,1728]{0,1:T(8,128)(2,1)} %all-gather.2.cloned.1.call-done) | data formatting | bytes 35389440
Async XLA Ops:
  7.2 1.7 copy-start
  7.2 63.0 %reduce-scatter.4.cloned.1.call-start = ((), (), s32[]{:S(2)}) async-start(), calls=%async_computation.2 | async-start | bytes 2064384 | tf_op jit(solution)/shard_map/reduce_scatter | solution.py:23
  8.9 17.6 %copy-start.1 = (bf16[512,1728]{0,1:T(8,128)(2,1)S(1)}, bf16[512,1728]{0,1:T(8,128)(2,1)}, u32[]{:S(2)}) copy-start(bf16[512,1728]{0,1:T(8,128)(2,1)} %param.7) | copy-start | bytes 5308420
  28.8 153.7 %all-gather.2.cloned.1.call-start = ((), (), s32[]{:S(2)}) async-start(), calls=%async_computation.1 | async-start | bytes 19906560 | tf_op jit(solution)/shard_map/all_gather | solution.py:41
Sparse Core Ops, SparseCore 0:
  28.9 41.2 reduce-scatter.3
  88.9 93.5 all-gather.1
where the time goes:
time: 205 us
  waiting for transfers between devices  135 us (66%)
  blocking collectives  26.2 us (13%)
  local copies, waits for them, and re-layouts  19 us (9%)
  between operations  14.1 us (7%)
  matrix products  8.57 us (4%)
  other arithmetic  2.05 us (1%)
    all_gather x1, waiting for transfers between devices, body(): lax.all_gather(master_new.astype(jnp.bfloat16), 'dp', axis=0, tiled=True)  93.7 us
    reduce_scatter x1, waiting for transfers between devices, body(): lax.psum_scatter(partial_value.astype(jnp.float32), 'dp', scatter_dimensi...  41.3 us
    unnamed x6, local copies, waits for them, and re-layouts  19 us
    all_gather x1, blocking collectives, body(): group_proj = lax.all_gather(projected, 'fsdp', axis=0, tiled=True)  15.6 us
    all_gather x1, blocking collectives, body(): piece = lax.all_gather(update, 'dp', axis=0, tiled=True)  10.6 us
    dot_general x1, matrix products, body(): jnp.dot(left_cols, piece, preferred_element_type=jnp.float32)  5.99 us
  transfers between devices with their start and end apart: 2, of which 2 were waited for; matrix products, arithmetic and copies ran while one was open for 0% of the time, Pallas kernels for 0%

commit v1 on v0

v1 whole, which is shorter than its diff:
```python
import functools

import jax
import jax.numpy as jnp
from jax import lax
from jax.experimental import pallas as pl
from jax.experimental.pallas import tpu as pltpu
from jax.sharding import PartitionSpec as P

STEP = 1000


BETA_ONE = 0.9
BETA_TWO = 0.999
ADAM_EPS = 1e-08
LEARN_RATE = 0.01
CORRECT_ONE = 1.0 - BETA_ONE**STEP
CORRECT_TWO = 1.0 - BETA_TWO**STEP

VMEM = pl.BlockSpec(memory_space=pltpu.VMEM)
SMEM = pl.BlockSpec(memory_space=pltpu.SMEM)
ANY = pl.BlockSpec(memory_space=pl.ANY)


def adam(grad, moment_one, moment_two):
    moment_one_new = BETA_ONE * moment_one + (1.0 - BETA_ONE) * grad
    moment_two_new = BETA_TWO * moment_two + (1.0 - BETA_TWO) * grad * grad
    update = (
        moment_one_new / CORRECT_ONE / (jnp.sqrt(moment_two_new / CORRECT_TWO) + ADAM_EPS)
    ).astype(jnp.bfloat16)
    return moment_one_new, moment_two_new, update


def plain_body(acts, grad_out, projection, moment_one, moment_two, master):
    projected = jnp.dot(acts, projection, preferred_element_type=jnp.float32).astype(jnp.bfloat16)
    group_proj = lax.all_gather(projected, "fsdp", axis=0, tiled=True)
    partial_value = jnp.einsum(
        "tr,tc->rc", group_proj, grad_out, preferred_element_type=jnp.float32
    )
    partial_value = lax.optimization_barrier(partial_value.astype(jnp.bfloat16))
    grad = lax.psum_scatter(
        partial_value.astype(jnp.float32), "dp", scatter_dimension=0, tiled=True
    )
    moment_one_new, moment_two_new, update = adam(grad, moment_one, moment_two)
    slab_rows = master.shape[0]
    proj_slab = lax.dynamic_slice_in_dim(projection, lax.axis_index("dp") * slab_rows, slab_rows, 0)
    piece = lax.all_gather(update, "dp", axis=0, tiled=True)
    expanded = jnp.dot(proj_slab, piece, preferred_element_type=jnp.float32)
    master_new = master - LEARN_RATE * expanded
    weight_cols = lax.all_gather(master_new.astype(jnp.bfloat16), "dp", axis=0, tiled=True)
    return (moment_one_new, moment_two_new, master_new, weight_cols)


def send(value, axis, size, mask):
    return lax.ppermute(value, axis, [(i, i ^ mask) for i in range(size)])


def partial_kernel(place, grad_t, *refs, n_fsdp, n_dp):
    pieces, outs, (tokens, result) = refs[:n_fsdp], refs[n_fsdp : n_fsdp + n_dp], refs[n_fsdp + n_dp :]
    count = pieces[0].shape[0]
    rows = outs[0].shape[0]
    for k in range(n_fsdp):
        tokens[pl.ds(pl.multiple_of((place[1] ^ k) * count, count), count), :] = pieces[k][...]
    result[...] = lax.dot_general(
        tokens[...].T, grad_t[...], (((1,), (1,)), ((), ())), preferred_element_type=jnp.float32
    ).astype(jnp.bfloat16)
    for k in range(n_dp):
        outs[k][...] = result[pl.ds(pl.multiple_of((place[0] ^ k) * rows, rows), rows), :]


def adam_kernel(moment_one, moment_two, *refs, n_dp):
    pieces, (one_new, two_new, update) = refs[:n_dp], refs[n_dp:]
    grad = pieces[0][...].astype(jnp.float32)
    for k in range(1, n_dp):
        grad = grad + pieces[k][...].astype(jnp.float32)
    one, two, value = adam(grad, moment_one[...], moment_two[...])
    one_new[...] = one
    two_new[...] = two
    cols = value.shape[1]
    update[...] = jnp.zeros_like(update)
    update[:, :cols] = value


def gather_update(place, pieces, wide, tall):
    rows = pieces[0].shape[0]
    for k, piece in enumerate(pieces):
        wide[pl.ds(pl.multiple_of((place[0] ^ k) * rows, rows), rows), :] = piece[...]
    tall[...] = wide[...].T


def expand(tall, slab, first, count):
    return lax.dot_general(
        tall[pl.ds(first, count), :], slab[...], (((1,), (1,)), ((), ())),
        preferred_element_type=jnp.float32,
    )


def weight_kernel(place, slab, master_t, *refs, n_dp, block):
    pieces, weight, (wide, tall) = refs[:n_dp], refs[n_dp], refs[n_dp + 1 :]
    step = pl.program_id(0)

    @pl.when(step == 0)
    def _():
        gather_update(place, pieces, wide, tall)

    first = pl.multiple_of(step * block, block)
    master_new = master_t[...] - LEARN_RATE * expand(tall, slab, first, block)
    weight[...] = master_new.astype(jnp.bfloat16)


def master_kernel(place, slab, master_t, *refs, n_dp, block):
    pieces, out, (wide, tall) = refs[:n_dp], refs[n_dp], refs[n_dp + 1 :]
    step = pl.program_id(0)

    @pl.when(step == 0)
    def _():
        gather_update(place, pieces, wide, tall)

    first = pl.multiple_of(step * block, block)
    out[...] = master_t[...] - LEARN_RATE * expand(tall, slab, first, block)


def expand_call(kernel, dtype, place, projection, master_t, pieces, block):
    cols, slab_rows = master_t.shape
    rank = projection.shape[1]
    wide = pieces[0].shape[1]
    n_dp = len(pieces)
    whole = pl.BlockSpec(pieces[0].shape, lambda i, s: (0, 0))
    return pl.pallas_call(
        functools.partial(kernel, n_dp=n_dp, block=block),
        out_shape=jax.ShapeDtypeStruct((cols, slab_rows), dtype),
        grid_spec=pltpu.PrefetchScalarGridSpec(
            num_scalar_prefetch=1,
            grid=(cols // block,),
            in_specs=[
                pl.BlockSpec((slab_rows, rank), lambda i, s: (s[0], 0)),
                pl.BlockSpec((block, slab_rows), lambda i, s: (i, 0)),
            ]
            + [whole] * n_dp,
            out_specs=pl.BlockSpec((block, slab_rows), lambda i, s: (i, 0)),
            scratch_shapes=[
                pltpu.VMEM((rank, wide), jnp.bfloat16),
                pltpu.VMEM((wide, rank), jnp.bfloat16),
            ],
        ),
        compiler_params=pltpu.CompilerParams(vmem_limit_bytes=32 * 2**20),
        cost_estimate=pl.CostEstimate(
            flops=2 * cols * slab_rows * rank, bytes_accessed=8 * cols * slab_rows, transcendentals=0
        ),
    )(place, projection, master_t, *pieces)


def lay_kernel(place, *refs, spots, fresh):
    refs = refs if fresh else refs[1:]
    pieces, out, sems = refs[: len(spots)], refs[len(spots)], refs[len(spots) + 1]
    copies = []
    for at, ((mask, first), piece) in enumerate(zip(spots, pieces)):
        count, width = piece.shape
        column = pl.multiple_of((place[0] ^ mask) * width, 128)
        copies.append(
            pltpu.make_async_copy(
                piece, out.at[pl.ds(first, count), pl.ds(column, width)], sems.at[at]
            )
        )
    for copy in copies:
        copy.start()
    for copy in copies:
        copy.wait()


def lay(place, out, shape, spots, pieces):
    fresh = out is None
    held = [] if fresh else [out]
    size = sum(2 * 2 * piece.size for piece in pieces)
    return pl.pallas_call(
        functools.partial(lay_kernel, spots=spots, fresh=fresh),
        out_shape=jax.ShapeDtypeStruct(shape, jnp.bfloat16),
        in_specs=[SMEM] + [ANY] * (len(held) + len(pieces)),
        out_specs=ANY,
        scratch_shapes=[pltpu.SemaphoreType.DMA((len(spots),))],
        input_output_aliases={} if fresh else {1: 0},
        cost_estimate=pl.CostEstimate(flops=0, bytes_accessed=size, transcendentals=0),
    )(place, *held, *pieces)


def kernel_body(acts, grad_out, projection, moment_one, moment_two, master, n_dp, n_fsdp):
    cols = grad_out.shape[1]
    rank = projection.shape[1]
    rows = moment_one.shape[0]
    slab_rows = master.shape[0]
    wide = -(-cols // 128) * 128
    place = jnp.stack([lax.axis_index("dp"), lax.axis_index("fsdp")]).astype(jnp.int32)
    master_t = master.T

    projected = jnp.dot(acts, projection, preferred_element_type=jnp.float32).astype(jnp.bfloat16)
    tokens = [projected] + [send(projected, "fsdp", n_fsdp, k) for k in range(1, n_fsdp)]
    parts = pl.pallas_call(
        functools.partial(partial_kernel, n_fsdp=n_fsdp, n_dp=n_dp),
        out_shape=[jax.ShapeDtypeStruct((rows, cols), jnp.bfloat16)] * n_dp,
        in_specs=[SMEM] + [VMEM] * (1 + n_fsdp),
        out_specs=[VMEM] * n_dp,
        scratch_shapes=[
            pltpu.VMEM((n_fsdp * projected.shape[0], rank), jnp.bfloat16),
            pltpu.VMEM((rank, cols), jnp.bfloat16),
        ],
        compiler_params=pltpu.CompilerParams(vmem_limit_bytes=32 * 2**20),
    )(place, grad_out.T, *tokens)
    parts = [parts[0]] + [send(parts[k], "dp", n_dp, k) for k in range(1, n_dp)]
    moment_one_new, moment_two_new, update = pl.pallas_call(
        functools.partial(adam_kernel, n_dp=n_dp),
        out_shape=[
            jax.ShapeDtypeStruct(moment_one.shape, jnp.float32),
            jax.ShapeDtypeStruct(moment_two.shape, jnp.float32),
            jax.ShapeDtypeStruct((rows, wide), jnp.bfloat16),
        ],
        in_specs=[VMEM] * (2 + n_dp),
        out_specs=[VMEM] * 3,
        compiler_params=pltpu.CompilerParams(vmem_limit_bytes=32 * 2**20),
    )(moment_one, moment_two, *parts)
    updates = [update] + [send(update, "dp", n_dp, k) for k in range(1, n_dp)]

    half = cols // 2
    weight = expand_call(weight_kernel, jnp.bfloat16, place, projection, master_t, updates, cols // 4)
    shape = (cols, n_dp * slab_rows)
    one, two = weight[:half], weight[half:]
    one_x, two_y = send(one, "dp", n_dp, 2), send(two, "dp", n_dp, 4)
    two_x, one_y = send(two, "dp", n_dp, 2), send(one, "dp", n_dp, 4)
    weight_c = send(weight, "dp", n_dp, 1)
    out = lay(place, None, shape, ((0, 0),), (weight,))
    one_xy, two_yx = send(one_x, "dp", n_dp, 4), send(two_y, "dp", n_dp, 2)
    one_xc, two_yc = send(one_x, "dp", n_dp, 1), send(two_y, "dp", n_dp, 1)
    master_new = expand_call(master_kernel, jnp.float32, place, projection, master_t, updates, cols // 4)
    out = lay(place, out, shape, ((2, 0), (4, half), (1, 0)), (one_x, two_y, weight_c))
    two_xc, one_yc = send(two_x, "dp", n_dp, 1), send(one_y, "dp", n_dp, 1)
    out = lay(
        place, out, shape, ((2, half), (4, 0), (3, 0), (5, half)), (two_x, one_y, one_xc, two_yc)
    )
    one_xyc, two_yxc = send(one_xy, "dp", n_dp, 1), send(two_yx, "dp", n_dp, 1)
    out = lay(place, out, shape, ((6, 0), (6, half), (3, half), (5, 0)), (one_xy, two_yx, two_xc, one_yc))
    out = lay(place, out, shape, ((7, 0), (7, half)), (one_xyc, two_yxc))
    return (moment_one_new, moment_two_new, master_new.T, out.T)


def solution(mesh):
    n_dp, n_fsdp = mesh.shape["dp"], mesh.shape["fsdp"]

    def body(acts, grad_out, projection, moment_one, moment_two, master):
        args = (acts, grad_out, projection, moment_one, moment_two, master)
        fits = n_dp == 8 and n_fsdp == 4 and moment_one.shape[0] % 32 == 0 and master.shape[0] % 128 == 0
        if fits and grad_out.shape[1] % 64 == 0 and acts.shape[0] % 128 == 0:
            return kernel_body(*args, n_dp, n_fsdp)
        return plain_body(*args)

    in_specs = (
        P(("dp", "fsdp"), None),
        P("dp", "fsdp"),
        P(),
        P("dp", "fsdp"),
        P("dp", "fsdp"),
        P("dp", "fsdp"),
    )
    out_specs = (P("dp", "fsdp"), P("dp", "fsdp"), P("dp", "fsdp"), P(None, "fsdp"))
    return jax.shard_map(body, mesh=mesh, in_specs=in_specs, out_specs=out_specs, check_vma=False)
```

time: 205 us -> 694 us (3.39)
  Pallas kernels: 0 us -> 554 us
  waiting for transfers between devices: 135 us -> 88.1 us
  starting transfers between devices: 0.08 us -> 27.8 us
  blocking collectives: 26.2 us -> 0 us
  between operations: 14.1 us -> 0.97 us
    pallas_call x0 -> x9, Pallas kernels: none -> 554 us  [the longest x5 545 us: lay(): pl.pallas_call(functools.partial(lay_kernel, spots=spots, fresh=fresh), o...]
    all_gather x1 -> x0, waiting for transfers between devices: 93.7 us -> none  [body(): lax.all_gather(master_new.astype(jnp.bfloat16), 'dp', axis=0, tiled=True)]
    ppermute x0 -> x30, waiting for transfers between devices: none -> 88.1 us  [send(): return lax.ppermute(value, axis, [(i, i ^ mask) for i in range(size)])]
    reduce_scatter x1 -> x0, waiting for transfers between devices: 41.3 us -> none  [body(): lax.psum_scatter(partial_value.astype(jnp.float32), 'dp', scatter_dimensi...]
    ppermute x0 -> x30, starting transfers between devices: none -> 27.8 us  [send(): return lax.ppermute(value, axis, [(i, i ^ mask) for i in range(size)])]
    all_gather x2 -> x0, blocking collectives: 26.2 us -> none  [the longest x1 15.6 us: body(): group_proj = lax.all_gather(projected, 'fsdp', axis=0, tiled=True)]
    unnamed x6 -> x64, local copies, waits for them, and re-layouts: 19 us -> 19.4 us
  transfers between devices with their start and end apart: 2 -> 30, of which waited for: 2 -> 14; matrix products, arithmetic and copies ran while one was open for 0% -> 0% of each run, Pallas kernels for 0% -> 69%
where the time goes in v1:
time: 694 us; the launch traced here: 693 us
  Pallas kernels  554 us (80%)
  waiting for transfers between devices  88.1 us (13%)
  starting transfers between devices  27.8 us (4%)
  local copies, waits for them, and re-layouts  19.6 us (3%)
    pallas_call x5, Pallas kernels, lay(): pl.pallas_call(functools.partial(lay_kernel, spots=spots, fresh=fresh), o...  545 us
    ppermute x30, waiting for transfers between devices, send(): return lax.ppermute(value, axis, [(i, i ^ mask) for i in range(size)])  88.1 us
    ppermute x30, starting transfers between devices, send(): return lax.ppermute(value, axis, [(i, i ^ mask) for i in range(size)])  27.8 us
    unnamed x64, local copies, waits for them, and re-layouts  19.4 us
  transfers between devices with their start and end apart: 30, of which 14 were waited for; matrix products, arithmetic and copies ran while one was open for 0% of the time, Pallas kernels for 69%

profile of v1, /device:TPU:0, one launch (start us, length us, event | category | flops | bytes accessed | tf_op | source)
XLA Modules:
  0.0 693.0 jit_solution(8422661273233810388)
XLA Ops:
  2.0 2.2 convolution_convert_fusion.refs_0_
  4.2 3.1 collective-permute-start
  7.3 2.6 collective-permute-start.1
  10.0 4.6 collective-permute-done.1.refs_2_
  16.1 1.8 shard_map.93
  21.5 2.4 collective-permute-start.8
  25.8 6.2 collective-permute-done.7.refs_5_
  36.8 2.5 collective-permute-start.15
  40.9 6.7 collective-permute-done.14.refs_5_
  47.6 2.3 copy-done.4
  50.0 2.5 shard_map.96.refs_0_
  58.1 23.2 %collective-permute-done.17.refs_1_ = bf16[864,640]{1,0:T(8,128)(2,1)S(1)} collective-permute-done((bf16[864,640]{1,0:T(8,128)(2,1)S(1)}, bf16[864,640]{1,0:T(8,128)(2,1)S(1)}, u32[]{:S(2)}, u32[]{:S(2)}) %collective-permute-start.17) | collective-permute-done | bytes 1105952 | tf_op jit(solution)/shard_map/ppermute | solution.py:55
  81.2 1.6 collective-permute-done.18.refs_2_
  84.4 20.1 %collective-permute-done.20.refs_1_ = bf16[864,640]{1,0:T(8,128)(2,1)} collective-permute-done((bf16[864,640]{1,0:T(8,128)(2,1)S(1)}, bf16[864,640]{1,0:T(8,128)(2,1)}, u32[]{:S(2)}, u32[]{:S(2)}) %collective-permute-start.20) | collective-permute-done | bytes 1105952 | tf_op jit(solution)/shard_map/ppermute | solution.py:55
  104.5 1.6 collective-permute-start.25
  108.5 20.9 %collective-permute-done.24.refs_1_ = bf16[864,640]{1,0:T(8,128)(2,1)} collective-permute-done((bf16[864,640]{1,0:T(8,128)(2,1)S(1)}, bf16[864,640]{1,0:T(8,128)(2,1)}, u32[]{:S(2)}, u32[]{:S(2)}) %collective-permute-start.24) | collective-permute-done | bytes 1105952 | tf_op jit(solution)/shard_map/ppermute | solution.py:55
  130.6 68.8 %shard_map.97.refs_0_ = bf16[1728,5120]{1,0:T(8,128)(2,1)} custom-call(s32[2]{0:T(128)} %copy-done.25, bf16[1728,640]{1,0:T(8,128)(2,1)} %copy-done.3), custom_call_target="tpu_custom_call" | custom-call | bytes 4423680 | tf_op jit(solution)/shard_map/pallas_call | solution.py:175
  199.4 1.7 copy-done.2
  201.2 2.3 copy-done.5
  210.6 4.0 shard_map.95
  214.7 135.8 %shard_map.98.refs_0_ = bf16[1728,5120]{1,0:T(8,128)(2,1)} custom-call(s32[2]{0:T(128)} %copy-done.25, bf16[1728,5120]{1,0:T(8,128)(2,1)} %shard_map.97.refs_0_, bf16[864,640]{1,0:T(8,128)(2,1)} %copy-done.28, bf16[864,640]{1,0:T(8,128)(2,1)} %collective-permute-done.18.refs_2_, bf16[1728,640]{1,0:T(8,128)(2,1)} %copy-done.27), custom_call_target="tpu_custom_call", output_to_operand_aliasing={{}: (1, {})} | custom-call | bytes 8847360 | tf_op jit(solution)/shard_map/pallas_call | solution.py:175
  350.5 135.8 %shard_map.99.refs_0_ = bf16[1728,5120]{1,0:T(8,128)(2,1)} custom-call(s32[2]{0:T(128)} %copy-done.25, bf16[1728,5120]{1,0:T(8,128)(2,1)} %shard_map.98.refs_0_, bf16[864,640]{1,0:T(8,128)(2,1)} %collective-permute-done.20.refs_1_, bf16[864,640]{1,0:T(8,128)(2,1)} %collective-permute-done.21.refs_2_, ...), custom_call_target="tpu_custom_call", output_to_operand_aliasing={{}: (1, {})} | custom-call | bytes 8847360 | tf_op jit(solution)/shard_map/pallas_call | solution.py:175
  487.3 135.8 %shard_map.100.refs_0_ = bf16[1728,5120]{1,0:T(8,128)(2,1)} custom-call(s32[2]{0:T(128)} %copy-done.25, bf16[1728,5120]{1,0:T(8,128)(2,1)} %shard_map.99.refs_0_, bf16[864,640]{1,0:T(8,128)(2,1)} %collective-permute-done.24.refs_1_, bf16[864,640]{1,0:T(8,128)(2,1)} %collective-permute-done.25.refs_2_, ...), custom_call_target="tpu_custom_call", output_to_operand_aliasing={{}: (1, {})} | custom-call | bytes 8847360 | tf_op jit(solution)/shard_map/pallas_call | solution.py:175
  624.2 68.8 %shard_map.101 = bf16[1728,5120]{1,0:T(8,128)(2,1)} custom-call(s32[2]{0:T(128)} %copy-done.25, bf16[1728,5120]{1,0:T(8,128)(2,1)} %shard_map.100.refs_0_, bf16[864,640]{1,0:T(8,128)(2,1)} %copy-done.31, bf16[864,640]{1,0:T(8,128)(2,1)} %collective-permute-done.29.refs_2_), custom_call_target="tpu_custom_call", output_to_operand_aliasing={{}: (1, {})} | custom-call | bytes 4423680 | tf_op jit(solution)/shard_map/pallas_call | solution.py:175
  (112 shorter events, 34.6 us)
Async XLA Ops:
  7.3 7.3 %collective-permute-start.1 = (bf16[128,256]{1,0:T(8,128)(2,1)S(1)}, bf16[128,256]{1,0:T(8,128)(2,1)S(1)}, u32[]{:S(2)}, u32[]{:S(2)}) collective-permute-start(bf16[128,256]{1,0:T(8,128)(2,1)S(1)} %convolution_convert_fusion.refs_0_), channel_id=1, source_target_pairs={{0,2},{1,3},{2,0},{3,1},{4,6},{5,7},{6,4},{7,5},{8,10},{9,11},{10,... | collective-permute-start | bytes 196616 | tf_op jit(solution)/shard_map/ppermute | solution.py:55
  9.9 6.2 collective-permute-start.2
  17.9 6.0 collective-permute-start.4
  19.5 6.0 collective-permute-start.5
  21.3 10.7 %collective-permute-start.7 = (bf16[32,1728]{1,0:T(8,128)(2,1)S(1)}, bf16[32,1728]{1,0:T(8,128)(2,1)S(1)}, u32[]{:S(2)}, u32[]{:S(2)}) collective-permute-start(bf16[32,1728]{1,0:T(8,128)(2,1)S(1)} %get-tuple-element.20), channel_id=1, source_target_pairs={{0,20},{4,16},{8,28},{12,24},{16,4},{20,0},{24,12},{28,8},{1,21},{... | collective-permute-start | bytes 331784 | tf_op jit(solution)/shard_map/ppermute | solution.py:55
  21.5 10.5 %collective-permute-start.8 = (bf16[32,1728]{1,0:T(8,128)(2,1)S(1)}, bf16[32,1728]{1,0:T(8,128)(2,1)S(1)}, u32[]{:S(2)}, u32[]{:S(2)}) collective-permute-start(bf16[32,1728]{1,0:T(8,128)(2,1)S(1)} %get-tuple-element.21), channel_id=1, source_target_pairs={{0,24},{4,28},{8,16},{12,20},{16,8},{20,12},{24,0},{28,4},{1,25},{... | collective-permute-start | bytes 331784 | tf_op jit(solution)/shard_map/ppermute | solution.py:55
  23.9 8.1 %collective-permute-start.9 = (bf16[32,1728]{1,0:T(8,128)(2,1)S(1)}, bf16[32,1728]{1,0:T(8,128)(2,1)S(1)}, u32[]{:S(2)}, u32[]{:S(2)}) collective-permute-start(bf16[32,1728]{1,0:T(8,128)(2,1)S(1)} %get-tuple-element.22), channel_id=1, source_target_pairs={{0,28},{4,24},{8,20},{12,16},{16,12},{20,8},{24,4},{28,0},{1,29},{... | collective-permute-start | bytes 331784 | tf_op jit(solution)/shard_map/ppermute | solution.py:55
  34.8 6.0 collective-permute-start.13
  36.4 11.2 %collective-permute-start.14 = (bf16[32,1792]{1,0:T(8,128)(2,1)S(1)}, bf16[32,1792]{1,0:T(8,128)(2,1)S(1)}, u32[]{:S(2)}, u32[]{:S(2)}) collective-permute-start(bf16[32,1792]{1,0:T(8,128)(2,1)S(1)} %get-tuple-element.25.refs_0_), channel_id=1, source_target_pairs={{0,20},{4,16},{8,28},{12,24},{16,4},{20,0},{24,12},{28,8},{1,21},{... | collective-permute-start | bytes 344072 | tf_op jit(solution)/shard_map/ppermute | solution.py:55
  36.8 10.7 %collective-permute-start.15 = (bf16[32,1792]{1,0:T(8,128)(2,1)S(1)}, bf16[32,1792]{1,0:T(8,128)(2,1)S(1)}, u32[]{:S(2)}, u32[]{:S(2)}) collective-permute-start(bf16[32,1792]{1,0:T(8,128)(2,1)S(1)} %get-tuple-element.25.refs_0_), channel_id=1, source_target_pairs={{0,24},{4,28},{8,16},{12,20},{16,8},{20,12},{24,0},{28,4},{1,25},{... | collective-permute-start | bytes 344072 | tf_op jit(solution)/shard_map/ppermute | solution.py:55
  39.3 8.2 %collective-permute-start.16 = (bf16[32,1792]{1,0:T(8,128)(2,1)S(1)}, bf16[32,1792]{1,0:T(8,128)(2,1)S(1)}, u32[]{:S(2)}, u32[]{:S(2)}) collective-permute-start(bf16[32,1792]{1,0:T(8,128)(2,1)S(1)} %get-tuple-element.25.refs_0_), channel_id=1, source_target_pairs={{0,28},{4,24},{8,20},{12,16},{16,12},{20,8},{24,4},{28,0},{1,29},{... | collective-permute-start | bytes 344072 | tf_op jit(solution)/shard_map/ppermute | solution.py:55
  53.9 52.7 %collective-permute-start.19 = (bf16[1728,640]{1,0:T(8,128)(2,1)S(1)}, bf16[1728,640]{1,0:T(8,128)(2,1)S(1)}, u32[]{:S(2)}, u32[]{:S(2)}) collective-permute-start(bf16[1728,640]{1,0:T(8,128)(2,1)S(1)} %shard_map.96.refs_0_), channel_id=1, source_target_pairs={{0,4},{4,0},{8,12},{12,8},{16,20},{20,16},{24,28},{28,24},{1,5},{5... | collective-permute-start | bytes 6635528 | tf_op jit(solution)/shard_map/ppermute | solution.py:55
  54.0 27.2 %collective-permute-start.17 = (bf16[864,640]{1,0:T(8,128)(2,1)S(1)}, bf16[864,640]{1,0:T(8,128)(2,1)S(1)}, u32[]{:S(2)}, u32[]{:S(2)}) collective-permute-start(bf16[864,640]{1,0:T(8,128)(2,1)S(1)} %get-tuple-element.27), channel_id=1, source_target_pairs={{0,8},{4,12},{8,0},{12,4},{16,24},{20,28},{24,16},{28,20},{1,9},{5... | collective-permute-start | bytes 3317768 | tf_op jit(solution)/shard_map/ppermute | solution.py:55
  55.5 27.3 %collective-permute-start.18 = (bf16[864,640]{1,0:T(8,128)(2,1)S(1)}, bf16[864,640]{1,0:T(8,128)(2,1)}, u32[]{:S(2)}, u32[]{:S(2)}) collective-permute-start(bf16[864,640]{1,0:T(8,128)(2,1)S(1)} %get-tuple-element.26), channel_id=1, source_target_pairs={{0,16},{4,20},{8,24},{12,28},{16,0},{20,4},{24,8},{28,12},{1,17},{... | collective-permute-start | bytes 3317768 | tf_op jit(solution)/shard_map/ppermute | solution.py:55
  57.1 47.4 %collective-permute-start.20 = (bf16[864,640]{1,0:T(8,128)(2,1)S(1)}, bf16[864,640]{1,0:T(8,128)(2,1)}, u32[]{:S(2)}, u32[]{:S(2)}) collective-permute-start(bf16[864,640]{1,0:T(8,128)(2,1)S(1)} %get-tuple-element.26), channel_id=1, source_target_pairs={{0,8},{4,12},{8,0},{12,4},{16,24},{20,28},{24,16},{28,20},{1,9},{5... | collective-permute-start | bytes 3317768 | tf_op jit(solution)/shard_map/ppermute | solution.py:55
  57.6 49.0 %collective-permute-start.21 = (bf16[864,640]{1,0:T(8,128)(2,1)S(1)}, bf16[864,640]{1,0:T(8,128)(2,1)}, u32[]{:S(2)}, u32[]{:S(2)}) collective-permute-start(bf16[864,640]{1,0:T(8,128)(2,1)S(1)} %get-tuple-element.27), channel_id=1, source_target_pairs={{0,16},{4,20},{8,24},{12,28},{16,0},{20,4},{24,8},{28,12},{1,17},{... | collective-permute-start | bytes 3317768 | tf_op jit(solution)/shard_map/ppermute | solution.py:55
  81.2 27.2 %collective-permute-start.22 = (bf16[864,640]{1,0:T(8,128)(2,1)S(1)}, bf16[864,640]{1,0:T(8,128)(2,1)S(1)}, u32[]{:S(2)}, u32[]{:S(2)}) collective-permute-start(bf16[864,640]{1,0:T(8,128)(2,1)S(1)} %collective-permute-done.17.refs_1_), channel_id=1, source_target_pairs={{0,4},{4,0},{8,12},{12,8},{16,20},{20,16},{24,28},{28,24},{1,5},{5... | collective-permute-start | bytes 3317768 | tf_op jit(solution)/shard_map/ppermute | solution.py:55
  82.9 46.6 %collective-permute-start.24 = (bf16[864,640]{1,0:T(8,128)(2,1)S(1)}, bf16[864,640]{1,0:T(8,128)(2,1)}, u32[]{:S(2)}, u32[]{:S(2)}) collective-permute-start(bf16[864,640]{1,0:T(8,128)(2,1)S(1)} %collective-permute-done.17.refs_1_), channel_id=1, source_target_pairs={{0,16},{4,20},{8,24},{12,28},{16,0},{20,4},{24,8},{28,12},{1,17},{... | collective-permute-start | bytes 3317768 | tf_op jit(solution)/shard_map/ppermute | solution.py:55
  104.5 26.2 %collective-permute-start.25 = (bf16[864,640]{1,0:T(8,128)(2,1)}, bf16[864,640]{1,0:T(8,128)(2,1)}, u32[]{:S(2)}, u32[]{:S(2)}) collective-permute-start(bf16[864,640]{1,0:T(8,128)(2,1)} %collective-permute-done.18.refs_2_), channel_id=1, source_target_pairs={{0,8},{4,12},{8,0},{12,4},{16,24},{20,28},{24,16},{28,20},{1,9},{5... | collective-permute-start | bytes 3317768 | tf_op jit(solution)/shard_map/ppermute | solution.py:55
  106.6 243.9 %collective-permute-start.23 = (bf16[864,640]{1,0:T(8,128)(2,1)}, bf16[864,640]{1,0:T(8,128)(2,1)}, u32[]{:S(2)}, u32[]{:S(2)}) collective-permute-start(bf16[864,640]{1,0:T(8,128)(2,1)} %collective-permute-done.18.refs_2_), channel_id=1, source_target_pairs={{0,4},{4,0},{8,12},{12,8},{16,20},{20,16},{24,28},{28,24},{1,5},{5... | collective-permute-start | bytes 3317768 | tf_op jit(solution)/shard_map/ppermute | solution.py:55
  108.0 378.4 %collective-permute-start.26 = (bf16[864,640]{1,0:T(8,128)(2,1)}, bf16[864,640]{1,0:T(8,128)(2,1)S(1)}, u32[]{:S(2)}, u32[]{:S(2)}) collective-permute-start(bf16[864,640]{1,0:T(8,128)(2,1)} %collective-permute-done.20.refs_1_), channel_id=1, source_target_pairs={{0,4},{4,0},{8,12},{12,8},{16,20},{20,16},{24,28},{28,24},{1,5},{5... | collective-permute-start | bytes 3317768 | tf_op jit(solution)/shard_map/ppermute | solution.py:55
  108.5 377.9 %collective-permute-start.27 = (bf16[864,640]{1,0:T(8,128)(2,1)}, bf16[864,640]{1,0:T(8,128)(2,1)}, u32[]{:S(2)}, u32[]{:S(2)}) collective-permute-start(bf16[864,640]{1,0:T(8,128)(2,1)} %collective-permute-done.21.refs_2_), channel_id=1, source_target_pairs={{0,4},{4,0},{8,12},{12,8},{16,20},{20,16},{24,28},{28,24},{1,5},{5... | collective-permute-start | bytes 3317768 | tf_op jit(solution)/shard_map/ppermute | solution.py:55
  129.5 493.7 %collective-permute-start.28 = (bf16[864,640]{1,0:T(8,128)(2,1)}, bf16[864,640]{1,0:T(8,128)(2,1)S(1)}, u32[]{:S(2)}, u32[]{:S(2)}) collective-permute-start(bf16[864,640]{1,0:T(8,128)(2,1)} %collective-permute-done.24.refs_1_), channel_id=1, source_target_pairs={{0,4},{4,0},{8,12},{12,8},{16,20},{20,16},{24,28},{28,24},{1,5},{5... | collective-permute-start | bytes 3317768 | tf_op jit(solution)/shard_map/ppermute | solution.py:55
  130.6 492.5 %collective-permute-start.29 = (bf16[864,640]{1,0:T(8,128)(2,1)}, bf16[864,640]{1,0:T(8,128)(2,1)}, u32[]{:S(2)}, u32[]{:S(2)}) collective-permute-start(bf16[864,640]{1,0:T(8,128)(2,1)} %collective-permute-done.25.refs_2_), channel_id=1, source_target_pairs={{0,4},{4,0},{8,12},{12,8},{16,20},{20,16},{24,28},{28,24},{1,5},{5... | collective-permute-start | bytes 3317768 | tf_op jit(solution)/shard_map/ppermute | solution.py:55
  (38 other events, 463.7 us)

commit v2 on v1

v2 whole, which is shorter than its diff:
```python
import functools

import jax
import jax.numpy as jnp
from jax import lax
from jax.experimental import pallas as pl
from jax.experimental.pallas import tpu as pltpu
from jax.sharding import PartitionSpec as P

STEP = 1000


BETA_ONE = 0.9
BETA_TWO = 0.999
ADAM_EPS = 1e-08
LEARN_RATE = 0.01
CORRECT_ONE = 1.0 - BETA_ONE**STEP
CORRECT_TWO = 1.0 - BETA_TWO**STEP

VMEM = pl.BlockSpec(memory_space=pltpu.VMEM)
SMEM = pl.BlockSpec(memory_space=pltpu.SMEM)
ANY = pl.BlockSpec(memory_space=pl.ANY)


def adam(grad, moment_one, moment_two):
    moment_one_new = BETA_ONE * moment_one + (1.0 - BETA_ONE) * grad
    moment_two_new = BETA_TWO * moment_two + (1.0 - BETA_TWO) * grad * grad
    update = (
        moment_one_new / CORRECT_ONE / (jnp.sqrt(moment_two_new / CORRECT_TWO) + ADAM_EPS)
    ).astype(jnp.bfloat16)
    return moment_one_new, moment_two_new, update


def plain_body(acts, grad_out, projection, moment_one, moment_two, master):
    projected = jnp.dot(acts, projection, preferred_element_type=jnp.float32).astype(jnp.bfloat16)
    group_proj = lax.all_gather(projected, "fsdp", axis=0, tiled=True)
    partial_value = jnp.einsum(
        "tr,tc->rc", group_proj, grad_out, preferred_element_type=jnp.float32
    )
    partial_value = lax.optimization_barrier(partial_value.astype(jnp.bfloat16))
    grad = lax.psum_scatter(
        partial_value.astype(jnp.float32), "dp", scatter_dimension=0, tiled=True
    )
    moment_one_new, moment_two_new, update = adam(grad, moment_one, moment_two)
    slab_rows = master.shape[0]
    proj_slab = lax.dynamic_slice_in_dim(projection, lax.axis_index("dp") * slab_rows, slab_rows, 0)
    piece = lax.all_gather(update, "dp", axis=0, tiled=True)
    expanded = jnp.dot(proj_slab, piece, preferred_element_type=jnp.float32)
    master_new = master - LEARN_RATE * expanded
    weight_cols = lax.all_gather(master_new.astype(jnp.bfloat16), "dp", axis=0, tiled=True)
    return (moment_one_new, moment_two_new, master_new, weight_cols)


def send(value, axis, size, mask):
    return lax.ppermute(value, axis, [(i, i ^ mask) for i in range(size)])


def order(size):
    return (0, 6, 7, 2, 4, 3, 5, 1) if size == 8 else (0, *reversed(range(1, size)))


def partial_kernel(place, grad_t, *refs, n_fsdp, n_dp):
    pieces, outs, (tokens, result) = refs[:n_fsdp], refs[n_fsdp : n_fsdp + n_dp], refs[n_fsdp + n_dp :]
    count = pieces[0].shape[0]
    rows = outs[0].shape[0]
    for k, piece in zip(order(n_fsdp), pieces):
        tokens[pl.ds(pl.multiple_of((place[1] ^ k) * count, count), count), :] = piece[...]
    result[...] = lax.dot_general(
        tokens[...].T, grad_t[...], (((1,), (1,)), ((), ())), preferred_element_type=jnp.float32
    ).astype(jnp.bfloat16)
    for k, out in enumerate(outs):
        out[...] = result[pl.ds(pl.multiple_of((place[0] ^ k) * rows, rows), rows), :]


def adam_kernel(moment_one, moment_two, *refs, n_dp):
    pieces, (one_new, two_new, update) = refs[:n_dp], refs[n_dp:]
    grad = pieces[0][...].astype(jnp.float32)
    for k in range(1, n_dp):
        grad = grad + pieces[k][...].astype(jnp.float32)
    one, two, value = adam(grad, moment_one[...], moment_two[...])
    one_new[...] = one
    two_new[...] = two
    cols = value.shape[1]
    update[...] = jnp.zeros_like(update)
    update[:, :cols] = value


def expand(tall, slab, first, count):
    return lax.dot_general(
        tall[pl.ds(first, count), :], slab, (((1,), (1,)), ((), ())),
        preferred_element_type=jnp.float32,
    )


def weight_kernel(place, projection, master_t, *refs, n_in, spans, block):
    pieces, outs = refs[:n_in], refs[n_in:]
    if n_in > 1:
        tall, wide = outs[0], outs[-1]
        outs = outs[1:-1]
        rows = pieces[0].shape[0]
        for k, piece in zip(order(n_in), pieces):
            wide[pl.ds(pl.multiple_of((place[0] ^ k) * rows, rows), rows), :] = piece[...]
        tall[...] = wide[...].T
    else:
        tall = pieces[0]
    slab_rows = master_t.shape[1]
    slab = projection[pl.ds(pl.multiple_of(place[0] * slab_rows, slab_rows), slab_rows), :]
    for (first, count), out in zip(spans, outs):
        for at in range(0, count, block):
            master_new = master_t[pl.ds(first + at, block), :] - LEARN_RATE * expand(
                tall, slab, first + at, block
            )
            out[pl.ds(at, block), :] = master_new.astype(jnp.bfloat16)


def weights(place, projection, master_t, pieces, spans, block):
    slab_rows = master_t.shape[1]
    rank = projection.shape[1]
    wide = pieces[0].shape[1]
    out_shape = [jax.ShapeDtypeStruct((count, slab_rows), jnp.bfloat16) for _, count in spans]
    scratch = []
    if len(pieces) > 1:
        out_shape = [jax.ShapeDtypeStruct((wide, rank), jnp.bfloat16)] + out_shape
        scratch = [pltpu.VMEM((rank, wide), jnp.bfloat16)]
    size = sum(count for _, count in spans) * slab_rows
    return pl.pallas_call(
        functools.partial(weight_kernel, n_in=len(pieces), spans=spans, block=block),
        out_shape=out_shape,
        in_specs=[SMEM] + [VMEM] * (2 + len(pieces)),
        out_specs=[VMEM] * len(out_shape),
        scratch_shapes=scratch,
        compiler_params=pltpu.CompilerParams(vmem_limit_bytes=20 * 2**20),
        cost_estimate=pl.CostEstimate(flops=2 * size * rank, bytes_accessed=4 * size, transcendentals=0),
    )(place, projection, master_t, *pieces)


def master_kernel(place, slab, master_t, tall, out):
    block = master_t.shape[0]
    first = pl.multiple_of(pl.program_id(0) * block, block)
    out[...] = master_t[...] - LEARN_RATE * expand(tall, slab[...], first, block)


def new_master(place, projection, master_t, tall, block):
    cols, slab_rows = master_t.shape
    rank = projection.shape[1]
    return pl.pallas_call(
        master_kernel,
        out_shape=jax.ShapeDtypeStruct((cols, slab_rows), jnp.float32),
        grid_spec=pltpu.PrefetchScalarGridSpec(
            num_scalar_prefetch=1,
            grid=(cols // block,),
            in_specs=[
                pl.BlockSpec((slab_rows, rank), lambda i, s: (s[0], 0)),
                pl.BlockSpec((block, slab_rows), lambda i, s: (i, 0)),
                pl.BlockSpec(tall.shape, lambda i, s: (0, 0)),
            ],
            out_specs=pl.BlockSpec((block, slab_rows), lambda i, s: (i, 0)),
        ),
        compiler_params=pltpu.CompilerParams(vmem_limit_bytes=12 * 2**20),
        cost_estimate=pl.CostEstimate(
            flops=2 * cols * slab_rows * rank, bytes_accessed=8 * cols * slab_rows, transcendentals=0
        ),
    )(place, projection, master_t, tall)


def lay_kernel(place, *refs, spans, block, fresh):
    refs = refs if fresh else refs[1:]
    n_in = sum(len(masks) for _, _, masks in spans)
    pieces, out, (held, sems) = refs[:n_in], refs[n_in], refs[n_in + 1 :]
    copies = [None, None]
    at = 0
    base = 0
    for first, count, masks in spans:
        for start in range(0, count, block):
            slot = at % 2
            if copies[slot] is not None:
                copies[slot].wait()
            for mask, piece in zip(masks, pieces[base : base + len(masks)]):
                width = piece.shape[1]
                column = pl.multiple_of((place[0] ^ mask) * width, 128)
                held[slot, :, pl.ds(column, width)] = piece[pl.ds(start, block), :]
            copies[slot] = pltpu.make_async_copy(
                held.at[slot], out.at[pl.ds(first + start, block), :], sems.at[slot]
            )
            copies[slot].start()
            at += 1
        base += len(masks)
    for copy in copies:
        if copy is not None:
            copy.wait()


def lay(place, out, shape, spans, pieces, block):
    fresh = out is None
    held = [] if fresh else [out]
    size = sum(2 * 2 * piece.size for piece in pieces)
    return pl.pallas_call(
        functools.partial(lay_kernel, spans=spans, block=block, fresh=fresh),
        out_shape=jax.ShapeDtypeStruct(shape, jnp.bfloat16),
        in_specs=[SMEM] + [ANY] * len(held) + [VMEM] * len(pieces),
        out_specs=ANY,
        scratch_shapes=[
            pltpu.VMEM((2, block, shape[1]), jnp.bfloat16),
            pltpu.SemaphoreType.DMA((2,)),
        ],
        input_output_aliases={} if fresh else {1: 0},
        compiler_params=pltpu.CompilerParams(vmem_limit_bytes=20 * 2**20),
        cost_estimate=pl.CostEstimate(flops=0, bytes_accessed=size, transcendentals=0),
    )(place, *held, *pieces)


def kernel_body(acts, grad_out, projection, moment_one, moment_two, master, n_dp, n_fsdp):
    cols = grad_out.shape[1]
    rank = projection.shape[1]
    rows = moment_one.shape[0]
    slab_rows = master.shape[0]
    wide = -(-cols // 128) * 128
    place = jnp.stack([lax.axis_index("dp"), lax.axis_index("fsdp")]).astype(jnp.int32)
    master_t = master.T

    projected = jnp.dot(acts, projection, preferred_element_type=jnp.float32).astype(jnp.bfloat16)
    tokens = [projected if k == 0 else send(projected, "fsdp", n_fsdp, k) for k in order(n_fsdp)]
    parts = pl.pallas_call(
        functools.partial(partial_kernel, n_fsdp=n_fsdp, n_dp=n_dp),
        out_shape=[jax.ShapeDtypeStruct((rows, cols), jnp.bfloat16)] * n_dp,
        in_specs=[SMEM] + [VMEM] * (1 + n_fsdp),
        out_specs=[VMEM] * n_dp,
        scratch_shapes=[
            pltpu.VMEM((n_fsdp * projected.shape[0], rank), jnp.bfloat16),
            pltpu.VMEM((rank, cols), jnp.bfloat16),
        ],
        compiler_params=pltpu.CompilerParams(vmem_limit_bytes=16 * 2**20),
    )(place, grad_out.T, *tokens)
    parts = [parts[k] if k == 0 else send(parts[k], "dp", n_dp, k) for k in order(n_dp)]
    moment_one_new, moment_two_new, update = pl.pallas_call(
        functools.partial(adam_kernel, n_dp=n_dp),
        out_shape=[
            jax.ShapeDtypeStruct(moment_one.shape, jnp.float32),
            jax.ShapeDtypeStruct(moment_two.shape, jnp.float32),
            jax.ShapeDtypeStruct((rows, wide), jnp.bfloat16),
        ],
        in_specs=[VMEM] * (2 + n_dp),
        out_specs=[VMEM] * 3,
        compiler_params=pltpu.CompilerParams(vmem_limit_bytes=16 * 2**20),
    )(moment_one, moment_two, *parts)
    updates = {0: update}
    for k in (6, 2, 4, 1):
        updates[k] = send(update, "dp", n_dp, k)
    for k in (2, 4, 6):
        updates[k ^ 1] = send(updates[k], "dp", n_dp, 1)
    updates = [updates[k] for k in order(n_dp)]

    half = cols // 2
    block = cols // 12
    counts = (4 * block, 2 * block)
    chunks = len(counts)
    starts = [sum(counts[:at]) for at in range(chunks)]
    spans = [((first, count), (half + first, count)) for first, count in zip(starts, counts)]
    tall, *early = weights(place, projection, master_t, updates, spans[0], block)
    own = [early]
    for span in spans[1:]:
        own.append(weights(place, projection, master_t, [tall], span, block))
    master_new = new_master(place, projection, master_t, tall, cols // 4)

    def hop(value, mask):
        return send(value, "dp", n_dp, mask)

    pairs, relays, own_relays, out = [], [], [], None
    shape = (cols, n_dp * slab_rows)
    for step in range(3 * chunks):
        phase, at = divmod(step, chunks)
        if phase < 2:
            both = (own[at][phase], own[at][1 - phase])
        else:
            both = (pairs[at][1], pairs[at][0])
        earlier = []
        if step >= 2:
            earlier += pairs[step - 2]
        if step >= 3:
            earlier += relays[step - 3]
            if step - 3 < chunks:
                earlier += own_relays[step - 3]
        if step == 2:
            earlier.append(master_new)
        both = lax.optimization_barrier((*both, *earlier))[:2]
        pair = (hop(both[0], 2), hop(both[1], 4))
        pairs.append(pair)
        if step < chunks:
            held = lax.optimization_barrier((*own[step], *pair))[:2]
            own_relays.append([hop(value, 1) for value in held])
        held = pair if out is None else lax.optimization_barrier((*pair, out))[:2]
        relays.append([hop(value, 1) for value in held])
        if phase == 2:
            from_x, from_y = pairs[at], pairs[chunks + at]
            over_x, over_y = relays[at], relays[chunks + at]
            first = (own[at][0], own_relays[at][0], from_x[0], over_x[0], from_y[1], over_y[1], pair[1], relays[step][1])
            second = (own[at][1], own_relays[at][1], from_y[0], over_y[0], from_x[1], over_x[1], pair[0], relays[step][0])
            masks = tuple(range(n_dp))
            placed = [(*spans[at][0], masks), (*spans[at][1], masks)]
            out = lay(place, out, shape, placed, first + second, block)
    return (moment_one_new, moment_two_new, master_new.T, out.T)


def solution(mesh):
    n_dp, n_fsdp = mesh.shape["dp"], mesh.shape["fsdp"]

    def body(acts, grad_out, projection, moment_one, moment_two, master):
        args = (acts, grad_out, projection, moment_one, moment_two, master)
        fits = n_dp == 8 and n_fsdp == 4 and moment_one.shape[0] % 32 == 0 and master.shape[0] % 128 == 0
        if fits and grad_out.shape[1] % 64 == 0 and acts.shape[0] % 128 == 0:
            return kernel_body(*args, n_dp, n_fsdp)
        return plain_body(*args)

    in_specs = (
        P(("dp", "fsdp"), None),
        P("dp", "fsdp"),
        P(),
        P("dp", "fsdp"),
        P("dp", "fsdp"),
        P("dp", "fsdp"),
    )
    out_specs = (P("dp", "fsdp"), P("dp", "fsdp"), P("dp", "fsdp"), P(None, "fsdp"))
    return jax.shard_map(body, mesh=mesh, in_specs=in_specs, out_specs=out_specs, check_vma=False)
```

time: 694 us -> 146 us (0.21)
  Pallas kernels: 554 us -> 18.3 us
  local copies, waits for them, and re-layouts: 19.6 us -> 4.5 us
    pallas_call x7 -> x5, Pallas kernels: 552 us -> 15.8 us  [the longest x2 9.45 us: lay(): pl.pallas_call(functools.partial(lay_kernel, spans=spans, block=block, fr...]
    unnamed x64 -> x12, local copies, waits for them, and re-layouts: 19.4 us -> 4.5 us
    ppermute x30 -> x45, starting transfers between devices: 27.8 us -> 29.7 us  [send(): return lax.ppermute(value, axis, [(i, i ^ mask) for i in range(size)])]
    ppermute x30 -> x45, waiting for transfers between devices: 88.1 us -> 90 us  [send(): return lax.ppermute(value, axis, [(i, i ^ mask) for i in range(size)])]
  transfers between devices with their start and end apart: 30 -> 45, of which waited for: 14 -> 25; matrix products, arithmetic and copies ran while one was open for 0% -> 0% of each run, Pallas kernels for 69% -> 7%
where the time goes in v2:
time: 146 us; the launch traced here: 145 us
  waiting for transfers between devices  90 us (62%)
  starting transfers between devices  29.7 us (20%)
  Pallas kernels  18.3 us (13%)
  local copies, waits for them, and re-layouts  4.5 us (3%)
  matrix products  2.25 us (2%)
    ppermute x45, waiting for transfers between devices, send(): return lax.ppermute(value, axis, [(i, i ^ mask) for i in range(size)])  90 us
    ppermute x45, starting transfers between devices, send(): return lax.ppermute(value, axis, [(i, i ^ mask) for i in range(size)])  29.7 us
    pallas_call x2, Pallas kernels, lay(): pl.pallas_call(functools.partial(lay_kernel, spans=spans, block=block, fr...  9.45 us
    unnamed x12, local copies, waits for them, and re-layouts  4.5 us
    pallas_call x1, Pallas kernels, new_master(): pl.pallas_call(master_kernel, out_shape=jax.ShapeDtypeStruct((cols, slab_...  3.68 us
  transfers between devices with their start and end apart: 45, of which 25 were waited for; matrix products, arithmetic and copies ran while one was open for 0% of the time, Pallas kernels for 7%

profile of v2, /device:TPU:0, one launch (start us, length us, event | category | flops | bytes accessed | tf_op | source)
XLA Modules:
  0.0 145.5 jit_solution(16294871558557123262)
XLA Ops:
  2.0 2.2 %convolution_convert_fusion.refs_0_ = bf16[128,256]{1,0:T(8,128)(2,1)S(1)} fusion(bf16[128,5120]{1,0:T(8,128)(2,1)S(1)} %copy-done, bf16[5120,256]{1,0:T(8,128)(2,1)} %projection.3), kind=kOutput, calls=%fused_computation | convolution fusion | flops 335577088 | bytes 3997696 | tf_op jit(solution)/shard_map/dot_general | solution.py:221
  4.2 3.1 %collective-permute-start.2 = (bf16[128,256]{1,0:T(8,128)(2,1)S(1)}, bf16[128,256]{1,0:T(8,128)(2,1)S(1)}, u32[]{:S(2)}, u32[]{:S(2)}) collective-permute-start(bf16[128,256]{1,0:T(8,128)(2,1)S(1)} %convolution_convert_fusion.refs_0_), channel_id=1, source_target_pairs={{0,1},{1,0},{2,3},{3,2},{4,5},{5,4},{6,7},{7,6},{8,9},{9,8},{10,11... | collective-permute-start | bytes 196616 | tf_op jit(solution)/shard_map/ppermute | solution.py:55
  7.3 2.6 %collective-permute-start.1 = (bf16[128,256]{1,0:T(8,128)(2,1)S(1)}, bf16[128,256]{1,0:T(8,128)(2,1)S(1)}, u32[]{:S(2)}, u32[]{:S(2)}) collective-permute-start(bf16[128,256]{1,0:T(8,128)(2,1)S(1)} %convolution_convert_fusion.refs_0_), channel_id=1, source_target_pairs={{0,2},{1,3},{2,0},{3,1},{4,6},{5,7},{6,4},{7,5},{8,10},{9,11},{10,... | collective-permute-start | bytes 196616 | tf_op jit(solution)/shard_map/ppermute | solution.py:55
  10.0 4.6 %collective-permute-done.1.refs_2_ = bf16[128,256]{1,0:T(8,128)(2,1)S(1)} collective-permute-done((bf16[128,256]{1,0:T(8,128)(2,1)S(1)}, bf16[128,256]{1,0:T(8,128)(2,1)S(1)}, u32[]{:S(2)}, u32[]{:S(2)}) %collective-permute-start.1) | collective-permute-done | bytes 65568 | tf_op jit(solution)/shard_map/ppermute | solution.py:55
  16.1 1.6 %shard_map.93 = (bf16[32,1728]{1,0:T(8,128)(2,1)S(1)}, bf16[32,1728]{1,0:T(8,128)(2,1)S(1)}, bf16[32,1728]{1,0:T(8,128)(2,1)S(1)}, bf16[32,1728]{1,0:T(8,128)(2,...) custom-call(s32[2]{0:T(128)S(1)} %pad_add_fusion.place, ...), custom_call_target="tpu_custom_call" | custom-call | tf_op jit(solution)/shard_map/pallas_call | solution.py:223
  17.7 2.5 %collective-permute-start.3 = (bf16[32,1728]{1,0:T(8,128)(2,1)S(1)}, bf16[32,1728]{1,0:T(8,128)(2,1)S(1)}, u32[]{:S(2)}, u32[]{:S(2)}) collective-permute-start(bf16[32,1728]{1,0:T(8,128)(2,1)S(1)} %get-tuple-element.39), channel_id=1, source_target_pairs={{0,24},{4,28},{8,16},{12,20},{16,8},{20,12},{24,0},{28,4},{1,25},{... | collective-permute-start | bytes 331784 | tf_op jit(solution)/shard_map/ppermute | solution.py:55
  21.3 2.1 %collective-permute-start.7 = (bf16[32,1728]{1,0:T(8,128)(2,1)S(1)}, bf16[32,1728]{1,0:T(8,128)(2,1)S(1)}, u32[]{:S(2)}, u32[]{:S(2)}) collective-permute-start(bf16[32,1728]{1,0:T(8,128)(2,1)S(1)} %get-tuple-element.43), channel_id=1, source_target_pairs={{0,12},{4,8},{8,4},{12,0},{16,28},{20,24},{24,20},{28,16},{1,13},{... | collective-permute-start | bytes 331784 | tf_op jit(solution)/shard_map/ppermute | solution.py:55
  24.0 2.6 %collective-permute-done.4.refs_2_ = bf16[32,1728]{1,0:T(8,128)(2,1)S(1)} collective-permute-done((bf16[32,1728]{1,0:T(8,128)(2,1)S(1)}, bf16[32,1728]{1,0:T(8,128)(2,1)S(1)}, u32[]{:S(2)}, u32[]{:S(2)}) %collective-permute-start.4) | collective-permute-done | bytes 110624 | tf_op jit(solution)/shard_map/ppermute | solution.py:55
  26.6 2.2 %collective-permute-done.5.refs_3_ = bf16[32,1728]{1,0:T(8,128)(2,1)S(1)} collective-permute-done((bf16[32,1728]{1,0:T(8,128)(2,1)S(1)}, bf16[32,1728]{1,0:T(8,128)(2,1)S(1)}, u32[]{:S(2)}, u32[]{:S(2)}) %collective-permute-start.5) | collective-permute-done | bytes 110624 | tf_op jit(solution)/shard_map/ppermute | solution.py:55
  28.8 1.7 %collective-permute-done.7.refs_5_ = bf16[32,1728]{1,0:T(8,128)(2,1)S(1)} collective-permute-done((bf16[32,1728]{1,0:T(8,128)(2,1)S(1)}, bf16[32,1728]{1,0:T(8,128)(2,1)S(1)}, u32[]{:S(2)}, u32[]{:S(2)}) %collective-permute-start.7) | collective-permute-done | bytes 110624 | tf_op jit(solution)/shard_map/ppermute | solution.py:55
  36.2 1.7 %collective-permute-done.13.refs_4_ = bf16[32,1792]{1,0:T(8,128)(2,1)S(1)} collective-permute-done((bf16[32,1792]{1,0:T(8,128)(2,1)S(1)}, bf16[32,1792]{1,0:T(8,128)(2,1)S(1)}, u32[]{:S(2)}, u32[]{:S(2)}) %collective-permute-start.13) | collective-permute-done | bytes 114720 | tf_op jit(solution)/shard_map/ppermute | solution.py:55
  37.9 2.3 %collective-permute-done.12.refs_3_ = bf16[32,1792]{1,0:T(8,128)(2,1)S(1)} collective-permute-done((bf16[32,1792]{1,0:T(8,128)(2,1)S(1)}, bf16[32,1792]{1,0:T(8,128)(2,1)S(1)}, u32[]{:S(2)}, u32[]{:S(2)}) %collective-permute-start.12) | collective-permute-done | bytes 114720 | tf_op jit(solution)/shard_map/ppermute | solution.py:55
  42.8 2.3 %copy-done.2 = f32[640,1728]{0,1:T(8,128)S(1)} copy-done((f32[640,1728]{0,1:T(8,128)S(1)}, f32[640,1728]{0,1:T(8,128)}, u32[]{:S(2)}) %copy-start.2) | copy-done | bytes 4423704
  45.1 1.6 %shard_map.95 = (bf16[1792,256]{1,0:T(8,128)(2,1)S(1)}, bf16[576,640]{1,0:T(8,128)(2,1)S(1)}, bf16[576,640]{1,0:T(8,128)(2,1)S(1)}) custom-call(s32[2]{0:T(128)S(1)} %pad_add_fusion.place, bf16[5120,256]{1,0:T(8,128)(2,1)S(1)} %copy-done.1, f32[1728,640]{1,0:T(8,128)S(1)} %bitcast.8, bf16[32,1792]{1,0:T(8,128)(2,1)S(1)} %get-tuple-element.48.refs_0_, ...), custom_call_target="tpu_custom_call" | custom-call | flops 377487360 | bytes 2949120 | tf_op jit(solution)/shard_map/pallas_call | solution.py:126
  51.9 3.7 %shard_map.96 = f32[1728,640]{1,0:T(8,128)} custom-call(s32[2]{0:T(128)S(1)} %pad_add_fusion.place, bf16[5120,256]{1,0:T(8,128)(2,1)S(1)} %copy-done.1, f32[1728,640]{1,0:T(8,128)S(1)} %bitcast.10, bf16[1792,256]{1,0:T(8,128)(2,1)S(1)} %get-tuple-element.49.tall.refs_0_), custom_call_target="tpu_custom_call" | custom-call | flops 566231040 | bytes 8847360 | tf_op jit(solution)/shard_map/pallas_call | solution.py:146
  55.6 10.4 %collective-permute-done.17.refs_2_ = bf16[576,640]{1,0:T(8,128)(2,1)S(1)} collective-permute-done((bf16[576,640]{1,0:T(8,128)(2,1)S(1)}, bf16[576,640]{1,0:T(8,128)(2,1)S(1)}, u32[]{:S(2)}, u32[]{:S(2)}) %collective-permute-start.17) | collective-permute-done | bytes 737312 | tf_op jit(solution)/shard_map/ppermute | solution.py:55
  69.0 4.2 %collective-permute-done.24.refs_3_ = bf16[288,640]{1,0:T(8,128)(2,1)S(1)} collective-permute-done((bf16[288,640]{1,0:T(8,128)(2,1)S(1)}, bf16[288,640]{1,0:T(8,128)(2,1)S(1)}, u32[]{:S(2)}, u32[]{:S(2)}) %collective-permute-start.24) | collective-permute-done | bytes 368672 | tf_op jit(solution)/shard_map/ppermute | solution.py:55
  73.2 2.2 %collective-permute-done.26.refs_13_ = bf16[288,640]{1,0:T(8,128)(2,1)S(1)} collective-permute-done((bf16[288,640]{1,0:T(8,128)(2,1)S(1)}, bf16[288,640]{1,0:T(8,128)(2,1)S(1)}, u32[]{:S(2)}, u32[]{:S(2)}) %collective-permute-start.26) | collective-permute-done | bytes 368672 | tf_op jit(solution)/shard_map/ppermute | solution.py:55
  78.3 11.8 %collective-permute-done.21.refs_4_ = bf16[576,640]{1,0:T(8,128)(2,1)S(1)} collective-permute-done((bf16[576,640]{1,0:T(8,128)(2,1)S(1)}, bf16[576,640]{1,0:T(8,128)(2,1)S(1)}, u32[]{:S(2)}, u32[]{:S(2)}) %collective-permute-start.21) | collective-permute-done | bytes 737312 | tf_op jit(solution)/shard_map/ppermute | solution.py:55
  90.1 4.7 %collective-permute-done.23.refs_10_ = bf16[576,640]{1,0:T(8,128)(2,1)S(1)} collective-permute-done((bf16[576,640]{1,0:T(8,128)(2,1)S(1)}, bf16[576,640]{1,0:T(8,128)(2,1)S(1)}, u32[]{:S(2)}, u32[]{:S(2)}) %collective-permute-start.23) | collective-permute-done | bytes 737312 | tf_op jit(solution)/shard_map/ppermute | solution.py:55
  98.1 22.8 %collective-permute-done.37.refs_5_ = bf16[288,640]{1,0:T(8,128)(2,1)S(1)} collective-permute-done((bf16[288,640]{1,0:T(8,128)(2,1)S(1)}, bf16[288,640]{1,0:T(8,128)(2,1)S(1)}, u32[]{:S(2)}, u32[]{:S(2)}) %collective-permute-start.37) | collective-permute-done | bytes 368672 | tf_op jit(solution)/shard_map/ppermute | solution.py:55
  122.0 8.2 %collective-permute-done.39.refs_11_ = bf16[288,640]{1,0:T(8,128)(2,1)S(1)} collective-permute-done((bf16[288,640]{1,0:T(8,128)(2,1)S(1)}, bf16[288,640]{1,0:T(8,128)(2,1)S(1)}, u32[]{:S(2)}, u32[]{:S(2)}) %collective-permute-start.39) | collective-permute-done | bytes 368672 | tf_op jit(solution)/shard_map/ppermute | solution.py:55
  132.7 6.0 %shard_map.98.refs_0_ = bf16[1728,5120]{1,0:T(8,128)(2,1)} custom-call(s32[2]{0:T(128)S(1)} %pad_add_fusion.place, bf16[576,640]{1,0:T(8,128)(2,1)S(1)} %get-tuple-element.55.refs_0_, bf16[576,640]{1,0:T(8,128)(2,1)S(1)} %collective-permute-done.19.refs_1_, bf16[576,640]{1,0:T(8,128)(2,1)S(1)} %collective-permute-done.17.refs_2_, ...), custom_call_target="tpu_custom_call" | custom-call | bytes 23592960 | tf_op jit(solution)/shard_map/pallas_call | solution.py:197
  142.0 3.5 %shard_map.99 = bf16[1728,5120]{1,0:T(8,128)(2,1)} custom-call(s32[2]{0:T(128)S(1)} %pad_add_fusion.place, bf16[1728,5120]{1,0:T(8,128)(2,1)} %shard_map.98.refs_0_, bf16[288,640]{1,0:T(8,128)(2,1)S(1)} %get-tuple-element.66.refs_1_, bf16[288,640]{1,0:T(8,128)(2,1)S(1)} %collective-permute-done.28.refs_2_, ...), custom_call_target="tpu_custom_call", output_to_operand_aliasing={{}: (1, {})} | custom-call | bytes 11796480 | tf_op jit(solution)/shard_map/pallas_call | solution.py:197
  (87 shorter events, 34.1 us)
Async XLA Ops:
  20.2 8.6 %collective-permute-start.5 = (bf16[32,1728]{1,0:T(8,128)(2,1)S(1)}, bf16[32,1728]{1,0:T(8,128)(2,1)S(1)}, u32[]{:S(2)}, u32[]{:S(2)}) collective-permute-start(bf16[32,1728]{1,0:T(8,128)(2,1)S(1)} %get-tuple-element.41), channel_id=1, source_target_pairs={{0,8},{4,12},{8,0},{12,4},{16,24},{20,28},{24,16},{28,20},{1,9},{5... | collective-permute-start | bytes 331784 | tf_op jit(solution)/shard_map/ppermute | solution.py:55
  20.7 8.1 %collective-permute-start.6 = (bf16[32,1728]{1,0:T(8,128)(2,1)S(1)}, bf16[32,1728]{1,0:T(8,128)(2,1)S(1)}, u32[]{:S(2)}, u32[]{:S(2)}) collective-permute-start(bf16[32,1728]{1,0:T(8,128)(2,1)S(1)} %get-tuple-element.42), channel_id=1, source_target_pairs={{0,16},{4,20},{8,24},{12,28},{16,0},{20,4},{24,8},{28,12},{1,17},{... | collective-permute-start | bytes 331784 | tf_op jit(solution)/shard_map/ppermute | solution.py:55
  21.3 9.3 %collective-permute-start.7 = (bf16[32,1728]{1,0:T(8,128)(2,1)S(1)}, bf16[32,1728]{1,0:T(8,128)(2,1)S(1)}, u32[]{:S(2)}, u32[]{:S(2)}) collective-permute-start(bf16[32,1728]{1,0:T(8,128)(2,1)S(1)} %get-tuple-element.43), channel_id=1, source_target_pairs={{0,12},{4,8},{8,4},{12,0},{16,28},{20,24},{24,20},{28,16},{1,13},{... | collective-permute-start | bytes 331784 | tf_op jit(solution)/shard_map/ppermute | solution.py:55
  46.7 19.4 %collective-permute-start.17 = (bf16[576,640]{1,0:T(8,128)(2,1)S(1)}, bf16[576,640]{1,0:T(8,128)(2,1)S(1)}, u32[]{:S(2)}, u32[]{:S(2)}) collective-permute-start(bf16[576,640]{1,0:T(8,128)(2,1)S(1)} %get-tuple-element.55.refs_0_), channel_id=1, source_target_pairs={{0,8},{4,12},{8,0},{12,4},{16,24},{20,28},{24,16},{28,20},{1,9},{5... | collective-permute-start | bytes 2211848 | tf_op jit(solution)/shard_map/ppermute | solution.py:55
  48.1 19.4 %collective-permute-start.18 = (bf16[576,640]{1,0:T(8,128)(2,1)S(1)}, bf16[576,640]{1,0:T(8,128)(2,1)S(1)}, u32[]{:S(2)}, u32[]{:S(2)}) collective-permute-start(bf16[576,640]{1,0:T(8,128)(2,1)S(1)} %get-tuple-element.64.refs_8_), channel_id=1, source_target_pairs={{0,16},{4,20},{8,24},{12,28},{16,0},{20,4},{24,8},{28,12},{1,17},{... | collective-permute-start | bytes 2211848 | tf_op jit(solution)/shard_map/ppermute | solution.py:55
  50.7 22.5 %collective-permute-start.24 = (bf16[288,640]{1,0:T(8,128)(2,1)S(1)}, bf16[288,640]{1,0:T(8,128)(2,1)S(1)}, u32[]{:S(2)}, u32[]{:S(2)}) collective-permute-start(bf16[288,640]{1,0:T(8,128)(2,1)S(1)} %get-tuple-element.66.refs_1_), channel_id=1, source_target_pairs={{0,8},{4,12},{8,0},{12,4},{16,24},{20,28},{24,16},{28,20},{1,9},{5... | collective-permute-start | bytes 1105928 | tf_op jit(solution)/shard_map/ppermute | solution.py:55
  51.3 24.1 %collective-permute-start.26 = (bf16[288,640]{1,0:T(8,128)(2,1)S(1)}, bf16[288,640]{1,0:T(8,128)(2,1)S(1)}, u32[]{:S(2)}, u32[]{:S(2)}) collective-permute-start(bf16[288,640]{1,0:T(8,128)(2,1)S(1)} %get-tuple-element.58), channel_id=1, source_target_pairs={{0,16},{4,20},{8,24},{12,28},{16,0},{20,4},{24,8},{28,12},{1,17},{... | collective-permute-start | bytes 1105928 | tf_op jit(solution)/shard_map/ppermute | solution.py:55
  67.5 22.6 %collective-permute-start.21 = (bf16[576,640]{1,0:T(8,128)(2,1)S(1)}, bf16[576,640]{1,0:T(8,128)(2,1)S(1)}, u32[]{:S(2)}, u32[]{:S(2)}) collective-permute-start(bf16[576,640]{1,0:T(8,128)(2,1)S(1)} %get-tuple-element.55.refs_0_), channel_id=1, source_target_pairs={{0,16},{4,20},{8,24},{12,28},{16,0},{20,4},{24,8},{28,12},{1,17},{... | collective-permute-start | bytes 2211848 | tf_op jit(solution)/shard_map/ppermute | solution.py:55
  75.9 18.9 %collective-permute-start.23 = (bf16[576,640]{1,0:T(8,128)(2,1)S(1)}, bf16[576,640]{1,0:T(8,128)(2,1)S(1)}, u32[]{:S(2)}, u32[]{:S(2)}) collective-permute-start(bf16[576,640]{1,0:T(8,128)(2,1)S(1)} %get-tuple-element.64.refs_8_), channel_id=1, source_target_pairs={{0,8},{4,12},{8,0},{12,4},{16,24},{20,28},{24,16},{28,20},{1,9},{5... | collective-permute-start | bytes 2211848 | tf_op jit(solution)/shard_map/ppermute | solution.py:55
  77.1 19.2 %collective-permute-start.20 = (bf16[576,640]{1,0:T(8,128)(2,1)S(1)}, bf16[576,640]{1,0:T(8,128)(2,1)S(1)}, u32[]{:S(2)}, u32[]{:S(2)}) collective-permute-start(bf16[576,640]{1,0:T(8,128)(2,1)S(1)} %collective-permute-done.17.refs_2_), channel_id=1, source_target_pairs={{0,4},{4,0},{8,12},{12,8},{16,20},{20,16},{24,28},{28,24},{1,5},{5... | collective-permute-start | bytes 2211848 | tf_op jit(solution)/shard_map/ppermute | solution.py:55
  77.6 19.2 %collective-permute-start.19 = (bf16[576,640]{1,0:T(8,128)(2,1)S(1)}, bf16[576,640]{1,0:T(8,128)(2,1)S(1)}, u32[]{:S(2)}, u32[]{:S(2)}) collective-permute-start(bf16[576,640]{1,0:T(8,128)(2,1)S(1)} %get-tuple-element.55.refs_0_), channel_id=1, source_target_pairs={{0,4},{4,0},{8,12},{12,8},{16,20},{20,16},{24,28},{28,24},{1,5},{5... | collective-permute-start | bytes 2211848 | tf_op jit(solution)/shard_map/ppermute | solution.py:55
  78.2 18.7 %collective-permute-start.32 = (bf16[576,640]{1,0:T(8,128)(2,1)S(1)}, bf16[576,640]{1,0:T(8,128)(2,1)S(1)}, u32[]{:S(2)}, u32[]{:S(2)}) collective-permute-start(bf16[576,640]{1,0:T(8,128)(2,1)S(1)} %get-tuple-element.64.refs_8_), channel_id=1, source_target_pairs={{0,4},{4,0},{8,12},{12,8},{16,20},{20,16},{24,28},{28,24},{1,5},{5... | collective-permute-start | bytes 2211848 | tf_op jit(solution)/shard_map/ppermute | solution.py:55
  94.8 26.6 %collective-permute-start.30 = (bf16[576,640]{1,0:T(8,128)(2,1)S(1)}, bf16[576,640]{1,0:T(8,128)(2,1)S(1)}, u32[]{:S(2)}, u32[]{:S(2)}) collective-permute-start(bf16[576,640]{1,0:T(8,128)(2,1)S(1)} %collective-permute-done.17.refs_2_), channel_id=1, source_target_pairs={{0,16},{4,20},{8,24},{12,28},{16,0},{20,4},{24,8},{28,12},{1,17},{... | collective-permute-start | bytes 2211848 | tf_op jit(solution)/shard_map/ppermute | solution.py:55
  96.3 25.2 %collective-permute-start.35 = (bf16[576,640]{1,0:T(8,128)(2,1)S(1)}, bf16[576,640]{1,0:T(8,128)(2,1)S(1)}, u32[]{:S(2)}, u32[]{:S(2)}) collective-permute-start(bf16[576,640]{1,0:T(8,128)(2,1)S(1)} %collective-permute-done.18.refs_12_), channel_id=1, source_target_pairs={{0,8},{4,12},{8,0},{12,4},{16,24},{20,28},{24,16},{28,20},{1,9},{5... | collective-permute-start | bytes 2211848 | tf_op jit(solution)/shard_map/ppermute | solution.py:55
  96.8 24.0 %collective-permute-start.37 = (bf16[288,640]{1,0:T(8,128)(2,1)S(1)}, bf16[288,640]{1,0:T(8,128)(2,1)S(1)}, u32[]{:S(2)}, u32[]{:S(2)}) collective-permute-start(bf16[288,640]{1,0:T(8,128)(2,1)S(1)} %get-tuple-element.66.refs_1_), channel_id=1, source_target_pairs={{0,16},{4,20},{8,24},{12,28},{16,0},{20,4},{24,8},{28,12},{1,17},{... | collective-permute-start | bytes 1105928 | tf_op jit(solution)/shard_map/ppermute | solution.py:55
  97.5 32.6 %collective-permute-start.22 = (bf16[576,640]{1,0:T(8,128)(2,1)S(1)}, bf16[576,640]{1,0:T(8,128)(2,1)S(1)}, u32[]{:S(2)}, u32[]{:S(2)}) collective-permute-start(bf16[576,640]{1,0:T(8,128)(2,1)S(1)} %collective-permute-done.21.refs_4_), channel_id=1, source_target_pairs={{0,4},{4,0},{8,12},{12,8},{16,20},{20,16},{24,28},{28,24},{1,5},{5... | collective-permute-start | bytes 2211848 | tf_op jit(solution)/shard_map/ppermute | solution.py:55
  97.5 32.6 %collective-permute-start.33 = (bf16[576,640]{1,0:T(8,128)(2,1)S(1)}, bf16[576,640]{1,0:T(8,128)(2,1)S(1)}, u32[]{:S(2)}, u32[]{:S(2)}) collective-permute-start(bf16[576,640]{1,0:T(8,128)(2,1)S(1)} %collective-permute-done.23.refs_10_), channel_id=1, source_target_pairs={{0,4},{4,0},{8,12},{12,8},{16,20},{20,16},{24,28},{28,24},{1,5},{5... | collective-permute-start | bytes 2211848 | tf_op jit(solution)/shard_map/ppermute | solution.py:55
  120.8 9.3 %collective-permute-start.39 = (bf16[288,640]{1,0:T(8,128)(2,1)S(1)}, bf16[288,640]{1,0:T(8,128)(2,1)S(1)}, u32[]{:S(2)}, u32[]{:S(2)}) collective-permute-start(bf16[288,640]{1,0:T(8,128)(2,1)S(1)} %get-tuple-element.58), channel_id=1, source_target_pairs={{0,8},{4,12},{8,0},{12,4},{16,24},{20,28},{24,16},{28,20},{1,9},{5... | collective-permute-start | bytes 1105928 | tf_op jit(solution)/shard_map/ppermute | solution.py:55
  121.5 10.7 %collective-permute-start.31 = (bf16[576,640]{1,0:T(8,128)(2,1)S(1)}, bf16[576,640]{1,0:T(8,128)(2,1)S(1)}, u32[]{:S(2)}, u32[]{:S(2)}) collective-permute-start(bf16[576,640]{1,0:T(8,128)(2,1)S(1)} %collective-permute-done.30.refs_6_), channel_id=1, source_target_pairs={{0,4},{4,0},{8,12},{12,8},{16,20},{20,16},{24,28},{28,24},{1,5},{5... | collective-permute-start | bytes 2211848 | tf_op jit(solution)/shard_map/ppermute | solution.py:55
  121.5 11.2 %collective-permute-start.36 = (bf16[576,640]{1,0:T(8,128)(2,1)S(1)}, bf16[576,640]{1,0:T(8,128)(2,1)S(1)}, u32[]{:S(2)}, u32[]{:S(2)}) collective-permute-start(bf16[576,640]{1,0:T(8,128)(2,1)S(1)} %collective-permute-done.35.refs_14_), channel_id=1, source_target_pairs={{0,4},{4,0},{8,12},{12,8},{16,20},{20,16},{24,28},{28,24},{1,5},{5... | collective-permute-start | bytes 2211848 | tf_op jit(solution)/shard_map/ppermute | solution.py:55
  130.2 8.5 %collective-permute-start.40 = (bf16[288,640]{1,0:T(8,128)(2,1)S(1)}, bf16[288,640]{1,0:T(8,128)(2,1)S(1)}, u32[]{:S(2)}, u32[]{:S(2)}) collective-permute-start(bf16[288,640]{1,0:T(8,128)(2,1)S(1)} %collective-permute-done.24.refs_3_), channel_id=1, source_target_pairs={{0,16},{4,20},{8,24},{12,28},{16,0},{20,4},{24,8},{28,12},{1,17},{... | collective-permute-start | bytes 1105928 | tf_op jit(solution)/shard_map/ppermute | solution.py:55
  131.6 8.1 %collective-permute-start.41 = (bf16[288,640]{1,0:T(8,128)(2,1)S(1)}, bf16[288,640]{1,0:T(8,128)(2,1)S(1)}, u32[]{:S(2)}, u32[]{:S(2)}) collective-permute-start(bf16[288,640]{1,0:T(8,128)(2,1)S(1)} %collective-permute-done.26.refs_13_), channel_id=1, source_target_pairs={{0,8},{4,12},{8,0},{12,4},{16,24},{20,28},{24,16},{28,20},{1,9},{5... | collective-permute-start | bytes 1105928 | tf_op jit(solution)/shard_map/ppermute | solution.py:55
  132.2 8.1 %collective-permute-start.38 = (bf16[288,640]{1,0:T(8,128)(2,1)S(1)}, bf16[288,640]{1,0:T(8,128)(2,1)S(1)}, u32[]{:S(2)}, u32[]{:S(2)}) collective-permute-start(bf16[288,640]{1,0:T(8,128)(2,1)S(1)} %collective-permute-done.37.refs_5_), channel_id=1, source_target_pairs={{0,4},{4,0},{8,12},{12,8},{16,20},{20,16},{24,28},{28,24},{1,5},{5... | collective-permute-start | bytes 1105928 | tf_op jit(solution)/shard_map/ppermute | solution.py:55
  132.2 8.1 %collective-permute-start.43 = (bf16[288,640]{1,0:T(8,128)(2,1)S(1)}, bf16[288,640]{1,0:T(8,128)(2,1)S(1)}, u32[]{:S(2)}, u32[]{:S(2)}) collective-permute-start(bf16[288,640]{1,0:T(8,128)(2,1)S(1)} %collective-permute-done.39.refs_11_), channel_id=1, source_target_pairs={{0,4},{4,0},{8,12},{12,8},{16,20},{20,16},{24,28},{28,24},{1,5},{5... | collective-permute-start | bytes 1105928 | tf_op jit(solution)/shard_map/ppermute | solution.py:55
  (27 other events, 174.3 us)

commit v3 on v2

v3 whole, which is shorter than its diff:
```python
import functools

import jax
import jax.numpy as jnp
from jax import lax
from jax.experimental import pallas as pl
from jax.experimental.pallas import tpu as pltpu
from jax.sharding import PartitionSpec as P

STEP = 1000


BETA_ONE = 0.9
BETA_TWO = 0.999
ADAM_EPS = 1e-08
LEARN_RATE = 0.01
CORRECT_ONE = 1.0 - BETA_ONE**STEP
CORRECT_TWO = 1.0 - BETA_TWO**STEP

VMEM = pl.BlockSpec(memory_space=pltpu.VMEM)
ANY = pl.BlockSpec(memory_space=pl.ANY)


def adam(grad, moment_one, moment_two):
    moment_one_new = BETA_ONE * moment_one + (1.0 - BETA_ONE) * grad
    moment_two_new = BETA_TWO * moment_two + (1.0 - BETA_TWO) * grad * grad
    update = (
        moment_one_new / CORRECT_ONE / (jnp.sqrt(moment_two_new / CORRECT_TWO) + ADAM_EPS)
    ).astype(jnp.bfloat16)
    return moment_one_new, moment_two_new, update


def plain_body(acts, grad_out, projection, moment_one, moment_two, master):
    projected = jnp.dot(acts, projection, preferred_element_type=jnp.float32).astype(jnp.bfloat16)
    group_proj = lax.all_gather(projected, "fsdp", axis=0, tiled=True)
    partial_value = jnp.einsum(
        "tr,tc->rc", group_proj, grad_out, preferred_element_type=jnp.float32
    )
    partial_value = lax.optimization_barrier(partial_value.astype(jnp.bfloat16))
    grad = lax.psum_scatter(
        partial_value.astype(jnp.float32), "dp", scatter_dimension=0, tiled=True
    )
    moment_one_new, moment_two_new, update = adam(grad, moment_one, moment_two)
    slab_rows = master.shape[0]
    proj_slab = lax.dynamic_slice_in_dim(projection, lax.axis_index("dp") * slab_rows, slab_rows, 0)
    piece = lax.all_gather(update, "dp", axis=0, tiled=True)
    expanded = jnp.dot(proj_slab, piece, preferred_element_type=jnp.float32)
    master_new = master - LEARN_RATE * expanded
    weight_cols = lax.all_gather(master_new.astype(jnp.bfloat16), "dp", axis=0, tiled=True)
    return (moment_one_new, moment_two_new, master_new, weight_cols)


def send(value, axis, size, mask):
    return lax.ppermute(value, axis, [(i, i ^ mask) for i in range(size)])


def order(size):
    return (0, *reversed(range(1, size)))


def partial_kernel(grad_t, *refs):
    pieces, out, tokens = refs[:-2], refs[-2], refs[-1]
    count = pieces[0].shape[0]
    me = lax.axis_index("fsdp")
    for k, piece in zip(order(len(pieces)), pieces):
        tokens[pl.ds(pl.multiple_of((me ^ k) * count, count), count), :] = piece[...]
    out[...] = lax.dot_general(
        tokens[...].T, grad_t[...], (((1,), (1,)), ((), ())), preferred_element_type=jnp.float32
    ).astype(jnp.bfloat16)


def adam_kernel(moment_one, moment_two, parts, one_new, two_new, update):
    rows, cols = moment_one.shape
    grad = parts[:rows, :].astype(jnp.float32)
    for first in range(rows, parts.shape[0], rows):
        grad = grad + parts[first : first + rows, :].astype(jnp.float32)
    one, two, value = adam(grad, moment_one[...], moment_two[...])
    one_new[...] = one
    two_new[...] = two
    update[...] = jnp.zeros_like(update)
    update[:, :cols] = value


def expand(tall, slab, first, count):
    return lax.dot_general(
        tall[pl.ds(first, count), :], slab, (((1,), (1,)), ((), ())),
        preferred_element_type=jnp.float32,
    )


def weight_kernel(projection, master_t, *refs, n_in, spans, block):
    pieces, outs = refs[:n_in], refs[n_in:]
    me = lax.axis_index("dp")
    if n_in > 1:
        tall, wide = outs[0], outs[-1]
        outs = outs[1:-1]
        rows = pieces[0].shape[0]
        for k, piece in enumerate(pieces):
            wide[pl.ds(pl.multiple_of((me ^ k) * rows, rows), rows), :] = piece[...]
        tall[...] = wide[...].T
    else:
        tall = pieces[0]
    slab_rows = master_t.shape[1]
    slab = projection[pl.ds(pl.multiple_of(me * slab_rows, slab_rows), slab_rows), :]
    for (first, count), out in zip(spans, outs):
        for at in range(0, count, block):
            master_new = master_t[pl.ds(first + at, block), :] - LEARN_RATE * expand(
                tall, slab, first + at, block
            )
            out[pl.ds(at, block), :] = master_new.astype(jnp.bfloat16)


def weights(projection, master_t, pieces, spans, block):
    slab_rows, rank = master_t.shape[1], projection.shape[1]
    wide = pieces[0].shape[1]
    out_shape = [jax.ShapeDtypeStruct((count, slab_rows), jnp.bfloat16) for _, count in spans]
    scratch = []
    if len(pieces) > 1:
        out_shape = [jax.ShapeDtypeStruct((wide, rank), jnp.bfloat16)] + out_shape
        scratch = [pltpu.VMEM((rank, wide), jnp.bfloat16)]
    size = sum(count for _, count in spans) * slab_rows
    return pl.pallas_call(
        functools.partial(weight_kernel, n_in=len(pieces), spans=spans, block=block),
        out_shape=out_shape,
        in_specs=[VMEM] * (2 + len(pieces)),
        out_specs=[VMEM] * len(out_shape),
        scratch_shapes=scratch,
        compiler_params=pltpu.CompilerParams(vmem_limit_bytes=20 * 2**20),
        cost_estimate=pl.CostEstimate(flops=2 * size * rank, bytes_accessed=4 * size, transcendentals=0),
    )(projection, master_t, *pieces)


def master_kernel(projection, master_t, tall, out):
    slab_rows = master_t.shape[1]
    first = pl.multiple_of(lax.axis_index("dp") * slab_rows, slab_rows)
    slab = projection[pl.ds(first, slab_rows), :]
    block = master_t.shape[0]
    first = pl.multiple_of(pl.program_id(0) * block, block)
    out[...] = master_t[...] - LEARN_RATE * expand(tall, slab, first, block)


def new_master(projection, master_t, tall, block):
    cols, slab_rows = master_t.shape
    rank = projection.shape[1]
    return pl.pallas_call(
        master_kernel,
        out_shape=jax.ShapeDtypeStruct((cols, slab_rows), jnp.float32),
        grid=(cols // block,),
        in_specs=[
            pl.BlockSpec(projection.shape, lambda i: (0, 0)),
            pl.BlockSpec((block, slab_rows), lambda i: (i, 0)),
            pl.BlockSpec(tall.shape, lambda i: (0, 0)),
        ],
        out_specs=pl.BlockSpec((block, slab_rows), lambda i: (i, 0)),
        compiler_params=pltpu.CompilerParams(vmem_limit_bytes=20 * 2**20),
        cost_estimate=pl.CostEstimate(
            flops=2 * cols * slab_rows * rank, bytes_accessed=8 * cols * slab_rows, transcendentals=0
        ),
    )(projection, master_t, tall)


def lay_kernel(*refs, spans, block, fresh):
    refs = refs if fresh else refs[1:]
    n_in = sum(len(masks) for _, _, masks in spans)
    pieces, out, (held, sems) = refs[:n_in], refs[n_in], refs[n_in + 1 :]
    copies = [None] * held.shape[0]
    me = lax.axis_index("dp")
    core = me & 1
    at = 0
    base = 0
    for first, count, masks in spans:
        for start in range(0, count, block):
            slot = at % len(copies)
            if copies[slot] is not None:
                copies[slot].wait()
            for mask, piece in zip(masks, pieces[base : base + len(masks)]):
                width = piece.shape[1]
                mask = jnp.where(core == 0, mask[0], mask[1])
                column = pl.multiple_of((me ^ mask) * width, 128)
                origin = start if piece.shape[0] == count else first + start
                held[slot, :, pl.ds(column, width)] = piece[pl.ds(origin, block), :]
            copies[slot] = pltpu.make_async_copy(
                held.at[slot], out.at[pl.ds(first + start, block), :], sems.at[slot]
            )
            copies[slot].start()
            at += 1
        base += len(masks)
    for copy in copies:
        if copy is not None:
            copy.wait()


def lay(out, shape, spans, pieces, block):
    fresh = out is None
    held = [] if fresh else [out]
    size = sum(2 * 2 * piece.size for piece in pieces)
    return pl.pallas_call(
        functools.partial(lay_kernel, spans=spans, block=block, fresh=fresh),
        out_shape=jax.ShapeDtypeStruct(shape, jnp.bfloat16),
        in_specs=[ANY] * len(held) + [VMEM] * len(pieces),
        out_specs=ANY,
        scratch_shapes=[
            pltpu.VMEM((4, block, shape[1]), jnp.bfloat16),
            pltpu.SemaphoreType.DMA((4,)),
        ],
        input_output_aliases={} if fresh else {0: 0},
        compiler_params=pltpu.CompilerParams(vmem_limit_bytes=20 * 2**20),
        cost_estimate=pl.CostEstimate(flops=0, bytes_accessed=size, transcendentals=0),
    )(*held, *pieces)


def kernel_body(acts, grad_out, projection, moment_one, moment_two, master, n_dp, n_fsdp):
    cols = grad_out.shape[1]
    rank = projection.shape[1]
    rows = moment_one.shape[0]
    slab_rows = master.shape[0]
    wide = -(-cols // 128) * 128
    master_t = master.T

    projected = jnp.dot(acts, projection, preferred_element_type=jnp.float32).astype(jnp.bfloat16)
    tokens = [projected if k == 0 else send(projected, "fsdp", n_fsdp, k) for k in order(n_fsdp)]
    parts = pl.pallas_call(
        partial_kernel,
        out_shape=jax.ShapeDtypeStruct((rank, cols), jnp.bfloat16),
        in_specs=[VMEM] * (1 + n_fsdp),
        out_specs=VMEM,
        scratch_shapes=[pltpu.VMEM((n_fsdp * projected.shape[0], rank), jnp.bfloat16)],
        compiler_params=pltpu.CompilerParams(vmem_limit_bytes=16 * 2**20),
    )(grad_out.T, *tokens)
    parts = lax.all_to_all(parts, "dp", split_axis=0, concat_axis=0, tiled=True)
    moment_one_new, moment_two_new, update = pl.pallas_call(
        adam_kernel,
        out_shape=[
            jax.ShapeDtypeStruct(moment_one.shape, jnp.float32),
            jax.ShapeDtypeStruct(moment_two.shape, jnp.float32),
            jax.ShapeDtypeStruct((rows, wide), jnp.bfloat16),
        ],
        in_specs=[VMEM] * 3,
        out_specs=[VMEM] * 3,
        compiler_params=pltpu.CompilerParams(vmem_limit_bytes=16 * 2**20),
    )(moment_one, moment_two, parts)

    def hop(value, mask):
        return send(value, "dp", n_dp, mask)

    updates = {0: update}
    for k in (6, 2, 4, 1):
        updates[k] = hop(update, k)
    for k in (2, 4, 6):
        updates[k ^ 1] = hop(updates[k], 1)
    updates = [updates[k] for k in range(n_dp)]

    def turn(value, which):
        masks = [(2, 4)[(i & 1) ^ which] for i in range(n_dp)]
        return lax.ppermute(value, "dp", [(i, i ^ masks[i]) for i in range(n_dp)])

    half = cols // 2
    block = cols // 18
    counts = (4 * block, 3 * block, 2 * block)
    chunks = len(counts)
    starts = [sum(counts[:at]) for at in range(chunks)]
    spans = [((first, count), (half + first, count)) for first, count in zip(starts, counts)]
    tall, *early = weights(projection, master_t, updates, spans[0], block)
    late = [span for both in spans[1:] for span in both]
    *late, whole = weights(projection, master_t, [tall], late + [(0, cols)], block)
    own = [early] + [late[2 * at : 2 * at + 2] for at in range(chunks - 1)]
    master_new = new_master(projection, master_t, tall, cols // 4)

    def after(value, earlier):
        return lax.optimization_barrier((value, *earlier))[0] if earlier else value

    got, over = [], []
    out = None
    shape = (cols, n_dp * slab_rows)
    whole_c = hop(whole, 1)
    for step in range(6 * chunks):
        phase, rest = divmod(step, 2 * chunks)
        at, part = divmod(rest, 2)
        if phase == 0:
            value, which = own[at][part], part
        elif phase == 1:
            value, which = own[at][1 - part], part
        else:
            value, which = got[2 * at + part], 1 - part
        earlier = got[step - 3 : step - 2] if step >= 3 else []
        if step == 3:
            earlier += [whole_c, master_new]
        if step >= 5 and part == 1:
            earlier += over[step - 5 : step - 3]
        got.append(turn(after(value, earlier), which))
        if part == 1:
            for which in (step - 1, step):
                over.append(hop(after(got[which], got[step - 1 :] + ([] if out is None else [out])), 1))
        if phase == 2 and part == 1:
            laid, placed = [], []
            for part, (first, count) in enumerate(spans[at]):
                one, two = 2 * at + part, 2 * chunks + 2 * at + 1 - part
                three = 4 * chunks + 2 * at + part
                laid += [whole, whole_c, got[one], over[one], got[two], over[two], got[three], over[three]]
                masks = ((0, 0), (1, 1), (2, 4), (5, 3), (4, 2), (3, 5), (6, 6), (7, 7))
                if part == 1:
                    masks = ((0, 0), (1, 1), (4, 2), (3, 5), (2, 4), (5, 3), (6, 6), (7, 7))
                placed.append((first, count, masks))
            out = lay(out, shape, placed, laid, block)
    return (moment_one_new, moment_two_new, master_new.T, out.T)


def solution(mesh):
    n_dp, n_fsdp = mesh.shape["dp"], mesh.shape["fsdp"]

    def body(acts, grad_out, projection, moment_one, moment_two, master):
        args = (acts, grad_out, projection, moment_one, moment_two, master)
        fits = n_dp == 8 and n_fsdp == 4 and moment_one.shape[0] % 32 == 0 and master.shape[0] % 128 == 0
        if fits and grad_out.shape[1] % 64 == 0 and acts.shape[0] % 128 == 0:
            return kernel_body(*args, n_dp, n_fsdp)
        return plain_body(*args)

    in_specs = (
        P(("dp", "fsdp"), None),
        P("dp", "fsdp"),
        P(),
        P("dp", "fsdp"),
        P("dp", "fsdp"),
        P("dp", "fsdp"),
    )
    out_specs = (P("dp", "fsdp"), P("dp", "fsdp"), P("dp", "fsdp"), P(None, "fsdp"))
    return jax.shard_map(body, mesh=mesh, in_specs=in_specs, out_specs=out_specs, check_vma=False)
```

time: 146 us -> 148 us (1.014)
  blocking collectives: 0 us -> 17.6 us
  waiting for transfers between devices: 90 us -> 76.1 us
  starting transfers between devices: 29.7 us -> 33 us
  local copies, waits for them, and re-layouts: 4.5 us -> 1.33 us
  Pallas kernels: 18.3 us -> 16.5 us
    ppermute x45 -> x29, waiting for transfers between devices: 90 us -> 12.8 us  [send(): return lax.ppermute(value, axis, [(i, i ^ mask) for i in range(size)])]
    ppermute x0 -> x18, waiting for transfers between devices: none -> 63.3 us  [turn(): return lax.ppermute(value, 'dp', [(i, i ^ masks[i]) for i in range(n_dp)])]
    ppermute x0 -> x18, starting transfers between devices: none -> 17.9 us  [turn(): return lax.ppermute(value, 'dp', [(i, i ^ masks[i]) for i in range(n_dp)])]
    all_to_all x0 -> x1, blocking collectives: none -> 17.6 us  [kernel_body(): parts = lax.all_to_all(parts, 'dp', split_axis=0, concat_axis=0, tiled=True)]
    ppermute x45 -> x29, starting transfers between devices: 29.7 us -> 15.1 us  [send(): return lax.ppermute(value, axis, [(i, i ^ mask) for i in range(size)])]
    unnamed x12, local copies, waits for them, and re-layouts: 4.5 us -> 1.33 us
    pallas_call x2 -> x3, Pallas kernels: 9.45 us -> 7.99 us  [lay(): pl.pallas_call(functools.partial(lay_kernel, spans=spans, block=block, fr...]
  transfers between devices with their start and end apart: 45 -> 47, of which waited for: 25 -> 22; matrix products, arithmetic and copies ran while one was open for 0% -> 0% of each run, Pallas kernels for 7% -> 6%
where the time goes in v3:
time: 148 us
  waiting for transfers between devices  76.1 us (51%)
  starting transfers between devices  33 us (22%)
  blocking collectives  17.6 us (12%)
  Pallas kernels  16.5 us (11%)
  matrix products  2.4 us (2%)
    ppermute x18, waiting for transfers between devices, turn(): return lax.ppermute(value, 'dp', [(i, i ^ masks[i]) for i in range(n_dp)])  63.3 us
    ppermute x18, starting transfers between devices, turn(): return lax.ppermute(value, 'dp', [(i, i ^ masks[i]) for i in range(n_dp)])  17.9 us
    all_to_all x1, blocking collectives, kernel_body(): parts = lax.all_to_all(parts, 'dp', split_axis=0, concat_axis=0, tiled=True)  17.6 us
    ppermute x29, starting transfers between devices, send(): return lax.ppermute(value, axis, [(i, i ^ mask) for i in range(size)])  15.1 us
    ppermute x29, waiting for transfers between devices, send(): return lax.ppermute(value, axis, [(i, i ^ mask) for i in range(size)])  12.8 us
    pallas_call x3, Pallas kernels, lay(): pl.pallas_call(functools.partial(lay_kernel, spans=spans, block=block, fr...  7.99 us
    pallas_call x2, Pallas kernels, weights(): pl.pallas_call(functools.partial(weight_kernel, n_in=len(pieces), spans=s...  3.73 us
    pallas_call x1, Pallas kernels, new_master(): pl.pallas_call(master_kernel, out_shape=jax.ShapeDtypeStruct((cols, slab_...  3.11 us
  transfers between devices with their start and end apart: 47, of which 22 were waited for; matrix products, arithmetic and copies ran while one was open for 0% of the time, Pallas kernels for 6%

profile of v3, /device:TPU:0, one launch (start us, length us, event | category | flops | bytes accessed | tf_op | source)
XLA Modules:
  0.0 147.7 jit_solution(9970520894704827533)
XLA Ops:
  2.0 2.4 %convolution_convert_fusion.refs_0_ = bf16[128,256]{1,0:T(8,128)(2,1)S(1)} fusion(bf16[128,5120]{1,0:T(8,128)(2,1)S(1)} %copy-done, bf16[5120,256]{1,0:T(8,128)(2,1)} %projection.5), kind=kOutput, calls=%fused_computation | convolution fusion | flops 335577088 | bytes 3997696 | tf_op jit(solution)/shard_map/dot_general | solution.py:220
  4.4 3.1 %collective-permute-start.2 = (bf16[128,256]{1,0:T(8,128)(2,1)S(1)}, bf16[128,256]{1,0:T(8,128)(2,1)S(1)}, u32[]{:S(2)}, u32[]{:S(2)}) collective-permute-start(bf16[128,256]{1,0:T(8,128)(2,1)S(1)} %convolution_convert_fusion.refs_0_), channel_id=1, source_target_pairs={{0,1},{1,0},{2,3},{3,2},{4,5},{5,4},{6,7},{7,6},{8,9},{9,8},{10,11... | collective-permute-start | bytes 196616 | tf_op jit(solution)/shard_map/ppermute | solution.py:54
  7.5 2.6 %collective-permute-start.1 = (bf16[128,256]{1,0:T(8,128)(2,1)S(1)}, bf16[128,256]{1,0:T(8,128)(2,1)S(1)}, u32[]{:S(2)}, u32[]{:S(2)}) collective-permute-start(bf16[128,256]{1,0:T(8,128)(2,1)S(1)} %convolution_convert_fusion.refs_0_), channel_id=1, source_target_pairs={{0,2},{1,3},{2,0},{3,1},{4,6},{5,7},{6,4},{7,5},{8,10},{9,11},{10,... | collective-permute-start | bytes 196616 | tf_op jit(solution)/shard_map/ppermute | solution.py:54
  10.1 4.7 %collective-permute-done.1.refs_2_ = bf16[128,256]{1,0:T(8,128)(2,1)S(1)} collective-permute-done((bf16[128,256]{1,0:T(8,128)(2,1)S(1)}, bf16[128,256]{1,0:T(8,128)(2,1)S(1)}, u32[]{:S(2)}, u32[]{:S(2)}) %collective-permute-start.1) | collective-permute-done | bytes 65568 | tf_op jit(solution)/shard_map/ppermute | solution.py:54
  16.9 17.6 %all_to_all.11 = bf16[8,32,1728]{2,1,0:T(8,128)(2,1)S(1)} all-to-all(bf16[8,32,1728]{2,1,0:T(8,128)(2,1)S(1)} %bitcast.11), channel_id=1, replica_groups=mesh['dp'=8,'fsdp'=4] {'dp'}, dimensions={0} | all-to-all | bytes 1769472 | tf_op jit(solution)/shard_map/all_to_all | solution.py:230
  37.4 1.5 collective-permute-start.4
  38.9 3.4 %collective-permute-done.8.refs_6_ = bf16[32,1792]{1,0:T(8,128)(2,1)S(1)} collective-permute-done((bf16[32,1792]{1,0:T(8,128)(2,1)S(1)}, bf16[32,1792]{1,0:T(8,128)(2,1)S(1)}, u32[]{:S(2)}, u32[]{:S(2)}) %collective-permute-start.8) | collective-permute-done | bytes 114720 | tf_op jit(solution)/shard_map/ppermute | solution.py:54
  45.4 2.8 %shard_map.97 = (bf16[288,640]{1,0:T(8,128)(2,1)S(1)}, bf16[288,640]{1,0:T(8,128)(2,1)S(1)}, bf16[192,640]{1,0:T(8,128)(2,1)S(1)}, bf16[192,640]{1,0:T(8,128)(2,1)S(1)}, bf16[1728,640]{1,0:T(8,128)(2,1)S(1)}) custom-call(bf16[5120,256]{1,0:T(8,128)(2,1)S(1)} %copy-done.1, f32[1728,640]{1,0:T(8,128)S(1)} %bitcast.9, ...), custom_call_target="tpu_custom_call" | custom-call | flops 880803840 | bytes 6881280 | tf_op jit(solution)/shard_map/pallas_call | solution.py:122
  50.4 12.3 %collective-permute-done.11.refs_2_ = bf16[384,640]{1,0:T(8,128)(2,1)S(1)} collective-permute-done((bf16[384,640]{1,0:T(8,128)(2,1)S(1)}, bf16[384,640]{1,0:T(8,128)(2,1)S(1)}, u32[]{:S(2)}, u32[]{:S(2)}) %collective-permute-start.11) | collective-permute-done | bytes 491552 | tf_op jit(solution)/shard_map/ppermute | solution.py:255
  63.9 3.1 %shard_map.96 = f32[1728,640]{1,0:T(8,128)} custom-call(bf16[5120,256]{1,0:T(8,128)(2,1)S(1)} %copy-done.1, f32[1728,640]{1,0:T(8,128)S(1)} %bitcast.10, bf16[1792,256]{1,0:T(8,128)(2,1)S(1)} %get-tuple-element.51.tall.refs_0_), custom_call_target="tpu_custom_call" | custom-call | flops 566231040 | bytes 8847360 | tf_op jit(solution)/shard_map/pallas_call | solution.py:145
  67.7 1.6 %collective-permute-start.14 = (bf16[192,640]{1,0:T(8,128)(2,1)S(1)}, bf16[192,640]{1,0:T(8,128)(2,1)S(1)}, u32[]{:S(2)}, u32[]{:S(2)}) collective-permute-start(bf16[192,640]{1,0:T(8,128)(2,1)S(1)} %get-tuple-element.81), channel_id=1, source_target_pairs={{0,8},{4,20},{8,0},{12,28},{16,24},{20,4},{24,16},{28,12},{1,9},{5... | collective-permute-start | bytes 737288 | tf_op jit(solution)/shard_map/ppermute | solution.py:255
  69.3 2.3 %collective-permute-done.15.refs_3_ = bf16[288,640]{1,0:T(8,128)(2,1)S(1)} collective-permute-done((bf16[288,640]{1,0:T(8,128)(2,1)S(1)}, bf16[288,640]{1,0:T(8,128)(2,1)S(1)}, u32[]{:S(2)}, u32[]{:S(2)}) %collective-permute-start.15) | collective-permute-done | bytes 368672 | tf_op jit(solution)/shard_map/ppermute | solution.py:255
  72.6 3.9 %collective-permute-done.16.refs_11_ = bf16[288,640]{1,0:T(8,128)(2,1)S(1)} collective-permute-done((bf16[288,640]{1,0:T(8,128)(2,1)S(1)}, bf16[288,640]{1,0:T(8,128)(2,1)S(1)}, u32[]{:S(2)}, u32[]{:S(2)}) %collective-permute-start.16) | collective-permute-done | bytes 368672 | tf_op jit(solution)/shard_map/ppermute | solution.py:255
  82.1 7.4 %collective-permute-done.20.refs_12_ = bf16[384,640]{1,0:T(8,128)(2,1)S(1)} collective-permute-done((bf16[384,640]{1,0:T(8,128)(2,1)S(1)}, bf16[384,640]{1,0:T(8,128)(2,1)S(1)}, u32[]{:S(2)}, u32[]{:S(2)}) %collective-permute-start.20) | collective-permute-done | bytes 491552 | tf_op jit(solution)/shard_map/ppermute | solution.py:255
  90.5 3.4 %collective-permute-done.19.refs_4_ = bf16[384,640]{1,0:T(8,128)(2,1)S(1)} collective-permute-done((bf16[384,640]{1,0:T(8,128)(2,1)S(1)}, bf16[384,640]{1,0:T(8,128)(2,1)S(1)}, u32[]{:S(2)}, u32[]{:S(2)}) %collective-permute-start.19) | collective-permute-done | bytes 491552 | tf_op jit(solution)/shard_map/ppermute | solution.py:255
  94.0 3.5 %collective-permute-done.29.refs_13_ = bf16[288,640]{1,0:T(8,128)(2,1)S(1)} collective-permute-done((bf16[288,640]{1,0:T(8,128)(2,1)S(1)}, bf16[288,640]{1,0:T(8,128)(2,1)S(1)}, u32[]{:S(2)}, u32[]{:S(2)}) %collective-permute-start.29) | collective-permute-done | bytes 368672 | tf_op jit(solution)/shard_map/ppermute | solution.py:255
  97.4 1.5 %collective-permute-done.26.refs_5_ = bf16[288,640]{1,0:T(8,128)(2,1)S(1)} collective-permute-done((bf16[288,640]{1,0:T(8,128)(2,1)S(1)}, bf16[288,640]{1,0:T(8,128)(2,1)S(1)}, u32[]{:S(2)}, u32[]{:S(2)}) %collective-permute-start.26) | collective-permute-done | bytes 368672 | tf_op jit(solution)/shard_map/ppermute | solution.py:255
  100.8 5.3 %collective-permute-done.28.refs_13_ = bf16[192,640]{1,0:T(8,128)(2,1)S(1)} collective-permute-done((bf16[192,640]{1,0:T(8,128)(2,1)S(1)}, bf16[192,640]{1,0:T(8,128)(2,1)S(1)}, u32[]{:S(2)}, u32[]{:S(2)}) %collective-permute-start.28) | collective-permute-done | bytes 245792 | tf_op jit(solution)/shard_map/ppermute | solution.py:255
  109.0 13.1 %collective-permute-done.36.refs_5_ = bf16[192,640]{1,0:T(8,128)(2,1)S(1)} collective-permute-done((bf16[192,640]{1,0:T(8,128)(2,1)S(1)}, bf16[192,640]{1,0:T(8,128)(2,1)S(1)}, u32[]{:S(2)}, u32[]{:S(2)}) %collective-permute-start.36) | collective-permute-done | bytes 245792 | tf_op jit(solution)/shard_map/ppermute | solution.py:255
  125.4 3.3 %shard_map.98.refs_0_ = bf16[1728,5120]{1,0:T(8,128)(2,1)} custom-call(bf16[1728,640]{1,0:T(8,128)(2,1)S(1)} %get-tuple-element.52.refs_0_.refs_8_.refs_1_.refs_9_, bf16[1728,640]{1,0:T(8,128)(2,1)S(1)} %collective-permute-done.10.refs_1_.refs_9_.refs_2_.refs_10_, bf16[384,640]{1,0:T(8,128)(2,1)S(1)} %collective-permute-done.11.refs_2_, ...), custom_call_target="tpu_custom_call" | custom-call | bytes 29491200 | tf_op jit(solution)/shard_map/pallas_call | solution.py:197
  128.7 5.9 %collective-permute-done.37.refs_7_ = bf16[288,640]{1,0:T(8,128)(2,1)S(1)} collective-permute-done((bf16[288,640]{1,0:T(8,128)(2,1)S(1)}, bf16[288,640]{1,0:T(8,128)(2,1)S(1)}, u32[]{:S(2)}, u32[]{:S(2)}) %collective-permute-start.37) | collective-permute-done | bytes 368672 | tf_op jit(solution)/shard_map/ppermute | solution.py:255
  137.1 2.7 %shard_map.99.refs_0_ = bf16[1728,5120]{1,0:T(8,128)(2,1)} custom-call(bf16[1728,5120]{1,0:T(8,128)(2,1)} %shard_map.98.refs_0_, bf16[1728,640]{1,0:T(8,128)(2,1)S(1)} %get-tuple-element.52.refs_0_.refs_8_.refs_1_.refs_9_, bf16[1728,640]{1,0:T(8,128)(2,1)S(1)} %collective-permute-done.10.refs_1_.refs_9_.refs_2_.refs_10_, ...), custom_call_target="tpu_custom_call", output_to_operand_aliasing={{}: (0, {})} | custom-call | bytes 26542080 | tf_op jit(solution)/shard_map/pallas_call | solution.py:197
  139.8 4.0 %collective-permute-done.43.refs_7_ = bf16[192,640]{1,0:T(8,128)(2,1)S(1)} collective-permute-done((bf16[192,640]{1,0:T(8,128)(2,1)S(1)}, bf16[192,640]{1,0:T(8,128)(2,1)S(1)}, u32[]{:S(2)}, u32[]{:S(2)}) %collective-permute-start.43) | collective-permute-done | bytes 245792 | tf_op jit(solution)/shard_map/ppermute | solution.py:255
  145.6 2.0 %shard_map.100 = bf16[1728,5120]{1,0:T(8,128)(2,1)} custom-call(bf16[1728,5120]{1,0:T(8,128)(2,1)} %shard_map.99.refs_0_, bf16[1728,640]{1,0:T(8,128)(2,1)S(1)} %get-tuple-element.52.refs_0_.refs_8_.refs_1_.refs_9_, bf16[1728,640]{1,0:T(8,128)(2,1)S(1)} %collective-permute-done.10.refs_1_.refs_9_.refs_2_.refs_10_, ...), custom_call_target="tpu_custom_call", output_to_operand_aliasing={{}: (0, {})} | custom-call | bytes 23592960 | tf_op jit(solution)/shard_map/pallas_call | solution.py:197
  (92 shorter events, 33.7 us)
Async XLA Ops:
  48.2 18.8 %collective-permute-start.10 = (bf16[1728,640]{1,0:T(8,128)(2,1)S(1)}, bf16[1728,640]{1,0:T(8,128)(2,1)S(1)}, u32[]{:S(2)}, u32[]{:S(2)}) collective-permute-start(bf16[1728,640]{1,0:T(8,128)(2,1)S(1)} %get-tuple-element.52.refs_0_.refs_8_.refs_1_.refs_9_), channel_id=1, source_target_pairs={{0,4},{4,0},{8,12},{12,8},{16,20},{20,16},{24,28},{28,24},{1,5},{5... | collective-permute-start | bytes 6635528 | tf_op jit(solution)/shard_map/ppermute | solution.py:54
  48.6 14.0 %collective-permute-start.11 = (bf16[384,640]{1,0:T(8,128)(2,1)S(1)}, bf16[384,640]{1,0:T(8,128)(2,1)S(1)}, u32[]{:S(2)}, u32[]{:S(2)}) collective-permute-start(bf16[384,640]{1,0:T(8,128)(2,1)S(1)} %get-tuple-element.63), channel_id=1, source_target_pairs={{0,8},{4,20},{8,0},{12,28},{16,24},{20,4},{24,16},{28,12},{1,9},{5... | collective-permute-start | bytes 1474568 | tf_op jit(solution)/shard_map/ppermute | solution.py:255
  49.8 12.9 %collective-permute-start.12 = (bf16[384,640]{1,0:T(8,128)(2,1)S(1)}, bf16[384,640]{1,0:T(8,128)(2,1)S(1)}, u32[]{:S(2)}, u32[]{:S(2)}) collective-permute-start(bf16[384,640]{1,0:T(8,128)(2,1)S(1)} %get-tuple-element.64), channel_id=1, source_target_pairs={{0,16},{4,12},{8,24},{12,4},{16,0},{20,28},{24,8},{28,20},{1,17},{... | collective-permute-start | bytes 1474568 | tf_op jit(solution)/shard_map/ppermute | solution.py:255
  62.6 9.0 %collective-permute-start.13 = (bf16[384,640]{1,0:T(8,128)(2,1)S(1)}, bf16[384,640]{1,0:T(8,128)(2,1)S(1)}, u32[]{:S(2)}, u32[]{:S(2)}) collective-permute-start(bf16[384,640]{1,0:T(8,128)(2,1)S(1)} %collective-permute-done.11.refs_2_), channel_id=1, source_target_pairs={{0,4},{4,0},{8,12},{12,8},{16,20},{20,16},{24,28},{28,24},{1,5},{5... | collective-permute-start | bytes 1474568 | tf_op jit(solution)/shard_map/ppermute | solution.py:54
  62.7 9.0 %collective-permute-start.22 = (bf16[384,640]{1,0:T(8,128)(2,1)S(1)}, bf16[384,640]{1,0:T(8,128)(2,1)S(1)}, u32[]{:S(2)}, u32[]{:S(2)}) collective-permute-start(bf16[384,640]{1,0:T(8,128)(2,1)S(1)} %collective-permute-done.12.refs_10_), channel_id=1, source_target_pairs={{0,4},{4,0},{8,12},{12,8},{16,20},{20,16},{24,28},{28,24},{1,5},{5... | collective-permute-start | bytes 1474568 | tf_op jit(solution)/shard_map/ppermute | solution.py:54
  63.2 8.5 %collective-permute-start.15 = (bf16[288,640]{1,0:T(8,128)(2,1)S(1)}, bf16[288,640]{1,0:T(8,128)(2,1)S(1)}, u32[]{:S(2)}, u32[]{:S(2)}) collective-permute-start(bf16[288,640]{1,0:T(8,128)(2,1)S(1)} %get-tuple-element.71), channel_id=1, source_target_pairs={{0,8},{4,20},{8,0},{12,28},{16,24},{20,4},{24,16},{28,12},{1,9},{5... | collective-permute-start | bytes 1105928 | tf_op jit(solution)/shard_map/ppermute | solution.py:255
  67.0 9.5 %collective-permute-start.16 = (bf16[288,640]{1,0:T(8,128)(2,1)S(1)}, bf16[288,640]{1,0:T(8,128)(2,1)S(1)}, u32[]{:S(2)}, u32[]{:S(2)}) collective-permute-start(bf16[288,640]{1,0:T(8,128)(2,1)S(1)} %get-tuple-element.74), channel_id=1, source_target_pairs={{0,16},{4,12},{8,24},{12,4},{16,0},{20,28},{24,8},{28,20},{1,17},{... | collective-permute-start | bytes 1105928 | tf_op jit(solution)/shard_map/ppermute | solution.py:255
  67.7 10.7 %collective-permute-start.14 = (bf16[192,640]{1,0:T(8,128)(2,1)S(1)}, bf16[192,640]{1,0:T(8,128)(2,1)S(1)}, u32[]{:S(2)}, u32[]{:S(2)}) collective-permute-start(bf16[192,640]{1,0:T(8,128)(2,1)S(1)} %get-tuple-element.81), channel_id=1, source_target_pairs={{0,8},{4,20},{8,0},{12,28},{16,24},{20,4},{24,16},{28,12},{1,9},{5... | collective-permute-start | bytes 737288 | tf_op jit(solution)/shard_map/ppermute | solution.py:255
  71.7 7.5 %collective-permute-start.23 = (bf16[192,640]{1,0:T(8,128)(2,1)S(1)}, bf16[192,640]{1,0:T(8,128)(2,1)S(1)}, u32[]{:S(2)}, u32[]{:S(2)}) collective-permute-start(bf16[192,640]{1,0:T(8,128)(2,1)S(1)} %get-tuple-element.73), channel_id=1, source_target_pairs={{0,16},{4,12},{8,24},{12,4},{16,0},{20,28},{24,8},{28,20},{1,17},{... | collective-permute-start | bytes 737288 | tf_op jit(solution)/shard_map/ppermute | solution.py:255
  77.4 12.1 %collective-permute-start.20 = (bf16[384,640]{1,0:T(8,128)(2,1)S(1)}, bf16[384,640]{1,0:T(8,128)(2,1)S(1)}, u32[]{:S(2)}, u32[]{:S(2)}) collective-permute-start(bf16[384,640]{1,0:T(8,128)(2,1)S(1)} %get-tuple-element.64), channel_id=1, source_target_pairs={{0,8},{4,20},{8,0},{12,28},{16,24},{20,4},{24,16},{28,12},{1,9},{5... | collective-permute-start | bytes 1474568 | tf_op jit(solution)/shard_map/ppermute | solution.py:255
  79.7 14.2 %collective-permute-start.19 = (bf16[384,640]{1,0:T(8,128)(2,1)S(1)}, bf16[384,640]{1,0:T(8,128)(2,1)S(1)}, u32[]{:S(2)}, u32[]{:S(2)}) collective-permute-start(bf16[384,640]{1,0:T(8,128)(2,1)S(1)} %get-tuple-element.63), channel_id=1, source_target_pairs={{0,16},{4,12},{8,24},{12,4},{16,0},{20,28},{24,8},{28,20},{1,17},{... | collective-permute-start | bytes 1474568 | tf_op jit(solution)/shard_map/ppermute | solution.py:255
  80.8 16.6 %collective-permute-start.29 = (bf16[288,640]{1,0:T(8,128)(2,1)S(1)}, bf16[288,640]{1,0:T(8,128)(2,1)S(1)}, u32[]{:S(2)}, u32[]{:S(2)}) collective-permute-start(bf16[288,640]{1,0:T(8,128)(2,1)S(1)} %get-tuple-element.74), channel_id=1, source_target_pairs={{0,8},{4,20},{8,0},{12,28},{16,24},{20,4},{24,16},{28,12},{1,9},{5... | collective-permute-start | bytes 1105928 | tf_op jit(solution)/shard_map/ppermute | solution.py:255
  89.5 9.4 %collective-permute-start.26 = (bf16[288,640]{1,0:T(8,128)(2,1)S(1)}, bf16[288,640]{1,0:T(8,128)(2,1)S(1)}, u32[]{:S(2)}, u32[]{:S(2)}) collective-permute-start(bf16[288,640]{1,0:T(8,128)(2,1)S(1)} %get-tuple-element.71), channel_id=1, source_target_pairs={{0,16},{4,12},{8,24},{12,4},{16,0},{20,28},{24,8},{28,20},{1,17},{... | collective-permute-start | bytes 1105928 | tf_op jit(solution)/shard_map/ppermute | solution.py:255
  98.9 8.2 %collective-permute-start.30 = (bf16[288,640]{1,0:T(8,128)(2,1)S(1)}, bf16[288,640]{1,0:T(8,128)(2,1)S(1)}, u32[]{:S(2)}, u32[]{:S(2)}) collective-permute-start(bf16[288,640]{1,0:T(8,128)(2,1)S(1)} %collective-permute-done.29.refs_13_), channel_id=1, source_target_pairs={{0,4},{4,0},{8,12},{12,8},{16,20},{20,16},{24,28},{28,24},{1,5},{5... | collective-permute-start | bytes 1105928 | tf_op jit(solution)/shard_map/ppermute | solution.py:54
  99.2 8.8 %collective-permute-start.21 = (bf16[384,640]{1,0:T(8,128)(2,1)S(1)}, bf16[384,640]{1,0:T(8,128)(2,1)S(1)}, u32[]{:S(2)}, u32[]{:S(2)}) collective-permute-start(bf16[384,640]{1,0:T(8,128)(2,1)S(1)} %collective-permute-done.19.refs_4_), channel_id=1, source_target_pairs={{0,4},{4,0},{8,12},{12,8},{16,20},{20,16},{24,28},{28,24},{1,5},{5... | collective-permute-start | bytes 1474568 | tf_op jit(solution)/shard_map/ppermute | solution.py:54
  99.4 8.6 %collective-permute-start.34 = (bf16[384,640]{1,0:T(8,128)(2,1)S(1)}, bf16[384,640]{1,0:T(8,128)(2,1)S(1)}, u32[]{:S(2)}, u32[]{:S(2)}) collective-permute-start(bf16[384,640]{1,0:T(8,128)(2,1)S(1)} %collective-permute-done.20.refs_12_), channel_id=1, source_target_pairs={{0,4},{4,0},{8,12},{12,8},{16,20},{20,16},{24,28},{28,24},{1,5},{5... | collective-permute-start | bytes 1474568 | tf_op jit(solution)/shard_map/ppermute | solution.py:54
  99.7 7.4 %collective-permute-start.31 = (bf16[288,640]{1,0:T(8,128)(2,1)S(1)}, bf16[288,640]{1,0:T(8,128)(2,1)S(1)}, u32[]{:S(2)}, u32[]{:S(2)}) collective-permute-start(bf16[288,640]{1,0:T(8,128)(2,1)S(1)} %collective-permute-done.26.refs_5_), channel_id=1, source_target_pairs={{0,4},{4,0},{8,12},{12,8},{16,20},{20,16},{24,28},{28,24},{1,5},{5... | collective-permute-start | bytes 1105928 | tf_op jit(solution)/shard_map/ppermute | solution.py:54
  106.1 16.5 %collective-permute-start.27 = (bf16[384,640]{1,0:T(8,128)(2,1)S(1)}, bf16[384,640]{1,0:T(8,128)(2,1)S(1)}, u32[]{:S(2)}, u32[]{:S(2)}) collective-permute-start(bf16[384,640]{1,0:T(8,128)(2,1)S(1)} %collective-permute-done.11.refs_2_), channel_id=1, source_target_pairs={{0,16},{4,12},{8,24},{12,4},{16,0},{20,28},{24,8},{28,20},{1,17},{... | collective-permute-start | bytes 1474568 | tf_op jit(solution)/shard_map/ppermute | solution.py:255
  107.1 15.5 %collective-permute-start.32 = (bf16[384,640]{1,0:T(8,128)(2,1)S(1)}, bf16[384,640]{1,0:T(8,128)(2,1)S(1)}, u32[]{:S(2)}, u32[]{:S(2)}) collective-permute-start(bf16[384,640]{1,0:T(8,128)(2,1)S(1)} %collective-permute-done.12.refs_10_), channel_id=1, source_target_pairs={{0,8},{4,20},{8,0},{12,28},{16,24},{20,4},{24,16},{28,12},{1,9},{5... | collective-permute-start | bytes 1474568 | tf_op jit(solution)/shard_map/ppermute | solution.py:255
  108.0 14.1 %collective-permute-start.36 = (bf16[192,640]{1,0:T(8,128)(2,1)S(1)}, bf16[192,640]{1,0:T(8,128)(2,1)S(1)}, u32[]{:S(2)}, u32[]{:S(2)}) collective-permute-start(bf16[192,640]{1,0:T(8,128)(2,1)S(1)} %get-tuple-element.81), channel_id=1, source_target_pairs={{0,16},{4,12},{8,24},{12,4},{16,0},{20,28},{24,8},{28,20},{1,17},{... | collective-permute-start | bytes 737288 | tf_op jit(solution)/shard_map/ppermute | solution.py:255
  123.2 11.4 %collective-permute-start.37 = (bf16[288,640]{1,0:T(8,128)(2,1)S(1)}, bf16[288,640]{1,0:T(8,128)(2,1)S(1)}, u32[]{:S(2)}, u32[]{:S(2)}) collective-permute-start(bf16[288,640]{1,0:T(8,128)(2,1)S(1)} %collective-permute-done.15.refs_3_), channel_id=1, source_target_pairs={{0,16},{4,12},{8,24},{12,4},{16,0},{20,28},{24,8},{28,20},{1,17},{... | collective-permute-start | bytes 1105928 | tf_op jit(solution)/shard_map/ppermute | solution.py:255
  124.2 10.4 %collective-permute-start.40 = (bf16[288,640]{1,0:T(8,128)(2,1)S(1)}, bf16[288,640]{1,0:T(8,128)(2,1)S(1)}, u32[]{:S(2)}, u32[]{:S(2)}) collective-permute-start(bf16[288,640]{1,0:T(8,128)(2,1)S(1)} %collective-permute-done.16.refs_11_), channel_id=1, source_target_pairs={{0,8},{4,20},{8,0},{12,28},{16,24},{20,4},{24,16},{28,12},{1,9},{5... | collective-permute-start | bytes 1105928 | tf_op jit(solution)/shard_map/ppermute | solution.py:255
  135.1 8.6 %collective-permute-start.43 = (bf16[192,640]{1,0:T(8,128)(2,1)S(1)}, bf16[192,640]{1,0:T(8,128)(2,1)S(1)}, u32[]{:S(2)}, u32[]{:S(2)}) collective-permute-start(bf16[192,640]{1,0:T(8,128)(2,1)S(1)} %collective-permute-done.14.refs_3_), channel_id=1, source_target_pairs={{0,16},{4,12},{8,24},{12,4},{16,0},{20,28},{24,8},{28,20},{1,17},{... | collective-permute-start | bytes 737288 | tf_op jit(solution)/shard_map/ppermute | solution.py:255
  136.2 7.6 %collective-permute-start.44 = (bf16[192,640]{1,0:T(8,128)(2,1)S(1)}, bf16[192,640]{1,0:T(8,128)(2,1)S(1)}, u32[]{:S(2)}, u32[]{:S(2)}) collective-permute-start(bf16[192,640]{1,0:T(8,128)(2,1)S(1)} %collective-permute-done.23.refs_11_), channel_id=1, source_target_pairs={{0,8},{4,20},{8,0},{12,28},{16,24},{20,4},{24,16},{28,12},{1,9},{5... | collective-permute-start | bytes 737288 | tf_op jit(solution)/shard_map/ppermute | solution.py:255
  (29 other events, 229.8 us)

commit v4 on v3

--- a/solution.py
+++ b/solution.py
@@ -54,29 +54,71 @@
     return lax.ppermute(value, axis, [(i, i ^ mask) for i in range(size)])
 
 
-def order(size):
-    return (0, *reversed(range(1, size)))
-
-
-def partial_kernel(grad_t, *refs):
-    pieces, out, tokens = refs[:-2], refs[-2], refs[-1]
+def project_kernel(acts, projection, out, total):
+    step = pl.program_id(0)
+    part = jnp.dot(acts[...], projection[...], preferred_element_type=jnp.float32)
+
+    @pl.when(step == 0)
+    def _():
+        total[...] = part
+
+    @pl.when(step > 0)
+    def _():
+        total[...] += part
+
+    @pl.when(step == pl.num_programs(0) - 1)
+    def _():
+        out[...] = total[...].astype(jnp.bfloat16)
+
+
+def project(acts, projection, depth):
+    tokens, width = acts.shape
+    rank = projection.shape[1]
+    return pl.pallas_call(
+        project_kernel,
+        out_shape=jax.ShapeDtypeStruct((tokens, rank), jnp.bfloat16),
+        grid=(width // depth,),
+        in_specs=[
+            pl.BlockSpec((tokens, depth), lambda i: (0, i)),
+            pl.BlockSpec((depth, rank), lambda i: (i, 0)),
+        ],
+        out_specs=VMEM,
+        scratch_shapes=[pltpu.VMEM((tokens, rank), jnp.float32)],
+        compiler_params=pltpu.CompilerParams(vmem_limit_bytes=56 * 2**20),
+        cost_estimate=pl.CostEstimate(
+            flops=2 * tokens * width * rank, bytes_accessed=2 * (tokens + rank) * width, transcendentals=0
+        ),
+    )(acts, projection)
+
+
+def partial_kernel(grad_t, *refs, n_fsdp, n_dp):
+    pieces, outs, (tokens, across) = refs[:n_fsdp], refs[n_fsdp : n_fsdp + n_dp], refs[n_fsdp + n_dp :]
     count = pieces[0].shape[0]
+    rows = outs[0].shape[0]
     me = lax.axis_index("fsdp")
-    for k, piece in zip(order(len(pieces)), pieces):
+    for k, piece in enumerate(pieces):
         tokens[pl.ds(pl.multiple_of((me ^ k) * count, count), count), :] = piece[...]
-    out[...] = lax.dot_general(
-        tokens[...].T, grad_t[...], (((1,), (1,)), ((), ())), preferred_element_type=jnp.float32
+    across[...] = tokens[...].T
+    me = lax.axis_index("dp")
+    left = jnp.concatenate(
+        [across[pl.ds(pl.multiple_of((me ^ k) * rows, rows), rows), :] for k in range(n_dp)], axis=0
+    )
+    result = lax.dot_general(
+        left, grad_t[...], (((1,), (1,)), ((), ())), preferred_element_type=jnp.float32
     ).astype(jnp.bfloat16)
-
-
-def adam_kernel(moment_one, moment_two, parts, one_new, two_new, update):
-    rows, cols = moment_one.shape
-    grad = parts[:rows, :].astype(jnp.float32)
-    for first in range(rows, parts.shape[0], rows):
-        grad = grad + parts[first : first + rows, :].astype(jnp.float32)
+    for k, out in enumerate(outs):
+        out[...] = result[k * rows : (k + 1) * rows, :]
+
+
+def adam_kernel(moment_one, moment_two, *refs):
+    parts, (one_new, two_new, update) = refs[:-3], refs[-3:]
+    grad = parts[0][...].astype(jnp.float32)
+    for part in parts[1:]:
+        grad = grad + part[...].astype(jnp.float32)
     one, two, value = adam(grad, moment_one[...], moment_two[...])
     one_new[...] = one
     two_new[...] = two
+    cols = value.shape[1]
     update[...] = jnp.zeros_like(update)
     update[:, :cols] = value
 
@@ -217,17 +259,20 @@
     wide = -(-cols // 128) * 128
     master_t = master.T
 
-    projected = jnp.dot(acts, projection, preferred_element_type=jnp.float32).astype(jnp.bfloat16)
-    tokens = [projected if k == 0 else send(projected, "fsdp", n_fsdp, k) for k in order(n_fsdp)]
+    projected = project(acts, projection, acts.shape[1] // 5)
+    tokens = [projected] + [send(projected, "fsdp", n_fsdp, k) for k in range(1, n_fsdp)]
     parts = pl.pallas_call(
-        partial_kernel,
-        out_shape=jax.ShapeDtypeStruct((rank, cols), jnp.bfloat16),
+        functools.partial(partial_kernel, n_fsdp=n_fsdp, n_dp=n_dp),
+        out_shape=[jax.ShapeDtypeStruct((rows, cols), jnp.bfloat16)] * n_dp,
         in_specs=[VMEM] * (1 + n_fsdp),
-        out_specs=VMEM,
-        scratch_shapes=[pltpu.VMEM((n_fsdp * projected.shape[0], rank), jnp.bfloat16)],
+        out_specs=[VMEM] * n_dp,
+        scratch_shapes=[
+            pltpu.VMEM((n_fsdp * projected.shape[0], rank), jnp.bfloat16),
+            pltpu.VMEM((rank, n_fsdp * projected.shape[0]), jnp.bfloat16),
+        ],
         compiler_params=pltpu.CompilerParams(vmem_limit_bytes=16 * 2**20),
     )(grad_out.T, *tokens)
-    parts = lax.all_to_all(parts, "dp", split_axis=0, concat_axis=0, tiled=True)
+    parts = [parts[k] if k == 0 else send(parts[k], "dp", n_dp, k) for k in (0, 2, 4, 6, 7, 3, 5, 1)]
     moment_one_new, moment_two_new, update = pl.pallas_call(
         adam_kernel,
         out_shape=[
@@ -235,10 +280,10 @@
             jax.ShapeDtypeStruct(moment_two.shape, jnp.float32),
             jax.ShapeDtypeStruct((rows, wide), jnp.bfloat16),
         ],
-        in_specs=[VMEM] * 3,
+        in_specs=[VMEM] * (2 + n_dp),
         out_specs=[VMEM] * 3,
         compiler_params=pltpu.CompilerParams(vmem_limit_bytes=16 * 2**20),
-    )(moment_one, moment_two, parts)
+    )(moment_one, moment_two, *parts)
 
     def hop(value, mask):
         return send(value, "dp", n_dp, mask)
@@ -255,14 +300,14 @@
         return lax.ppermute(value, "dp", [(i, i ^ masks[i]) for i in range(n_dp)])
 
     half = cols // 2
-    block = cols // 18
-    counts = (4 * block, 3 * block, 2 * block)
+    block = cols // 12
+    counts = (3 * block, 3 * block)
     chunks = len(counts)
     starts = [sum(counts[:at]) for at in range(chunks)]
     spans = [((first, count), (half + first, count)) for first, count in zip(starts, counts)]
     tall, *early = weights(projection, master_t, updates, spans[0], block)
     late = [span for both in spans[1:] for span in both]
-    *late, whole = weights(projection, master_t, [tall], late + [(0, cols)], block)
+    late = weights(projection, master_t, [tall], late, block)
     own = [early] + [late[2 * at : 2 * at + 2] for at in range(chunks - 1)]
     master_new = new_master(projection, master_t, tall, cols // 4)
 
@@ -272,7 +317,6 @@
     got, over = [], []
     out = None
     shape = (cols, n_dp * slab_rows)
-    whole_c = hop(whole, 1)
     for step in range(6 * chunks):
         phase, rest = divmod(step, 2 * chunks)
         at, part = divmod(rest, 2)
@@ -282,15 +326,17 @@
             value, which = own[at][1 - part], part
         else:
             value, which = got[2 * at + part], 1 - part
-        earlier = got[step - 3 : step - 2] if step >= 3 else []
-        if step == 3:
-            earlier += [whole_c, master_new]
-        if step >= 5 and part == 1:
-            earlier += over[step - 5 : step - 3]
+        earlier = got[step - 2 : step - 1] if step >= 2 else []
+        earlier += over[step - 4 : step - 3] if step >= 4 else []
+        if step == 4:
+            earlier.append(master_new)
+        if step == 10:
+            earlier.append(whole_c)
         got.append(turn(after(value, earlier), which))
-        if part == 1:
-            for which in (step - 1, step):
-                over.append(hop(after(got[which], got[step - 1 :] + ([] if out is None else [out])), 1))
+        over.append(hop(after(got[step], [] if out is None else [out]), 1))
+        if step == 0:
+            (whole,) = weights(projection, master_t, [after(tall, got)], [(0, cols)], block)
+            whole_c = hop(whole, 1)
         if phase == 2 and part == 1:
             laid, placed = [], []
             for part, (first, count) in enumerate(spans[at]):
@@ -301,7 +347,7 @@
                 if part == 1:
                     masks = ((0, 0), (1, 1), (4, 2), (3, 5), (2, 4), (5, 3), (6, 6), (7, 7))
                 placed.append((first, count, masks))
-            out = lay(out, shape, placed, laid, block)
+            out = lay(out, shape, placed, laid, block // 2 if block % 32 == 0 else block)
     return (moment_one_new, moment_two_new, master_new.T, out.T)
 
 

time: 148 us -> 144 us (0.973)
  blocking collectives: 17.6 us -> 0 us
  waiting for transfers between devices: 76.1 us -> 89.6 us
  starting transfers between devices: 33 us -> 29.1 us
  Pallas kernels: 16.5 us -> 20.1 us
  local copies, waits for them, and re-layouts: 1.33 us -> 4.2 us
  matrix products: 2.4 us -> 0 us
    all_to_all x1 -> x0, blocking collectives: 17.6 us -> none  [kernel_body(): parts = lax.all_to_all(parts, 'dp', split_axis=0, concat_axis=0, tiled=True)]
    ppermute x29 -> x30, waiting for transfers between devices: 12.8 us -> 21.8 us  [send(): return lax.ppermute(value, axis, [(i, i ^ mask) for i in range(size)])]
    ppermute x18 -> x12, starting transfers between devices: 17.9 us -> 9.79 us  [turn(): return lax.ppermute(value, 'dp', [(i, i ^ masks[i]) for i in range(n_dp)])]
    pallas_call x1 -> x2, Pallas kernels: 0.71 us -> 5.93 us  [the longest x1 5.18 us: project(): pl.pallas_call(project_kernel, out_shape=jax.ShapeDtypeStruct((tokens, ra...]
    ppermute x18 -> x12, waiting for transfers between devices: 63.3 us -> 67.7 us  [turn(): return lax.ppermute(value, 'dp', [(i, i ^ masks[i]) for i in range(n_dp)])]
    ppermute x29 -> x30, starting transfers between devices: 15.1 us -> 19.4 us  [send(): return lax.ppermute(value, axis, [(i, i ^ mask) for i in range(size)])]
    unnamed x12, local copies, waits for them, and re-layouts: 1.33 us -> 4.2 us
    dot_general x1 -> x0, matrix products: 2.4 us -> none  [kernel_body(): jnp.dot(acts, projection, preferred_element_type=jnp.float32)]
  transfers between devices with their start and end apart: 47 -> 42, of which waited for: 22 -> 19; matrix products, arithmetic and copies ran while one was open for 0% -> 0% of each run, Pallas kernels for 6% -> 6%
where the time goes in v4:
time: 144 us
  waiting for transfers between devices  89.6 us (62%)
  starting transfers between devices  29.1 us (20%)
  Pallas kernels  20.1 us (14%)
  local copies, waits for them, and re-layouts  4.2 us (3%)
    ppermute x12, waiting for transfers between devices, turn(): return lax.ppermute(value, 'dp', [(i, i ^ masks[i]) for i in range(n_dp)])  67.7 us
    ppermute x30, waiting for transfers between devices, send(): return lax.ppermute(value, axis, [(i, i ^ mask) for i in range(size)])  21.8 us
    ppermute x30, starting transfers between devices, send(): return lax.ppermute(value, axis, [(i, i ^ mask) for i in range(size)])  19.4 us
    ppermute x12, starting transfers between devices, turn(): return lax.ppermute(value, 'dp', [(i, i ^ masks[i]) for i in range(n_dp)])  9.79 us
    pallas_call x2, Pallas kernels, lay(): pl.pallas_call(functools.partial(lay_kernel, spans=spans, block=block, fr...  7.23 us
    pallas_call x1, Pallas kernels, project(): pl.pallas_call(project_kernel, out_shape=jax.ShapeDtypeStruct((tokens, ra...  5.18 us
    unnamed x12, local copies, waits for them, and re-layouts  4.2 us
    pallas_call x1, Pallas kernels, new_master(): pl.pallas_call(master_kernel, out_shape=jax.ShapeDtypeStruct((cols, slab_...  3.15 us
  transfers between devices with their start and end apart: 42, of which 19 were waited for; matrix products, arithmetic and copies ran while one was open for 0% of the time, Pallas kernels for 6%

profile of v4, /device:TPU:0, one launch (start us, length us, event | category | flops | bytes accessed | tf_op | source)
XLA Modules:
  0.0 143.8 jit_solution(14111186370702431222)
XLA Ops:
  0.6 5.2 %shard_map.93.refs_0_ = bf16[128,256]{1,0:T(8,128)(2,1)} custom-call(bf16[128,5120]{1,0:T(8,128)(2,1)} %acts.1, bf16[5120,256]{1,0:T(8,128)(2,1)} %projection.9), custom_call_target="tpu_custom_call" | custom-call | flops 335544320 | bytes 3932160 | tf_op jit(solution)/shard_map/pallas_call | solution.py:77
  5.8 5.0 %collective-permute-start.2 = (bf16[128,256]{1,0:T(8,128)(2,1)}, bf16[128,256]{1,0:T(8,128)(2,1)S(1)}, u32[]{:S(2)}, u32[]{:S(2)}) collective-permute-start(bf16[128,256]{1,0:T(8,128)(2,1)} %shard_map.93.refs_0_), channel_id=1, source_target_pairs={{0,3},{1,2},{2,1},{3,0},{4,7},{5,6},{6,5},{7,4},{8,11},{9,10},{10,... | collective-permute-start | bytes 196616 | tf_op jit(solution)/shard_map/ppermute | solution.py:54
  11.4 2.2 %collective-permute-done.2.refs_3_ = bf16[128,256]{1,0:T(8,128)(2,1)S(1)} collective-permute-done((bf16[128,256]{1,0:T(8,128)(2,1)}, bf16[128,256]{1,0:T(8,128)(2,1)S(1)}, u32[]{:S(2)}, u32[]{:S(2)}) %collective-permute-start.2) | collective-permute-done | bytes 65568 | tf_op jit(solution)/shard_map/ppermute | solution.py:54
  13.7 3.0 %collective-permute-done.1.refs_2_ = bf16[128,256]{1,0:T(8,128)(2,1)S(1)} collective-permute-done((bf16[128,256]{1,0:T(8,128)(2,1)}, bf16[128,256]{1,0:T(8,128)(2,1)S(1)}, u32[]{:S(2)}, u32[]{:S(2)}) %collective-permute-start.1) | collective-permute-done | bytes 65568 | tf_op jit(solution)/shard_map/ppermute | solution.py:54
  16.7 1.5 %copy-done.2 = bf16[512,1728]{0,1:T(8,128)(2,1)S(1)} copy-done((bf16[512,1728]{0,1:T(8,128)(2,1)S(1)}, bf16[512,1728]{0,1:T(8,128)(2,1)}, u32[]{:S(2)}) %copy-start.2) | copy-done | bytes 1769496
  19.8 1.6 %collective-permute-start.3 = (bf16[32,1728]{1,0:T(8,128)(2,1)S(1)}, bf16[32,1728]{1,0:T(8,128)(2,1)S(1)}, u32[]{:S(2)}, u32[]{:S(2)}) collective-permute-start(bf16[32,1728]{1,0:T(8,128)(2,1)S(1)} %get-tuple-element.34), channel_id=1, source_target_pairs={{0,8},{4,12},{8,0},{12,4},{16,24},{20,28},{24,16},{28,20},{1,9},{5... | collective-permute-start | bytes 331784 | tf_op jit(solution)/shard_map/ppermute | solution.py:54
  21.3 1.5 %collective-permute-start.4 = (bf16[32,1728]{1,0:T(8,128)(2,1)S(1)}, bf16[32,1728]{1,0:T(8,128)(2,1)S(1)}, u32[]{:S(2)}, u32[]{:S(2)}) collective-permute-start(bf16[32,1728]{1,0:T(8,128)(2,1)S(1)} %get-tuple-element.35), channel_id=1, source_target_pairs={{0,16},{4,20},{8,24},{12,28},{16,0},{20,4},{24,8},{28,12},{1,17},{... | collective-permute-start | bytes 331784 | tf_op jit(solution)/shard_map/ppermute | solution.py:54
  24.4 1.6 %collective-permute-start.7 = (bf16[32,1728]{1,0:T(8,128)(2,1)S(1)}, bf16[32,1728]{1,0:T(8,128)(2,1)S(1)}, u32[]{:S(2)}, u32[]{:S(2)}) collective-permute-start(bf16[32,1728]{1,0:T(8,128)(2,1)S(1)} %get-tuple-element.38), channel_id=1, source_target_pairs={{0,12},{4,8},{8,4},{12,0},{16,28},{20,24},{24,20},{28,16},{1,13},{... | collective-permute-start | bytes 331784 | tf_op jit(solution)/shard_map/ppermute | solution.py:54
  26.1 4.6 %collective-permute-done.4.refs_2_ = bf16[32,1728]{1,0:T(8,128)(2,1)S(1)} collective-permute-done((bf16[32,1728]{1,0:T(8,128)(2,1)S(1)}, bf16[32,1728]{1,0:T(8,128)(2,1)S(1)}, u32[]{:S(2)}, u32[]{:S(2)}) %collective-permute-start.4) | collective-permute-done | bytes 110624 | tf_op jit(solution)/shard_map/ppermute | solution.py:54
  30.7 1.5 %collective-permute-done.7.refs_5_ = bf16[32,1728]{1,0:T(8,128)(2,1)S(1)} collective-permute-done((bf16[32,1728]{1,0:T(8,128)(2,1)S(1)}, bf16[32,1728]{1,0:T(8,128)(2,1)S(1)}, u32[]{:S(2)}, u32[]{:S(2)}) %collective-permute-start.7) | collective-permute-done | bytes 110624 | tf_op jit(solution)/shard_map/ppermute | solution.py:54
  39.7 3.4 %collective-permute-done.15.refs_6_ = bf16[32,1792]{1,0:T(8,128)(2,1)S(1)} collective-permute-done((bf16[32,1792]{1,0:T(8,128)(2,1)S(1)}, bf16[32,1792]{1,0:T(8,128)(2,1)S(1)}, u32[]{:S(2)}, u32[]{:S(2)}) %collective-permute-start.15) | collective-permute-done | bytes 114720 | tf_op jit(solution)/shard_map/ppermute | solution.py:54
  43.2 1.6 %collective-permute-done.13.refs_4_ = bf16[32,1792]{1,0:T(8,128)(2,1)S(1)} collective-permute-done((bf16[32,1792]{1,0:T(8,128)(2,1)S(1)}, bf16[32,1792]{1,0:T(8,128)(2,1)S(1)}, u32[]{:S(2)}, u32[]{:S(2)}) %collective-permute-start.13) | collective-permute-done | bytes 114720 | tf_op jit(solution)/shard_map/ppermute | solution.py:54
  49.7 12.7 %collective-permute-done.17.refs_2_ = bf16[432,640]{1,0:T(8,128)(2,1)S(1)} collective-permute-done((bf16[432,640]{1,0:T(8,128)(2,1)S(1)}, bf16[432,640]{1,0:T(8,128)(2,1)S(1)}, u32[]{:S(2)}, u32[]{:S(2)}) %collective-permute-start.17) | collective-permute-done | bytes 552992 | tf_op jit(solution)/shard_map/ppermute | solution.py:300
  64.5 1.4 shard_map.98.refs_0_.refs_8_.refs_1_.refs_9_
  65.9 3.2 %shard_map.97 = f32[1728,640]{1,0:T(8,128)} custom-call(bf16[5120,256]{1,0:T(8,128)(2,1)S(1)} %copy-done.1, f32[1728,640]{1,0:T(8,128)S(1)} %bitcast.7, bf16[1792,256]{1,0:T(8,128)(2,1)S(1)} %get-tuple-element.46.tall.refs_0_), custom_call_target="tpu_custom_call" | custom-call | flops 566231040 | bytes 8847360 | tf_op jit(solution)/shard_map/pallas_call | solution.py:187
  69.1 7.9 %collective-permute-done.21.refs_11_ = bf16[432,640]{1,0:T(8,128)(2,1)S(1)} collective-permute-done((bf16[432,640]{1,0:T(8,128)(2,1)S(1)}, bf16[432,640]{1,0:T(8,128)(2,1)S(1)}, u32[]{:S(2)}, u32[]{:S(2)}) %collective-permute-start.21) | collective-permute-done | bytes 552992 | tf_op jit(solution)/shard_map/ppermute | solution.py:300
  79.7 11.9 %collective-permute-done.23.refs_4_ = bf16[432,640]{1,0:T(8,128)(2,1)S(1)} collective-permute-done((bf16[432,640]{1,0:T(8,128)(2,1)S(1)}, bf16[432,640]{1,0:T(8,128)(2,1)S(1)}, u32[]{:S(2)}, u32[]{:S(2)}) %collective-permute-start.23) | collective-permute-done | bytes 552992 | tf_op jit(solution)/shard_map/ppermute | solution.py:300
  91.6 1.6 %collective-permute-start.33 = (bf16[432,640]{1,0:T(8,128)(2,1)S(1)}, bf16[432,640]{1,0:T(8,128)(2,1)S(1)}, u32[]{:S(2)}, u32[]{:S(2)}) collective-permute-start(bf16[432,640]{1,0:T(8,128)(2,1)S(1)} %get-tuple-element.56), channel_id=1, source_target_pairs={{0,16},{4,12},{8,24},{12,4},{16,0},{20,28},{24,8},{28,20},{1,17},{... | collective-permute-start | bytes 1658888 | tf_op jit(solution)/shard_map/ppermute | solution.py:300
  93.5 13.3 %collective-permute-done.33.refs_5_ = bf16[432,640]{1,0:T(8,128)(2,1)S(1)} collective-permute-done((bf16[432,640]{1,0:T(8,128)(2,1)S(1)}, bf16[432,640]{1,0:T(8,128)(2,1)S(1)}, u32[]{:S(2)}, u32[]{:S(2)}) %collective-permute-start.33) | collective-permute-done | bytes 552992 | tf_op jit(solution)/shard_map/ppermute | solution.py:300
  109.1 13.0 %collective-permute-done.34.refs_14_ = bf16[432,640]{1,0:T(8,128)(2,1)S(1)} collective-permute-done((bf16[432,640]{1,0:T(8,128)(2,1)S(1)}, bf16[432,640]{1,0:T(8,128)(2,1)S(1)}, u32[]{:S(2)}, u32[]{:S(2)}) %collective-permute-start.34) | collective-permute-done | bytes 552992 | tf_op jit(solution)/shard_map/ppermute | solution.py:300
  124.8 3.6 %shard_map.100.refs_0_ = bf16[1728,5120]{1,0:T(8,128)(2,1)} custom-call(bf16[1728,640]{1,0:T(8,128)(2,1)S(1)} %shard_map.98.refs_0_.refs_8_.refs_1_.refs_9_, bf16[1728,640]{1,0:T(8,128)(2,1)S(1)} %collective-permute-done.18.refs_1_.refs_9_.refs_2_.refs_10_, bf16[432,640]{1,0:T(8,128)(2,1)S(1)} %collective-permute-done.17.refs_2_, ...), custom_call_target="tpu_custom_call" | custom-call | bytes 30965760 | tf_op jit(solution)/shard_map/pallas_call | solution.py:239
  128.5 9.0 %collective-permute-done.40.refs_15_ = bf16[432,640]{1,0:T(8,128)(2,1)S(1)} collective-permute-done((bf16[432,640]{1,0:T(8,128)(2,1)S(1)}, bf16[432,640]{1,0:T(8,128)(2,1)S(1)}, u32[]{:S(2)}, u32[]{:S(2)}) %collective-permute-start.40) | collective-permute-done | bytes 552992 | tf_op jit(solution)/shard_map/ppermute | solution.py:300
  137.9 1.4 %collective-permute-done.39.refs_8_ = bf16[432,640]{1,0:T(8,128)(2,1)S(1)} collective-permute-done((bf16[432,640]{1,0:T(8,128)(2,1)S(1)}, bf16[432,640]{1,0:T(8,128)(2,1)S(1)}, u32[]{:S(2)}, u32[]{:S(2)}) %collective-permute-start.39) | collective-permute-done | bytes 552992 | tf_op jit(solution)/shard_map/ppermute | solution.py:54
  140.2 3.6 %shard_map.101 = bf16[1728,5120]{1,0:T(8,128)(2,1)} custom-call(bf16[1728,5120]{1,0:T(8,128)(2,1)} %shard_map.100.refs_0_, bf16[1728,640]{1,0:T(8,128)(2,1)S(1)} %shard_map.98.refs_0_.refs_8_.refs_1_.refs_9_, bf16[1728,640]{1,0:T(8,128)(2,1)S(1)} %collective-permute-done.18.refs_1_.refs_9_.refs_2_.refs_10_, ...), custom_call_target="tpu_custom_call", output_to_operand_aliasing={{}: (0, {})} | custom-call | bytes 30965760 | tf_op jit(solution)/shard_map/pallas_call | solution.py:239
  (81 shorter events, 27.7 us)
Async XLA Ops:
  5.8 7.9 %collective-permute-start.2 = (bf16[128,256]{1,0:T(8,128)(2,1)}, bf16[128,256]{1,0:T(8,128)(2,1)S(1)}, u32[]{:S(2)}, u32[]{:S(2)}) collective-permute-start(bf16[128,256]{1,0:T(8,128)(2,1)} %shard_map.93.refs_0_), channel_id=1, source_target_pairs={{0,3},{1,2},{2,1},{3,0},{4,7},{5,6},{6,5},{7,4},{8,11},{9,10},{10,... | collective-permute-start | bytes 196616 | tf_op jit(solution)/shard_map/ppermute | solution.py:54
  21.3 9.3 %collective-permute-start.4 = (bf16[32,1728]{1,0:T(8,128)(2,1)S(1)}, bf16[32,1728]{1,0:T(8,128)(2,1)S(1)}, u32[]{:S(2)}, u32[]{:S(2)}) collective-permute-start(bf16[32,1728]{1,0:T(8,128)(2,1)S(1)} %get-tuple-element.35), channel_id=1, source_target_pairs={{0,16},{4,20},{8,24},{12,28},{16,0},{20,4},{24,8},{28,12},{1,17},{... | collective-permute-start | bytes 331784 | tf_op jit(solution)/shard_map/ppermute | solution.py:54
  22.8 7.8 %collective-permute-start.5 = (bf16[32,1728]{1,0:T(8,128)(2,1)S(1)}, bf16[32,1728]{1,0:T(8,128)(2,1)S(1)}, u32[]{:S(2)}, u32[]{:S(2)}) collective-permute-start(bf16[32,1728]{1,0:T(8,128)(2,1)S(1)} %get-tuple-element.36), channel_id=1, source_target_pairs={{0,24},{4,28},{8,16},{12,20},{16,8},{20,12},{24,0},{28,4},{1,25},{... | collective-permute-start | bytes 331784 | tf_op jit(solution)/shard_map/ppermute | solution.py:54
  24.4 7.8 %collective-permute-start.7 = (bf16[32,1728]{1,0:T(8,128)(2,1)S(1)}, bf16[32,1728]{1,0:T(8,128)(2,1)S(1)}, u32[]{:S(2)}, u32[]{:S(2)}) collective-permute-start(bf16[32,1728]{1,0:T(8,128)(2,1)S(1)} %get-tuple-element.38), channel_id=1, source_target_pairs={{0,12},{4,8},{8,4},{12,0},{16,28},{20,24},{24,20},{28,16},{1,13},{... | collective-permute-start | bytes 331784 | tf_op jit(solution)/shard_map/ppermute | solution.py:54
  26.0 7.4 %collective-permute-start.8 = (bf16[32,1728]{1,0:T(8,128)(2,1)S(1)}, bf16[32,1728]{1,0:T(8,128)(2,1)S(1)}, u32[]{:S(2)}, u32[]{:S(2)}) collective-permute-start(bf16[32,1728]{1,0:T(8,128)(2,1)S(1)} %get-tuple-element.39), channel_id=1, source_target_pairs={{0,20},{4,16},{8,28},{12,24},{16,4},{20,0},{24,12},{28,8},{1,21},{... | collective-permute-start | bytes 331784 | tf_op jit(solution)/shard_map/ppermute | solution.py:54
  47.1 15.3 %collective-permute-start.17 = (bf16[432,640]{1,0:T(8,128)(2,1)S(1)}, bf16[432,640]{1,0:T(8,128)(2,1)S(1)}, u32[]{:S(2)}, u32[]{:S(2)}) collective-permute-start(bf16[432,640]{1,0:T(8,128)(2,1)S(1)} %get-tuple-element.50), channel_id=1, source_target_pairs={{0,8},{4,20},{8,0},{12,28},{16,24},{20,4},{24,16},{28,12},{1,9},{5... | collective-permute-start | bytes 1658888 | tf_op jit(solution)/shard_map/ppermute | solution.py:300
  48.2 14.2 %collective-permute-start.20 = (bf16[432,640]{1,0:T(8,128)(2,1)S(1)}, bf16[432,640]{1,0:T(8,128)(2,1)S(1)}, u32[]{:S(2)}, u32[]{:S(2)}) collective-permute-start(bf16[432,640]{1,0:T(8,128)(2,1)S(1)} %get-tuple-element.53), channel_id=1, source_target_pairs={{0,16},{4,12},{8,24},{12,4},{16,0},{20,28},{24,8},{28,20},{1,17},{... | collective-permute-start | bytes 1658888 | tf_op jit(solution)/shard_map/ppermute | solution.py:300
  62.4 15.8 %collective-permute-start.25 = (bf16[432,640]{1,0:T(8,128)(2,1)S(1)}, bf16[432,640]{1,0:T(8,128)(2,1)S(1)}, u32[]{:S(2)}, u32[]{:S(2)}) collective-permute-start(bf16[432,640]{1,0:T(8,128)(2,1)S(1)} %get-tuple-element.56), channel_id=1, source_target_pairs={{0,8},{4,20},{8,0},{12,28},{16,24},{20,4},{24,16},{28,12},{1,9},{5... | collective-permute-start | bytes 1658888 | tf_op jit(solution)/shard_map/ppermute | solution.py:300
  63.4 13.5 %collective-permute-start.21 = (bf16[432,640]{1,0:T(8,128)(2,1)S(1)}, bf16[432,640]{1,0:T(8,128)(2,1)S(1)}, u32[]{:S(2)}, u32[]{:S(2)}) collective-permute-start(bf16[432,640]{1,0:T(8,128)(2,1)S(1)} %get-tuple-element.54), channel_id=1, source_target_pairs={{0,16},{4,12},{8,24},{12,4},{16,0},{20,28},{24,8},{28,20},{1,17},{... | collective-permute-start | bytes 1658888 | tf_op jit(solution)/shard_map/ppermute | solution.py:300
  64.0 14.2 %collective-permute-start.19 = (bf16[432,640]{1,0:T(8,128)(2,1)S(1)}, bf16[432,640]{1,0:T(8,128)(2,1)S(1)}, u32[]{:S(2)}, u32[]{:S(2)}) collective-permute-start(bf16[432,640]{1,0:T(8,128)(2,1)S(1)} %collective-permute-done.17.refs_2_), channel_id=1, source_target_pairs={{0,4},{4,0},{8,12},{12,8},{16,20},{20,16},{24,28},{28,24},{1,5},{5... | collective-permute-start | bytes 1658888 | tf_op jit(solution)/shard_map/ppermute | solution.py:54
  65.8 56.8 %collective-permute-start.18 = (bf16[1728,640]{1,0:T(8,128)(2,1)S(1)}, bf16[1728,640]{1,0:T(8,128)(2,1)S(1)}, u32[]{:S(2)}, u32[]{:S(2)}) collective-permute-start(bf16[1728,640]{1,0:T(8,128)(2,1)S(1)} %shard_map.98.refs_0_.refs_8_.refs_1_.refs_9_), channel_id=1, source_target_pairs={{0,4},{4,0},{8,12},{12,8},{16,20},{20,16},{24,28},{28,24},{1,5},{5... | collective-permute-start | bytes 6635528 | tf_op jit(solution)/shard_map/ppermute | solution.py:54
  76.9 14.6 %collective-permute-start.23 = (bf16[432,640]{1,0:T(8,128)(2,1)S(1)}, bf16[432,640]{1,0:T(8,128)(2,1)S(1)}, u32[]{:S(2)}, u32[]{:S(2)}) collective-permute-start(bf16[432,640]{1,0:T(8,128)(2,1)S(1)} %get-tuple-element.50), channel_id=1, source_target_pairs={{0,16},{4,12},{8,24},{12,4},{16,0},{20,28},{24,8},{28,20},{1,17},{... | collective-permute-start | bytes 1658888 | tf_op jit(solution)/shard_map/ppermute | solution.py:300
  78.1 13.4 %collective-permute-start.32 = (bf16[432,640]{1,0:T(8,128)(2,1)S(1)}, bf16[432,640]{1,0:T(8,128)(2,1)S(1)}, u32[]{:S(2)}, u32[]{:S(2)}) collective-permute-start(bf16[432,640]{1,0:T(8,128)(2,1)S(1)} %collective-permute-done.21.refs_11_), channel_id=1, source_target_pairs={{0,4},{4,0},{8,12},{12,8},{16,20},{20,16},{24,28},{28,24},{1,5},{5... | collective-permute-start | bytes 1658888 | tf_op jit(solution)/shard_map/ppermute | solution.py:54
  78.2 15.0 %collective-permute-start.27 = (bf16[432,640]{1,0:T(8,128)(2,1)S(1)}, bf16[432,640]{1,0:T(8,128)(2,1)S(1)}, u32[]{:S(2)}, u32[]{:S(2)}) collective-permute-start(bf16[432,640]{1,0:T(8,128)(2,1)S(1)} %collective-permute-done.25.refs_3_), channel_id=1, source_target_pairs={{0,4},{4,0},{8,12},{12,8},{16,20},{20,16},{24,28},{28,24},{1,5},{5... | collective-permute-start | bytes 1658888 | tf_op jit(solution)/shard_map/ppermute | solution.py:54
  78.7 14.5 %collective-permute-start.26 = (bf16[432,640]{1,0:T(8,128)(2,1)S(1)}, bf16[432,640]{1,0:T(8,128)(2,1)S(1)}, u32[]{:S(2)}, u32[]{:S(2)}) collective-permute-start(bf16[432,640]{1,0:T(8,128)(2,1)S(1)} %get-tuple-element.53), channel_id=1, source_target_pairs={{0,8},{4,20},{8,0},{12,28},{16,24},{20,4},{24,16},{28,12},{1,9},{5... | collective-permute-start | bytes 1658888 | tf_op jit(solution)/shard_map/ppermute | solution.py:300
  91.6 15.3 %collective-permute-start.33 = (bf16[432,640]{1,0:T(8,128)(2,1)S(1)}, bf16[432,640]{1,0:T(8,128)(2,1)S(1)}, u32[]{:S(2)}, u32[]{:S(2)}) collective-permute-start(bf16[432,640]{1,0:T(8,128)(2,1)S(1)} %get-tuple-element.56), channel_id=1, source_target_pairs={{0,16},{4,12},{8,24},{12,4},{16,0},{20,28},{24,8},{28,20},{1,17},{... | collective-permute-start | bytes 1658888 | tf_op jit(solution)/shard_map/ppermute | solution.py:300
  93.2 13.9 %collective-permute-start.28 = (bf16[432,640]{1,0:T(8,128)(2,1)S(1)}, bf16[432,640]{1,0:T(8,128)(2,1)S(1)}, u32[]{:S(2)}, u32[]{:S(2)}) collective-permute-start(bf16[432,640]{1,0:T(8,128)(2,1)S(1)} %get-tuple-element.54), channel_id=1, source_target_pairs={{0,8},{4,20},{8,0},{12,28},{16,24},{20,4},{24,16},{28,12},{1,9},{5... | collective-permute-start | bytes 1658888 | tf_op jit(solution)/shard_map/ppermute | solution.py:300
  93.2 13.9 %collective-permute-start.29 = (bf16[432,640]{1,0:T(8,128)(2,1)S(1)}, bf16[432,640]{1,0:T(8,128)(2,1)S(1)}, u32[]{:S(2)}, u32[]{:S(2)}) collective-permute-start(bf16[432,640]{1,0:T(8,128)(2,1)S(1)} %collective-permute-done.26.refs_12_), channel_id=1, source_target_pairs={{0,4},{4,0},{8,12},{12,8},{16,20},{20,16},{24,28},{28,24},{1,5},{5... | collective-permute-start | bytes 1658888 | tf_op jit(solution)/shard_map/ppermute | solution.py:54
  106.8 15.2 %collective-permute-start.34 = (bf16[432,640]{1,0:T(8,128)(2,1)S(1)}, bf16[432,640]{1,0:T(8,128)(2,1)S(1)}, u32[]{:S(2)}, u32[]{:S(2)}) collective-permute-start(bf16[432,640]{1,0:T(8,128)(2,1)S(1)} %collective-permute-done.20.refs_10_), channel_id=1, source_target_pairs={{0,8},{4,20},{8,0},{12,28},{16,24},{20,4},{24,16},{28,12},{1,9},{5... | collective-permute-start | bytes 1658888 | tf_op jit(solution)/shard_map/ppermute | solution.py:300
  106.8 15.2 %collective-permute-start.36 = (bf16[432,640]{1,0:T(8,128)(2,1)S(1)}, bf16[432,640]{1,0:T(8,128)(2,1)S(1)}, u32[]{:S(2)}, u32[]{:S(2)}) collective-permute-start(bf16[432,640]{1,0:T(8,128)(2,1)S(1)} %collective-permute-done.33.refs_5_), channel_id=1, source_target_pairs={{0,4},{4,0},{8,12},{12,8},{16,20},{20,16},{24,28},{28,24},{1,5},{5... | collective-permute-start | bytes 1658888 | tf_op jit(solution)/shard_map/ppermute | solution.py:54
  107.1 15.0 %collective-permute-start.30 = (bf16[432,640]{1,0:T(8,128)(2,1)S(1)}, bf16[432,640]{1,0:T(8,128)(2,1)S(1)}, u32[]{:S(2)}, u32[]{:S(2)}) collective-permute-start(bf16[432,640]{1,0:T(8,128)(2,1)S(1)} %collective-permute-done.17.refs_2_), channel_id=1, source_target_pairs={{0,16},{4,12},{8,24},{12,4},{16,0},{20,28},{24,8},{28,20},{1,17},{... | collective-permute-start | bytes 1658888 | tf_op jit(solution)/shard_map/ppermute | solution.py:300
  108.3 14.3 %collective-permute-start.37 = (bf16[432,640]{1,0:T(8,128)(2,1)S(1)}, bf16[432,640]{1,0:T(8,128)(2,1)S(1)}, u32[]{:S(2)}, u32[]{:S(2)}) collective-permute-start(bf16[432,640]{1,0:T(8,128)(2,1)S(1)} %collective-permute-done.28.refs_13_), channel_id=1, source_target_pairs={{0,4},{4,0},{8,12},{12,8},{16,20},{20,16},{24,28},{28,24},{1,5},{5... | collective-permute-start | bytes 1658888 | tf_op jit(solution)/shard_map/ppermute | solution.py:54
  122.1 15.3 %collective-permute-start.40 = (bf16[432,640]{1,0:T(8,128)(2,1)S(1)}, bf16[432,640]{1,0:T(8,128)(2,1)S(1)}, u32[]{:S(2)}, u32[]{:S(2)}) collective-permute-start(bf16[432,640]{1,0:T(8,128)(2,1)S(1)} %collective-permute-done.21.refs_11_), channel_id=1, source_target_pairs={{0,8},{4,20},{8,0},{12,28},{16,24},{20,4},{24,16},{28,12},{1,9},{5... | collective-permute-start | bytes 1658888 | tf_op jit(solution)/shard_map/ppermute | solution.py:300
  122.6 14.8 %collective-permute-start.38 = (bf16[432,640]{1,0:T(8,128)(2,1)S(1)}, bf16[432,640]{1,0:T(8,128)(2,1)S(1)}, u32[]{:S(2)}, u32[]{:S(2)}) collective-permute-start(bf16[432,640]{1,0:T(8,128)(2,1)S(1)} %collective-permute-done.25.refs_3_), channel_id=1, source_target_pairs={{0,16},{4,12},{8,24},{12,4},{16,0},{20,28},{24,8},{28,20},{1,17},{... | collective-permute-start | bytes 1658888 | tf_op jit(solution)/shard_map/ppermute | solution.py:300
  (24 other events, 165.4 us)

commit v5 on v4

--- a/solution.py
+++ b/solution.py
@@ -19,6 +19,15 @@
 
 VMEM = pl.BlockSpec(memory_space=pltpu.VMEM)
 ANY = pl.BlockSpec(memory_space=pl.ANY)
+
+
+TURN_MASKS = ((2, 4), (4, 2))
+OWNER_MASKS = ((0, 0), (1, 1), (2, 4), (5, 3), (4, 2), (3, 5), (6, 6), (7, 7))
+
+
+def chunk_sizes(cols):
+    rest = -(-cols * 7 // 18 // 16) * 16
+    return (cols - 2 * rest, rest, rest)
 
 
 def adam(grad, moment_one, moment_two):
@@ -54,41 +63,21 @@
     return lax.ppermute(value, axis, [(i, i ^ mask) for i in range(size)])
 
 
-def project_kernel(acts, projection, out, total):
-    step = pl.program_id(0)
-    part = jnp.dot(acts[...], projection[...], preferred_element_type=jnp.float32)
-
-    @pl.when(step == 0)
-    def _():
-        total[...] = part
-
-    @pl.when(step > 0)
-    def _():
-        total[...] += part
-
-    @pl.when(step == pl.num_programs(0) - 1)
-    def _():
-        out[...] = total[...].astype(jnp.bfloat16)
-
-
-def project(acts, projection, depth):
-    tokens, width = acts.shape
-    rank = projection.shape[1]
+def take_kernel(source, out, sem):
+    copy = pltpu.make_async_copy(source.at[pl.ds(0, out.shape[0]), :], out, sem)
+    copy.start()
+    copy.wait()
+
+
+def take(array, count):
     return pl.pallas_call(
-        project_kernel,
-        out_shape=jax.ShapeDtypeStruct((tokens, rank), jnp.bfloat16),
-        grid=(width // depth,),
-        in_specs=[
-            pl.BlockSpec((tokens, depth), lambda i: (0, i)),
-            pl.BlockSpec((depth, rank), lambda i: (i, 0)),
-        ],
+        take_kernel,
+        out_shape=jax.ShapeDtypeStruct((count, array.shape[1]), array.dtype),
+        in_specs=[ANY],
         out_specs=VMEM,
-        scratch_shapes=[pltpu.VMEM((tokens, rank), jnp.float32)],
-        compiler_params=pltpu.CompilerParams(vmem_limit_bytes=56 * 2**20),
-        cost_estimate=pl.CostEstimate(
-            flops=2 * tokens * width * rank, bytes_accessed=2 * (tokens + rank) * width, transcendentals=0
-        ),
-    )(acts, projection)
+        scratch_shapes=[pltpu.SemaphoreType.DMA],
+        compiler_params=pltpu.CompilerParams(vmem_limit_bytes=60 * 2**20),
+    )(array)
 
 
 def partial_kernel(grad_t, *refs, n_fsdp, n_dp):
@@ -130,7 +119,7 @@
     )
 
 
-def weight_kernel(projection, master_t, *refs, n_in, spans, block):
+def weight_kernel(projection, master_t, *refs, n_in, masks, spans, block):
     pieces, outs = refs[:n_in], refs[n_in:]
     me = lax.axis_index("dp")
     if n_in > 1:
@@ -143,16 +132,18 @@
     else:
         tall = pieces[0]
     slab_rows = master_t.shape[1]
-    slab = projection[pl.ds(pl.multiple_of(me * slab_rows, slab_rows), slab_rows), :]
+    owner = me ^ jnp.where((me & 1) == 0, masks[0], masks[1])
+    slab = projection[pl.ds(pl.multiple_of(owner * slab_rows, slab_rows), slab_rows), :]
     for (first, count), out in zip(spans, outs):
         for at in range(0, count, block):
-            master_new = master_t[pl.ds(first + at, block), :] - LEARN_RATE * expand(
-                tall, slab, first + at, block
+            size = min(block, count - at)
+            master_new = master_t[pl.ds(first + at, size), :] - LEARN_RATE * expand(
+                tall, slab, first + at, size
             )
-            out[pl.ds(at, block), :] = master_new.astype(jnp.bfloat16)
-
-
-def weights(projection, master_t, pieces, spans, block):
+            out[pl.ds(at, size), :] = master_new.astype(jnp.bfloat16)
+
+
+def weights(projection, master_t, pieces, spans, masks=(0, 0)):
     slab_rows, rank = master_t.shape[1], projection.shape[1]
     wide = pieces[0].shape[1]
     out_shape = [jax.ShapeDtypeStruct((count, slab_rows), jnp.bfloat16) for _, count in spans]
@@ -162,7 +153,7 @@
         scratch = [pltpu.VMEM((rank, wide), jnp.bfloat16)]
     size = sum(count for _, count in spans) * slab_rows
     return pl.pallas_call(
-        functools.partial(weight_kernel, n_in=len(pieces), spans=spans, block=block),
+        functools.partial(weight_kernel, n_in=len(pieces), masks=masks, spans=spans, block=144),
         out_shape=out_shape,
         in_specs=[VMEM] * (2 + len(pieces)),
         out_specs=[VMEM] * len(out_shape),
@@ -201,43 +192,37 @@
     )(projection, master_t, tall)
 
 
-def lay_kernel(*refs, spans, block, fresh):
+def lay_kernel(*refs, first, count, block, fresh):
     refs = refs if fresh else refs[1:]
-    n_in = sum(len(masks) for _, _, masks in spans)
-    pieces, out, (held, sems) = refs[:n_in], refs[n_in], refs[n_in + 1 :]
+    pieces, out, (held, sems) = refs[:-3], refs[-3], refs[-2:]
     copies = [None] * held.shape[0]
     me = lax.axis_index("dp")
     core = me & 1
-    at = 0
-    base = 0
-    for first, count, masks in spans:
-        for start in range(0, count, block):
-            slot = at % len(copies)
-            if copies[slot] is not None:
-                copies[slot].wait()
-            for mask, piece in zip(masks, pieces[base : base + len(masks)]):
-                width = piece.shape[1]
-                mask = jnp.where(core == 0, mask[0], mask[1])
-                column = pl.multiple_of((me ^ mask) * width, 128)
-                origin = start if piece.shape[0] == count else first + start
-                held[slot, :, pl.ds(column, width)] = piece[pl.ds(origin, block), :]
-            copies[slot] = pltpu.make_async_copy(
-                held.at[slot], out.at[pl.ds(first + start, block), :], sems.at[slot]
-            )
-            copies[slot].start()
-            at += 1
-        base += len(masks)
+    for at in range(0, count, block):
+        slot = at // block % len(copies)
+        size = min(block, count - at)
+        if copies[slot] is not None:
+            copies[slot].wait()
+        for masks, piece in zip(OWNER_MASKS, pieces):
+            width = piece.shape[1]
+            column = pl.multiple_of((me ^ jnp.where(core == 0, masks[0], masks[1])) * width, 128)
+            origin = at if piece.shape[0] == count else first + at
+            held[slot, pl.ds(0, size), pl.ds(column, width)] = piece[pl.ds(origin, size), :]
+        copies[slot] = pltpu.make_async_copy(
+            held.at[slot, pl.ds(0, size), :], out.at[pl.ds(first + at, size), :], sems.at[slot]
+        )
+        copies[slot].start()
     for copy in copies:
         if copy is not None:
             copy.wait()
 
 
-def lay(out, shape, spans, pieces, block):
+def lay(out, shape, span, pieces, block=96):
     fresh = out is None
     held = [] if fresh else [out]
-    size = sum(2 * 2 * piece.size for piece in pieces)
+    first, count = span
     return pl.pallas_call(
-        functools.partial(lay_kernel, spans=spans, block=block, fresh=fresh),
+        functools.partial(lay_kernel, first=first, count=count, block=block, fresh=fresh),
         out_shape=jax.ShapeDtypeStruct(shape, jnp.bfloat16),
         in_specs=[ANY] * len(held) + [VMEM] * len(pieces),
         out_specs=ANY,
@@ -247,7 +232,7 @@
         ],
         input_output_aliases={} if fresh else {0: 0},
         compiler_params=pltpu.CompilerParams(vmem_limit_bytes=20 * 2**20),
-        cost_estimate=pl.CostEstimate(flops=0, bytes_accessed=size, transcendentals=0),
+        cost_estimate=pl.CostEstimate(flops=0, bytes_accessed=4 * count * shape[1], transcendentals=0),
     )(*held, *pieces)
 
 
@@ -259,7 +244,24 @@
     wide = -(-cols // 128) * 128
     master_t = master.T
 
-    projected = project(acts, projection, acts.shape[1] // 5)
+    def hop(value, mask):
+        return send(value, "dp", n_dp, mask)
+
+    def turn(value, which):
+        masks = [TURN_MASKS[which][i & 1] for i in range(n_dp)]
+        return lax.ppermute(value, "dp", [(i, i ^ masks[i]) for i in range(n_dp)])
+
+    def after(value, earlier):
+        return lax.optimization_barrier((value, *earlier))[0] if earlier else value
+
+    counts = chunk_sizes(cols)
+    chunks = len(counts)
+    spans = [(sum(counts[:at]), count) for at, count in enumerate(counts)]
+    taken = take(master_t, counts[0])
+    ahead = turn(taken, 0)
+    acts = after(acts, [taken])
+
+    projected = jnp.dot(acts, projection, preferred_element_type=jnp.float32).astype(jnp.bfloat16)
     tokens = [projected] + [send(projected, "fsdp", n_fsdp, k) for k in range(1, n_fsdp)]
     parts = pl.pallas_call(
         functools.partial(partial_kernel, n_fsdp=n_fsdp, n_dp=n_dp),
@@ -272,6 +274,7 @@
         ],
         compiler_params=pltpu.CompilerParams(vmem_limit_bytes=16 * 2**20),
     )(grad_out.T, *tokens)
+    parts = lax.optimization_barrier((*parts, ahead))[:-1]
     parts = [parts[k] if k == 0 else send(parts[k], "dp", n_dp, k) for k in (0, 2, 4, 6, 7, 3, 5, 1)]
     moment_one_new, moment_two_new, update = pl.pallas_call(
         adam_kernel,
@@ -285,9 +288,6 @@
         compiler_params=pltpu.CompilerParams(vmem_limit_bytes=16 * 2**20),
     )(moment_one, moment_two, *parts)
 
-    def hop(value, mask):
-        return send(value, "dp", n_dp, mask)
-
     updates = {0: update}
     for k in (6, 2, 4, 1):
         updates[k] = hop(update, k)
@@ -295,60 +295,34 @@
         updates[k ^ 1] = hop(updates[k], 1)
     updates = [updates[k] for k in range(n_dp)]
 
-    def turn(value, which):
-        masks = [(2, 4)[(i & 1) ^ which] for i in range(n_dp)]
-        return lax.ppermute(value, "dp", [(i, i ^ masks[i]) for i in range(n_dp)])
-
-    half = cols // 2
-    block = cols // 12
-    counts = (3 * block, 3 * block)
-    chunks = len(counts)
-    starts = [sum(counts[:at]) for at in range(chunks)]
-    spans = [((first, count), (half + first, count)) for first, count in zip(starts, counts)]
-    tall, *early = weights(projection, master_t, updates, spans[0], block)
-    late = [span for both in spans[1:] for span in both]
-    late = weights(projection, master_t, [tall], late, block)
-    own = [early] + [late[2 * at : 2 * at + 2] for at in range(chunks - 1)]
+    tall, *own = weights(projection, master_t, updates, spans[1:])
+    own_last, whole = weights(projection, master_t, [tall], spans[:1] + [(0, cols)])
+    own = [own_last] + own
+    (ahead_got,) = weights(projection, ahead, [tall], spans[:1], TURN_MASKS[0])
+    ahead_over = hop(ahead_got, 1)
     master_new = new_master(projection, master_t, tall, cols // 4)
 
-    def after(value, earlier):
-        return lax.optimization_barrier((value, *earlier))[0] if earlier else value
-
-    got, over = [], []
-    out = None
-    shape = (cols, n_dp * slab_rows)
-    for step in range(6 * chunks):
-        phase, rest = divmod(step, 2 * chunks)
-        at, part = divmod(rest, 2)
-        if phase == 0:
-            value, which = own[at][part], part
-        elif phase == 1:
-            value, which = own[at][1 - part], part
-        else:
-            value, which = got[2 * at + part], 1 - part
-        earlier = got[step - 2 : step - 1] if step >= 2 else []
-        earlier += over[step - 4 : step - 3] if step >= 4 else []
-        if step == 4:
+    later = range(1, chunks)
+    steps = [(0, at) for at in later] + [(1, at) for at in later] + [(2, at) for at in later] + [(1, 0), (2, 0)]
+    got, over = {(0, 0): ahead_got}, {(0, 0): ahead_over}
+    outs = [None]
+    for step, (phase, at) in enumerate(steps):
+        value = got[(0, at)] if phase == 2 else own[at]
+        earlier = [got[steps[step - 2]]] if step >= 2 else []
+        earlier += [over[steps[step - 4]]] if step >= 4 else []
+        if step == 2:
             earlier.append(master_new)
-        if step == 10:
-            earlier.append(whole_c)
-        got.append(turn(after(value, earlier), which))
-        over.append(hop(after(got[step], [] if out is None else [out]), 1))
-        if step == 0:
-            (whole,) = weights(projection, master_t, [after(tall, got)], [(0, cols)], block)
-            whole_c = hop(whole, 1)
-        if phase == 2 and part == 1:
-            laid, placed = [], []
-            for part, (first, count) in enumerate(spans[at]):
-                one, two = 2 * at + part, 2 * chunks + 2 * at + 1 - part
-                three = 4 * chunks + 2 * at + part
-                laid += [whole, whole_c, got[one], over[one], got[two], over[two], got[three], over[three]]
-                masks = ((0, 0), (1, 1), (2, 4), (5, 3), (4, 2), (3, 5), (6, 6), (7, 7))
-                if part == 1:
-                    masks = ((0, 0), (1, 1), (4, 2), (3, 5), (2, 4), (5, 3), (6, 6), (7, 7))
-                placed.append((first, count, masks))
-            out = lay(out, shape, placed, laid, block // 2 if block % 32 == 0 else block)
-    return (moment_one_new, moment_two_new, master_new.T, out.T)
+        got[(phase, at)] = turn(after(value, earlier), min(phase, 1))
+        held = outs[step - len(steps) + 3 : step - len(steps) + 4] if step >= len(steps) - 2 else []
+        over[(phase, at)] = hop(after(got[(phase, at)], held), 1)
+        if step == 1:
+            whole_c = hop(after(whole, [got[steps[1]]]), 1)
+        if phase == 2:
+            pieces = [whole, whole_c]
+            for which in range(3):
+                pieces += [got[(which, at)], over[(which, at)]]
+            outs.append(lay(outs[-1], (cols, n_dp * slab_rows), spans[at], pieces))
+    return (moment_one_new, moment_two_new, master_new.T, outs[-1].T)
 
 
 def solution(mesh):

time: 144 us -> 125 us (0.87)
  waiting for transfers between devices: 89.6 us -> 75.1 us
  local copies, waits for them, and re-layouts: 4.2 us -> 0.03 us
  matrix products: 0 us -> 2.4 us
  Pallas kernels: 20.1 us -> 18.3 us
    ppermute x12 -> x9, waiting for transfers between devices: 67.7 us -> 54 us  [turn(): return lax.ppermute(value, 'dp', [(i, i ^ masks[i]) for i in range(n_dp)])]
    unnamed x12, local copies, waits for them, and re-layouts: 4.2 us -> 0.03 us
    ppermute x30 -> x27, starting transfers between devices: 19.4 us -> 16.5 us  [send(): return lax.ppermute(value, axis, [(i, i ^ mask) for i in range(size)])]
    dot_general x0 -> x1, matrix products: none -> 2.4 us  [kernel_body(): jnp.dot(acts, projection, preferred_element_type=jnp.float32)]
    ppermute x12 -> x9, starting transfers between devices: 9.79 us -> 11.7 us  [turn(): return lax.ppermute(value, 'dp', [(i, i ^ masks[i]) for i in range(n_dp)])]
    pallas_call x6 -> x7, Pallas kernels: 15.3 us -> 13.5 us  [the longest x3 8 us: lay(): pl.pallas_call(functools.partial(lay_kernel, first=first, count=count, bl...]
    ppermute x30 -> x27, waiting for transfers between devices: 21.8 us -> 21.1 us  [send(): return lax.ppermute(value, axis, [(i, i ^ mask) for i in range(size)])]
  transfers between devices with their start and end apart: 42 -> 36, of which waited for: 19 -> 19; matrix products, arithmetic and copies ran while one was open for 0% -> 2% of each run, Pallas kernels for 6% -> 10%
where the time goes in v5:
time: 125 us
  waiting for transfers between devices  75.1 us (60%)
  starting transfers between devices  28.1 us (22%)
  Pallas kernels  18.3 us (15%)
  matrix products  2.4 us (2%)
    ppermute x9, waiting for transfers between devices, turn(): return lax.ppermute(value, 'dp', [(i, i ^ masks[i]) for i in range(n_dp)])  54 us
    ppermute x27, waiting for transfers between devices, send(): return lax.ppermute(value, axis, [(i, i ^ mask) for i in range(size)])  21.1 us
    ppermute x27, starting transfers between devices, send(): return lax.ppermute(value, axis, [(i, i ^ mask) for i in range(size)])  16.5 us
    ppermute x9, starting transfers between devices, turn(): return lax.ppermute(value, 'dp', [(i, i ^ masks[i]) for i in range(n_dp)])  11.7 us
    pallas_call x3, Pallas kernels, lay(): pl.pallas_call(functools.partial(lay_kernel, first=first, count=count, bl...  8 us
    pallas_call x3, Pallas kernels, weights(): pl.pallas_call(functools.partial(weight_kernel, n_in=len(pieces), masks=m...  3.24 us
    pallas_call x1, Pallas kernels, new_master(): pl.pallas_call(master_kernel, out_shape=jax.ShapeDtypeStruct((cols, slab_...  3.12 us
  transfers between devices with their start and end apart: 36, of which 19 were waited for; matrix products, arithmetic and copies ran while one was open for 2% of the time, Pallas kernels for 10%

profile of v5, /device:TPU:0, one launch (start us, length us, event | category | flops | bytes accessed | tf_op | source)
XLA Modules:
  0.0 124.7 jit_solution(4527107513519560216)
XLA Ops:
  0.7 2.3 %shard_map.93 = f32[384,640]{1,0:T(8,128)} custom-call(f32[1728,640]{1,0:T(8,128)} %bitcast.6), custom_call_target="tpu_custom_call" | custom-call | tf_op jit(solution)/shard_map/pallas_call | solution.py:73
  3.0 3.0 %collective-permute-start.3 = (f32[384,640]{1,0:T(8,128)}, f32[384,640]{1,0:T(8,128)S(1)}, u32[]{:S(2)}, u32[]{:S(2)}) collective-permute-start(f32[384,640]{1,0:T(8,128)} %shard_map.93), channel_id=1, source_target_pairs={{0,8},{4,20},{8,0},{12,28},{16,24},{20,4},{24,16},{28,12},{1,9},{5... | collective-permute-start | bytes 2949128 | tf_op jit(solution)/shard_map/ppermute | solution.py:252
  6.0 2.4 %convolution_convert_fusion.refs_0_ = bf16[128,256]{1,0:T(8,128)(2,1)S(1)} fusion(bf16[128,5120]{1,0:T(8,128)(2,1)S(1)} %copy-done, bf16[5120,256]{1,0:T(8,128)(2,1)} %projection.7), kind=kOutput, calls=%fused_computation | convolution fusion | flops 335577088 | bytes 3997696 | tf_op jit(solution)/shard_map/dot_general | solution.py:264
  8.4 1.6 %collective-permute-start = (bf16[128,256]{1,0:T(8,128)(2,1)S(1)}, bf16[128,256]{1,0:T(8,128)(2,1)S(1)}, u32[]{:S(2)}, u32[]{:S(2)}) collective-permute-start(bf16[128,256]{1,0:T(8,128)(2,1)S(1)} %convolution_convert_fusion.refs_0_), channel_id=1, source_target_pairs={{0,1},{1,0},{2,3},{3,2},{4,5},{5,4},{6,7},{7,6},{8,9},{9,8},{10,11... | collective-permute-start | bytes 196616 | tf_op jit(solution)/shard_map/ppermute | solution.py:63
  10.1 2.6 %collective-permute-start.1 = (bf16[128,256]{1,0:T(8,128)(2,1)S(1)}, bf16[128,256]{1,0:T(8,128)(2,1)S(1)}, u32[]{:S(2)}, u32[]{:S(2)}) collective-permute-start(bf16[128,256]{1,0:T(8,128)(2,1)S(1)} %convolution_convert_fusion.refs_0_), channel_id=1, source_target_pairs={{0,2},{1,3},{2,0},{3,1},{4,6},{5,7},{6,4},{7,5},{8,10},{9,11},{10,... | collective-permute-start | bytes 196616 | tf_op jit(solution)/shard_map/ppermute | solution.py:63
  12.9 4.2 %collective-permute-done.1.refs_2_ = bf16[128,256]{1,0:T(8,128)(2,1)S(1)} collective-permute-done((bf16[128,256]{1,0:T(8,128)(2,1)S(1)}, bf16[128,256]{1,0:T(8,128)(2,1)S(1)}, u32[]{:S(2)}, u32[]{:S(2)}) %collective-permute-start.1) | collective-permute-done | bytes 65568 | tf_op jit(solution)/shard_map/ppermute | solution.py:63
  17.1 1.6 %collective-permute-done.2.refs_3_ = bf16[128,256]{1,0:T(8,128)(2,1)S(1)} collective-permute-done((bf16[128,256]{1,0:T(8,128)(2,1)S(1)}, bf16[128,256]{1,0:T(8,128)(2,1)S(1)}, u32[]{:S(2)}, u32[]{:S(2)}) %collective-permute-start.2) | collective-permute-done | bytes 65568 | tf_op jit(solution)/shard_map/ppermute | solution.py:63
  24.0 1.8 %collective-permute-start.8 = (bf16[32,1728]{1,0:T(8,128)(2,1)S(1)}, bf16[32,1728]{1,0:T(8,128)(2,1)S(1)}, u32[]{:S(2)}, u32[]{:S(2)}) collective-permute-start(bf16[32,1728]{1,0:T(8,128)(2,1)S(1)} %get-tuple-element.52), channel_id=1, source_target_pairs={{0,12},{4,8},{8,4},{12,0},{16,28},{20,24},{24,20},{28,16},{1,13},{... | collective-permute-start | bytes 331784 | tf_op jit(solution)/shard_map/ppermute | solution.py:63
  25.9 3.8 %collective-permute-done.5.refs_2_ = bf16[32,1728]{1,0:T(8,128)(2,1)S(1)} collective-permute-done((bf16[32,1728]{1,0:T(8,128)(2,1)S(1)}, bf16[32,1728]{1,0:T(8,128)(2,1)S(1)}, u32[]{:S(2)}, u32[]{:S(2)}) %collective-permute-start.5) | collective-permute-done | bytes 110624 | tf_op jit(solution)/shard_map/ppermute | solution.py:63
  35.9 2.0 %collective-permute-start.16 = (bf16[32,1792]{1,0:T(8,128)(2,1)S(1)}, bf16[32,1792]{1,0:T(8,128)(2,1)S(1)}, u32[]{:S(2)}, u32[]{:S(2)}) collective-permute-start(bf16[32,1792]{1,0:T(8,128)(2,1)S(1)} %get-tuple-element.57.refs_0_), channel_id=1, source_target_pairs={{0,24},{4,28},{8,16},{12,20},{16,8},{20,12},{24,0},{28,4},{1,25},{... | collective-permute-start | bytes 344072 | tf_op jit(solution)/shard_map/ppermute | solution.py:63
  37.9 2.4 %collective-permute-done.12.refs_2_ = bf16[32,1792]{1,0:T(8,128)(2,1)S(1)} collective-permute-done((bf16[32,1792]{1,0:T(8,128)(2,1)S(1)}, bf16[32,1792]{1,0:T(8,128)(2,1)S(1)}, u32[]{:S(2)}, u32[]{:S(2)}) %collective-permute-start.12) | collective-permute-done | bytes 114720 | tf_op jit(solution)/shard_map/ppermute | solution.py:63
  40.3 2.2 %collective-permute-done.14.refs_4_ = bf16[32,1792]{1,0:T(8,128)(2,1)S(1)} collective-permute-done((bf16[32,1792]{1,0:T(8,128)(2,1)S(1)}, bf16[32,1792]{1,0:T(8,128)(2,1)S(1)}, u32[]{:S(2)}, u32[]{:S(2)}) %collective-permute-start.14) | collective-permute-done | bytes 114720 | tf_op jit(solution)/shard_map/ppermute | solution.py:63
  47.3 3.1 %shard_map.97 = f32[1728,640]{1,0:T(8,128)} custom-call(bf16[5120,256]{1,0:T(8,128)(2,1)S(1)} %copy-done.2, f32[1728,640]{1,0:T(8,128)S(1)} %bitcast.8, bf16[1792,256]{1,0:T(8,128)(2,1)S(1)} %get-tuple-element.58.tall.refs_0_), custom_call_target="tpu_custom_call" | custom-call | flops 566231040 | bytes 8847360 | tf_op jit(solution)/shard_map/pallas_call | solution.py:178
  50.4 7.6 %collective-permute-done.20.refs_2_ = bf16[672,640]{1,0:T(8,128)(2,1)S(1)} collective-permute-done((bf16[672,640]{1,0:T(8,128)(2,1)S(1)}, bf16[672,640]{1,0:T(8,128)(2,1)S(1)}, u32[]{:S(2)}, u32[]{:S(2)}) %collective-permute-start.20) | collective-permute-done | bytes 860192 | tf_op jit(solution)/shard_map/ppermute | solution.py:252
  59.3 15.0 %collective-permute-done.18.refs_3_ = bf16[672,640]{1,0:T(8,128)(2,1)S(1)} collective-permute-done((bf16[672,640]{1,0:T(8,128)(2,1)S(1)}, bf16[672,640]{1,0:T(8,128)(2,1)S(1)}, u32[]{:S(2)}, u32[]{:S(2)}) %collective-permute-start.18) | collective-permute-done | bytes 860192 | tf_op jit(solution)/shard_map/ppermute | solution.py:252
  75.5 1.6 %shard_map.98 = (bf16[384,640]{1,0:T(8,128)(2,1)S(1)}, bf16[1728,640]{1,0:T(8,128)(2,1)S(1)}) custom-call(bf16[5120,256]{1,0:T(8,128)(2,1)S(1)} %copy-done.2, f32[1728,640]{1,0:T(8,128)S(1)} %bitcast.9, bf16[1792,256]{1,0:T(8,128)(2,1)S(1)} %get-tuple-element.58.tall.refs_0_), custom_call_target="tpu_custom_call" | custom-call | flops 692060160 | bytes 5406720 | tf_op jit(solution)/shard_map/pallas_call | solution.py:155
  78.5 8.5 %collective-permute-done.27.refs_5_ = bf16[672,640]{1,0:T(8,128)(2,1)S(1)} collective-permute-done((bf16[672,640]{1,0:T(8,128)(2,1)S(1)}, bf16[672,640]{1,0:T(8,128)(2,1)S(1)}, u32[]{:S(2)}, u32[]{:S(2)}) %collective-permute-start.27) | collective-permute-done | bytes 860192 | tf_op jit(solution)/shard_map/ppermute | solution.py:252
  88.8 7.5 %collective-permute-done.24.refs_6_ = bf16[672,640]{1,0:T(8,128)(2,1)S(1)} collective-permute-done((bf16[672,640]{1,0:T(8,128)(2,1)S(1)}, bf16[672,640]{1,0:T(8,128)(2,1)S(1)}, u32[]{:S(2)}, u32[]{:S(2)}) %collective-permute-start.24) | collective-permute-done | bytes 860192 | tf_op jit(solution)/shard_map/ppermute | solution.py:252
  96.3 9.2 %collective-permute-done.29.refs_7_ = bf16[672,640]{1,0:T(8,128)(2,1)S(1)} collective-permute-done((bf16[672,640]{1,0:T(8,128)(2,1)S(1)}, bf16[672,640]{1,0:T(8,128)(2,1)S(1)}, u32[]{:S(2)}, u32[]{:S(2)}) %collective-permute-start.29) | collective-permute-done | bytes 860192 | tf_op jit(solution)/shard_map/ppermute | solution.py:252
  108.1 3.0 %shard_map.99.refs_0_ = bf16[1728,5120]{1,0:T(8,128)(2,1)} custom-call(bf16[1728,640]{1,0:T(8,128)(2,1)S(1)} %get-tuple-element.61.refs_0_.refs_1_, bf16[1728,640]{1,0:T(8,128)(2,1)S(1)} %collective-permute-done.19.refs_1_.refs_2_, bf16[672,640]{1,0:T(8,128)(2,1)S(1)} %collective-permute-done.20.refs_2_, ...), custom_call_target="tpu_custom_call" | custom-call | bytes 13762560 | tf_op jit(solution)/shard_map/pallas_call | solution.py:224
  111.1 3.8 %collective-permute-done.32.refs_5_ = bf16[384,640]{1,0:T(8,128)(2,1)S(1)} collective-permute-done((bf16[384,640]{1,0:T(8,128)(2,1)S(1)}, bf16[384,640]{1,0:T(8,128)(2,1)S(1)}, u32[]{:S(2)}, u32[]{:S(2)}) %collective-permute-start.32) | collective-permute-done | bytes 491552 | tf_op jit(solution)/shard_map/ppermute | solution.py:252
  114.9 3.0 %shard_map.100.refs_0_ = bf16[1728,5120]{1,0:T(8,128)(2,1)} custom-call(bf16[1728,5120]{1,0:T(8,128)(2,1)} %shard_map.99.refs_0_, bf16[1728,640]{1,0:T(8,128)(2,1)S(1)} %get-tuple-element.61.refs_0_.refs_1_, bf16[1728,640]{1,0:T(8,128)(2,1)S(1)} %collective-permute-done.19.refs_1_.refs_2_, ...), custom_call_target="tpu_custom_call", output_to_operand_aliasing={{}: (0, {})} | custom-call | bytes 13762560 | tf_op jit(solution)/shard_map/pallas_call | solution.py:224
  117.9 2.3 %collective-permute-done.34.refs_7_ = bf16[384,640]{1,0:T(8,128)(2,1)S(1)} collective-permute-done((bf16[384,640]{1,0:T(8,128)(2,1)S(1)}, bf16[384,640]{1,0:T(8,128)(2,1)S(1)}, u32[]{:S(2)}, u32[]{:S(2)}) %collective-permute-start.34) | collective-permute-done | bytes 491552 | tf_op jit(solution)/shard_map/ppermute | solution.py:252
  122.7 2.0 %shard_map.102 = bf16[1728,5120]{1,0:T(8,128)(2,1)} custom-call(bf16[1728,5120]{1,0:T(8,128)(2,1)} %shard_map.100.refs_0_, bf16[1728,640]{1,0:T(8,128)(2,1)S(1)} %get-tuple-element.61.refs_0_.refs_1_, bf16[1728,640]{1,0:T(8,128)(2,1)S(1)} %collective-permute-done.19.refs_1_.refs_2_, ...), custom_call_target="tpu_custom_call", output_to_operand_aliasing={{}: (0, {})} | custom-call | bytes 7864320 | tf_op jit(solution)/shard_map/pallas_call | solution.py:224
  (71 shorter events, 27.2 us)
Async XLA Ops:
  3.0 16.5 %collective-permute-start.3 = (f32[384,640]{1,0:T(8,128)}, f32[384,640]{1,0:T(8,128)S(1)}, u32[]{:S(2)}, u32[]{:S(2)}) collective-permute-start(f32[384,640]{1,0:T(8,128)} %shard_map.93), channel_id=1, source_target_pairs={{0,8},{4,20},{8,0},{12,28},{16,24},{20,4},{24,16},{28,12},{1,9},{5... | collective-permute-start | bytes 2949128 | tf_op jit(solution)/shard_map/ppermute | solution.py:252
  10.1 7.0 %collective-permute-start.1 = (bf16[128,256]{1,0:T(8,128)(2,1)S(1)}, bf16[128,256]{1,0:T(8,128)(2,1)S(1)}, u32[]{:S(2)}, u32[]{:S(2)}) collective-permute-start(bf16[128,256]{1,0:T(8,128)(2,1)S(1)} %convolution_convert_fusion.refs_0_), channel_id=1, source_target_pairs={{0,2},{1,3},{2,0},{3,1},{4,6},{5,7},{6,4},{7,5},{8,10},{9,11},{10,... | collective-permute-start | bytes 196616 | tf_op jit(solution)/shard_map/ppermute | solution.py:63
  20.3 9.4 %collective-permute-start.5 = (bf16[32,1728]{1,0:T(8,128)(2,1)S(1)}, bf16[32,1728]{1,0:T(8,128)(2,1)S(1)}, u32[]{:S(2)}, u32[]{:S(2)}) collective-permute-start(bf16[32,1728]{1,0:T(8,128)(2,1)S(1)} %get-tuple-element.49), channel_id=1, source_target_pairs={{0,16},{4,20},{8,24},{12,28},{16,0},{20,4},{24,8},{28,12},{1,17},{... | collective-permute-start | bytes 331784 | tf_op jit(solution)/shard_map/ppermute | solution.py:63
  21.8 7.9 %collective-permute-start.6 = (bf16[32,1728]{1,0:T(8,128)(2,1)S(1)}, bf16[32,1728]{1,0:T(8,128)(2,1)S(1)}, u32[]{:S(2)}, u32[]{:S(2)}) collective-permute-start(bf16[32,1728]{1,0:T(8,128)(2,1)S(1)} %get-tuple-element.50), channel_id=1, source_target_pairs={{0,24},{4,28},{8,16},{12,20},{16,8},{20,12},{24,0},{28,4},{1,25},{... | collective-permute-start | bytes 331784 | tf_op jit(solution)/shard_map/ppermute | solution.py:63
  23.1 7.5 %collective-permute-start.7 = (bf16[32,1728]{1,0:T(8,128)(2,1)S(1)}, bf16[32,1728]{1,0:T(8,128)(2,1)S(1)}, u32[]{:S(2)}, u32[]{:S(2)}) collective-permute-start(bf16[32,1728]{1,0:T(8,128)(2,1)S(1)} %get-tuple-element.51), channel_id=1, source_target_pairs={{0,28},{4,24},{8,20},{12,16},{16,12},{20,8},{24,4},{28,0},{1,29},{... | collective-permute-start | bytes 331784 | tf_op jit(solution)/shard_map/ppermute | solution.py:63
  24.0 8.1 %collective-permute-start.8 = (bf16[32,1728]{1,0:T(8,128)(2,1)S(1)}, bf16[32,1728]{1,0:T(8,128)(2,1)S(1)}, u32[]{:S(2)}, u32[]{:S(2)}) collective-permute-start(bf16[32,1728]{1,0:T(8,128)(2,1)S(1)} %get-tuple-element.52), channel_id=1, source_target_pairs={{0,12},{4,8},{8,4},{12,0},{16,28},{20,24},{24,20},{28,16},{1,13},{... | collective-permute-start | bytes 331784 | tf_op jit(solution)/shard_map/ppermute | solution.py:63
  25.8 7.6 %collective-permute-start.9 = (bf16[32,1728]{1,0:T(8,128)(2,1)S(1)}, bf16[32,1728]{1,0:T(8,128)(2,1)S(1)}, u32[]{:S(2)}, u32[]{:S(2)}) collective-permute-start(bf16[32,1728]{1,0:T(8,128)(2,1)S(1)} %get-tuple-element.53), channel_id=1, source_target_pairs={{0,20},{4,16},{8,28},{12,24},{16,4},{20,0},{24,12},{28,8},{1,21},{... | collective-permute-start | bytes 331784 | tf_op jit(solution)/shard_map/ppermute | solution.py:63
  35.2 7.3 %collective-permute-start.14 = (bf16[32,1792]{1,0:T(8,128)(2,1)S(1)}, bf16[32,1792]{1,0:T(8,128)(2,1)S(1)}, u32[]{:S(2)}, u32[]{:S(2)}) collective-permute-start(bf16[32,1792]{1,0:T(8,128)(2,1)S(1)} %get-tuple-element.57.refs_0_), channel_id=1, source_target_pairs={{0,16},{4,20},{8,24},{12,28},{16,0},{20,4},{24,8},{28,12},{1,17},{... | collective-permute-start | bytes 344072 | tf_op jit(solution)/shard_map/ppermute | solution.py:63
  45.2 12.8 %collective-permute-start.20 = (bf16[672,640]{1,0:T(8,128)(2,1)S(1)}, bf16[672,640]{1,0:T(8,128)(2,1)S(1)}, u32[]{:S(2)}, u32[]{:S(2)}) collective-permute-start(bf16[672,640]{1,0:T(8,128)(2,1)S(1)} %get-tuple-element.63), channel_id=1, source_target_pairs={{0,8},{4,20},{8,0},{12,28},{16,24},{20,4},{24,16},{28,12},{1,9},{5... | collective-permute-start | bytes 2580488 | tf_op jit(solution)/shard_map/ppermute | solution.py:252
  46.5 27.8 %collective-permute-start.18 = (bf16[672,640]{1,0:T(8,128)(2,1)S(1)}, bf16[672,640]{1,0:T(8,128)(2,1)S(1)}, u32[]{:S(2)}, u32[]{:S(2)}) collective-permute-start(bf16[672,640]{1,0:T(8,128)(2,1)S(1)} %get-tuple-element.65), channel_id=1, source_target_pairs={{0,8},{4,20},{8,0},{12,28},{16,24},{20,4},{24,16},{28,12},{1,9},{5... | collective-permute-start | bytes 2580488 | tf_op jit(solution)/shard_map/ppermute | solution.py:252
  58.0 19.7 %collective-permute-start.22 = (bf16[672,640]{1,0:T(8,128)(2,1)S(1)}, bf16[672,640]{1,0:T(8,128)(2,1)S(1)}, u32[]{:S(2)}, u32[]{:S(2)}) collective-permute-start(bf16[672,640]{1,0:T(8,128)(2,1)S(1)} %get-tuple-element.63), channel_id=1, source_target_pairs={{0,16},{4,12},{8,24},{12,4},{16,0},{20,28},{24,8},{28,20},{1,17},{... | collective-permute-start | bytes 2580488 | tf_op jit(solution)/shard_map/ppermute | solution.py:252
  59.3 18.5 %collective-permute-start.21 = (bf16[672,640]{1,0:T(8,128)(2,1)S(1)}, bf16[672,640]{1,0:T(8,128)(2,1)S(1)}, u32[]{:S(2)}, u32[]{:S(2)}) collective-permute-start(bf16[672,640]{1,0:T(8,128)(2,1)S(1)} %collective-permute-done.20.refs_2_), channel_id=1, source_target_pairs={{0,4},{4,0},{8,12},{12,8},{16,20},{20,16},{24,28},{28,24},{1,5},{5... | collective-permute-start | bytes 2580488 | tf_op jit(solution)/shard_map/ppermute | solution.py:63
  74.3 12.8 %collective-permute-start.27 = (bf16[672,640]{1,0:T(8,128)(2,1)S(1)}, bf16[672,640]{1,0:T(8,128)(2,1)S(1)}, u32[]{:S(2)}, u32[]{:S(2)}) collective-permute-start(bf16[672,640]{1,0:T(8,128)(2,1)S(1)} %get-tuple-element.65), channel_id=1, source_target_pairs={{0,16},{4,12},{8,24},{12,4},{16,0},{20,28},{24,8},{28,20},{1,17},{... | collective-permute-start | bytes 2580488 | tf_op jit(solution)/shard_map/ppermute | solution.py:252
  75.5 11.6 %collective-permute-start.26 = (bf16[672,640]{1,0:T(8,128)(2,1)S(1)}, bf16[672,640]{1,0:T(8,128)(2,1)S(1)}, u32[]{:S(2)}, u32[]{:S(2)}) collective-permute-start(bf16[672,640]{1,0:T(8,128)(2,1)S(1)} %collective-permute-done.18.refs_3_), channel_id=1, source_target_pairs={{0,4},{4,0},{8,12},{12,8},{16,20},{20,16},{24,28},{28,24},{1,5},{5... | collective-permute-start | bytes 2580488 | tf_op jit(solution)/shard_map/ppermute | solution.py:63
  77.2 30.9 %collective-permute-start.19 = (bf16[1728,640]{1,0:T(8,128)(2,1)S(1)}, bf16[1728,640]{1,0:T(8,128)(2,1)S(1)}, u32[]{:S(2)}, u32[]{:S(2)}) collective-permute-start(bf16[1728,640]{1,0:T(8,128)(2,1)S(1)} %get-tuple-element.61.refs_0_.refs_1_), channel_id=1, source_target_pairs={{0,4},{4,0},{8,12},{12,8},{16,20},{20,16},{24,28},{28,24},{1,5},{5... | collective-permute-start | bytes 6635528 | tf_op jit(solution)/shard_map/ppermute | solution.py:63
  77.7 18.6 %collective-permute-start.24 = (bf16[672,640]{1,0:T(8,128)(2,1)S(1)}, bf16[672,640]{1,0:T(8,128)(2,1)S(1)}, u32[]{:S(2)}, u32[]{:S(2)}) collective-permute-start(bf16[672,640]{1,0:T(8,128)(2,1)S(1)} %collective-permute-done.20.refs_2_), channel_id=1, source_target_pairs={{0,16},{4,12},{8,24},{12,4},{16,0},{20,28},{24,8},{28,20},{1,17},{... | collective-permute-start | bytes 2580488 | tf_op jit(solution)/shard_map/ppermute | solution.py:252
  87.1 18.4 %collective-permute-start.29 = (bf16[672,640]{1,0:T(8,128)(2,1)S(1)}, bf16[672,640]{1,0:T(8,128)(2,1)S(1)}, u32[]{:S(2)}, u32[]{:S(2)}) collective-permute-start(bf16[672,640]{1,0:T(8,128)(2,1)S(1)} %collective-permute-done.18.refs_3_), channel_id=1, source_target_pairs={{0,16},{4,12},{8,24},{12,4},{16,0},{20,28},{24,8},{28,20},{1,17},{... | collective-permute-start | bytes 2580488 | tf_op jit(solution)/shard_map/ppermute | solution.py:252
  88.3 17.6 %collective-permute-start.23 = (bf16[672,640]{1,0:T(8,128)(2,1)S(1)}, bf16[672,640]{1,0:T(8,128)(2,1)S(1)}, u32[]{:S(2)}, u32[]{:S(2)}) collective-permute-start(bf16[672,640]{1,0:T(8,128)(2,1)S(1)} %collective-permute-done.22.refs_4_), channel_id=1, source_target_pairs={{0,4},{4,0},{8,12},{12,8},{16,20},{20,16},{24,28},{28,24},{1,5},{5... | collective-permute-start | bytes 2580488 | tf_op jit(solution)/shard_map/ppermute | solution.py:63
  88.3 19.0 %collective-permute-start.28 = (bf16[672,640]{1,0:T(8,128)(2,1)S(1)}, bf16[672,640]{1,0:T(8,128)(2,1)S(1)}, u32[]{:S(2)}, u32[]{:S(2)}) collective-permute-start(bf16[672,640]{1,0:T(8,128)(2,1)S(1)} %collective-permute-done.27.refs_5_), channel_id=1, source_target_pairs={{0,4},{4,0},{8,12},{12,8},{16,20},{20,16},{24,28},{28,24},{1,5},{5... | collective-permute-start | bytes 2580488 | tf_op jit(solution)/shard_map/ppermute | solution.py:63
  96.3 11.8 %collective-permute-start.25 = (bf16[672,640]{1,0:T(8,128)(2,1)S(1)}, bf16[672,640]{1,0:T(8,128)(2,1)S(1)}, u32[]{:S(2)}, u32[]{:S(2)}) collective-permute-start(bf16[672,640]{1,0:T(8,128)(2,1)S(1)} %collective-permute-done.24.refs_6_), channel_id=1, source_target_pairs={{0,4},{4,0},{8,12},{12,8},{16,20},{20,16},{24,28},{28,24},{1,5},{5... | collective-permute-start | bytes 2580488 | tf_op jit(solution)/shard_map/ppermute | solution.py:63
  105.5 9.4 %collective-permute-start.30 = (bf16[672,640]{1,0:T(8,128)(2,1)S(1)}, bf16[672,640]{1,0:T(8,128)(2,1)S(1)}, u32[]{:S(2)}, u32[]{:S(2)}) collective-permute-start(bf16[672,640]{1,0:T(8,128)(2,1)S(1)} %collective-permute-done.29.refs_7_), channel_id=1, source_target_pairs={{0,4},{4,0},{8,12},{12,8},{16,20},{20,16},{24,28},{28,24},{1,5},{5... | collective-permute-start | bytes 2580488 | tf_op jit(solution)/shard_map/ppermute | solution.py:63
  106.0 8.9 %collective-permute-start.32 = (bf16[384,640]{1,0:T(8,128)(2,1)S(1)}, bf16[384,640]{1,0:T(8,128)(2,1)S(1)}, u32[]{:S(2)}, u32[]{:S(2)}) collective-permute-start(bf16[384,640]{1,0:T(8,128)(2,1)S(1)} %get-tuple-element.68), channel_id=1, source_target_pairs={{0,16},{4,12},{8,24},{12,4},{16,0},{20,28},{24,8},{28,20},{1,17},{... | collective-permute-start | bytes 1474568 | tf_op jit(solution)/shard_map/ppermute | solution.py:252
  107.3 12.9 %collective-permute-start.34 = (bf16[384,640]{1,0:T(8,128)(2,1)S(1)}, bf16[384,640]{1,0:T(8,128)(2,1)S(1)}, u32[]{:S(2)}, u32[]{:S(2)}) collective-permute-start(bf16[384,640]{1,0:T(8,128)(2,1)S(1)} %shard_map.101.refs_3_), channel_id=1, source_target_pairs={{0,16},{4,12},{8,24},{12,4},{16,0},{20,28},{24,8},{28,20},{1,17},{... | collective-permute-start | bytes 1474568 | tf_op jit(solution)/shard_map/ppermute | solution.py:252
  108.1 12.6 %collective-permute-start.31 = (bf16[384,640]{1,0:T(8,128)(2,1)S(1)}, bf16[384,640]{1,0:T(8,128)(2,1)S(1)}, u32[]{:S(2)}, u32[]{:S(2)}) collective-permute-start(bf16[384,640]{1,0:T(8,128)(2,1)S(1)} %shard_map.101.refs_3_), channel_id=1, source_target_pairs={{0,4},{4,0},{8,12},{12,8},{16,20},{20,16},{24,28},{28,24},{1,5},{5... | collective-permute-start | bytes 1474568 | tf_op jit(solution)/shard_map/ppermute | solution.py:63
  (18 other events, 209.3 us)

commit v6 on v5

--- a/solution.py
+++ b/solution.py
@@ -26,8 +26,8 @@
 
 
 def chunk_sizes(cols):
-    rest = -(-cols * 7 // 18 // 16) * 16
-    return (cols - 2 * rest, rest, rest)
+    rest = cols // 80 * 16
+    return (cols - 4 * rest, rest, rest, rest, rest)
 
 
 def adam(grad, moment_one, moment_two):
@@ -63,10 +63,16 @@
     return lax.ppermute(value, axis, [(i, i ^ mask) for i in range(size)])
 
 
-def take_kernel(source, out, sem):
-    copy = pltpu.make_async_copy(source.at[pl.ds(0, out.shape[0]), :], out, sem)
-    copy.start()
-    copy.wait()
+def take_kernel(source, out, sems):
+    count = out.shape[0] // sems.shape[0]
+    copies = []
+    for at in range(sems.shape[0]):
+        rows = pl.ds(at * count, count)
+        copies.append(pltpu.make_async_copy(source.at[rows, :], out.at[rows, :], sems.at[at]))
+    for copy in copies:
+        copy.start()
+    for copy in copies:
+        copy.wait()
 
 
 def take(array, count):
@@ -75,7 +81,7 @@
         out_shape=jax.ShapeDtypeStruct((count, array.shape[1]), array.dtype),
         in_specs=[ANY],
         out_specs=VMEM,
-        scratch_shapes=[pltpu.SemaphoreType.DMA],
+        scratch_shapes=[pltpu.SemaphoreType.DMA((count // 16,))],
         compiler_params=pltpu.CompilerParams(vmem_limit_bytes=60 * 2**20),
     )(array)
 
@@ -126,8 +132,9 @@
         tall, wide = outs[0], outs[-1]
         outs = outs[1:-1]
         rows = pieces[0].shape[0]
-        for k, piece in enumerate(pieces):
-            wide[pl.ds(pl.multiple_of((me ^ k) * rows, rows), rows), :] = piece[...]
+        for piece_masks, piece in zip(OWNER_MASKS, pieces):
+            owner = me ^ jnp.where((me & 1) == 0, piece_masks[0], piece_masks[1])
+            wide[pl.ds(pl.multiple_of(owner * rows, rows), rows), :] = piece[...]
         tall[...] = wide[...].T
     else:
         tall = pieces[0]
@@ -288,12 +295,11 @@
         compiler_params=pltpu.CompilerParams(vmem_limit_bytes=16 * 2**20),
     )(moment_one, moment_two, *parts)
 
-    updates = {0: update}
-    for k in (6, 2, 4, 1):
-        updates[k] = hop(update, k)
-    for k in (2, 4, 6):
-        updates[k ^ 1] = hop(updates[k], 1)
-    updates = [updates[k] for k in range(n_dp)]
+    brought = [turn(update, 0), turn(update, 1)]
+    brought.append(turn(brought[0], 1))
+    updates = []
+    for value in [update] + brought:
+        updates += [value, hop(value, 1)]
 
     tall, *own = weights(projection, master_t, updates, spans[1:])
     own_last, whole = weights(projection, master_t, [tall], spans[:1] + [(0, cols)])
@@ -313,7 +319,7 @@
         if step == 2:
             earlier.append(master_new)
         got[(phase, at)] = turn(after(value, earlier), min(phase, 1))
-        held = outs[step - len(steps) + 3 : step - len(steps) + 4] if step >= len(steps) - 2 else []
+        held = [outs[chunks + step - len(steps)]] if step >= len(steps) - 2 else []
         over[(phase, at)] = hop(after(got[(phase, at)], held), 1)
         if step == 1:
             whole_c = hop(after(whole, [got[steps[1]]]), 1)

time: 125 us -> 122 us (0.976)
  waiting for transfers between devices: 75.1 us -> 67.5 us
  starting transfers between devices: 28.1 us -> 32.5 us
  Pallas kernels: 18.3 us -> 20.2 us
  matrix products: 2.4 us -> 0.51 us
    ppermute x9 -> x18, starting transfers between devices: 11.7 us -> 19.1 us  [turn(): return lax.ppermute(value, 'dp', [(i, i ^ masks[i]) for i in range(n_dp)])]
    ppermute x27 -> x30, waiting for transfers between devices: 21.1 us -> 16.2 us  [send(): return lax.ppermute(value, axis, [(i, i ^ mask) for i in range(size)])]
    ppermute x27 -> x30, starting transfers between devices: 16.5 us -> 13.4 us  [send(): return lax.ppermute(value, axis, [(i, i ^ mask) for i in range(size)])]
    ppermute x9 -> x18, waiting for transfers between devices: 54 us -> 51.3 us  [turn(): return lax.ppermute(value, 'dp', [(i, i ^ masks[i]) for i in range(n_dp)])]
    dot_general x1, matrix products: 2.4 us -> 0.51 us  [kernel_body(): jnp.dot(acts, projection, preferred_element_type=jnp.float32)]
    pallas_call x3 -> x5, Pallas kernels: 8 us -> 9.53 us  [lay(): pl.pallas_call(functools.partial(lay_kernel, first=first, count=count, bl...]
  transfers between devices with their start and end apart: 36 -> 48, of which waited for: 19 -> 22; matrix products, arithmetic and copies ran while one was open for 2% -> 0% of each run, Pallas kernels for 10% -> 11%
where the time goes in v6:
time: 122 us
  waiting for transfers between devices  67.5 us (55%)
  starting transfers between devices  32.5 us (27%)
  Pallas kernels  20.2 us (17%)
    ppermute x18, waiting for transfers between devices, turn(): return lax.ppermute(value, 'dp', [(i, i ^ masks[i]) for i in range(n_dp)])  51.3 us
    ppermute x18, starting transfers between devices, turn(): return lax.ppermute(value, 'dp', [(i, i ^ masks[i]) for i in range(n_dp)])  19.1 us
    ppermute x30, waiting for transfers between devices, send(): return lax.ppermute(value, axis, [(i, i ^ mask) for i in range(size)])  16.2 us
    ppermute x30, starting transfers between devices, send(): return lax.ppermute(value, axis, [(i, i ^ mask) for i in range(size)])  13.4 us
    pallas_call x5, Pallas kernels, lay(): pl.pallas_call(functools.partial(lay_kernel, first=first, count=count, bl...  9.53 us
    pallas_call x3, Pallas kernels, weights(): pl.pallas_call(functools.partial(weight_kernel, n_in=len(pieces), masks=m...  3.41 us
    pallas_call x1, Pallas kernels, new_master(): pl.pallas_call(master_kernel, out_shape=jax.ShapeDtypeStruct((cols, slab_...  3.11 us
    pallas_call x1, Pallas kernels, take(): pl.pallas_call(take_kernel, out_shape=jax.ShapeDtypeStruct((count, array....  2.46 us
  transfers between devices with their start and end apart: 48, of which 22 were waited for; matrix products, arithmetic and copies ran while one was open for 0% of the time, Pallas kernels for 11%

profile of v6, /device:TPU:0, one launch (start us, length us, event | category | flops | bytes accessed | tf_op | source)
XLA Modules:
  0.0 121.5 jit_solution(11786538954012093286)
XLA Ops:
  0.7 2.5 %shard_map.93 = f32[384,640]{1,0:T(8,128)} custom-call(f32[1728,640]{1,0:T(8,128)} %bitcast.6), custom_call_target="tpu_custom_call" | custom-call | tf_op jit(solution)/shard_map/pallas_call | solution.py:79
  3.2 3.0 %collective-permute-start.3 = (f32[384,640]{1,0:T(8,128)}, f32[384,640]{1,0:T(8,128)S(1)}, u32[]{:S(2)}, u32[]{:S(2)}) collective-permute-start(f32[384,640]{1,0:T(8,128)} %shard_map.93), channel_id=1, source_target_pairs={{0,8},{4,20},{8,0},{12,28},{16,24},{20,4},{24,16},{28,12},{1,9},{5... | collective-permute-start | bytes 2949128 | tf_op jit(solution)/shard_map/ppermute | solution.py:259
  8.3 2.6 %collective-permute-start.1 = (bf16[128,256]{1,0:T(8,128)(2,1)S(1)}, bf16[128,256]{1,0:T(8,128)(2,1)S(1)}, u32[]{:S(2)}, u32[]{:S(2)}) collective-permute-start(bf16[128,256]{1,0:T(8,128)(2,1)S(1)} %convolution_convert_fusion.refs_0_), channel_id=1, source_target_pairs={{0,2},{1,3},{2,0},{3,1},{4,6},{5,7},{6,4},{7,5},{8,10},{9,11},{10,... | collective-permute-start | bytes 196616 | tf_op jit(solution)/shard_map/ppermute | solution.py:63
  11.1 4.2 %collective-permute-done.1.refs_2_ = bf16[128,256]{1,0:T(8,128)(2,1)S(1)} collective-permute-done((bf16[128,256]{1,0:T(8,128)(2,1)S(1)}, bf16[128,256]{1,0:T(8,128)(2,1)S(1)}, u32[]{:S(2)}, u32[]{:S(2)}) %collective-permute-start.1) | collective-permute-done | bytes 65568 | tf_op jit(solution)/shard_map/ppermute | solution.py:63
  18.5 2.0 %collective-permute-start.4 = (bf16[32,1728]{1,0:T(8,128)(2,1)S(1)}, bf16[32,1728]{1,0:T(8,128)(2,1)S(1)}, u32[]{:S(2)}, u32[]{:S(2)}) collective-permute-start(bf16[32,1728]{1,0:T(8,128)(2,1)S(1)} %get-tuple-element.56), channel_id=1, source_target_pairs={{0,8},{4,12},{8,0},{12,4},{16,24},{20,28},{24,16},{28,20},{1,9},{5... | collective-permute-start | bytes 331784 | tf_op jit(solution)/shard_map/ppermute | solution.py:63
  22.7 2.5 %collective-permute-start.8 = (bf16[32,1728]{1,0:T(8,128)(2,1)S(1)}, bf16[32,1728]{1,0:T(8,128)(2,1)S(1)}, u32[]{:S(2)}, u32[]{:S(2)}) collective-permute-start(bf16[32,1728]{1,0:T(8,128)(2,1)S(1)} %get-tuple-element.60), channel_id=1, source_target_pairs={{0,12},{4,8},{8,4},{12,0},{16,28},{20,24},{24,20},{28,16},{1,13},{... | collective-permute-start | bytes 331784 | tf_op jit(solution)/shard_map/ppermute | solution.py:63
  25.2 3.8 %collective-permute-done.5.refs_2_ = bf16[32,1728]{1,0:T(8,128)(2,1)S(1)} collective-permute-done((bf16[32,1728]{1,0:T(8,128)(2,1)S(1)}, bf16[32,1728]{1,0:T(8,128)(2,1)S(1)}, u32[]{:S(2)}, u32[]{:S(2)}) %collective-permute-start.5) | collective-permute-done | bytes 110624 | tf_op jit(solution)/shard_map/ppermute | solution.py:63
  29.0 2.3 %collective-permute-done.8.refs_5_ = bf16[32,1728]{1,0:T(8,128)(2,1)S(1)} collective-permute-done((bf16[32,1728]{1,0:T(8,128)(2,1)S(1)}, bf16[32,1728]{1,0:T(8,128)(2,1)S(1)}, u32[]{:S(2)}, u32[]{:S(2)}) %collective-permute-start.8) | collective-permute-done | bytes 110624 | tf_op jit(solution)/shard_map/ppermute | solution.py:63
  34.5 4.6 %collective-permute-done.12.refs_2_ = bf16[32,1792]{1,0:T(8,128)(2,1)S(1)} collective-permute-done((bf16[32,1792]{1,0:T(8,128)(2,1)S(1)}, bf16[32,1792]{1,0:T(8,128)(2,1)S(1)}, u32[]{:S(2)}, u32[]{:S(2)}) %collective-permute-start.12) | collective-permute-done | bytes 114720 | tf_op jit(solution)/shard_map/ppermute | solution.py:259
  40.7 3.2 %collective-permute-done.16.refs_6_ = bf16[32,1792]{1,0:T(8,128)(2,1)S(1)} collective-permute-done((bf16[32,1792]{1,0:T(8,128)(2,1)S(1)}, bf16[32,1792]{1,0:T(8,128)(2,1)S(1)}, u32[]{:S(2)}, u32[]{:S(2)}) %collective-permute-start.16) | collective-permute-done | bytes 114720 | tf_op jit(solution)/shard_map/ppermute | solution.py:259
  48.7 3.1 %shard_map.97 = f32[1728,640]{1,0:T(8,128)} custom-call(bf16[5120,256]{1,0:T(8,128)(2,1)S(1)} %copy-done.2, f32[1728,640]{1,0:T(8,128)S(1)} %bitcast.8, bf16[1792,256]{1,0:T(8,128)(2,1)S(1)} %get-tuple-element.66.tall.refs_0_), custom_call_target="tpu_custom_call" | custom-call | flops 566231040 | bytes 8847360 | tf_op jit(solution)/shard_map/pallas_call | solution.py:185
  51.8 3.0 %collective-permute-done.20.refs_2_ = bf16[336,640]{1,0:T(8,128)(2,1)S(1)} collective-permute-done((bf16[336,640]{1,0:T(8,128)(2,1)S(1)}, bf16[336,640]{1,0:T(8,128)(2,1)S(1)}, u32[]{:S(2)}, u32[]{:S(2)}) %collective-permute-start.20) | collective-permute-done | bytes 430112 | tf_op jit(solution)/shard_map/ppermute | solution.py:259
  55.1 4.3 %collective-permute-done.18.refs_3_ = bf16[336,640]{1,0:T(8,128)(2,1)S(1)} collective-permute-done((bf16[336,640]{1,0:T(8,128)(2,1)S(1)}, bf16[336,640]{1,0:T(8,128)(2,1)S(1)}, u32[]{:S(2)}, u32[]{:S(2)}) %collective-permute-start.18) | collective-permute-done | bytes 430112 | tf_op jit(solution)/shard_map/ppermute | solution.py:259
  59.7 4.3 %collective-permute-done.22.refs_3_ = bf16[336,640]{1,0:T(8,128)(2,1)S(1)} collective-permute-done((bf16[336,640]{1,0:T(8,128)(2,1)S(1)}, bf16[336,640]{1,0:T(8,128)(2,1)S(1)}, u32[]{:S(2)}, u32[]{:S(2)}) %collective-permute-start.22) | collective-permute-done | bytes 430112 | tf_op jit(solution)/shard_map/ppermute | solution.py:259
  65.1 6.1 %collective-permute-done.30.refs_3_ = bf16[336,640]{1,0:T(8,128)(2,1)S(1)} collective-permute-done((bf16[336,640]{1,0:T(8,128)(2,1)S(1)}, bf16[336,640]{1,0:T(8,128)(2,1)S(1)}, u32[]{:S(2)}, u32[]{:S(2)}) %collective-permute-start.30) | collective-permute-done | bytes 430112 | tf_op jit(solution)/shard_map/ppermute | solution.py:259
  75.6 3.8 %collective-permute-done.31.refs_5_ = bf16[336,640]{1,0:T(8,128)(2,1)S(1)} collective-permute-done((bf16[336,640]{1,0:T(8,128)(2,1)S(1)}, bf16[336,640]{1,0:T(8,128)(2,1)S(1)}, u32[]{:S(2)}, u32[]{:S(2)}) %collective-permute-start.31) | collective-permute-done | bytes 430112 | tf_op jit(solution)/shard_map/ppermute | solution.py:259
  80.6 3.5 %collective-permute-done.26.refs_5_ = bf16[336,640]{1,0:T(8,128)(2,1)S(1)} collective-permute-done((bf16[336,640]{1,0:T(8,128)(2,1)S(1)}, bf16[336,640]{1,0:T(8,128)(2,1)S(1)}, u32[]{:S(2)}, u32[]{:S(2)}) %collective-permute-start.26) | collective-permute-done | bytes 430112 | tf_op jit(solution)/shard_map/ppermute | solution.py:259
  85.2 3.5 %collective-permute-done.34.refs_5_ = bf16[336,640]{1,0:T(8,128)(2,1)S(1)} collective-permute-done((bf16[336,640]{1,0:T(8,128)(2,1)S(1)}, bf16[336,640]{1,0:T(8,128)(2,1)S(1)}, u32[]{:S(2)}, u32[]{:S(2)}) %collective-permute-start.34) | collective-permute-done | bytes 430112 | tf_op jit(solution)/shard_map/ppermute | solution.py:259
  89.8 3.5 %collective-permute-done.27.refs_6_ = bf16[336,640]{1,0:T(8,128)(2,1)S(1)} collective-permute-done((bf16[336,640]{1,0:T(8,128)(2,1)S(1)}, bf16[336,640]{1,0:T(8,128)(2,1)S(1)}, u32[]{:S(2)}, u32[]{:S(2)}) %collective-permute-start.27) | collective-permute-done | bytes 430112 | tf_op jit(solution)/shard_map/ppermute | solution.py:259
  94.4 3.5 %collective-permute-done.35.refs_7_ = bf16[336,640]{1,0:T(8,128)(2,1)S(1)} collective-permute-done((bf16[336,640]{1,0:T(8,128)(2,1)S(1)}, bf16[336,640]{1,0:T(8,128)(2,1)S(1)}, u32[]{:S(2)}, u32[]{:S(2)}) %collective-permute-start.35) | collective-permute-done | bytes 430112 | tf_op jit(solution)/shard_map/ppermute | solution.py:259
  99.0 3.5 %collective-permute-done.38.refs_7_ = bf16[336,640]{1,0:T(8,128)(2,1)S(1)} collective-permute-done((bf16[336,640]{1,0:T(8,128)(2,1)S(1)}, bf16[336,640]{1,0:T(8,128)(2,1)S(1)}, u32[]{:S(2)}, u32[]{:S(2)}) %collective-permute-start.38) | collective-permute-done | bytes 430112 | tf_op jit(solution)/shard_map/ppermute | solution.py:259
  104.0 3.0 %collective-permute-done.41.refs_7_ = bf16[336,640]{1,0:T(8,128)(2,1)S(1)} collective-permute-done((bf16[336,640]{1,0:T(8,128)(2,1)S(1)}, bf16[336,640]{1,0:T(8,128)(2,1)S(1)}, u32[]{:S(2)}, u32[]{:S(2)}) %collective-permute-start.41) | collective-permute-done | bytes 430112 | tf_op jit(solution)/shard_map/ppermute | solution.py:259
  110.6 1.9 %shard_map.100.refs_0_ = bf16[1728,5120]{1,0:T(8,128)(2,1)} custom-call(bf16[1728,5120]{1,0:T(8,128)(2,1)} %shard_map.99.refs_0_, bf16[1728,640]{1,0:T(8,128)(2,1)S(1)} %get-tuple-element.69.refs_0_.refs_1_, bf16[1728,640]{1,0:T(8,128)(2,1)S(1)} %collective-permute-done.19.refs_1_.refs_2_, ...), custom_call_target="tpu_custom_call", output_to_operand_aliasing={{}: (0, {})} | custom-call | bytes 6881280 | tf_op jit(solution)/shard_map/pallas_call | solution.py:231
  119.5 2.0 %shard_map.104 = bf16[1728,5120]{1,0:T(8,128)(2,1)} custom-call(bf16[1728,5120]{1,0:T(8,128)(2,1)} %shard_map.102.refs_0_, bf16[1728,640]{1,0:T(8,128)(2,1)S(1)} %get-tuple-element.69.refs_0_.refs_1_, bf16[1728,640]{1,0:T(8,128)(2,1)S(1)} %collective-permute-done.19.refs_1_.refs_2_, ...), custom_call_target="tpu_custom_call", output_to_operand_aliasing={{}: (0, {})} | custom-call | bytes 7864320 | tf_op jit(solution)/shard_map/pallas_call | solution.py:231
  (97 shorter events, 40.9 us)
Async XLA Ops:
  3.2 15.3 %collective-permute-start.3 = (f32[384,640]{1,0:T(8,128)}, f32[384,640]{1,0:T(8,128)S(1)}, u32[]{:S(2)}, u32[]{:S(2)}) collective-permute-start(f32[384,640]{1,0:T(8,128)} %shard_map.93), channel_id=1, source_target_pairs={{0,8},{4,20},{8,0},{12,28},{16,24},{20,4},{24,16},{28,12},{1,9},{5... | collective-permute-start | bytes 2949128 | tf_op jit(solution)/shard_map/ppermute | solution.py:259
  20.5 8.5 %collective-permute-start.5 = (bf16[32,1728]{1,0:T(8,128)(2,1)S(1)}, bf16[32,1728]{1,0:T(8,128)(2,1)S(1)}, u32[]{:S(2)}, u32[]{:S(2)}) collective-permute-start(bf16[32,1728]{1,0:T(8,128)(2,1)S(1)} %get-tuple-element.57), channel_id=1, source_target_pairs={{0,16},{4,20},{8,24},{12,28},{16,0},{20,4},{24,8},{28,12},{1,17},{... | collective-permute-start | bytes 331784 | tf_op jit(solution)/shard_map/ppermute | solution.py:63
  22.7 8.7 %collective-permute-start.8 = (bf16[32,1728]{1,0:T(8,128)(2,1)S(1)}, bf16[32,1728]{1,0:T(8,128)(2,1)S(1)}, u32[]{:S(2)}, u32[]{:S(2)}) collective-permute-start(bf16[32,1728]{1,0:T(8,128)(2,1)S(1)} %get-tuple-element.60), channel_id=1, source_target_pairs={{0,12},{4,8},{8,4},{12,0},{16,28},{20,24},{24,20},{28,16},{1,13},{... | collective-permute-start | bytes 331784 | tf_op jit(solution)/shard_map/ppermute | solution.py:63
  46.6 8.2 %collective-permute-start.20 = (bf16[336,640]{1,0:T(8,128)(2,1)S(1)}, bf16[336,640]{1,0:T(8,128)(2,1)S(1)}, u32[]{:S(2)}, u32[]{:S(2)}) collective-permute-start(bf16[336,640]{1,0:T(8,128)(2,1)S(1)} %get-tuple-element.73), channel_id=1, source_target_pairs={{0,8},{4,20},{8,0},{12,28},{16,24},{20,4},{24,16},{28,12},{1,9},{5... | collective-permute-start | bytes 1290248 | tf_op jit(solution)/shard_map/ppermute | solution.py:259
  47.0 12.4 %collective-permute-start.18 = (bf16[336,640]{1,0:T(8,128)(2,1)S(1)}, bf16[336,640]{1,0:T(8,128)(2,1)S(1)}, u32[]{:S(2)}, u32[]{:S(2)}) collective-permute-start(bf16[336,640]{1,0:T(8,128)(2,1)S(1)} %get-tuple-element.78), channel_id=1, source_target_pairs={{0,8},{4,20},{8,0},{12,28},{16,24},{20,4},{24,16},{28,12},{1,9},{5... | collective-permute-start | bytes 1290248 | tf_op jit(solution)/shard_map/ppermute | solution.py:259
  54.8 9.2 %collective-permute-start.22 = (bf16[336,640]{1,0:T(8,128)(2,1)S(1)}, bf16[336,640]{1,0:T(8,128)(2,1)S(1)}, u32[]{:S(2)}, u32[]{:S(2)}) collective-permute-start(bf16[336,640]{1,0:T(8,128)(2,1)S(1)} %get-tuple-element.74), channel_id=1, source_target_pairs={{0,8},{4,20},{8,0},{12,28},{16,24},{20,4},{24,16},{28,12},{1,9},{5... | collective-permute-start | bytes 1290248 | tf_op jit(solution)/shard_map/ppermute | solution.py:259
  55.1 8.9 %collective-permute-start.21 = (bf16[336,640]{1,0:T(8,128)(2,1)S(1)}, bf16[336,640]{1,0:T(8,128)(2,1)S(1)}, u32[]{:S(2)}, u32[]{:S(2)}) collective-permute-start(bf16[336,640]{1,0:T(8,128)(2,1)S(1)} %collective-permute-done.20.refs_2_), channel_id=1, source_target_pairs={{0,4},{4,0},{8,12},{12,8},{16,20},{20,16},{24,28},{28,24},{1,5},{5... | collective-permute-start | bytes 1290248 | tf_op jit(solution)/shard_map/ppermute | solution.py:63
  59.4 11.9 %collective-permute-start.30 = (bf16[336,640]{1,0:T(8,128)(2,1)S(1)}, bf16[336,640]{1,0:T(8,128)(2,1)S(1)}, u32[]{:S(2)}, u32[]{:S(2)}) collective-permute-start(bf16[336,640]{1,0:T(8,128)(2,1)S(1)} %get-tuple-element.79), channel_id=1, source_target_pairs={{0,8},{4,20},{8,0},{12,28},{16,24},{20,4},{24,16},{28,12},{1,9},{5... | collective-permute-start | bytes 1290248 | tf_op jit(solution)/shard_map/ppermute | solution.py:259
  64.0 10.6 %collective-permute-start.23 = (bf16[336,640]{1,0:T(8,128)(2,1)S(1)}, bf16[336,640]{1,0:T(8,128)(2,1)S(1)}, u32[]{:S(2)}, u32[]{:S(2)}) collective-permute-start(bf16[336,640]{1,0:T(8,128)(2,1)S(1)} %get-tuple-element.73), channel_id=1, source_target_pairs={{0,16},{4,12},{8,24},{12,4},{16,0},{20,28},{24,8},{28,20},{1,17},{... | collective-permute-start | bytes 1290248 | tf_op jit(solution)/shard_map/ppermute | solution.py:259
  71.3 8.2 %collective-permute-start.31 = (bf16[336,640]{1,0:T(8,128)(2,1)S(1)}, bf16[336,640]{1,0:T(8,128)(2,1)S(1)}, u32[]{:S(2)}, u32[]{:S(2)}) collective-permute-start(bf16[336,640]{1,0:T(8,128)(2,1)S(1)} %get-tuple-element.78), channel_id=1, source_target_pairs={{0,16},{4,12},{8,24},{12,4},{16,0},{20,28},{24,8},{28,20},{1,17},{... | collective-permute-start | bytes 1290248 | tf_op jit(solution)/shard_map/ppermute | solution.py:259
  74.5 34.2 %collective-permute-start.19 = (bf16[1728,640]{1,0:T(8,128)(2,1)S(1)}, bf16[1728,640]{1,0:T(8,128)(2,1)S(1)}, u32[]{:S(2)}, u32[]{:S(2)}) collective-permute-start(bf16[1728,640]{1,0:T(8,128)(2,1)S(1)} %get-tuple-element.69.refs_0_.refs_1_), channel_id=1, source_target_pairs={{0,4},{4,0},{8,12},{12,8},{16,20},{20,16},{24,28},{28,24},{1,5},{5... | collective-permute-start | bytes 6635528 | tf_op jit(solution)/shard_map/ppermute | solution.py:63
  74.6 9.4 %collective-permute-start.26 = (bf16[336,640]{1,0:T(8,128)(2,1)S(1)}, bf16[336,640]{1,0:T(8,128)(2,1)S(1)}, u32[]{:S(2)}, u32[]{:S(2)}) collective-permute-start(bf16[336,640]{1,0:T(8,128)(2,1)S(1)} %get-tuple-element.74), channel_id=1, source_target_pairs={{0,16},{4,12},{8,24},{12,4},{16,0},{20,28},{24,8},{28,20},{1,17},{... | collective-permute-start | bytes 1290248 | tf_op jit(solution)/shard_map/ppermute | solution.py:259
  75.6 8.5 %collective-permute-start.24 = (bf16[336,640]{1,0:T(8,128)(2,1)S(1)}, bf16[336,640]{1,0:T(8,128)(2,1)S(1)}, u32[]{:S(2)}, u32[]{:S(2)}) collective-permute-start(bf16[336,640]{1,0:T(8,128)(2,1)S(1)} %collective-permute-done.23.refs_4_), channel_id=1, source_target_pairs={{0,4},{4,0},{8,12},{12,8},{16,20},{20,16},{24,28},{28,24},{1,5},{5... | collective-permute-start | bytes 1290248 | tf_op jit(solution)/shard_map/ppermute | solution.py:63
  79.4 9.2 %collective-permute-start.34 = (bf16[336,640]{1,0:T(8,128)(2,1)S(1)}, bf16[336,640]{1,0:T(8,128)(2,1)S(1)}, u32[]{:S(2)}, u32[]{:S(2)}) collective-permute-start(bf16[336,640]{1,0:T(8,128)(2,1)S(1)} %get-tuple-element.79), channel_id=1, source_target_pairs={{0,16},{4,12},{8,24},{12,4},{16,0},{20,28},{24,8},{28,20},{1,17},{... | collective-permute-start | bytes 1290248 | tf_op jit(solution)/shard_map/ppermute | solution.py:259
  84.1 9.2 %collective-permute-start.27 = (bf16[336,640]{1,0:T(8,128)(2,1)S(1)}, bf16[336,640]{1,0:T(8,128)(2,1)S(1)}, u32[]{:S(2)}, u32[]{:S(2)}) collective-permute-start(bf16[336,640]{1,0:T(8,128)(2,1)S(1)} %collective-permute-done.20.refs_2_), channel_id=1, source_target_pairs={{0,16},{4,12},{8,24},{12,4},{16,0},{20,28},{24,8},{28,20},{1,17},{... | collective-permute-start | bytes 1290248 | tf_op jit(solution)/shard_map/ppermute | solution.py:259
  85.2 8.1 %collective-permute-start.37 = (bf16[336,640]{1,0:T(8,128)(2,1)S(1)}, bf16[336,640]{1,0:T(8,128)(2,1)S(1)}, u32[]{:S(2)}, u32[]{:S(2)}) collective-permute-start(bf16[336,640]{1,0:T(8,128)(2,1)S(1)} %collective-permute-done.26.refs_5_), channel_id=1, source_target_pairs={{0,4},{4,0},{8,12},{12,8},{16,20},{20,16},{24,28},{28,24},{1,5},{5... | collective-permute-start | bytes 1290248 | tf_op jit(solution)/shard_map/ppermute | solution.py:63
  88.7 9.2 %collective-permute-start.35 = (bf16[336,640]{1,0:T(8,128)(2,1)S(1)}, bf16[336,640]{1,0:T(8,128)(2,1)S(1)}, u32[]{:S(2)}, u32[]{:S(2)}) collective-permute-start(bf16[336,640]{1,0:T(8,128)(2,1)S(1)} %collective-permute-done.18.refs_3_), channel_id=1, source_target_pairs={{0,16},{4,12},{8,24},{12,4},{16,0},{20,28},{24,8},{28,20},{1,17},{... | collective-permute-start | bytes 1290248 | tf_op jit(solution)/shard_map/ppermute | solution.py:259
  89.8 8.1 %collective-permute-start.40 = (bf16[336,640]{1,0:T(8,128)(2,1)S(1)}, bf16[336,640]{1,0:T(8,128)(2,1)S(1)}, u32[]{:S(2)}, u32[]{:S(2)}) collective-permute-start(bf16[336,640]{1,0:T(8,128)(2,1)S(1)} %collective-permute-done.34.refs_5_), channel_id=1, source_target_pairs={{0,4},{4,0},{8,12},{12,8},{16,20},{20,16},{24,28},{28,24},{1,5},{5... | collective-permute-start | bytes 1290248 | tf_op jit(solution)/shard_map/ppermute | solution.py:63
  93.3 9.2 %collective-permute-start.38 = (bf16[336,640]{1,0:T(8,128)(2,1)S(1)}, bf16[336,640]{1,0:T(8,128)(2,1)S(1)}, u32[]{:S(2)}, u32[]{:S(2)}) collective-permute-start(bf16[336,640]{1,0:T(8,128)(2,1)S(1)} %collective-permute-done.22.refs_3_), channel_id=1, source_target_pairs={{0,16},{4,12},{8,24},{12,4},{16,0},{20,28},{24,8},{28,20},{1,17},{... | collective-permute-start | bytes 1290248 | tf_op jit(solution)/shard_map/ppermute | solution.py:259
  94.4 8.1 %collective-permute-start.28 = (bf16[336,640]{1,0:T(8,128)(2,1)S(1)}, bf16[336,640]{1,0:T(8,128)(2,1)S(1)}, u32[]{:S(2)}, u32[]{:S(2)}) collective-permute-start(bf16[336,640]{1,0:T(8,128)(2,1)S(1)} %collective-permute-done.27.refs_6_), channel_id=1, source_target_pairs={{0,4},{4,0},{8,12},{12,8},{16,20},{20,16},{24,28},{28,24},{1,5},{5... | collective-permute-start | bytes 1290248 | tf_op jit(solution)/shard_map/ppermute | solution.py:63
  97.9 9.2 %collective-permute-start.41 = (bf16[336,640]{1,0:T(8,128)(2,1)S(1)}, bf16[336,640]{1,0:T(8,128)(2,1)S(1)}, u32[]{:S(2)}, u32[]{:S(2)}) collective-permute-start(bf16[336,640]{1,0:T(8,128)(2,1)S(1)} %collective-permute-done.30.refs_3_), channel_id=1, source_target_pairs={{0,16},{4,12},{8,24},{12,4},{16,0},{20,28},{24,8},{28,20},{1,17},{... | collective-permute-start | bytes 1290248 | tf_op jit(solution)/shard_map/ppermute | solution.py:259
  102.5 11.9 %collective-permute-start.44 = (bf16[384,640]{1,0:T(8,128)(2,1)S(1)}, bf16[384,640]{1,0:T(8,128)(2,1)S(1)}, u32[]{:S(2)}, u32[]{:S(2)}) collective-permute-start(bf16[384,640]{1,0:T(8,128)(2,1)S(1)} %get-tuple-element.84), channel_id=1, source_target_pairs={{0,16},{4,12},{8,24},{12,4},{16,0},{20,28},{24,8},{28,20},{1,17},{... | collective-permute-start | bytes 1474568 | tf_op jit(solution)/shard_map/ppermute | solution.py:259
  107.1 10.5 %collective-permute-start.46 = (bf16[384,640]{1,0:T(8,128)(2,1)S(1)}, bf16[384,640]{1,0:T(8,128)(2,1)S(1)}, u32[]{:S(2)}, u32[]{:S(2)}) collective-permute-start(bf16[384,640]{1,0:T(8,128)(2,1)S(1)} %shard_map.103.refs_3_), channel_id=1, source_target_pairs={{0,16},{4,12},{8,24},{12,4},{16,0},{20,28},{24,8},{28,20},{1,17},{... | collective-permute-start | bytes 1474568 | tf_op jit(solution)/shard_map/ppermute | solution.py:259
  108.7 8.9 %collective-permute-start.43 = (bf16[384,640]{1,0:T(8,128)(2,1)S(1)}, bf16[384,640]{1,0:T(8,128)(2,1)S(1)}, u32[]{:S(2)}, u32[]{:S(2)}) collective-permute-start(bf16[384,640]{1,0:T(8,128)(2,1)S(1)} %shard_map.103.refs_3_), channel_id=1, source_target_pairs={{0,4},{4,0},{8,12},{12,8},{16,20},{20,16},{24,28},{28,24},{1,5},{5... | collective-permute-start | bytes 1474568 | tf_op jit(solution)/shard_map/ppermute | solution.py:63
  (30 other events, 243.4 us)

commit v7 on v5

--- a/solution.py
+++ b/solution.py
@@ -22,12 +22,15 @@
 
 
 TURN_MASKS = ((2, 4), (4, 2))
+UPDATE_MASKS = tuple((k, k) for k in range(8))
+SWAP_MASKS = ((0, 0), (4, 2), (2, 4), (6, 6), (7, 7), (5, 3), (3, 5), (1, 1))
 OWNER_MASKS = ((0, 0), (1, 1), (2, 4), (5, 3), (4, 2), (3, 5), (6, 6), (7, 7))
 
 
 def chunk_sizes(cols):
-    rest = -(-cols * 7 // 18 // 16) * 16
-    return (cols - 2 * rest, rest, rest)
+    small = cols // 80 * 16
+    part = -(-(cols - 2 * small) // 48) * 16
+    return (small,), (small, part, part, cols - 2 * part - 2 * small, small)
 
 
 def adam(grad, moment_one, moment_two):
@@ -63,19 +66,29 @@
     return lax.ppermute(value, axis, [(i, i ^ mask) for i in range(size)])
 
 
-def take_kernel(source, out, sem):
-    copy = pltpu.make_async_copy(source.at[pl.ds(0, out.shape[0]), :], out, sem)
-    copy.start()
-    copy.wait()
-
-
-def take(array, count):
-    return pl.pallas_call(
-        take_kernel,
+def other(me, masks):
+    return me ^ jnp.where((me & 1) == 0, masks[0], masks[1])
+
+
+def take_kernel(source, out, sems, *, first):
+    count = out.shape[0] // sems.shape[0]
+    copies = []
+    for at in range(sems.shape[0]):
+        part = source.at[pl.ds(first + at * count, count), :]
+        copies.append(pltpu.make_async_copy(part, out.at[pl.ds(at * count, count), :], sems.at[at]))
+    for copy in copies:
+        copy.start()
+    for copy in copies:
+        copy.wait()
+
+
+def take(array, first, count):
+    return pl.pallas_call(
+        functools.partial(take_kernel, first=first),
         out_shape=jax.ShapeDtypeStruct((count, array.shape[1]), array.dtype),
         in_specs=[ANY],
         out_specs=VMEM,
-        scratch_shapes=[pltpu.SemaphoreType.DMA],
+        scratch_shapes=[pltpu.SemaphoreType.DMA((count // 16,))],
         compiler_params=pltpu.CompilerParams(vmem_limit_bytes=60 * 2**20),
     )(array)
 
@@ -90,7 +103,7 @@
     across[...] = tokens[...].T
     me = lax.axis_index("dp")
     left = jnp.concatenate(
-        [across[pl.ds(pl.multiple_of((me ^ k) * rows, rows), rows), :] for k in range(n_dp)], axis=0
+        [across[pl.ds(pl.multiple_of(other(me, masks) * rows, rows), rows), :] for masks in SWAP_MASKS], axis=0
     )
     result = lax.dot_general(
         left, grad_t[...], (((1,), (1,)), ((), ())), preferred_element_type=jnp.float32
@@ -119,7 +132,7 @@
     )
 
 
-def weight_kernel(projection, master_t, *refs, n_in, masks, spans, block):
+def weight_kernel(projection, master_t, *refs, n_in, spans, block):
     pieces, outs = refs[:n_in], refs[n_in:]
     me = lax.axis_index("dp")
     if n_in > 1:
@@ -132,8 +145,7 @@
     else:
         tall = pieces[0]
     slab_rows = master_t.shape[1]
-    owner = me ^ jnp.where((me & 1) == 0, masks[0], masks[1])
-    slab = projection[pl.ds(pl.multiple_of(owner * slab_rows, slab_rows), slab_rows), :]
+    slab = projection[pl.ds(pl.multiple_of(me * slab_rows, slab_rows), slab_rows), :]
     for (first, count), out in zip(spans, outs):
         for at in range(0, count, block):
             size = min(block, count - at)
@@ -143,7 +155,7 @@
             out[pl.ds(at, size), :] = master_new.astype(jnp.bfloat16)
 
 
-def weights(projection, master_t, pieces, spans, masks=(0, 0)):
+def weights(projection, master_t, pieces, spans):
     slab_rows, rank = master_t.shape[1], projection.shape[1]
     wide = pieces[0].shape[1]
     out_shape = [jax.ShapeDtypeStruct((count, slab_rows), jnp.bfloat16) for _, count in spans]
@@ -153,7 +165,7 @@
         scratch = [pltpu.VMEM((rank, wide), jnp.bfloat16)]
     size = sum(count for _, count in spans) * slab_rows
     return pl.pallas_call(
-        functools.partial(weight_kernel, n_in=len(pieces), masks=masks, spans=spans, block=144),
+        functools.partial(weight_kernel, n_in=len(pieces), spans=spans, block=144),
         out_shape=out_shape,
         in_specs=[VMEM] * (2 + len(pieces)),
         out_specs=[VMEM] * len(out_shape),
@@ -161,6 +173,35 @@
         compiler_params=pltpu.CompilerParams(vmem_limit_bytes=20 * 2**20),
         cost_estimate=pl.CostEstimate(flops=2 * size * rank, bytes_accessed=4 * size, transcendentals=0),
     )(projection, master_t, *pieces)
+
+
+def ahead_kernel(projection, tall, *refs, block):
+    parts, out = refs[:-1], refs[-1]
+    slab_rows = out.shape[1]
+    owner = other(lax.axis_index("dp"), TURN_MASKS[0])
+    slab = projection[pl.ds(pl.multiple_of(owner * slab_rows, slab_rows), slab_rows), :]
+    first = 0
+    for part in parts:
+        for at in range(0, part.shape[0], block):
+            size = min(block, part.shape[0] - at)
+            master_new = part[pl.ds(at, size), :] - LEARN_RATE * expand(tall, slab, first, size)
+            out[pl.ds(first, size), :] = master_new.astype(jnp.bfloat16)
+            first += size
+
+
+def ahead_weights(projection, tall, parts):
+    shape = (sum(part.shape[0] for part in parts), parts[0].shape[1])
+    size = shape[0] * shape[1]
+    return pl.pallas_call(
+        functools.partial(ahead_kernel, block=144),
+        out_shape=jax.ShapeDtypeStruct(shape, jnp.bfloat16),
+        in_specs=[VMEM] * (2 + len(parts)),
+        out_specs=VMEM,
+        compiler_params=pltpu.CompilerParams(vmem_limit_bytes=20 * 2**20),
+        cost_estimate=pl.CostEstimate(
+            flops=2 * size * projection.shape[1], bytes_accessed=4 * size, transcendentals=0
+        ),
+    )(projection, tall, *parts)
 
 
 def master_kernel(projection, master_t, tall, out):
@@ -197,7 +238,6 @@
     pieces, out, (held, sems) = refs[:-3], refs[-3], refs[-2:]
     copies = [None] * held.shape[0]
     me = lax.axis_index("dp")
-    core = me & 1
     for at in range(0, count, block):
         slot = at // block % len(copies)
         size = min(block, count - at)
@@ -205,7 +245,7 @@
             copies[slot].wait()
         for masks, piece in zip(OWNER_MASKS, pieces):
             width = piece.shape[1]
-            column = pl.multiple_of((me ^ jnp.where(core == 0, masks[0], masks[1])) * width, 128)
+            column = pl.multiple_of(other(me, masks) * width, 128)
             origin = at if piece.shape[0] == count else first + at
             held[slot, pl.ds(0, size), pl.ds(column, width)] = piece[pl.ds(origin, size), :]
         copies[slot] = pltpu.make_async_copy(
@@ -247,18 +287,16 @@
     def hop(value, mask):
         return send(value, "dp", n_dp, mask)
 
-    def turn(value, which):
-        masks = [TURN_MASKS[which][i & 1] for i in range(n_dp)]
-        return lax.ppermute(value, "dp", [(i, i ^ masks[i]) for i in range(n_dp)])
+    def turn(value, masks):
+        return lax.ppermute(value, "dp", [(i, i ^ masks[i & 1]) for i in range(n_dp)])
 
     def after(value, earlier):
         return lax.optimization_barrier((value, *earlier))[0] if earlier else value
 
-    counts = chunk_sizes(cols)
-    chunks = len(counts)
+    early, counts = chunk_sizes(cols)
     spans = [(sum(counts[:at]), count) for at, count in enumerate(counts)]
-    taken = take(master_t, counts[0])
-    ahead = turn(taken, 0)
+    taken = take(master_t, 0, early[0])
+    ahead = [turn(taken, TURN_MASKS[0])]
     acts = after(acts, [taken])
 
     projected = jnp.dot(acts, projection, preferred_element_type=jnp.float32).astype(jnp.bfloat16)
@@ -274,8 +312,8 @@
         ],
         compiler_params=pltpu.CompilerParams(vmem_limit_bytes=16 * 2**20),
     )(grad_out.T, *tokens)
-    parts = lax.optimization_barrier((*parts, ahead))[:-1]
-    parts = [parts[k] if k == 0 else send(parts[k], "dp", n_dp, k) for k in (0, 2, 4, 6, 7, 3, 5, 1)]
+    parts = lax.optimization_barrier((*parts, *ahead))[:n_dp]
+    parts = [part if masks == (0, 0) else turn(part, masks) for part, masks in zip(parts, SWAP_MASKS)]
     moment_one_new, moment_two_new, update = pl.pallas_call(
         adam_kernel,
         out_shape=[
@@ -295,16 +333,15 @@
         updates[k ^ 1] = hop(updates[k], 1)
     updates = [updates[k] for k in range(n_dp)]
 
-    tall, *own = weights(projection, master_t, updates, spans[1:])
-    own_last, whole = weights(projection, master_t, [tall], spans[:1] + [(0, cols)])
-    own = [own_last] + own
-    (ahead_got,) = weights(projection, ahead, [tall], spans[:1], TURN_MASKS[0])
-    ahead_over = hop(ahead_got, 1)
+    tall, *own = weights(projection, master_t, updates, spans[1:3])
+    *late, own_first, whole = weights(projection, master_t, [tall], spans[3:] + spans[:1] + [(0, cols)])
+    own = [own_first] + own + late
+    got = {(0, 0): ahead_weights(projection, tall, ahead)}
+    over = {(0, 0): hop(got[(0, 0)], 1)}
     master_new = new_master(projection, master_t, tall, cols // 4)
 
-    later = range(1, chunks)
-    steps = [(0, at) for at in later] + [(1, at) for at in later] + [(2, at) for at in later] + [(1, 0), (2, 0)]
-    got, over = {(0, 0): ahead_got}, {(0, 0): ahead_over}
+    later = range(1, len(counts))
+    steps = [(phase, at) for phase in range(3) for at in later] + [(1, 0), (2, 0)]
     outs = [None]
     for step, (phase, at) in enumerate(steps):
         value = got[(0, at)] if phase == 2 else own[at]
@@ -312,8 +349,8 @@
         earlier += [over[steps[step - 4]]] if step >= 4 else []
         if step == 2:
             earlier.append(master_new)
-        got[(phase, at)] = turn(after(value, earlier), min(phase, 1))
-        held = outs[step - len(steps) + 3 : step - len(steps) + 4] if step >= len(steps) - 2 else []
+        got[(phase, at)] = turn(after(value, earlier), TURN_MASKS[min(phase, 1)])
+        held = [outs[len(counts) + step - len(steps)]] if step >= len(steps) - 2 else []
         over[(phase, at)] = hop(after(got[(phase, at)], held), 1)
         if step == 1:
             whole_c = hop(after(whole, [got[steps[1]]]), 1)

time: 125 us -> 118 us (0.944)
  waiting for transfers between devices: 75.1 us -> 58.8 us
  starting transfers between devices: 28.1 us -> 37.4 us
  matrix products: 2.4 us -> 0.51 us
  Pallas kernels: 18.3 us -> 20.1 us
    ppermute x9 -> x22, starting transfers between devices: 11.7 us -> 26.6 us  [turn(): lax.ppermute(value, 'dp', [(i, i ^ masks[i & 1]) for i in range(n_dp)])]
    ppermute x27 -> x26, waiting for transfers between devices: 21.1 us -> 12.8 us  [send(): return lax.ppermute(value, axis, [(i, i ^ mask) for i in range(size)])]
    ppermute x9 -> x22, waiting for transfers between devices: 54 us -> 46 us  [turn(): lax.ppermute(value, 'dp', [(i, i ^ masks[i & 1]) for i in range(n_dp)])]
    ppermute x27 -> x26, starting transfers between devices: 16.5 us -> 10.9 us  [send(): return lax.ppermute(value, axis, [(i, i ^ mask) for i in range(size)])]
    dot_general x1, matrix products: 2.4 us -> 0.51 us  [kernel_body(): jnp.dot(acts, projection, preferred_element_type=jnp.float32)]
    pallas_call x3 -> x5, Pallas kernels: 8 us -> 9.53 us  [lay(): pl.pallas_call(functools.partial(lay_kernel, first=first, count=count, bl...]
  transfers between devices with their start and end apart: 36 -> 48, of which waited for: 19 -> 24; matrix products, arithmetic and copies ran while one was open for 2% -> 0% of each run, Pallas kernels for 10% -> 12%
where the time goes in v7:
time: 118 us
  waiting for transfers between devices  58.8 us (50%)
  starting transfers between devices  37.4 us (32%)
  Pallas kernels  20.1 us (17%)
    ppermute x22, waiting for transfers between devices, turn(): lax.ppermute(value, 'dp', [(i, i ^ masks[i & 1]) for i in range(n_dp)])  46 us
    ppermute x22, starting transfers between devices, turn(): lax.ppermute(value, 'dp', [(i, i ^ masks[i & 1]) for i in range(n_dp)])  26.6 us
    ppermute x26, waiting for transfers between devices, send(): return lax.ppermute(value, axis, [(i, i ^ mask) for i in range(size)])  12.8 us
    ppermute x26, starting transfers between devices, send(): return lax.ppermute(value, axis, [(i, i ^ mask) for i in range(size)])  10.9 us
    pallas_call x5, Pallas kernels, lay(): pl.pallas_call(functools.partial(lay_kernel, first=first, count=count, bl...  9.53 us
    pallas_call x1, Pallas kernels, new_master(): pl.pallas_call(master_kernel, out_shape=jax.ShapeDtypeStruct((cols, slab_...  3.12 us
    pallas_call x2, Pallas kernels, weights(): pl.pallas_call(functools.partial(weight_kernel, n_in=len(pieces), spans=s...  3.03 us
    pallas_call x1, Pallas kernels, take(): pl.pallas_call(functools.partial(take_kernel, first=first), out_shape=jax...  2.36 us
  transfers between devices with their start and end apart: 48, of which 24 were waited for; matrix products, arithmetic and copies ran while one was open for 0% of the time, Pallas kernels for 12%

profile of v7, /device:TPU:0, one launch (start us, length us, event | category | flops | bytes accessed | tf_op | source)
XLA Modules:
  0.0 117.7 jit_solution(13676609558147970494)
XLA Ops:
  0.7 2.4 %shard_map.93 = f32[336,640]{1,0:T(8,128)} custom-call(f32[1728,640]{1,0:T(8,128)} %bitcast.6), custom_call_target="tpu_custom_call" | custom-call | tf_op jit(solution)/shard_map/pallas_call | solution.py:86
  3.1 3.0 %collective-permute-start.3 = (f32[336,640]{1,0:T(8,128)}, f32[336,640]{1,0:T(8,128)S(1)}, u32[]{:S(2)}, u32[]{:S(2)}) collective-permute-start(f32[336,640]{1,0:T(8,128)} %shard_map.93), channel_id=1, source_target_pairs={{0,8},{4,20},{8,0},{12,28},{16,24},{20,4},{24,16},{28,12},{1,9},{5... | collective-permute-start | bytes 2580488 | tf_op jit(solution)/shard_map/ppermute | solution.py:291
  8.2 2.6 %collective-permute-start.1 = (bf16[128,256]{1,0:T(8,128)(2,1)S(1)}, bf16[128,256]{1,0:T(8,128)(2,1)S(1)}, u32[]{:S(2)}, u32[]{:S(2)}) collective-permute-start(bf16[128,256]{1,0:T(8,128)(2,1)S(1)} %convolution_convert_fusion.refs_0_), channel_id=1, source_target_pairs={{0,2},{1,3},{2,0},{3,1},{4,6},{5,7},{6,4},{7,5},{8,10},{9,11},{10,... | collective-permute-start | bytes 196616 | tf_op jit(solution)/shard_map/ppermute | solution.py:66
  11.0 4.2 %collective-permute-done.1.refs_2_ = bf16[128,256]{1,0:T(8,128)(2,1)S(1)} collective-permute-done((bf16[128,256]{1,0:T(8,128)(2,1)S(1)}, bf16[128,256]{1,0:T(8,128)(2,1)S(1)}, u32[]{:S(2)}, u32[]{:S(2)}) %collective-permute-start.1) | collective-permute-done | bytes 65568 | tf_op jit(solution)/shard_map/ppermute | solution.py:66
  21.3 2.5 %collective-permute-start.8 = (bf16[32,1728]{1,0:T(8,128)(2,1)S(1)}, bf16[32,1728]{1,0:T(8,128)(2,1)S(1)}, u32[]{:S(2)}, u32[]{:S(2)}) collective-permute-start(bf16[32,1728]{1,0:T(8,128)(2,1)S(1)} %get-tuple-element.60), channel_id=1, source_target_pairs={{0,20},{4,8},{8,28},{12,0},{16,4},{20,24},{24,12},{28,16},{1,21},{... | collective-permute-start | bytes 331784 | tf_op jit(solution)/shard_map/ppermute | solution.py:291
  27.6 2.5 %collective-permute-done.8.refs_5_ = bf16[32,1728]{1,0:T(8,128)(2,1)S(1)} collective-permute-done((bf16[32,1728]{1,0:T(8,128)(2,1)S(1)}, bf16[32,1728]{1,0:T(8,128)(2,1)S(1)}, u32[]{:S(2)}, u32[]{:S(2)}) %collective-permute-start.8) | collective-permute-done | bytes 110624 | tf_op jit(solution)/shard_map/ppermute | solution.py:291
  35.6 2.5 %collective-permute-done.12.refs_2_ = bf16[32,1792]{1,0:T(8,128)(2,1)S(1)} collective-permute-done((bf16[32,1792]{1,0:T(8,128)(2,1)S(1)}, bf16[32,1792]{1,0:T(8,128)(2,1)S(1)}, u32[]{:S(2)}, u32[]{:S(2)}) %collective-permute-start.12) | collective-permute-done | bytes 114720 | tf_op jit(solution)/shard_map/ppermute | solution.py:66
  38.1 2.0 %collective-permute-done.14.refs_4_ = bf16[32,1792]{1,0:T(8,128)(2,1)S(1)} collective-permute-done((bf16[32,1792]{1,0:T(8,128)(2,1)S(1)}, bf16[32,1792]{1,0:T(8,128)(2,1)S(1)}, u32[]{:S(2)}, u32[]{:S(2)}) %collective-permute-start.14) | collective-permute-done | bytes 114720 | tf_op jit(solution)/shard_map/ppermute | solution.py:66
  44.5 3.1 %shard_map.97 = f32[1728,640]{1,0:T(8,128)} custom-call(bf16[5120,256]{1,0:T(8,128)(2,1)S(1)} %copy-done.2, f32[1728,640]{1,0:T(8,128)S(1)} %bitcast.8, bf16[1792,256]{1,0:T(8,128)(2,1)S(1)} %get-tuple-element.66.tall.refs_0_), custom_call_target="tpu_custom_call" | custom-call | flops 566231040 | bytes 8847360 | tf_op jit(solution)/shard_map/pallas_call | solution.py:219
  47.6 2.2 %shard_map.98 = (bf16[352,640]{1,0:T(8,128)(2,1)S(1)}, bf16[336,640]{1,0:T(8,128)(2,1)S(1)}, bf16[336,640]{1,0:T(8,128)(2,1)S(1)}, bf16[1728,640]{1,0:T(8,128)(2,1)S(1)}) custom-call(bf16[5120,256]{1,0:T(8,128)(2,1)S(1)} %copy-done.2, f32[1728,640]{1,0:T(8,128)S(1)} %bitcast.9, bf16[1792,256]{1,0:T(8,128)(2,1)S(1)} %get-tuple-element.66.tall.refs_0_), custom_call_target="tpu_custom_call" | custom-call | flops 901775360 | bytes 7045120 | tf_op jit(solution)/shard_map/pallas_call | solution.py:167
  52.2 3.4 %collective-permute-done.18.refs_3_ = bf16[352,640]{1,0:T(8,128)(2,1)S(1)} collective-permute-done((bf16[352,640]{1,0:T(8,128)(2,1)S(1)}, bf16[352,640]{1,0:T(8,128)(2,1)S(1)}, u32[]{:S(2)}, u32[]{:S(2)}) %collective-permute-start.18) | collective-permute-done | bytes 450592 | tf_op jit(solution)/shard_map/ppermute | solution.py:291
  57.1 3.4 %collective-permute-done.22.refs_3_ = bf16[352,640]{1,0:T(8,128)(2,1)S(1)} collective-permute-done((bf16[352,640]{1,0:T(8,128)(2,1)S(1)}, bf16[352,640]{1,0:T(8,128)(2,1)S(1)}, u32[]{:S(2)}, u32[]{:S(2)}) %collective-permute-start.22) | collective-permute-done | bytes 450592 | tf_op jit(solution)/shard_map/ppermute | solution.py:291
  61.4 6.1 %collective-permute-done.30.refs_3_ = bf16[336,640]{1,0:T(8,128)(2,1)S(1)} collective-permute-done((bf16[336,640]{1,0:T(8,128)(2,1)S(1)}, bf16[336,640]{1,0:T(8,128)(2,1)S(1)}, u32[]{:S(2)}, u32[]{:S(2)}) %collective-permute-start.30) | collective-permute-done | bytes 430112 | tf_op jit(solution)/shard_map/ppermute | solution.py:291
  70.9 5.1 %collective-permute-done.31.refs_5_ = bf16[352,640]{1,0:T(8,128)(2,1)S(1)} collective-permute-done((bf16[352,640]{1,0:T(8,128)(2,1)S(1)}, bf16[352,640]{1,0:T(8,128)(2,1)S(1)}, u32[]{:S(2)}, u32[]{:S(2)}) %collective-permute-start.31) | collective-permute-done | bytes 450592 | tf_op jit(solution)/shard_map/ppermute | solution.py:291
  77.1 3.7 %collective-permute-done.26.refs_5_ = bf16[352,640]{1,0:T(8,128)(2,1)S(1)} collective-permute-done((bf16[352,640]{1,0:T(8,128)(2,1)S(1)}, bf16[352,640]{1,0:T(8,128)(2,1)S(1)}, u32[]{:S(2)}, u32[]{:S(2)}) %collective-permute-start.26) | collective-permute-done | bytes 450592 | tf_op jit(solution)/shard_map/ppermute | solution.py:291
  81.9 3.5 %collective-permute-done.34.refs_5_ = bf16[336,640]{1,0:T(8,128)(2,1)S(1)} collective-permute-done((bf16[336,640]{1,0:T(8,128)(2,1)S(1)}, bf16[336,640]{1,0:T(8,128)(2,1)S(1)}, u32[]{:S(2)}, u32[]{:S(2)}) %collective-permute-start.34) | collective-permute-done | bytes 430112 | tf_op jit(solution)/shard_map/ppermute | solution.py:291
  86.5 3.7 %collective-permute-done.27.refs_6_ = bf16[352,640]{1,0:T(8,128)(2,1)S(1)} collective-permute-done((bf16[352,640]{1,0:T(8,128)(2,1)S(1)}, bf16[352,640]{1,0:T(8,128)(2,1)S(1)}, u32[]{:S(2)}, u32[]{:S(2)}) %collective-permute-start.27) | collective-permute-done | bytes 450592 | tf_op jit(solution)/shard_map/ppermute | solution.py:291
  91.4 3.7 %collective-permute-done.35.refs_7_ = bf16[352,640]{1,0:T(8,128)(2,1)S(1)} collective-permute-done((bf16[352,640]{1,0:T(8,128)(2,1)S(1)}, bf16[352,640]{1,0:T(8,128)(2,1)S(1)}, u32[]{:S(2)}, u32[]{:S(2)}) %collective-permute-start.35) | collective-permute-done | bytes 450592 | tf_op jit(solution)/shard_map/ppermute | solution.py:291
  96.2 3.7 %collective-permute-done.38.refs_7_ = bf16[352,640]{1,0:T(8,128)(2,1)S(1)} collective-permute-done((bf16[352,640]{1,0:T(8,128)(2,1)S(1)}, bf16[352,640]{1,0:T(8,128)(2,1)S(1)}, u32[]{:S(2)}, u32[]{:S(2)}) %collective-permute-start.38) | collective-permute-done | bytes 450592 | tf_op jit(solution)/shard_map/ppermute | solution.py:291
  101.5 3.0 %collective-permute-done.41.refs_7_ = bf16[336,640]{1,0:T(8,128)(2,1)S(1)} collective-permute-done((bf16[336,640]{1,0:T(8,128)(2,1)S(1)}, bf16[336,640]{1,0:T(8,128)(2,1)S(1)}, u32[]{:S(2)}, u32[]{:S(2)}) %collective-permute-start.41) | collective-permute-done | bytes 430112 | tf_op jit(solution)/shard_map/ppermute | solution.py:291
  106.1 1.9 %shard_map.99.refs_0_ = bf16[1728,5120]{1,0:T(8,128)(2,1)} custom-call(bf16[1728,640]{1,0:T(8,128)(2,1)S(1)} %get-tuple-element.69.refs_0_.refs_1_, bf16[1728,640]{1,0:T(8,128)(2,1)S(1)} %collective-permute-done.19.refs_1_.refs_2_, bf16[352,640]{1,0:T(8,128)(2,1)S(1)} %collective-permute-done.20.refs_2_, ...), custom_call_target="tpu_custom_call" | custom-call | bytes 7208960 | tf_op jit(solution)/shard_map/pallas_call | solution.py:264
  108.0 1.9 %shard_map.100.refs_0_ = bf16[1728,5120]{1,0:T(8,128)(2,1)} custom-call(bf16[1728,5120]{1,0:T(8,128)(2,1)} %shard_map.99.refs_0_, bf16[1728,640]{1,0:T(8,128)(2,1)S(1)} %get-tuple-element.69.refs_0_.refs_1_, bf16[1728,640]{1,0:T(8,128)(2,1)S(1)} %collective-permute-done.19.refs_1_.refs_2_, ...), custom_call_target="tpu_custom_call", output_to_operand_aliasing={{}: (0, {})} | custom-call | bytes 7208960 | tf_op jit(solution)/shard_map/pallas_call | solution.py:264
  110.0 1.9 %shard_map.101.refs_0_ = bf16[1728,5120]{1,0:T(8,128)(2,1)} custom-call(bf16[1728,5120]{1,0:T(8,128)(2,1)} %shard_map.100.refs_0_, bf16[1728,640]{1,0:T(8,128)(2,1)S(1)} %get-tuple-element.69.refs_0_.refs_1_, bf16[1728,640]{1,0:T(8,128)(2,1)S(1)} %collective-permute-done.19.refs_1_.refs_2_, ...), custom_call_target="tpu_custom_call", output_to_operand_aliasing={{}: (0, {})} | custom-call | bytes 7208960 | tf_op jit(solution)/shard_map/pallas_call | solution.py:264
  112.0 1.9 %shard_map.102.refs_0_ = bf16[1728,5120]{1,0:T(8,128)(2,1)} custom-call(bf16[1728,5120]{1,0:T(8,128)(2,1)} %shard_map.101.refs_0_, bf16[1728,640]{1,0:T(8,128)(2,1)S(1)} %get-tuple-element.69.refs_0_.refs_1_, bf16[1728,640]{1,0:T(8,128)(2,1)S(1)} %collective-permute-done.19.refs_1_.refs_2_, ...), custom_call_target="tpu_custom_call", output_to_operand_aliasing={{}: (0, {})} | custom-call | bytes 6881280 | tf_op jit(solution)/shard_map/pallas_call | solution.py:264
  (97 shorter events, 42.9 us)
Async XLA Ops:
  3.1 14.6 %collective-permute-start.3 = (f32[336,640]{1,0:T(8,128)}, f32[336,640]{1,0:T(8,128)S(1)}, u32[]{:S(2)}, u32[]{:S(2)}) collective-permute-start(f32[336,640]{1,0:T(8,128)} %shard_map.93), channel_id=1, source_target_pairs={{0,8},{4,20},{8,0},{12,28},{16,24},{20,4},{24,16},{28,12},{1,9},{5... | collective-permute-start | bytes 2580488 | tf_op jit(solution)/shard_map/ppermute | solution.py:291
  21.3 8.9 %collective-permute-start.8 = (bf16[32,1728]{1,0:T(8,128)(2,1)S(1)}, bf16[32,1728]{1,0:T(8,128)(2,1)S(1)}, u32[]{:S(2)}, u32[]{:S(2)}) collective-permute-start(bf16[32,1728]{1,0:T(8,128)(2,1)S(1)} %get-tuple-element.60), channel_id=1, source_target_pairs={{0,20},{4,8},{8,28},{12,0},{16,4},{20,24},{24,12},{28,16},{1,21},{... | collective-permute-start | bytes 331784 | tf_op jit(solution)/shard_map/ppermute | solution.py:291
  42.4 8.5 %collective-permute-start.20 = (bf16[352,640]{1,0:T(8,128)(2,1)S(1)}, bf16[352,640]{1,0:T(8,128)(2,1)S(1)}, u32[]{:S(2)}, u32[]{:S(2)}) collective-permute-start(bf16[352,640]{1,0:T(8,128)(2,1)S(1)} %get-tuple-element.73), channel_id=1, source_target_pairs={{0,8},{4,20},{8,0},{12,28},{16,24},{20,4},{24,16},{28,12},{1,9},{5... | collective-permute-start | bytes 1351688 | tf_op jit(solution)/shard_map/ppermute | solution.py:291
  43.8 11.8 %collective-permute-start.18 = (bf16[352,640]{1,0:T(8,128)(2,1)S(1)}, bf16[352,640]{1,0:T(8,128)(2,1)S(1)}, u32[]{:S(2)}, u32[]{:S(2)}) collective-permute-start(bf16[352,640]{1,0:T(8,128)(2,1)S(1)} %get-tuple-element.78), channel_id=1, source_target_pairs={{0,8},{4,20},{8,0},{12,28},{16,24},{20,4},{24,16},{28,12},{1,9},{5... | collective-permute-start | bytes 1351688 | tf_op jit(solution)/shard_map/ppermute | solution.py:291
  50.9 9.7 %collective-permute-start.22 = (bf16[352,640]{1,0:T(8,128)(2,1)S(1)}, bf16[352,640]{1,0:T(8,128)(2,1)S(1)}, u32[]{:S(2)}, u32[]{:S(2)}) collective-permute-start(bf16[352,640]{1,0:T(8,128)(2,1)S(1)} %get-tuple-element.74), channel_id=1, source_target_pairs={{0,8},{4,20},{8,0},{12,28},{16,24},{20,4},{24,16},{28,12},{1,9},{5... | collective-permute-start | bytes 1351688 | tf_op jit(solution)/shard_map/ppermute | solution.py:291
  55.7 11.9 %collective-permute-start.29 = (bf16[352,640]{1,0:T(8,128)(2,1)S(1)}, bf16[352,640]{1,0:T(8,128)(2,1)S(1)}, u32[]{:S(2)}, u32[]{:S(2)}) collective-permute-start(bf16[352,640]{1,0:T(8,128)(2,1)S(1)} %collective-permute-done.18.refs_3_), channel_id=1, source_target_pairs={{0,4},{4,0},{8,12},{12,8},{16,20},{20,16},{24,28},{28,24},{1,5},{5... | collective-permute-start | bytes 1351688 | tf_op jit(solution)/shard_map/ppermute | solution.py:66
  55.7 11.9 %collective-permute-start.30 = (bf16[336,640]{1,0:T(8,128)(2,1)S(1)}, bf16[336,640]{1,0:T(8,128)(2,1)S(1)}, u32[]{:S(2)}, u32[]{:S(2)}) collective-permute-start(bf16[336,640]{1,0:T(8,128)(2,1)S(1)} %get-tuple-element.79), channel_id=1, source_target_pairs={{0,8},{4,20},{8,0},{12,28},{16,24},{20,4},{24,16},{28,12},{1,9},{5... | collective-permute-start | bytes 1290248 | tf_op jit(solution)/shard_map/ppermute | solution.py:291
  60.5 8.8 %collective-permute-start.23 = (bf16[352,640]{1,0:T(8,128)(2,1)S(1)}, bf16[352,640]{1,0:T(8,128)(2,1)S(1)}, u32[]{:S(2)}, u32[]{:S(2)}) collective-permute-start(bf16[352,640]{1,0:T(8,128)(2,1)S(1)} %get-tuple-element.73), channel_id=1, source_target_pairs={{0,16},{4,12},{8,24},{12,4},{16,0},{20,28},{24,8},{28,20},{1,17},{... | collective-permute-start | bytes 1351688 | tf_op jit(solution)/shard_map/ppermute | solution.py:291
  68.7 36.9 %collective-permute-start.19 = (bf16[1728,640]{1,0:T(8,128)(2,1)S(1)}, bf16[1728,640]{1,0:T(8,128)(2,1)S(1)}, u32[]{:S(2)}, u32[]{:S(2)}) collective-permute-start(bf16[1728,640]{1,0:T(8,128)(2,1)S(1)} %get-tuple-element.69.refs_0_.refs_1_), channel_id=1, source_target_pairs={{0,4},{4,0},{8,12},{12,8},{16,20},{20,16},{24,28},{28,24},{1,5},{5... | collective-permute-start | bytes 6635528 | tf_op jit(solution)/shard_map/ppermute | solution.py:66
  69.3 11.5 %collective-permute-start.26 = (bf16[352,640]{1,0:T(8,128)(2,1)S(1)}, bf16[352,640]{1,0:T(8,128)(2,1)S(1)}, u32[]{:S(2)}, u32[]{:S(2)}) collective-permute-start(bf16[352,640]{1,0:T(8,128)(2,1)S(1)} %get-tuple-element.74), channel_id=1, source_target_pairs={{0,16},{4,12},{8,24},{12,4},{16,0},{20,28},{24,8},{28,20},{1,17},{... | collective-permute-start | bytes 1351688 | tf_op jit(solution)/shard_map/ppermute | solution.py:291
  70.1 10.7 %collective-permute-start.24 = (bf16[352,640]{1,0:T(8,128)(2,1)S(1)}, bf16[352,640]{1,0:T(8,128)(2,1)S(1)}, u32[]{:S(2)}, u32[]{:S(2)}) collective-permute-start(bf16[352,640]{1,0:T(8,128)(2,1)S(1)} %collective-permute-done.23.refs_4_), channel_id=1, source_target_pairs={{0,4},{4,0},{8,12},{12,8},{16,20},{20,16},{24,28},{28,24},{1,5},{5... | collective-permute-start | bytes 1351688 | tf_op jit(solution)/shard_map/ppermute | solution.py:66
  76.0 9.4 %collective-permute-start.32 = (bf16[352,640]{1,0:T(8,128)(2,1)S(1)}, bf16[352,640]{1,0:T(8,128)(2,1)S(1)}, u32[]{:S(2)}, u32[]{:S(2)}) collective-permute-start(bf16[352,640]{1,0:T(8,128)(2,1)S(1)} %collective-permute-done.31.refs_5_), channel_id=1, source_target_pairs={{0,4},{4,0},{8,12},{12,8},{16,20},{20,16},{24,28},{28,24},{1,5},{5... | collective-permute-start | bytes 1351688 | tf_op jit(solution)/shard_map/ppermute | solution.py:66
  76.0 9.4 %collective-permute-start.34 = (bf16[336,640]{1,0:T(8,128)(2,1)S(1)}, bf16[336,640]{1,0:T(8,128)(2,1)S(1)}, u32[]{:S(2)}, u32[]{:S(2)}) collective-permute-start(bf16[336,640]{1,0:T(8,128)(2,1)S(1)} %get-tuple-element.79), channel_id=1, source_target_pairs={{0,16},{4,12},{8,24},{12,4},{16,0},{20,28},{24,8},{28,20},{1,17},{... | collective-permute-start | bytes 1290248 | tf_op jit(solution)/shard_map/ppermute | solution.py:291
  80.8 9.4 %collective-permute-start.27 = (bf16[352,640]{1,0:T(8,128)(2,1)S(1)}, bf16[352,640]{1,0:T(8,128)(2,1)S(1)}, u32[]{:S(2)}, u32[]{:S(2)}) collective-permute-start(bf16[352,640]{1,0:T(8,128)(2,1)S(1)} %collective-permute-done.20.refs_2_), channel_id=1, source_target_pairs={{0,16},{4,12},{8,24},{12,4},{16,0},{20,28},{24,8},{28,20},{1,17},{... | collective-permute-start | bytes 1351688 | tf_op jit(solution)/shard_map/ppermute | solution.py:291
  85.4 9.7 %collective-permute-start.35 = (bf16[352,640]{1,0:T(8,128)(2,1)S(1)}, bf16[352,640]{1,0:T(8,128)(2,1)S(1)}, u32[]{:S(2)}, u32[]{:S(2)}) collective-permute-start(bf16[352,640]{1,0:T(8,128)(2,1)S(1)} %collective-permute-done.18.refs_3_), channel_id=1, source_target_pairs={{0,16},{4,12},{8,24},{12,4},{16,0},{20,28},{24,8},{28,20},{1,17},{... | collective-permute-start | bytes 1351688 | tf_op jit(solution)/shard_map/ppermute | solution.py:291
  86.5 8.5 %collective-permute-start.40 = (bf16[336,640]{1,0:T(8,128)(2,1)S(1)}, bf16[336,640]{1,0:T(8,128)(2,1)S(1)}, u32[]{:S(2)}, u32[]{:S(2)}) collective-permute-start(bf16[336,640]{1,0:T(8,128)(2,1)S(1)} %collective-permute-done.34.refs_5_), channel_id=1, source_target_pairs={{0,4},{4,0},{8,12},{12,8},{16,20},{20,16},{24,28},{28,24},{1,5},{5... | collective-permute-start | bytes 1290248 | tf_op jit(solution)/shard_map/ppermute | solution.py:66
  90.2 9.7 %collective-permute-start.38 = (bf16[352,640]{1,0:T(8,128)(2,1)S(1)}, bf16[352,640]{1,0:T(8,128)(2,1)S(1)}, u32[]{:S(2)}, u32[]{:S(2)}) collective-permute-start(bf16[352,640]{1,0:T(8,128)(2,1)S(1)} %collective-permute-done.22.refs_3_), channel_id=1, source_target_pairs={{0,16},{4,12},{8,24},{12,4},{16,0},{20,28},{24,8},{28,20},{1,17},{... | collective-permute-start | bytes 1351688 | tf_op jit(solution)/shard_map/ppermute | solution.py:291
  91.4 9.0 %collective-permute-start.28 = (bf16[352,640]{1,0:T(8,128)(2,1)S(1)}, bf16[352,640]{1,0:T(8,128)(2,1)S(1)}, u32[]{:S(2)}, u32[]{:S(2)}) collective-permute-start(bf16[352,640]{1,0:T(8,128)(2,1)S(1)} %collective-permute-done.27.refs_6_), channel_id=1, source_target_pairs={{0,4},{4,0},{8,12},{12,8},{16,20},{20,16},{24,28},{28,24},{1,5},{5... | collective-permute-start | bytes 1351688 | tf_op jit(solution)/shard_map/ppermute | solution.py:66
  95.0 9.4 %collective-permute-start.36 = (bf16[352,640]{1,0:T(8,128)(2,1)S(1)}, bf16[352,640]{1,0:T(8,128)(2,1)S(1)}, u32[]{:S(2)}, u32[]{:S(2)}) collective-permute-start(bf16[352,640]{1,0:T(8,128)(2,1)S(1)} %collective-permute-done.35.refs_7_), channel_id=1, source_target_pairs={{0,4},{4,0},{8,12},{12,8},{16,20},{20,16},{24,28},{28,24},{1,5},{5... | collective-permute-start | bytes 1351688 | tf_op jit(solution)/shard_map/ppermute | solution.py:66
  95.1 9.4 %collective-permute-start.41 = (bf16[336,640]{1,0:T(8,128)(2,1)S(1)}, bf16[336,640]{1,0:T(8,128)(2,1)S(1)}, u32[]{:S(2)}, u32[]{:S(2)}) collective-permute-start(bf16[336,640]{1,0:T(8,128)(2,1)S(1)} %collective-permute-done.30.refs_3_), channel_id=1, source_target_pairs={{0,16},{4,12},{8,24},{12,4},{16,0},{20,28},{24,8},{28,20},{1,17},{... | collective-permute-start | bytes 1290248 | tf_op jit(solution)/shard_map/ppermute | solution.py:291
  99.9 10.1 %collective-permute-start.39 = (bf16[352,640]{1,0:T(8,128)(2,1)S(1)}, bf16[352,640]{1,0:T(8,128)(2,1)S(1)}, u32[]{:S(2)}, u32[]{:S(2)}) collective-permute-start(bf16[352,640]{1,0:T(8,128)(2,1)S(1)} %collective-permute-done.38.refs_7_), channel_id=1, source_target_pairs={{0,4},{4,0},{8,12},{12,8},{16,20},{20,16},{24,28},{28,24},{1,5},{5... | collective-permute-start | bytes 1351688 | tf_op jit(solution)/shard_map/ppermute | solution.py:66
  100.3 11.6 %collective-permute-start.44 = (bf16[336,640]{1,0:T(8,128)(2,1)S(1)}, bf16[336,640]{1,0:T(8,128)(2,1)S(1)}, u32[]{:S(2)}, u32[]{:S(2)}) collective-permute-start(bf16[336,640]{1,0:T(8,128)(2,1)S(1)} %get-tuple-element.84), channel_id=1, source_target_pairs={{0,16},{4,12},{8,24},{12,4},{16,0},{20,28},{24,8},{28,20},{1,17},{... | collective-permute-start | bytes 1290248 | tf_op jit(solution)/shard_map/ppermute | solution.py:291
  104.5 9.4 %collective-permute-start.46 = (bf16[336,640]{1,0:T(8,128)(2,1)S(1)}, bf16[336,640]{1,0:T(8,128)(2,1)S(1)}, u32[]{:S(2)}, u32[]{:S(2)}) collective-permute-start(bf16[336,640]{1,0:T(8,128)(2,1)S(1)} %shard_map.103.refs_3_), channel_id=1, source_target_pairs={{0,16},{4,12},{8,24},{12,4},{16,0},{20,28},{24,8},{28,20},{1,17},{... | collective-permute-start | bytes 1290248 | tf_op jit(solution)/shard_map/ppermute | solution.py:291
  105.6 8.9 %collective-permute-start.43 = (bf16[336,640]{1,0:T(8,128)(2,1)S(1)}, bf16[336,640]{1,0:T(8,128)(2,1)S(1)}, u32[]{:S(2)}, u32[]{:S(2)}) collective-permute-start(bf16[336,640]{1,0:T(8,128)(2,1)S(1)} %shard_map.103.refs_3_), channel_id=1, source_target_pairs={{0,4},{4,0},{8,12},{12,8},{16,20},{20,16},{24,28},{28,24},{1,5},{5... | collective-permute-start | bytes 1290248 | tf_op jit(solution)/shard_map/ppermute | solution.py:66
  (30 other events, 254.9 us)

commit v8 on v7

--- a/solution.py
+++ b/solution.py
@@ -28,9 +28,10 @@
 
 
 def chunk_sizes(cols):
-    small = cols // 80 * 16
-    part = -(-(cols - 2 * small) // 48) * 16
-    return (small,), (small, part, part, cols - 2 * part - 2 * small, small)
+    ahead = (cols // 120 * 16, cols // 112 * 16)
+    rest = cols - sum(ahead)
+    part = -(-rest // 64) * 16
+    return ahead, (sum(ahead), part, part, part, rest - 3 * part)
 
 
 def adam(grad, moment_one, moment_two):
@@ -82,14 +83,14 @@
         copy.wait()
 
 
-def take(array, first, count):
+def take(array, first, count, limit):
     return pl.pallas_call(
         functools.partial(take_kernel, first=first),
         out_shape=jax.ShapeDtypeStruct((count, array.shape[1]), array.dtype),
         in_specs=[ANY],
         out_specs=VMEM,
         scratch_shapes=[pltpu.SemaphoreType.DMA((count // 16,))],
-        compiler_params=pltpu.CompilerParams(vmem_limit_bytes=60 * 2**20),
+        compiler_params=pltpu.CompilerParams(vmem_limit_bytes=limit * 2**20),
     )(array)
 
 
@@ -295,7 +296,7 @@
 
     early, counts = chunk_sizes(cols)
     spans = [(sum(counts[:at]), count) for at, count in enumerate(counts)]
-    taken = take(master_t, 0, early[0])
+    taken = take(master_t, 0, early[0], 60)
     ahead = [turn(taken, TURN_MASKS[0])]
     acts = after(acts, [taken])
 
@@ -331,6 +332,8 @@
         updates[k] = hop(update, k)
     for k in (2, 4, 6):
         updates[k ^ 1] = hop(updates[k], 1)
+    second = take(after(master_t, [update]), *early, 8)
+    ahead.append(turn(after(second, [updates[k] for k in (2, 4, 6)]), TURN_MASKS[0]))
     updates = [updates[k] for k in range(n_dp)]
 
     tall, *own = weights(projection, master_t, updates, spans[1:3])
@@ -349,6 +352,8 @@
         earlier += [over[steps[step - 4]]] if step >= 4 else []
         if step == 2:
             earlier.append(master_new)
+        if step == 3:
+            earlier.append(ahead[1])
         got[(phase, at)] = turn(after(value, earlier), TURN_MASKS[min(phase, 1)])
         held = [outs[len(counts) + step - len(steps)]] if step >= len(steps) - 2 else []
         over[(phase, at)] = hop(after(got[(phase, at)], held), 1)

time: 118 us -> 122 us (1.034)
  waiting for transfers between devices: 58.8 us -> 68.6 us
  starting transfers between devices: 37.4 us -> 30.8 us
    ppermute x22 -> x23, waiting for transfers between devices: 46 us -> 55.4 us  [turn(): lax.ppermute(value, 'dp', [(i, i ^ masks[i & 1]) for i in range(n_dp)])]
    ppermute x22 -> x23, starting transfers between devices: 26.6 us -> 20.2 us  [turn(): lax.ppermute(value, 'dp', [(i, i ^ masks[i & 1]) for i in range(n_dp)])]
    pallas_call x1 -> x2, Pallas kernels: 2.36 us -> 3.05 us  [take(): pl.pallas_call(functools.partial(take_kernel, first=first), out_shape=jax...]
  transfers between devices with their start and end apart: 48 -> 49, of which waited for: 24 -> 27; matrix products, arithmetic and copies ran while one was open for 0% -> 0% of each run, Pallas kernels for 12% -> 13%
where the time goes in v8:
time: 122 us
  waiting for transfers between devices  68.6 us (56%)
  starting transfers between devices  30.8 us (25%)
  Pallas kernels  21 us (17%)
    ppermute x23, waiting for transfers between devices, turn(): lax.ppermute(value, 'dp', [(i, i ^ masks[i & 1]) for i in range(n_dp)])  55.4 us
    ppermute x23, starting transfers between devices, turn(): lax.ppermute(value, 'dp', [(i, i ^ masks[i & 1]) for i in range(n_dp)])  20.2 us
    ppermute x26, waiting for transfers between devices, send(): return lax.ppermute(value, axis, [(i, i ^ mask) for i in range(size)])  13.2 us
    ppermute x26, starting transfers between devices, send(): return lax.ppermute(value, axis, [(i, i ^ mask) for i in range(size)])  10.6 us
    pallas_call x5, Pallas kernels, lay(): pl.pallas_call(functools.partial(lay_kernel, first=first, count=count, bl...  9.53 us
    pallas_call x1, Pallas kernels, new_master(): pl.pallas_call(master_kernel, out_shape=jax.ShapeDtypeStruct((cols, slab_...  3.12 us
    pallas_call x2, Pallas kernels, weights(): pl.pallas_call(functools.partial(weight_kernel, n_in=len(pieces), spans=s...  3.1 us
    pallas_call x2, Pallas kernels, take(): pl.pallas_call(functools.partial(take_kernel, first=first), out_shape=jax...  3.05 us
  transfers between devices with their start and end apart: 49, of which 27 were waited for; matrix products, arithmetic and copies ran while one was open for 0% of the time, Pallas kernels for 13%

profile of v8, /device:TPU:0, one launch (start us, length us, event | category | flops | bytes accessed | tf_op | source)
XLA Modules:
  0.0 121.8 jit_solution(13354662908143133284)
XLA Ops:
  0.7 2.1 %shard_map.93 = f32[224,640]{1,0:T(8,128)} custom-call(f32[1728,640]{1,0:T(8,128)} %bitcast.6), custom_call_target="tpu_custom_call" | custom-call | tf_op jit(solution)/shard_map/pallas_call | solution.py:87
  2.8 3.0 %collective-permute-start.3 = (f32[224,640]{1,0:T(8,128)}, f32[224,640]{1,0:T(8,128)S(1)}, u32[]{:S(2)}, u32[]{:S(2)}) collective-permute-start(f32[224,640]{1,0:T(8,128)} %shard_map.93), channel_id=1, source_target_pairs={{0,8},{4,20},{8,0},{12,28},{16,24},{20,4},{24,16},{28,12},{1,9},{5... | collective-permute-start | bytes 1720328 | tf_op jit(solution)/shard_map/ppermute | solution.py:292
  8.0 2.6 %collective-permute-start.1 = (bf16[128,256]{1,0:T(8,128)(2,1)S(1)}, bf16[128,256]{1,0:T(8,128)(2,1)S(1)}, u32[]{:S(2)}, u32[]{:S(2)}) collective-permute-start(bf16[128,256]{1,0:T(8,128)(2,1)S(1)} %convolution_convert_fusion.refs_0_), channel_id=1, source_target_pairs={{0,2},{1,3},{2,0},{3,1},{4,6},{5,7},{6,4},{7,5},{8,10},{9,11},{10,... | collective-permute-start | bytes 196616 | tf_op jit(solution)/shard_map/ppermute | solution.py:67
  10.8 4.2 %collective-permute-done.1.refs_2_ = bf16[128,256]{1,0:T(8,128)(2,1)S(1)} collective-permute-done((bf16[128,256]{1,0:T(8,128)(2,1)S(1)}, bf16[128,256]{1,0:T(8,128)(2,1)S(1)}, u32[]{:S(2)}, u32[]{:S(2)}) %collective-permute-start.1) | collective-permute-done | bytes 65568 | tf_op jit(solution)/shard_map/ppermute | solution.py:67
  27.4 2.5 %collective-permute-done.8.refs_5_ = bf16[32,1728]{1,0:T(8,128)(2,1)S(1)} collective-permute-done((bf16[32,1728]{1,0:T(8,128)(2,1)S(1)}, bf16[32,1728]{1,0:T(8,128)(2,1)S(1)}, u32[]{:S(2)}, u32[]{:S(2)}) %collective-permute-start.8) | collective-permute-done | bytes 110624 | tf_op jit(solution)/shard_map/ppermute | solution.py:292
  36.3 3.6 %collective-permute-done.14.refs_4_ = bf16[32,1792]{1,0:T(8,128)(2,1)S(1)} collective-permute-done((bf16[32,1792]{1,0:T(8,128)(2,1)S(1)}, bf16[32,1792]{1,0:T(8,128)(2,1)S(1)}, u32[]{:S(2)}, u32[]{:S(2)}) %collective-permute-start.14) | collective-permute-done | bytes 114720 | tf_op jit(solution)/shard_map/ppermute | solution.py:67
  45.3 3.1 %shard_map.97 = f32[1728,640]{1,0:T(8,128)} custom-call(bf16[5120,256]{1,0:T(8,128)(2,1)S(1)} %copy-done.2, f32[1728,640]{1,0:T(8,128)S(1)} %bitcast.9, bf16[1792,256]{1,0:T(8,128)(2,1)S(1)} %get-tuple-element.68.tall.refs_0_), custom_call_target="tpu_custom_call" | custom-call | flops 566231040 | bytes 8847360 | tf_op jit(solution)/shard_map/pallas_call | solution.py:220
  48.4 2.3 %shard_map.98 = (bf16[320,640]{1,0:T(8,128)(2,1)S(1)}, bf16[304,640]{1,0:T(8,128)(2,1)S(1)}, bf16[464,640]{1,0:T(8,128)(2,1)S(1)}, bf16[1728,640]{1,0:T(8,128)(2,1)S(1)}) custom-call(bf16[5120,256]{1,0:T(8,128)(2,1)S(1)} %copy-done.2, f32[1728,640]{1,0:T(8,128)S(1)} %bitcast.10, bf16[1792,256]{1,0:T(8,128)(2,1)S(1)} %get-tuple-element.68.tall.refs_0_), custom_call_target="tpu_custom_call" | custom-call | flops 922746880 | bytes 7208960 | tf_op jit(solution)/shard_map/pallas_call | solution.py:168
  50.8 3.6 %collective-permute-done.20.refs_2_ = bf16[320,640]{1,0:T(8,128)(2,1)S(1)} collective-permute-done((bf16[320,640]{1,0:T(8,128)(2,1)S(1)}, bf16[320,640]{1,0:T(8,128)(2,1)S(1)}, u32[]{:S(2)}, u32[]{:S(2)}) %collective-permute-start.20) | collective-permute-done | bytes 409632 | tf_op jit(solution)/shard_map/ppermute | solution.py:292
  55.0 3.8 %collective-permute-done.18.refs_3_ = bf16[320,640]{1,0:T(8,128)(2,1)S(1)} collective-permute-done((bf16[320,640]{1,0:T(8,128)(2,1)S(1)}, bf16[320,640]{1,0:T(8,128)(2,1)S(1)}, u32[]{:S(2)}, u32[]{:S(2)}) %collective-permute-start.18) | collective-permute-done | bytes 409632 | tf_op jit(solution)/shard_map/ppermute | solution.py:292
  59.4 3.8 %collective-permute-done.22.refs_3_ = bf16[320,640]{1,0:T(8,128)(2,1)S(1)} collective-permute-done((bf16[320,640]{1,0:T(8,128)(2,1)S(1)}, bf16[320,640]{1,0:T(8,128)(2,1)S(1)}, u32[]{:S(2)}, u32[]{:S(2)}) %collective-permute-start.22) | collective-permute-done | bytes 409632 | tf_op jit(solution)/shard_map/ppermute | solution.py:292
  63.7 7.2 %collective-permute-done.31.refs_3_ = bf16[304,640]{1,0:T(8,128)(2,1)S(1)} collective-permute-done((bf16[304,640]{1,0:T(8,128)(2,1)S(1)}, bf16[304,640]{1,0:T(8,128)(2,1)S(1)}, u32[]{:S(2)}, u32[]{:S(2)}) %collective-permute-start.31) | collective-permute-done | bytes 389152 | tf_op jit(solution)/shard_map/ppermute | solution.py:292
  73.5 5.4 %collective-permute-done.32.refs_5_ = bf16[320,640]{1,0:T(8,128)(2,1)S(1)} collective-permute-done((bf16[320,640]{1,0:T(8,128)(2,1)S(1)}, bf16[320,640]{1,0:T(8,128)(2,1)S(1)}, u32[]{:S(2)}, u32[]{:S(2)}) %collective-permute-start.32) | collective-permute-done | bytes 409632 | tf_op jit(solution)/shard_map/ppermute | solution.py:292
  79.5 3.8 %collective-permute-done.26.refs_5_ = bf16[320,640]{1,0:T(8,128)(2,1)S(1)} collective-permute-done((bf16[320,640]{1,0:T(8,128)(2,1)S(1)}, bf16[320,640]{1,0:T(8,128)(2,1)S(1)}, u32[]{:S(2)}, u32[]{:S(2)}) %collective-permute-start.26) | collective-permute-done | bytes 409632 | tf_op jit(solution)/shard_map/ppermute | solution.py:292
  83.9 3.6 %collective-permute-done.35.refs_5_ = bf16[304,640]{1,0:T(8,128)(2,1)S(1)} collective-permute-done((bf16[304,640]{1,0:T(8,128)(2,1)S(1)}, bf16[304,640]{1,0:T(8,128)(2,1)S(1)}, u32[]{:S(2)}, u32[]{:S(2)}) %collective-permute-start.35) | collective-permute-done | bytes 389152 | tf_op jit(solution)/shard_map/ppermute | solution.py:292
  88.0 3.8 %collective-permute-done.27.refs_6_ = bf16[320,640]{1,0:T(8,128)(2,1)S(1)} collective-permute-done((bf16[320,640]{1,0:T(8,128)(2,1)S(1)}, bf16[320,640]{1,0:T(8,128)(2,1)S(1)}, u32[]{:S(2)}, u32[]{:S(2)}) %collective-permute-start.27) | collective-permute-done | bytes 409632 | tf_op jit(solution)/shard_map/ppermute | solution.py:292
  92.4 3.8 %collective-permute-done.36.refs_7_ = bf16[320,640]{1,0:T(8,128)(2,1)S(1)} collective-permute-done((bf16[320,640]{1,0:T(8,128)(2,1)S(1)}, bf16[320,640]{1,0:T(8,128)(2,1)S(1)}, u32[]{:S(2)}, u32[]{:S(2)}) %collective-permute-start.36) | collective-permute-done | bytes 409632 | tf_op jit(solution)/shard_map/ppermute | solution.py:292
  96.8 3.8 %collective-permute-done.39.refs_7_ = bf16[320,640]{1,0:T(8,128)(2,1)S(1)} collective-permute-done((bf16[320,640]{1,0:T(8,128)(2,1)S(1)}, bf16[320,640]{1,0:T(8,128)(2,1)S(1)}, u32[]{:S(2)}, u32[]{:S(2)}) %collective-permute-start.39) | collective-permute-done | bytes 409632 | tf_op jit(solution)/shard_map/ppermute | solution.py:292
  101.7 3.0 %collective-permute-done.42.refs_7_ = bf16[304,640]{1,0:T(8,128)(2,1)S(1)} collective-permute-done((bf16[304,640]{1,0:T(8,128)(2,1)S(1)}, bf16[304,640]{1,0:T(8,128)(2,1)S(1)}, u32[]{:S(2)}, u32[]{:S(2)}) %collective-permute-start.42) | collective-permute-done | bytes 389152 | tf_op jit(solution)/shard_map/ppermute | solution.py:292
  107.7 1.8 %shard_map.101.refs_0_ = bf16[1728,5120]{1,0:T(8,128)(2,1)} custom-call(bf16[1728,5120]{1,0:T(8,128)(2,1)} %shard_map.99.refs_0_, bf16[1728,640]{1,0:T(8,128)(2,1)S(1)} %get-tuple-element.71.refs_0_.refs_1_, bf16[1728,640]{1,0:T(8,128)(2,1)S(1)} %collective-permute-done.19.refs_1_.refs_2_, ...), custom_call_target="tpu_custom_call", output_to_operand_aliasing={{}: (0, {})} | custom-call | bytes 6553600 | tf_op jit(solution)/shard_map/pallas_call | solution.py:265
  109.5 1.8 %shard_map.102.refs_0_ = bf16[1728,5120]{1,0:T(8,128)(2,1)} custom-call(bf16[1728,5120]{1,0:T(8,128)(2,1)} %shard_map.101.refs_0_, bf16[1728,640]{1,0:T(8,128)(2,1)S(1)} %get-tuple-element.71.refs_0_.refs_1_, bf16[1728,640]{1,0:T(8,128)(2,1)S(1)} %collective-permute-done.19.refs_1_.refs_2_, ...), custom_call_target="tpu_custom_call", output_to_operand_aliasing={{}: (0, {})} | custom-call | bytes 6553600 | tf_op jit(solution)/shard_map/pallas_call | solution.py:265
  113.7 3.8 %collective-permute-done.47.refs_7_ = bf16[464,640]{1,0:T(8,128)(2,1)S(1)} collective-permute-done((bf16[464,640]{1,0:T(8,128)(2,1)S(1)}, bf16[464,640]{1,0:T(8,128)(2,1)S(1)}, u32[]{:S(2)}, u32[]{:S(2)}) %collective-permute-start.47) | collective-permute-done | bytes 593952 | tf_op jit(solution)/shard_map/ppermute | solution.py:292
  117.5 2.0 %collective-permute-done.48.refs_8_ = bf16[464,640]{1,0:T(8,128)(2,1)S(1)} collective-permute-done((bf16[464,640]{1,0:T(8,128)(2,1)S(1)}, bf16[464,640]{1,0:T(8,128)(2,1)S(1)}, u32[]{:S(2)}, u32[]{:S(2)}) %collective-permute-start.48) | collective-permute-done | bytes 593952 | tf_op jit(solution)/shard_map/ppermute | solution.py:67
  119.5 2.3 %shard_map.105 = bf16[1728,5120]{1,0:T(8,128)(2,1)} custom-call(bf16[1728,5120]{1,0:T(8,128)(2,1)} %shard_map.103.refs_0_, bf16[1728,640]{1,0:T(8,128)(2,1)S(1)} %get-tuple-element.71.refs_0_.refs_1_, bf16[1728,640]{1,0:T(8,128)(2,1)S(1)} %collective-permute-done.19.refs_1_.refs_2_, ...), custom_call_target="tpu_custom_call", output_to_operand_aliasing={{}: (0, {})} | custom-call | bytes 9502720 | tf_op jit(solution)/shard_map/pallas_call | solution.py:265
  (100 shorter events, 40.1 us)
Async XLA Ops:
  2.8 14.6 %collective-permute-start.3 = (f32[224,640]{1,0:T(8,128)}, f32[224,640]{1,0:T(8,128)S(1)}, u32[]{:S(2)}, u32[]{:S(2)}) collective-permute-start(f32[224,640]{1,0:T(8,128)} %shard_map.93), channel_id=1, source_target_pairs={{0,8},{4,20},{8,0},{12,28},{16,24},{20,4},{24,16},{28,12},{1,9},{5... | collective-permute-start | bytes 1720328 | tf_op jit(solution)/shard_map/ppermute | solution.py:292
  21.0 9.0 %collective-permute-start.8 = (bf16[32,1728]{1,0:T(8,128)(2,1)S(1)}, bf16[32,1728]{1,0:T(8,128)(2,1)S(1)}, u32[]{:S(2)}, u32[]{:S(2)}) collective-permute-start(bf16[32,1728]{1,0:T(8,128)(2,1)S(1)} %get-tuple-element.62), channel_id=1, source_target_pairs={{0,20},{4,8},{8,28},{12,0},{16,4},{20,24},{24,12},{28,16},{1,21},{... | collective-permute-start | bytes 331784 | tf_op jit(solution)/shard_map/ppermute | solution.py:292
  39.9 18.9 %collective-permute-start.30 = (f32[240,640]{1,0:T(8,128)S(1)}, f32[240,640]{1,0:T(8,128)S(1)}, u32[]{:S(2)}, u32[]{:S(2)}) collective-permute-start(f32[240,640]{1,0:T(8,128)S(1)} %shard_map.100), channel_id=1, source_target_pairs={{0,8},{4,20},{8,0},{12,28},{16,24},{20,4},{24,16},{28,12},{1,9},{5... | collective-permute-start | bytes 1843208 | tf_op jit(solution)/shard_map/ppermute | solution.py:292
  43.2 11.2 %collective-permute-start.20 = (bf16[320,640]{1,0:T(8,128)(2,1)S(1)}, bf16[320,640]{1,0:T(8,128)(2,1)S(1)}, u32[]{:S(2)}, u32[]{:S(2)}) collective-permute-start(bf16[320,640]{1,0:T(8,128)(2,1)S(1)} %get-tuple-element.75), channel_id=1, source_target_pairs={{0,8},{4,20},{8,0},{12,28},{16,24},{20,4},{24,16},{28,12},{1,9},{5... | collective-permute-start | bytes 1228808 | tf_op jit(solution)/shard_map/ppermute | solution.py:292
  44.7 14.1 %collective-permute-start.18 = (bf16[320,640]{1,0:T(8,128)(2,1)S(1)}, bf16[320,640]{1,0:T(8,128)(2,1)S(1)}, u32[]{:S(2)}, u32[]{:S(2)}) collective-permute-start(bf16[320,640]{1,0:T(8,128)(2,1)S(1)} %get-tuple-element.82), channel_id=1, source_target_pairs={{0,8},{4,20},{8,0},{12,28},{16,24},{20,4},{24,16},{28,12},{1,9},{5... | collective-permute-start | bytes 1228808 | tf_op jit(solution)/shard_map/ppermute | solution.py:292
  54.4 8.8 %collective-permute-start.22 = (bf16[320,640]{1,0:T(8,128)(2,1)S(1)}, bf16[320,640]{1,0:T(8,128)(2,1)S(1)}, u32[]{:S(2)}, u32[]{:S(2)}) collective-permute-start(bf16[320,640]{1,0:T(8,128)(2,1)S(1)} %get-tuple-element.76), channel_id=1, source_target_pairs={{0,8},{4,20},{8,0},{12,28},{16,24},{20,4},{24,16},{28,12},{1,9},{5... | collective-permute-start | bytes 1228808 | tf_op jit(solution)/shard_map/ppermute | solution.py:292
  55.0 8.2 %collective-permute-start.21 = (bf16[320,640]{1,0:T(8,128)(2,1)S(1)}, bf16[320,640]{1,0:T(8,128)(2,1)S(1)}, u32[]{:S(2)}, u32[]{:S(2)}) collective-permute-start(bf16[320,640]{1,0:T(8,128)(2,1)S(1)} %collective-permute-done.20.refs_2_), channel_id=1, source_target_pairs={{0,4},{4,0},{8,12},{12,8},{16,20},{20,16},{24,28},{28,24},{1,5},{5... | collective-permute-start | bytes 1228808 | tf_op jit(solution)/shard_map/ppermute | solution.py:67
  58.8 12.1 %collective-permute-start.31 = (bf16[304,640]{1,0:T(8,128)(2,1)S(1)}, bf16[304,640]{1,0:T(8,128)(2,1)S(1)}, u32[]{:S(2)}, u32[]{:S(2)}) collective-permute-start(bf16[304,640]{1,0:T(8,128)(2,1)S(1)} %get-tuple-element.83), channel_id=1, source_target_pairs={{0,8},{4,20},{8,0},{12,28},{16,24},{20,4},{24,16},{28,12},{1,9},{5... | collective-permute-start | bytes 1167368 | tf_op jit(solution)/shard_map/ppermute | solution.py:292
  63.2 8.8 %collective-permute-start.23 = (bf16[320,640]{1,0:T(8,128)(2,1)S(1)}, bf16[320,640]{1,0:T(8,128)(2,1)S(1)}, u32[]{:S(2)}, u32[]{:S(2)}) collective-permute-start(bf16[320,640]{1,0:T(8,128)(2,1)S(1)} %get-tuple-element.75), channel_id=1, source_target_pairs={{0,16},{4,12},{8,24},{12,4},{16,0},{20,28},{24,8},{28,20},{1,17},{... | collective-permute-start | bytes 1228808 | tf_op jit(solution)/shard_map/ppermute | solution.py:292
  63.7 8.3 %collective-permute-start.25 = (bf16[320,640]{1,0:T(8,128)(2,1)S(1)}, bf16[320,640]{1,0:T(8,128)(2,1)S(1)}, u32[]{:S(2)}, u32[]{:S(2)}) collective-permute-start(bf16[320,640]{1,0:T(8,128)(2,1)S(1)} %collective-permute-done.22.refs_3_), channel_id=1, source_target_pairs={{0,4},{4,0},{8,12},{12,8},{16,20},{20,16},{24,28},{28,24},{1,5},{5... | collective-permute-start | bytes 1228808 | tf_op jit(solution)/shard_map/ppermute | solution.py:67
  71.5 34.4 %collective-permute-start.19 = (bf16[1728,640]{1,0:T(8,128)(2,1)S(1)}, bf16[1728,640]{1,0:T(8,128)(2,1)S(1)}, u32[]{:S(2)}, u32[]{:S(2)}) collective-permute-start(bf16[1728,640]{1,0:T(8,128)(2,1)S(1)} %get-tuple-element.71.refs_0_.refs_1_), channel_id=1, source_target_pairs={{0,4},{4,0},{8,12},{12,8},{16,20},{20,16},{24,28},{28,24},{1,5},{5... | collective-permute-start | bytes 6635528 | tf_op jit(solution)/shard_map/ppermute | solution.py:67
  72.0 11.2 %collective-permute-start.26 = (bf16[320,640]{1,0:T(8,128)(2,1)S(1)}, bf16[320,640]{1,0:T(8,128)(2,1)S(1)}, u32[]{:S(2)}, u32[]{:S(2)}) collective-permute-start(bf16[320,640]{1,0:T(8,128)(2,1)S(1)} %get-tuple-element.76), channel_id=1, source_target_pairs={{0,16},{4,12},{8,24},{12,4},{16,0},{20,28},{24,8},{28,20},{1,17},{... | collective-permute-start | bytes 1228808 | tf_op jit(solution)/shard_map/ppermute | solution.py:292
  73.5 9.8 %collective-permute-start.24 = (bf16[320,640]{1,0:T(8,128)(2,1)S(1)}, bf16[320,640]{1,0:T(8,128)(2,1)S(1)}, u32[]{:S(2)}, u32[]{:S(2)}) collective-permute-start(bf16[320,640]{1,0:T(8,128)(2,1)S(1)} %collective-permute-done.23.refs_4_), channel_id=1, source_target_pairs={{0,4},{4,0},{8,12},{12,8},{16,20},{20,16},{24,28},{28,24},{1,5},{5... | collective-permute-start | bytes 1228808 | tf_op jit(solution)/shard_map/ppermute | solution.py:67
  78.9 8.6 %collective-permute-start.33 = (bf16[320,640]{1,0:T(8,128)(2,1)S(1)}, bf16[320,640]{1,0:T(8,128)(2,1)S(1)}, u32[]{:S(2)}, u32[]{:S(2)}) collective-permute-start(bf16[320,640]{1,0:T(8,128)(2,1)S(1)} %collective-permute-done.32.refs_5_), channel_id=1, source_target_pairs={{0,4},{4,0},{8,12},{12,8},{16,20},{20,16},{24,28},{28,24},{1,5},{5... | collective-permute-start | bytes 1228808 | tf_op jit(solution)/shard_map/ppermute | solution.py:67
  78.9 8.6 %collective-permute-start.35 = (bf16[304,640]{1,0:T(8,128)(2,1)S(1)}, bf16[304,640]{1,0:T(8,128)(2,1)S(1)}, u32[]{:S(2)}, u32[]{:S(2)}) collective-permute-start(bf16[304,640]{1,0:T(8,128)(2,1)S(1)} %get-tuple-element.83), channel_id=1, source_target_pairs={{0,16},{4,12},{8,24},{12,4},{16,0},{20,28},{24,8},{28,20},{1,17},{... | collective-permute-start | bytes 1167368 | tf_op jit(solution)/shard_map/ppermute | solution.py:292
  83.3 8.6 %collective-permute-start.27 = (bf16[320,640]{1,0:T(8,128)(2,1)S(1)}, bf16[320,640]{1,0:T(8,128)(2,1)S(1)}, u32[]{:S(2)}, u32[]{:S(2)}) collective-permute-start(bf16[320,640]{1,0:T(8,128)(2,1)S(1)} %collective-permute-done.20.refs_2_), channel_id=1, source_target_pairs={{0,16},{4,12},{8,24},{12,4},{16,0},{20,28},{24,8},{28,20},{1,17},{... | collective-permute-start | bytes 1228808 | tf_op jit(solution)/shard_map/ppermute | solution.py:292
  87.4 8.8 %collective-permute-start.36 = (bf16[320,640]{1,0:T(8,128)(2,1)S(1)}, bf16[320,640]{1,0:T(8,128)(2,1)S(1)}, u32[]{:S(2)}, u32[]{:S(2)}) collective-permute-start(bf16[320,640]{1,0:T(8,128)(2,1)S(1)} %collective-permute-done.18.refs_3_), channel_id=1, source_target_pairs={{0,16},{4,12},{8,24},{12,4},{16,0},{20,28},{24,8},{28,20},{1,17},{... | collective-permute-start | bytes 1228808 | tf_op jit(solution)/shard_map/ppermute | solution.py:292
  88.0 8.2 %collective-permute-start.41 = (bf16[304,640]{1,0:T(8,128)(2,1)S(1)}, bf16[304,640]{1,0:T(8,128)(2,1)S(1)}, u32[]{:S(2)}, u32[]{:S(2)}) collective-permute-start(bf16[304,640]{1,0:T(8,128)(2,1)S(1)} %collective-permute-done.35.refs_5_), channel_id=1, source_target_pairs={{0,4},{4,0},{8,12},{12,8},{16,20},{20,16},{24,28},{28,24},{1,5},{5... | collective-permute-start | bytes 1167368 | tf_op jit(solution)/shard_map/ppermute | solution.py:67
  91.8 8.8 %collective-permute-start.39 = (bf16[320,640]{1,0:T(8,128)(2,1)S(1)}, bf16[320,640]{1,0:T(8,128)(2,1)S(1)}, u32[]{:S(2)}, u32[]{:S(2)}) collective-permute-start(bf16[320,640]{1,0:T(8,128)(2,1)S(1)} %collective-permute-done.22.refs_3_), channel_id=1, source_target_pairs={{0,16},{4,12},{8,24},{12,4},{16,0},{20,28},{24,8},{28,20},{1,17},{... | collective-permute-start | bytes 1228808 | tf_op jit(solution)/shard_map/ppermute | solution.py:292
  96.2 8.6 %collective-permute-start.37 = (bf16[320,640]{1,0:T(8,128)(2,1)S(1)}, bf16[320,640]{1,0:T(8,128)(2,1)S(1)}, u32[]{:S(2)}, u32[]{:S(2)}) collective-permute-start(bf16[320,640]{1,0:T(8,128)(2,1)S(1)} %collective-permute-done.36.refs_7_), channel_id=1, source_target_pairs={{0,4},{4,0},{8,12},{12,8},{16,20},{20,16},{24,28},{28,24},{1,5},{5... | collective-permute-start | bytes 1228808 | tf_op jit(solution)/shard_map/ppermute | solution.py:67
  96.2 8.6 %collective-permute-start.42 = (bf16[304,640]{1,0:T(8,128)(2,1)S(1)}, bf16[304,640]{1,0:T(8,128)(2,1)S(1)}, u32[]{:S(2)}, u32[]{:S(2)}) collective-permute-start(bf16[304,640]{1,0:T(8,128)(2,1)S(1)} %collective-permute-done.31.refs_3_), channel_id=1, source_target_pairs={{0,16},{4,12},{8,24},{12,4},{16,0},{20,28},{24,8},{28,20},{1,17},{... | collective-permute-start | bytes 1167368 | tf_op jit(solution)/shard_map/ppermute | solution.py:292
  100.6 10.8 %collective-permute-start.45 = (bf16[464,640]{1,0:T(8,128)(2,1)S(1)}, bf16[464,640]{1,0:T(8,128)(2,1)S(1)}, u32[]{:S(2)}, u32[]{:S(2)}) collective-permute-start(bf16[464,640]{1,0:T(8,128)(2,1)S(1)} %get-tuple-element.88), channel_id=1, source_target_pairs={{0,16},{4,12},{8,24},{12,4},{16,0},{20,28},{24,8},{28,20},{1,17},{... | collective-permute-start | bytes 1781768 | tf_op jit(solution)/shard_map/ppermute | solution.py:292
  104.8 12.7 %collective-permute-start.47 = (bf16[464,640]{1,0:T(8,128)(2,1)S(1)}, bf16[464,640]{1,0:T(8,128)(2,1)S(1)}, u32[]{:S(2)}, u32[]{:S(2)}) collective-permute-start(bf16[464,640]{1,0:T(8,128)(2,1)S(1)} %shard_map.104.refs_3_), channel_id=1, source_target_pairs={{0,16},{4,12},{8,24},{12,4},{16,0},{20,28},{24,8},{28,20},{1,17},{... | collective-permute-start | bytes 1781768 | tf_op jit(solution)/shard_map/ppermute | solution.py:292
  105.9 11.6 %collective-permute-start.44 = (bf16[464,640]{1,0:T(8,128)(2,1)S(1)}, bf16[464,640]{1,0:T(8,128)(2,1)S(1)}, u32[]{:S(2)}, u32[]{:S(2)}) collective-permute-start(bf16[464,640]{1,0:T(8,128)(2,1)S(1)} %shard_map.104.refs_3_), channel_id=1, source_target_pairs={{0,4},{4,0},{8,12},{12,8},{16,20},{20,16},{24,28},{28,24},{1,5},{5... | collective-permute-start | bytes 1781768 | tf_op jit(solution)/shard_map/ppermute | solution.py:67
  (31 other events, 241.9 us)

commit v9 on v7

--- a/solution.py
+++ b/solution.py
@@ -22,7 +22,6 @@
 
 
 TURN_MASKS = ((2, 4), (4, 2))
-UPDATE_MASKS = tuple((k, k) for k in range(8))
 SWAP_MASKS = ((0, 0), (4, 2), (2, 4), (6, 6), (7, 7), (5, 3), (3, 5), (1, 1))
 OWNER_MASKS = ((0, 0), (1, 1), (2, 4), (5, 3), (4, 2), (3, 5), (6, 6), (7, 7))
 
@@ -68,29 +67,6 @@
 
 def other(me, masks):
     return me ^ jnp.where((me & 1) == 0, masks[0], masks[1])
-
-
-def take_kernel(source, out, sems, *, first):
-    count = out.shape[0] // sems.shape[0]
-    copies = []
-    for at in range(sems.shape[0]):
-        part = source.at[pl.ds(first + at * count, count), :]
-        copies.append(pltpu.make_async_copy(part, out.at[pl.ds(at * count, count), :], sems.at[at]))
-    for copy in copies:
-        copy.start()
-    for copy in copies:
-        copy.wait()
-
-
-def take(array, first, count):
-    return pl.pallas_call(
-        functools.partial(take_kernel, first=first),
-        out_shape=jax.ShapeDtypeStruct((count, array.shape[1]), array.dtype),
-        in_specs=[ANY],
-        out_specs=VMEM,
-        scratch_shapes=[pltpu.SemaphoreType.DMA((count // 16,))],
-        compiler_params=pltpu.CompilerParams(vmem_limit_bytes=60 * 2**20),
-    )(array)
 
 
 def partial_kernel(grad_t, *refs, n_fsdp, n_dp):
@@ -139,8 +115,8 @@
         tall, wide = outs[0], outs[-1]
         outs = outs[1:-1]
         rows = pieces[0].shape[0]
-        for k, piece in enumerate(pieces):
-            wide[pl.ds(pl.multiple_of((me ^ k) * rows, rows), rows), :] = piece[...]
+        for masks, piece in zip(OWNER_MASKS, pieces):
+            wide[pl.ds(pl.multiple_of(other(me, masks) * rows, rows), rows), :] = piece[...]
         tall[...] = wide[...].T
     else:
         tall = pieces[0]
@@ -295,7 +271,7 @@
 
     early, counts = chunk_sizes(cols)
     spans = [(sum(counts[:at]), count) for at, count in enumerate(counts)]
-    taken = take(master_t, 0, early[0])
+    taken = lax.slice_in_dim(master_t, 0, early[0], axis=0)
     ahead = [turn(taken, TURN_MASKS[0])]
     acts = after(acts, [taken])
 
@@ -326,12 +302,11 @@
         compiler_params=pltpu.CompilerParams(vmem_limit_bytes=16 * 2**20),
     )(moment_one, moment_two, *parts)
 
-    updates = {0: update}
-    for k in (6, 2, 4, 1):
-        updates[k] = hop(update, k)
-    for k in (2, 4, 6):
-        updates[k ^ 1] = hop(updates[k], 1)
-    updates = [updates[k] for k in range(n_dp)]
+    updates = {(0, 0): update, (1, 1): hop(update, 1)}
+    for masks, relayed in (((6, 6), (7, 7)), ((2, 4), (5, 3)), ((4, 2), (3, 5))):
+        updates[masks] = turn(update, masks)
+        updates[relayed] = hop(updates[masks], 1)
+    updates = [updates[masks] for masks in OWNER_MASKS]
 
     tall, *own = weights(projection, master_t, updates, spans[1:3])
     *late, own_first, whole = weights(projection, master_t, [tall], spans[3:] + spans[:1] + [(0, cols)])

time: 118 us -> 120 us (1.017)
  starting transfers between devices: 37.4 us -> 34.9 us
  waiting for transfers between devices: 58.8 us -> 61.2 us
  Pallas kernels: 20.1 us -> 17.8 us
  local copies, waits for them, and re-layouts: 0.04 us -> 2.33 us
  matrix products: 0.51 us -> 2.4 us
    ppermute x22 -> x25, waiting for transfers between devices: 46 us -> 52.5 us  [turn(): lax.ppermute(value, 'dp', [(i, i ^ masks[i & 1]) for i in range(n_dp)])]
    ppermute x26 -> x23, starting transfers between devices: 10.9 us -> 6.18 us  [send(): return lax.ppermute(value, axis, [(i, i ^ mask) for i in range(size)])]
    ppermute x26 -> x23, waiting for transfers between devices: 12.8 us -> 8.76 us  [send(): return lax.ppermute(value, axis, [(i, i ^ mask) for i in range(size)])]
    pallas_call x1 -> x0, Pallas kernels: 2.36 us -> none  [take(): pl.pallas_call(functools.partial(take_kernel, first=first), out_shape=jax...]
    ppermute x22 -> x25, starting transfers between devices: 26.6 us -> 28.7 us  [turn(): lax.ppermute(value, 'dp', [(i, i ^ masks[i & 1]) for i in range(n_dp)])]
    dot_general x1, matrix products: 0.51 us -> 2.4 us  [kernel_body(): jnp.dot(acts, projection, preferred_element_type=jnp.float32)]
    slice x0 -> x1, local copies, waits for them, and re-layouts: none -> 1.37 us  [kernel_body(): taken = lax.slice_in_dim(master_t, 0, early[0], axis=0)]
  transfers between devices with their start and end apart: 48 -> 48, of which waited for: 24 -> 24; matrix products, arithmetic and copies ran while one was open for 0% -> 2% of each run, Pallas kernels for 12% -> 12%
where the time goes in v9:
time: 120 us
  waiting for transfers between devices  61.2 us (51%)
  starting transfers between devices  34.9 us (29%)
  Pallas kernels  17.8 us (15%)
  matrix products  2.4 us (2%)
  local copies, waits for them, and re-layouts  2.33 us (2%)
    ppermute x25, waiting for transfers between devices, turn(): lax.ppermute(value, 'dp', [(i, i ^ masks[i & 1]) for i in range(n_dp)])  52.5 us
    ppermute x25, starting transfers between devices, turn(): lax.ppermute(value, 'dp', [(i, i ^ masks[i & 1]) for i in range(n_dp)])  28.7 us
    pallas_call x5, Pallas kernels, lay(): pl.pallas_call(functools.partial(lay_kernel, first=first, count=count, bl...  9.53 us
    ppermute x23, waiting for transfers between devices, send(): return lax.ppermute(value, axis, [(i, i ^ mask) for i in range(size)])  8.76 us
    ppermute x23, starting transfers between devices, send(): return lax.ppermute(value, axis, [(i, i ^ mask) for i in range(size)])  6.18 us
    pallas_call x1, Pallas kernels, new_master(): pl.pallas_call(master_kernel, out_shape=jax.ShapeDtypeStruct((cols, slab_...  3.12 us
    pallas_call x2, Pallas kernels, weights(): pl.pallas_call(functools.partial(weight_kernel, n_in=len(pieces), spans=s...  3.04 us
  transfers between devices with their start and end apart: 48, of which 24 were waited for; matrix products, arithmetic and copies ran while one was open for 2% of the time, Pallas kernels for 12%

profile of v9, /device:TPU:0, one launch (start us, length us, event | category | flops | bytes accessed | tf_op | source)
XLA Modules:
  0.0 119.5 jit_solution(18017172411359294183)
XLA Ops:
  2.0 3.0 %collective-permute-start.3 = (f32[336,640]{1,0:T(8,128)S(1)}, f32[336,640]{1,0:T(8,128)S(1)}, u32[]{:S(2)}, u32[]{:S(2)}) collective-permute-start(f32[336,640]{1,0:T(8,128)S(1)} %slice.4), channel_id=1, source_target_pairs={{0,8},{4,20},{8,0},{12,28},{16,24},{20,4},{24,16},{28,12},{1,9},{5... | collective-permute-start | bytes 2580488 | tf_op jit(solution)/shard_map/ppermute | solution.py:267
  5.0 2.4 %convolution_convert_fusion.refs_0_ = bf16[128,256]{1,0:T(8,128)(2,1)S(1)} fusion(bf16[128,5120]{1,0:T(8,128)(2,1)S(1)} %copy-done, bf16[5120,256]{1,0:T(8,128)(2,1)} %projection.7), kind=kOutput, calls=%fused_computation | convolution fusion | flops 335577088 | bytes 3997696 | tf_op jit(solution)/shard_map/dot_general | solution.py:278
  9.1 2.6 %collective-permute-start.1 = (bf16[128,256]{1,0:T(8,128)(2,1)S(1)}, bf16[128,256]{1,0:T(8,128)(2,1)S(1)}, u32[]{:S(2)}, u32[]{:S(2)}) collective-permute-start(bf16[128,256]{1,0:T(8,128)(2,1)S(1)} %convolution_convert_fusion.refs_0_), channel_id=1, source_target_pairs={{0,2},{1,3},{2,0},{3,1},{4,6},{5,7},{6,4},{7,5},{8,10},{9,11},{10,... | collective-permute-start | bytes 196616 | tf_op jit(solution)/shard_map/ppermute | solution.py:65
  11.9 4.2 %collective-permute-done.1.refs_2_ = bf16[128,256]{1,0:T(8,128)(2,1)S(1)} collective-permute-done((bf16[128,256]{1,0:T(8,128)(2,1)S(1)}, bf16[128,256]{1,0:T(8,128)(2,1)S(1)}, u32[]{:S(2)}, u32[]{:S(2)}) %collective-permute-start.1) | collective-permute-done | bytes 65568 | tf_op jit(solution)/shard_map/ppermute | solution.py:65
  28.5 2.5 %collective-permute-done.8.refs_5_ = bf16[32,1728]{1,0:T(8,128)(2,1)S(1)} collective-permute-done((bf16[32,1728]{1,0:T(8,128)(2,1)S(1)}, bf16[32,1728]{1,0:T(8,128)(2,1)S(1)}, u32[]{:S(2)}, u32[]{:S(2)}) %collective-permute-start.8) | collective-permute-done | bytes 110624 | tf_op jit(solution)/shard_map/ppermute | solution.py:267
  36.6 2.5 %collective-permute-done.12.refs_2_ = bf16[32,1792]{1,0:T(8,128)(2,1)S(1)} collective-permute-done((bf16[32,1792]{1,0:T(8,128)(2,1)S(1)}, bf16[32,1792]{1,0:T(8,128)(2,1)S(1)}, u32[]{:S(2)}, u32[]{:S(2)}) %collective-permute-start.12) | collective-permute-done | bytes 114720 | tf_op jit(solution)/shard_map/ppermute | solution.py:267
  39.6 2.3 %collective-permute-done.16.refs_6_ = bf16[32,1792]{1,0:T(8,128)(2,1)S(1)} collective-permute-done((bf16[32,1792]{1,0:T(8,128)(2,1)S(1)}, bf16[32,1792]{1,0:T(8,128)(2,1)S(1)}, u32[]{:S(2)}, u32[]{:S(2)}) %collective-permute-start.16) | collective-permute-done | bytes 114720 | tf_op jit(solution)/shard_map/ppermute | solution.py:267
  46.1 3.1 %shard_map.96 = f32[1728,640]{1,0:T(8,128)} custom-call(bf16[5120,256]{1,0:T(8,128)(2,1)S(1)} %copy-done.1, f32[1728,640]{1,0:T(8,128)S(1)} %bitcast.8, bf16[1792,256]{1,0:T(8,128)(2,1)S(1)} %get-tuple-element.66.tall.refs_0_), custom_call_target="tpu_custom_call" | custom-call | flops 566231040 | bytes 8847360 | tf_op jit(solution)/shard_map/pallas_call | solution.py:195
  49.3 2.2 %shard_map.97 = (bf16[352,640]{1,0:T(8,128)(2,1)S(1)}, bf16[336,640]{1,0:T(8,128)(2,1)S(1)}, bf16[336,640]{1,0:T(8,128)(2,1)S(1)}, bf16[1728,640]{1,0:T(8,128)(2,1)S(1)}) custom-call(bf16[5120,256]{1,0:T(8,128)(2,1)S(1)} %copy-done.1, f32[1728,640]{1,0:T(8,128)S(1)} %bitcast.9, bf16[1792,256]{1,0:T(8,128)(2,1)S(1)} %get-tuple-element.66.tall.refs_0_), custom_call_target="tpu_custom_call" | custom-call | flops 901775360 | bytes 7045120 | tf_op jit(solution)/shard_map/pallas_call | solution.py:143
  53.6 3.7 %collective-permute-done.18.refs_3_ = bf16[352,640]{1,0:T(8,128)(2,1)S(1)} collective-permute-done((bf16[352,640]{1,0:T(8,128)(2,1)S(1)}, bf16[352,640]{1,0:T(8,128)(2,1)S(1)}, u32[]{:S(2)}, u32[]{:S(2)}) %collective-permute-start.18) | collective-permute-done | bytes 450592 | tf_op jit(solution)/shard_map/ppermute | solution.py:267
  58.5 3.7 %collective-permute-done.22.refs_3_ = bf16[352,640]{1,0:T(8,128)(2,1)S(1)} collective-permute-done((bf16[352,640]{1,0:T(8,128)(2,1)S(1)}, bf16[352,640]{1,0:T(8,128)(2,1)S(1)}, u32[]{:S(2)}, u32[]{:S(2)}) %collective-permute-start.22) | collective-permute-done | bytes 450592 | tf_op jit(solution)/shard_map/ppermute | solution.py:267
  63.3 6.1 %collective-permute-done.30.refs_3_ = bf16[336,640]{1,0:T(8,128)(2,1)S(1)} collective-permute-done((bf16[336,640]{1,0:T(8,128)(2,1)S(1)}, bf16[336,640]{1,0:T(8,128)(2,1)S(1)}, u32[]{:S(2)}, u32[]{:S(2)}) %collective-permute-start.30) | collective-permute-done | bytes 430112 | tf_op jit(solution)/shard_map/ppermute | solution.py:267
  72.3 5.6 %collective-permute-done.31.refs_5_ = bf16[352,640]{1,0:T(8,128)(2,1)S(1)} collective-permute-done((bf16[352,640]{1,0:T(8,128)(2,1)S(1)}, bf16[352,640]{1,0:T(8,128)(2,1)S(1)}, u32[]{:S(2)}, u32[]{:S(2)}) %collective-permute-start.31) | collective-permute-done | bytes 450592 | tf_op jit(solution)/shard_map/ppermute | solution.py:267
  79.0 3.7 %collective-permute-done.26.refs_5_ = bf16[352,640]{1,0:T(8,128)(2,1)S(1)} collective-permute-done((bf16[352,640]{1,0:T(8,128)(2,1)S(1)}, bf16[352,640]{1,0:T(8,128)(2,1)S(1)}, u32[]{:S(2)}, u32[]{:S(2)}) %collective-permute-start.26) | collective-permute-done | bytes 450592 | tf_op jit(solution)/shard_map/ppermute | solution.py:267
  83.8 3.5 %collective-permute-done.34.refs_5_ = bf16[336,640]{1,0:T(8,128)(2,1)S(1)} collective-permute-done((bf16[336,640]{1,0:T(8,128)(2,1)S(1)}, bf16[336,640]{1,0:T(8,128)(2,1)S(1)}, u32[]{:S(2)}, u32[]{:S(2)}) %collective-permute-start.34) | collective-permute-done | bytes 430112 | tf_op jit(solution)/shard_map/ppermute | solution.py:267
  88.4 3.7 %collective-permute-done.27.refs_6_ = bf16[352,640]{1,0:T(8,128)(2,1)S(1)} collective-permute-done((bf16[352,640]{1,0:T(8,128)(2,1)S(1)}, bf16[352,640]{1,0:T(8,128)(2,1)S(1)}, u32[]{:S(2)}, u32[]{:S(2)}) %collective-permute-start.27) | collective-permute-done | bytes 450592 | tf_op jit(solution)/shard_map/ppermute | solution.py:267
  93.2 3.7 %collective-permute-done.35.refs_7_ = bf16[352,640]{1,0:T(8,128)(2,1)S(1)} collective-permute-done((bf16[352,640]{1,0:T(8,128)(2,1)S(1)}, bf16[352,640]{1,0:T(8,128)(2,1)S(1)}, u32[]{:S(2)}, u32[]{:S(2)}) %collective-permute-start.35) | collective-permute-done | bytes 450592 | tf_op jit(solution)/shard_map/ppermute | solution.py:267
  98.1 3.7 %collective-permute-done.38.refs_7_ = bf16[352,640]{1,0:T(8,128)(2,1)S(1)} collective-permute-done((bf16[352,640]{1,0:T(8,128)(2,1)S(1)}, bf16[352,640]{1,0:T(8,128)(2,1)S(1)}, u32[]{:S(2)}, u32[]{:S(2)}) %collective-permute-start.38) | collective-permute-done | bytes 450592 | tf_op jit(solution)/shard_map/ppermute | solution.py:267
  103.4 3.0 %collective-permute-done.41.refs_7_ = bf16[336,640]{1,0:T(8,128)(2,1)S(1)} collective-permute-done((bf16[336,640]{1,0:T(8,128)(2,1)S(1)}, bf16[336,640]{1,0:T(8,128)(2,1)S(1)}, u32[]{:S(2)}, u32[]{:S(2)}) %collective-permute-start.41) | collective-permute-done | bytes 430112 | tf_op jit(solution)/shard_map/ppermute | solution.py:267
  107.7 1.9 %shard_map.98.refs_0_ = bf16[1728,5120]{1,0:T(8,128)(2,1)} custom-call(bf16[1728,640]{1,0:T(8,128)(2,1)S(1)} %get-tuple-element.69.refs_0_.refs_1_, bf16[1728,640]{1,0:T(8,128)(2,1)S(1)} %collective-permute-done.19.refs_1_.refs_2_, bf16[352,640]{1,0:T(8,128)(2,1)S(1)} %collective-permute-done.20.refs_2_, ...), custom_call_target="tpu_custom_call" | custom-call | bytes 7208960 | tf_op jit(solution)/shard_map/pallas_call | solution.py:240
  109.6 1.9 %shard_map.99.refs_0_ = bf16[1728,5120]{1,0:T(8,128)(2,1)} custom-call(bf16[1728,5120]{1,0:T(8,128)(2,1)} %shard_map.98.refs_0_, bf16[1728,640]{1,0:T(8,128)(2,1)S(1)} %get-tuple-element.69.refs_0_.refs_1_, bf16[1728,640]{1,0:T(8,128)(2,1)S(1)} %collective-permute-done.19.refs_1_.refs_2_, ...), custom_call_target="tpu_custom_call", output_to_operand_aliasing={{}: (0, {})} | custom-call | bytes 7208960 | tf_op jit(solution)/shard_map/pallas_call | solution.py:240
  111.6 1.9 %shard_map.100.refs_0_ = bf16[1728,5120]{1,0:T(8,128)(2,1)} custom-call(bf16[1728,5120]{1,0:T(8,128)(2,1)} %shard_map.99.refs_0_, bf16[1728,640]{1,0:T(8,128)(2,1)S(1)} %get-tuple-element.69.refs_0_.refs_1_, bf16[1728,640]{1,0:T(8,128)(2,1)S(1)} %collective-permute-done.19.refs_1_.refs_2_, ...), custom_call_target="tpu_custom_call", output_to_operand_aliasing={{}: (0, {})} | custom-call | bytes 7208960 | tf_op jit(solution)/shard_map/pallas_call | solution.py:240
  113.9 1.9 %shard_map.101.refs_0_ = bf16[1728,5120]{1,0:T(8,128)(2,1)} custom-call(bf16[1728,5120]{1,0:T(8,128)(2,1)} %shard_map.100.refs_0_, bf16[1728,640]{1,0:T(8,128)(2,1)S(1)} %get-tuple-element.69.refs_0_.refs_1_, bf16[1728,640]{1,0:T(8,128)(2,1)S(1)} %collective-permute-done.19.refs_1_.refs_2_, ...), custom_call_target="tpu_custom_call", output_to_operand_aliasing={{}: (0, {})} | custom-call | bytes 6881280 | tf_op jit(solution)/shard_map/pallas_call | solution.py:240
  117.6 1.9 %shard_map.103 = bf16[1728,5120]{1,0:T(8,128)(2,1)} custom-call(bf16[1728,5120]{1,0:T(8,128)(2,1)} %shard_map.101.refs_0_, bf16[1728,640]{1,0:T(8,128)(2,1)S(1)} %get-tuple-element.69.refs_0_.refs_1_, bf16[1728,640]{1,0:T(8,128)(2,1)S(1)} %collective-permute-done.19.refs_1_.refs_2_, ...), custom_call_target="tpu_custom_call", output_to_operand_aliasing={{}: (0, {})} | custom-call | bytes 6881280 | tf_op jit(solution)/shard_map/pallas_call | solution.py:240
  (97 shorter events, 44.0 us)
Async XLA Ops:
  2.0 16.5 %collective-permute-start.3 = (f32[336,640]{1,0:T(8,128)S(1)}, f32[336,640]{1,0:T(8,128)S(1)}, u32[]{:S(2)}, u32[]{:S(2)}) collective-permute-start(f32[336,640]{1,0:T(8,128)S(1)} %slice.4), channel_id=1, source_target_pairs={{0,8},{4,20},{8,0},{12,28},{16,24},{20,4},{24,16},{28,12},{1,9},{5... | collective-permute-start | bytes 2580488 | tf_op jit(solution)/shard_map/ppermute | solution.py:267
  22.1 9.0 %collective-permute-start.8 = (bf16[32,1728]{1,0:T(8,128)(2,1)S(1)}, bf16[32,1728]{1,0:T(8,128)(2,1)S(1)}, u32[]{:S(2)}, u32[]{:S(2)}) collective-permute-start(bf16[32,1728]{1,0:T(8,128)(2,1)S(1)} %get-tuple-element.60), channel_id=1, source_target_pairs={{0,20},{4,8},{8,28},{12,0},{16,4},{20,24},{24,12},{28,16},{1,21},{... | collective-permute-start | bytes 331784 | tf_op jit(solution)/shard_map/ppermute | solution.py:267
  45.2 12.1 %collective-permute-start.18 = (bf16[352,640]{1,0:T(8,128)(2,1)S(1)}, bf16[352,640]{1,0:T(8,128)(2,1)S(1)}, u32[]{:S(2)}, u32[]{:S(2)}) collective-permute-start(bf16[352,640]{1,0:T(8,128)(2,1)S(1)} %get-tuple-element.78), channel_id=1, source_target_pairs={{0,8},{4,20},{8,0},{12,28},{16,24},{20,4},{24,16},{28,12},{1,9},{5... | collective-permute-start | bytes 1351688 | tf_op jit(solution)/shard_map/ppermute | solution.py:267
  52.5 9.7 %collective-permute-start.22 = (bf16[352,640]{1,0:T(8,128)(2,1)S(1)}, bf16[352,640]{1,0:T(8,128)(2,1)S(1)}, u32[]{:S(2)}, u32[]{:S(2)}) collective-permute-start(bf16[352,640]{1,0:T(8,128)(2,1)S(1)} %get-tuple-element.74), channel_id=1, source_target_pairs={{0,8},{4,20},{8,0},{12,28},{16,24},{20,4},{24,16},{28,12},{1,9},{5... | collective-permute-start | bytes 1351688 | tf_op jit(solution)/shard_map/ppermute | solution.py:267
  53.6 8.5 %collective-permute-start.21 = (bf16[352,640]{1,0:T(8,128)(2,1)S(1)}, bf16[352,640]{1,0:T(8,128)(2,1)S(1)}, u32[]{:S(2)}, u32[]{:S(2)}) collective-permute-start(bf16[352,640]{1,0:T(8,128)(2,1)S(1)} %collective-permute-done.20.refs_2_), channel_id=1, source_target_pairs={{0,4},{4,0},{8,12},{12,8},{16,20},{20,16},{24,28},{28,24},{1,5},{5... | collective-permute-start | bytes 1351688 | tf_op jit(solution)/shard_map/ppermute | solution.py:65
  57.3 12.1 %collective-permute-start.29 = (bf16[352,640]{1,0:T(8,128)(2,1)S(1)}, bf16[352,640]{1,0:T(8,128)(2,1)S(1)}, u32[]{:S(2)}, u32[]{:S(2)}) collective-permute-start(bf16[352,640]{1,0:T(8,128)(2,1)S(1)} %collective-permute-done.18.refs_3_), channel_id=1, source_target_pairs={{0,4},{4,0},{8,12},{12,8},{16,20},{20,16},{24,28},{28,24},{1,5},{5... | collective-permute-start | bytes 1351688 | tf_op jit(solution)/shard_map/ppermute | solution.py:65
  57.3 12.1 %collective-permute-start.30 = (bf16[336,640]{1,0:T(8,128)(2,1)S(1)}, bf16[336,640]{1,0:T(8,128)(2,1)S(1)}, u32[]{:S(2)}, u32[]{:S(2)}) collective-permute-start(bf16[336,640]{1,0:T(8,128)(2,1)S(1)} %get-tuple-element.79), channel_id=1, source_target_pairs={{0,8},{4,20},{8,0},{12,28},{16,24},{20,4},{24,16},{28,12},{1,9},{5... | collective-permute-start | bytes 1290248 | tf_op jit(solution)/shard_map/ppermute | solution.py:267
  62.2 8.9 %collective-permute-start.23 = (bf16[352,640]{1,0:T(8,128)(2,1)S(1)}, bf16[352,640]{1,0:T(8,128)(2,1)S(1)}, u32[]{:S(2)}, u32[]{:S(2)}) collective-permute-start(bf16[352,640]{1,0:T(8,128)(2,1)S(1)} %get-tuple-element.73), channel_id=1, source_target_pairs={{0,16},{4,12},{8,24},{12,4},{16,0},{20,28},{24,8},{28,20},{1,17},{... | collective-permute-start | bytes 1351688 | tf_op jit(solution)/shard_map/ppermute | solution.py:267
  70.6 36.9 %collective-permute-start.19 = (bf16[1728,640]{1,0:T(8,128)(2,1)S(1)}, bf16[1728,640]{1,0:T(8,128)(2,1)S(1)}, u32[]{:S(2)}, u32[]{:S(2)}) collective-permute-start(bf16[1728,640]{1,0:T(8,128)(2,1)S(1)} %get-tuple-element.69.refs_0_.refs_1_), channel_id=1, source_target_pairs={{0,4},{4,0},{8,12},{12,8},{16,20},{20,16},{24,28},{28,24},{1,5},{5... | collective-permute-start | bytes 6635528 | tf_op jit(solution)/shard_map/ppermute | solution.py:65
  71.1 11.6 %collective-permute-start.26 = (bf16[352,640]{1,0:T(8,128)(2,1)S(1)}, bf16[352,640]{1,0:T(8,128)(2,1)S(1)}, u32[]{:S(2)}, u32[]{:S(2)}) collective-permute-start(bf16[352,640]{1,0:T(8,128)(2,1)S(1)} %get-tuple-element.74), channel_id=1, source_target_pairs={{0,16},{4,12},{8,24},{12,4},{16,0},{20,28},{24,8},{28,20},{1,17},{... | collective-permute-start | bytes 1351688 | tf_op jit(solution)/shard_map/ppermute | solution.py:267
  72.0 10.7 %collective-permute-start.24 = (bf16[352,640]{1,0:T(8,128)(2,1)S(1)}, bf16[352,640]{1,0:T(8,128)(2,1)S(1)}, u32[]{:S(2)}, u32[]{:S(2)}) collective-permute-start(bf16[352,640]{1,0:T(8,128)(2,1)S(1)} %collective-permute-done.23.refs_4_), channel_id=1, source_target_pairs={{0,4},{4,0},{8,12},{12,8},{16,20},{20,16},{24,28},{28,24},{1,5},{5... | collective-permute-start | bytes 1351688 | tf_op jit(solution)/shard_map/ppermute | solution.py:65
  77.8 9.4 %collective-permute-start.32 = (bf16[352,640]{1,0:T(8,128)(2,1)S(1)}, bf16[352,640]{1,0:T(8,128)(2,1)S(1)}, u32[]{:S(2)}, u32[]{:S(2)}) collective-permute-start(bf16[352,640]{1,0:T(8,128)(2,1)S(1)} %collective-permute-done.31.refs_5_), channel_id=1, source_target_pairs={{0,4},{4,0},{8,12},{12,8},{16,20},{20,16},{24,28},{28,24},{1,5},{5... | collective-permute-start | bytes 1351688 | tf_op jit(solution)/shard_map/ppermute | solution.py:65
  77.8 9.4 %collective-permute-start.34 = (bf16[336,640]{1,0:T(8,128)(2,1)S(1)}, bf16[336,640]{1,0:T(8,128)(2,1)S(1)}, u32[]{:S(2)}, u32[]{:S(2)}) collective-permute-start(bf16[336,640]{1,0:T(8,128)(2,1)S(1)} %get-tuple-element.79), channel_id=1, source_target_pairs={{0,16},{4,12},{8,24},{12,4},{16,0},{20,28},{24,8},{28,20},{1,17},{... | collective-permute-start | bytes 1290248 | tf_op jit(solution)/shard_map/ppermute | solution.py:267
  82.6 9.4 %collective-permute-start.27 = (bf16[352,640]{1,0:T(8,128)(2,1)S(1)}, bf16[352,640]{1,0:T(8,128)(2,1)S(1)}, u32[]{:S(2)}, u32[]{:S(2)}) collective-permute-start(bf16[352,640]{1,0:T(8,128)(2,1)S(1)} %collective-permute-done.20.refs_2_), channel_id=1, source_target_pairs={{0,16},{4,12},{8,24},{12,4},{16,0},{20,28},{24,8},{28,20},{1,17},{... | collective-permute-start | bytes 1351688 | tf_op jit(solution)/shard_map/ppermute | solution.py:267
  87.3 9.7 %collective-permute-start.35 = (bf16[352,640]{1,0:T(8,128)(2,1)S(1)}, bf16[352,640]{1,0:T(8,128)(2,1)S(1)}, u32[]{:S(2)}, u32[]{:S(2)}) collective-permute-start(bf16[352,640]{1,0:T(8,128)(2,1)S(1)} %collective-permute-done.18.refs_3_), channel_id=1, source_target_pairs={{0,16},{4,12},{8,24},{12,4},{16,0},{20,28},{24,8},{28,20},{1,17},{... | collective-permute-start | bytes 1351688 | tf_op jit(solution)/shard_map/ppermute | solution.py:267
  88.4 8.5 %collective-permute-start.40 = (bf16[336,640]{1,0:T(8,128)(2,1)S(1)}, bf16[336,640]{1,0:T(8,128)(2,1)S(1)}, u32[]{:S(2)}, u32[]{:S(2)}) collective-permute-start(bf16[336,640]{1,0:T(8,128)(2,1)S(1)} %collective-permute-done.34.refs_5_), channel_id=1, source_target_pairs={{0,4},{4,0},{8,12},{12,8},{16,20},{20,16},{24,28},{28,24},{1,5},{5... | collective-permute-start | bytes 1290248 | tf_op jit(solution)/shard_map/ppermute | solution.py:65
  92.1 9.7 %collective-permute-start.38 = (bf16[352,640]{1,0:T(8,128)(2,1)S(1)}, bf16[352,640]{1,0:T(8,128)(2,1)S(1)}, u32[]{:S(2)}, u32[]{:S(2)}) collective-permute-start(bf16[352,640]{1,0:T(8,128)(2,1)S(1)} %collective-permute-done.22.refs_3_), channel_id=1, source_target_pairs={{0,16},{4,12},{8,24},{12,4},{16,0},{20,28},{24,8},{28,20},{1,17},{... | collective-permute-start | bytes 1351688 | tf_op jit(solution)/shard_map/ppermute | solution.py:267
  93.2 9.0 %collective-permute-start.28 = (bf16[352,640]{1,0:T(8,128)(2,1)S(1)}, bf16[352,640]{1,0:T(8,128)(2,1)S(1)}, u32[]{:S(2)}, u32[]{:S(2)}) collective-permute-start(bf16[352,640]{1,0:T(8,128)(2,1)S(1)} %collective-permute-done.27.refs_6_), channel_id=1, source_target_pairs={{0,4},{4,0},{8,12},{12,8},{16,20},{20,16},{24,28},{28,24},{1,5},{5... | collective-permute-start | bytes 1351688 | tf_op jit(solution)/shard_map/ppermute | solution.py:65
  96.9 9.4 %collective-permute-start.36 = (bf16[352,640]{1,0:T(8,128)(2,1)S(1)}, bf16[352,640]{1,0:T(8,128)(2,1)S(1)}, u32[]{:S(2)}, u32[]{:S(2)}) collective-permute-start(bf16[352,640]{1,0:T(8,128)(2,1)S(1)} %collective-permute-done.35.refs_7_), channel_id=1, source_target_pairs={{0,4},{4,0},{8,12},{12,8},{16,20},{20,16},{24,28},{28,24},{1,5},{5... | collective-permute-start | bytes 1351688 | tf_op jit(solution)/shard_map/ppermute | solution.py:65
  96.9 9.4 %collective-permute-start.41 = (bf16[336,640]{1,0:T(8,128)(2,1)S(1)}, bf16[336,640]{1,0:T(8,128)(2,1)S(1)}, u32[]{:S(2)}, u32[]{:S(2)}) collective-permute-start(bf16[336,640]{1,0:T(8,128)(2,1)S(1)} %collective-permute-done.30.refs_3_), channel_id=1, source_target_pairs={{0,16},{4,12},{8,24},{12,4},{16,0},{20,28},{24,8},{28,20},{1,17},{... | collective-permute-start | bytes 1290248 | tf_op jit(solution)/shard_map/ppermute | solution.py:267
  101.7 9.8 %collective-permute-start.39 = (bf16[352,640]{1,0:T(8,128)(2,1)S(1)}, bf16[352,640]{1,0:T(8,128)(2,1)S(1)}, u32[]{:S(2)}, u32[]{:S(2)}) collective-permute-start(bf16[352,640]{1,0:T(8,128)(2,1)S(1)} %collective-permute-done.38.refs_7_), channel_id=1, source_target_pairs={{0,4},{4,0},{8,12},{12,8},{16,20},{20,16},{24,28},{28,24},{1,5},{5... | collective-permute-start | bytes 1351688 | tf_op jit(solution)/shard_map/ppermute | solution.py:65
  102.2 11.3 %collective-permute-start.44 = (bf16[336,640]{1,0:T(8,128)(2,1)S(1)}, bf16[336,640]{1,0:T(8,128)(2,1)S(1)}, u32[]{:S(2)}, u32[]{:S(2)}) collective-permute-start(bf16[336,640]{1,0:T(8,128)(2,1)S(1)} %get-tuple-element.84), channel_id=1, source_target_pairs={{0,16},{4,12},{8,24},{12,4},{16,0},{20,28},{24,8},{28,20},{1,17},{... | collective-permute-start | bytes 1290248 | tf_op jit(solution)/shard_map/ppermute | solution.py:267
  106.4 9.4 %collective-permute-start.46 = (bf16[336,640]{1,0:T(8,128)(2,1)S(1)}, bf16[336,640]{1,0:T(8,128)(2,1)S(1)}, u32[]{:S(2)}, u32[]{:S(2)}) collective-permute-start(bf16[336,640]{1,0:T(8,128)(2,1)S(1)} %shard_map.102.refs_3_), channel_id=1, source_target_pairs={{0,16},{4,12},{8,24},{12,4},{16,0},{20,28},{24,8},{28,20},{1,17},{... | collective-permute-start | bytes 1290248 | tf_op jit(solution)/shard_map/ppermute | solution.py:267
  107.5 8.6 %collective-permute-start.43 = (bf16[336,640]{1,0:T(8,128)(2,1)S(1)}, bf16[336,640]{1,0:T(8,128)(2,1)S(1)}, u32[]{:S(2)}, u32[]{:S(2)}) collective-permute-start(bf16[336,640]{1,0:T(8,128)(2,1)S(1)} %shard_map.102.refs_3_), channel_id=1, source_target_pairs={{0,4},{4,0},{8,12},{12,8},{16,20},{20,16},{24,28},{28,24},{1,5},{5... | collective-permute-start | bytes 1290248 | tf_op jit(solution)/shard_map/ppermute | solution.py:65
  (30 other events, 261.4 us)

commit v10 on v7

--- a/solution.py
+++ b/solution.py
@@ -87,7 +87,7 @@
         functools.partial(take_kernel, first=first),
         out_shape=jax.ShapeDtypeStruct((count, array.shape[1]), array.dtype),
         in_specs=[ANY],
-        out_specs=VMEM,
+        out_specs=ANY,
         scratch_shapes=[pltpu.SemaphoreType.DMA((count // 16,))],
         compiler_params=pltpu.CompilerParams(vmem_limit_bytes=60 * 2**20),
     )(array)

time: 118 us -> 143 us (1.21)
  Pallas kernels: 20.1 us -> 45.1 us
    pallas_call x1, Pallas kernels: 2.36 us -> 27.4 us  [take(): pl.pallas_call(functools.partial(take_kernel, first=first), out_shape=jax...]
  transfers between devices with their start and end apart: 48 -> 48, of which waited for: 24 -> 24; matrix products, arithmetic and copies ran while one was open for 0% -> 0% of each run, Pallas kernels for 12% -> 10%
where the time goes in v10:
time: 143 us
  waiting for transfers between devices  58.6 us (41%)
  Pallas kernels  45.1 us (32%)
  starting transfers between devices  37.6 us (26%)
    ppermute x22, waiting for transfers between devices, turn(): lax.ppermute(value, 'dp', [(i, i ^ masks[i & 1]) for i in range(n_dp)])  45.9 us
    pallas_call x1, Pallas kernels, take(): pl.pallas_call(functools.partial(take_kernel, first=first), out_shape=jax...  27.4 us
    ppermute x22, starting transfers between devices, turn(): lax.ppermute(value, 'dp', [(i, i ^ masks[i & 1]) for i in range(n_dp)])  26.7 us
    ppermute x26, waiting for transfers between devices, send(): return lax.ppermute(value, axis, [(i, i ^ mask) for i in range(size)])  12.8 us
    ppermute x26, starting transfers between devices, send(): return lax.ppermute(value, axis, [(i, i ^ mask) for i in range(size)])  10.9 us
    pallas_call x5, Pallas kernels, lay(): pl.pallas_call(functools.partial(lay_kernel, first=first, count=count, bl...  9.53 us
    pallas_call x1, Pallas kernels, new_master(): pl.pallas_call(master_kernel, out_shape=jax.ShapeDtypeStruct((cols, slab_...  3.12 us
    pallas_call x2, Pallas kernels, weights(): pl.pallas_call(functools.partial(weight_kernel, n_in=len(pieces), spans=s...  3.03 us
  transfers between devices with their start and end apart: 48, of which 24 were waited for; matrix products, arithmetic and copies ran while one was open for 0% of the time, Pallas kernels for 10%

profile of v10, /device:TPU:0, one launch (start us, length us, event | category | flops | bytes accessed | tf_op | source)
XLA Modules:
  0.0 142.7 jit_solution(14027478144444833827)
XLA Ops:
  0.7 27.4 %shard_map.93 = f32[336,640]{1,0:T(8,128)} custom-call(f32[1728,640]{1,0:T(8,128)} %bitcast.6), custom_call_target="tpu_custom_call" | custom-call | tf_op jit(solution)/shard_map/pallas_call | solution.py:86
  28.1 3.0 %collective-permute-start.3 = (f32[336,640]{1,0:T(8,128)}, f32[336,640]{1,0:T(8,128)S(1)}, u32[]{:S(2)}, u32[]{:S(2)}) collective-permute-start(f32[336,640]{1,0:T(8,128)} %shard_map.93), channel_id=1, source_target_pairs={{0,8},{4,20},{8,0},{12,28},{16,24},{20,4},{24,16},{28,12},{1,9},{5... | collective-permute-start | bytes 2580488 | tf_op jit(solution)/shard_map/ppermute | solution.py:291
  33.2 2.6 %collective-permute-start.1 = (bf16[128,256]{1,0:T(8,128)(2,1)S(1)}, bf16[128,256]{1,0:T(8,128)(2,1)S(1)}, u32[]{:S(2)}, u32[]{:S(2)}) collective-permute-start(bf16[128,256]{1,0:T(8,128)(2,1)S(1)} %convolution_convert_fusion.refs_0_), channel_id=1, source_target_pairs={{0,2},{1,3},{2,0},{3,1},{4,6},{5,7},{6,4},{7,5},{8,10},{9,11},{10,... | collective-permute-start | bytes 196616 | tf_op jit(solution)/shard_map/ppermute | solution.py:66
  36.0 4.2 %collective-permute-done.1.refs_2_ = bf16[128,256]{1,0:T(8,128)(2,1)S(1)} collective-permute-done((bf16[128,256]{1,0:T(8,128)(2,1)S(1)}, bf16[128,256]{1,0:T(8,128)(2,1)S(1)}, u32[]{:S(2)}, u32[]{:S(2)}) %collective-permute-start.1) | collective-permute-done | bytes 65568 | tf_op jit(solution)/shard_map/ppermute | solution.py:66
  46.3 2.5 %collective-permute-start.8 = (bf16[32,1728]{1,0:T(8,128)(2,1)S(1)}, bf16[32,1728]{1,0:T(8,128)(2,1)S(1)}, u32[]{:S(2)}, u32[]{:S(2)}) collective-permute-start(bf16[32,1728]{1,0:T(8,128)(2,1)S(1)} %get-tuple-element.60), channel_id=1, source_target_pairs={{0,20},{4,8},{8,28},{12,0},{16,4},{20,24},{24,12},{28,16},{1,21},{... | collective-permute-start | bytes 331784 | tf_op jit(solution)/shard_map/ppermute | solution.py:291
  52.6 2.5 %collective-permute-done.8.refs_5_ = bf16[32,1728]{1,0:T(8,128)(2,1)S(1)} collective-permute-done((bf16[32,1728]{1,0:T(8,128)(2,1)S(1)}, bf16[32,1728]{1,0:T(8,128)(2,1)S(1)}, u32[]{:S(2)}, u32[]{:S(2)}) %collective-permute-start.8) | collective-permute-done | bytes 110624 | tf_op jit(solution)/shard_map/ppermute | solution.py:291
  60.6 2.5 %collective-permute-done.12.refs_2_ = bf16[32,1792]{1,0:T(8,128)(2,1)S(1)} collective-permute-done((bf16[32,1792]{1,0:T(8,128)(2,1)S(1)}, bf16[32,1792]{1,0:T(8,128)(2,1)S(1)}, u32[]{:S(2)}, u32[]{:S(2)}) %collective-permute-start.12) | collective-permute-done | bytes 114720 | tf_op jit(solution)/shard_map/ppermute | solution.py:66
  63.1 2.0 %collective-permute-done.14.refs_4_ = bf16[32,1792]{1,0:T(8,128)(2,1)S(1)} collective-permute-done((bf16[32,1792]{1,0:T(8,128)(2,1)S(1)}, bf16[32,1792]{1,0:T(8,128)(2,1)S(1)}, u32[]{:S(2)}, u32[]{:S(2)}) %collective-permute-start.14) | collective-permute-done | bytes 114720 | tf_op jit(solution)/shard_map/ppermute | solution.py:66
  69.5 3.1 %shard_map.97 = f32[1728,640]{1,0:T(8,128)} custom-call(bf16[5120,256]{1,0:T(8,128)(2,1)S(1)} %copy-done.2, f32[1728,640]{1,0:T(8,128)S(1)} %bitcast.8, bf16[1792,256]{1,0:T(8,128)(2,1)S(1)} %get-tuple-element.66.tall.refs_0_), custom_call_target="tpu_custom_call" | custom-call | flops 566231040 | bytes 8847360 | tf_op jit(solution)/shard_map/pallas_call | solution.py:219
  72.6 2.2 %shard_map.98 = (bf16[352,640]{1,0:T(8,128)(2,1)S(1)}, bf16[336,640]{1,0:T(8,128)(2,1)S(1)}, bf16[336,640]{1,0:T(8,128)(2,1)S(1)}, bf16[1728,640]{1,0:T(8,128)(2,1)S(1)}) custom-call(bf16[5120,256]{1,0:T(8,128)(2,1)S(1)} %copy-done.2, f32[1728,640]{1,0:T(8,128)S(1)} %bitcast.9, bf16[1792,256]{1,0:T(8,128)(2,1)S(1)} %get-tuple-element.66.tall.refs_0_), custom_call_target="tpu_custom_call" | custom-call | flops 901775360 | bytes 7045120 | tf_op jit(solution)/shard_map/pallas_call | solution.py:167
  77.2 3.4 %collective-permute-done.18.refs_3_ = bf16[352,640]{1,0:T(8,128)(2,1)S(1)} collective-permute-done((bf16[352,640]{1,0:T(8,128)(2,1)S(1)}, bf16[352,640]{1,0:T(8,128)(2,1)S(1)}, u32[]{:S(2)}, u32[]{:S(2)}) %collective-permute-start.18) | collective-permute-done | bytes 450592 | tf_op jit(solution)/shard_map/ppermute | solution.py:291
  82.1 3.4 %collective-permute-done.22.refs_3_ = bf16[352,640]{1,0:T(8,128)(2,1)S(1)} collective-permute-done((bf16[352,640]{1,0:T(8,128)(2,1)S(1)}, bf16[352,640]{1,0:T(8,128)(2,1)S(1)}, u32[]{:S(2)}, u32[]{:S(2)}) %collective-permute-start.22) | collective-permute-done | bytes 450592 | tf_op jit(solution)/shard_map/ppermute | solution.py:291
  86.4 6.1 %collective-permute-done.30.refs_3_ = bf16[336,640]{1,0:T(8,128)(2,1)S(1)} collective-permute-done((bf16[336,640]{1,0:T(8,128)(2,1)S(1)}, bf16[336,640]{1,0:T(8,128)(2,1)S(1)}, u32[]{:S(2)}, u32[]{:S(2)}) %collective-permute-start.30) | collective-permute-done | bytes 430112 | tf_op jit(solution)/shard_map/ppermute | solution.py:291
  95.9 5.1 %collective-permute-done.31.refs_5_ = bf16[352,640]{1,0:T(8,128)(2,1)S(1)} collective-permute-done((bf16[352,640]{1,0:T(8,128)(2,1)S(1)}, bf16[352,640]{1,0:T(8,128)(2,1)S(1)}, u32[]{:S(2)}, u32[]{:S(2)}) %collective-permute-start.31) | collective-permute-done | bytes 450592 | tf_op jit(solution)/shard_map/ppermute | solution.py:291
  102.1 3.7 %collective-permute-done.26.refs_5_ = bf16[352,640]{1,0:T(8,128)(2,1)S(1)} collective-permute-done((bf16[352,640]{1,0:T(8,128)(2,1)S(1)}, bf16[352,640]{1,0:T(8,128)(2,1)S(1)}, u32[]{:S(2)}, u32[]{:S(2)}) %collective-permute-start.26) | collective-permute-done | bytes 450592 | tf_op jit(solution)/shard_map/ppermute | solution.py:291
  106.9 3.5 %collective-permute-done.34.refs_5_ = bf16[336,640]{1,0:T(8,128)(2,1)S(1)} collective-permute-done((bf16[336,640]{1,0:T(8,128)(2,1)S(1)}, bf16[336,640]{1,0:T(8,128)(2,1)S(1)}, u32[]{:S(2)}, u32[]{:S(2)}) %collective-permute-start.34) | collective-permute-done | bytes 430112 | tf_op jit(solution)/shard_map/ppermute | solution.py:291
  111.5 3.7 %collective-permute-done.27.refs_6_ = bf16[352,640]{1,0:T(8,128)(2,1)S(1)} collective-permute-done((bf16[352,640]{1,0:T(8,128)(2,1)S(1)}, bf16[352,640]{1,0:T(8,128)(2,1)S(1)}, u32[]{:S(2)}, u32[]{:S(2)}) %collective-permute-start.27) | collective-permute-done | bytes 450592 | tf_op jit(solution)/shard_map/ppermute | solution.py:291
  116.4 3.7 %collective-permute-done.35.refs_7_ = bf16[352,640]{1,0:T(8,128)(2,1)S(1)} collective-permute-done((bf16[352,640]{1,0:T(8,128)(2,1)S(1)}, bf16[352,640]{1,0:T(8,128)(2,1)S(1)}, u32[]{:S(2)}, u32[]{:S(2)}) %collective-permute-start.35) | collective-permute-done | bytes 450592 | tf_op jit(solution)/shard_map/ppermute | solution.py:291
  121.2 3.7 %collective-permute-done.38.refs_7_ = bf16[352,640]{1,0:T(8,128)(2,1)S(1)} collective-permute-done((bf16[352,640]{1,0:T(8,128)(2,1)S(1)}, bf16[352,640]{1,0:T(8,128)(2,1)S(1)}, u32[]{:S(2)}, u32[]{:S(2)}) %collective-permute-start.38) | collective-permute-done | bytes 450592 | tf_op jit(solution)/shard_map/ppermute | solution.py:291
  126.5 3.0 %collective-permute-done.41.refs_7_ = bf16[336,640]{1,0:T(8,128)(2,1)S(1)} collective-permute-done((bf16[336,640]{1,0:T(8,128)(2,1)S(1)}, bf16[336,640]{1,0:T(8,128)(2,1)S(1)}, u32[]{:S(2)}, u32[]{:S(2)}) %collective-permute-start.41) | collective-permute-done | bytes 430112 | tf_op jit(solution)/shard_map/ppermute | solution.py:291
  131.1 1.9 %shard_map.99.refs_0_ = bf16[1728,5120]{1,0:T(8,128)(2,1)} custom-call(bf16[1728,640]{1,0:T(8,128)(2,1)S(1)} %get-tuple-element.69.refs_0_.refs_1_, bf16[1728,640]{1,0:T(8,128)(2,1)S(1)} %collective-permute-done.19.refs_1_.refs_2_, bf16[352,640]{1,0:T(8,128)(2,1)S(1)} %collective-permute-done.20.refs_2_, ...), custom_call_target="tpu_custom_call" | custom-call | bytes 7208960 | tf_op jit(solution)/shard_map/pallas_call | solution.py:264
  133.0 1.9 %shard_map.100.refs_0_ = bf16[1728,5120]{1,0:T(8,128)(2,1)} custom-call(bf16[1728,5120]{1,0:T(8,128)(2,1)} %shard_map.99.refs_0_, bf16[1728,640]{1,0:T(8,128)(2,1)S(1)} %get-tuple-element.69.refs_0_.refs_1_, bf16[1728,640]{1,0:T(8,128)(2,1)S(1)} %collective-permute-done.19.refs_1_.refs_2_, ...), custom_call_target="tpu_custom_call", output_to_operand_aliasing={{}: (0, {})} | custom-call | bytes 7208960 | tf_op jit(solution)/shard_map/pallas_call | solution.py:264
  135.0 1.9 %shard_map.101.refs_0_ = bf16[1728,5120]{1,0:T(8,128)(2,1)} custom-call(bf16[1728,5120]{1,0:T(8,128)(2,1)} %shard_map.100.refs_0_, bf16[1728,640]{1,0:T(8,128)(2,1)S(1)} %get-tuple-element.69.refs_0_.refs_1_, bf16[1728,640]{1,0:T(8,128)(2,1)S(1)} %collective-permute-done.19.refs_1_.refs_2_, ...), custom_call_target="tpu_custom_call", output_to_operand_aliasing={{}: (0, {})} | custom-call | bytes 7208960 | tf_op jit(solution)/shard_map/pallas_call | solution.py:264
  137.0 1.9 %shard_map.102.refs_0_ = bf16[1728,5120]{1,0:T(8,128)(2,1)} custom-call(bf16[1728,5120]{1,0:T(8,128)(2,1)} %shard_map.101.refs_0_, bf16[1728,640]{1,0:T(8,128)(2,1)S(1)} %get-tuple-element.69.refs_0_.refs_1_, bf16[1728,640]{1,0:T(8,128)(2,1)S(1)} %collective-permute-done.19.refs_1_.refs_2_, ...), custom_call_target="tpu_custom_call", output_to_operand_aliasing={{}: (0, {})} | custom-call | bytes 6881280 | tf_op jit(solution)/shard_map/pallas_call | solution.py:264
  (97 shorter events, 43.1 us)
Async XLA Ops:
  28.1 14.6 %collective-permute-start.3 = (f32[336,640]{1,0:T(8,128)}, f32[336,640]{1,0:T(8,128)S(1)}, u32[]{:S(2)}, u32[]{:S(2)}) collective-permute-start(f32[336,640]{1,0:T(8,128)} %shard_map.93), channel_id=1, source_target_pairs={{0,8},{4,20},{8,0},{12,28},{16,24},{20,4},{24,16},{28,12},{1,9},{5... | collective-permute-start | bytes 2580488 | tf_op jit(solution)/shard_map/ppermute | solution.py:291
  46.3 8.9 %collective-permute-start.8 = (bf16[32,1728]{1,0:T(8,128)(2,1)S(1)}, bf16[32,1728]{1,0:T(8,128)(2,1)S(1)}, u32[]{:S(2)}, u32[]{:S(2)}) collective-permute-start(bf16[32,1728]{1,0:T(8,128)(2,1)S(1)} %get-tuple-element.60), channel_id=1, source_target_pairs={{0,20},{4,8},{8,28},{12,0},{16,4},{20,24},{24,12},{28,16},{1,21},{... | collective-permute-start | bytes 331784 | tf_op jit(solution)/shard_map/ppermute | solution.py:291
  67.4 8.5 %collective-permute-start.20 = (bf16[352,640]{1,0:T(8,128)(2,1)S(1)}, bf16[352,640]{1,0:T(8,128)(2,1)S(1)}, u32[]{:S(2)}, u32[]{:S(2)}) collective-permute-start(bf16[352,640]{1,0:T(8,128)(2,1)S(1)} %get-tuple-element.73), channel_id=1, source_target_pairs={{0,8},{4,20},{8,0},{12,28},{16,24},{20,4},{24,16},{28,12},{1,9},{5... | collective-permute-start | bytes 1351688 | tf_op jit(solution)/shard_map/ppermute | solution.py:291
  68.8 11.8 %collective-permute-start.18 = (bf16[352,640]{1,0:T(8,128)(2,1)S(1)}, bf16[352,640]{1,0:T(8,128)(2,1)S(1)}, u32[]{:S(2)}, u32[]{:S(2)}) collective-permute-start(bf16[352,640]{1,0:T(8,128)(2,1)S(1)} %get-tuple-element.78), channel_id=1, source_target_pairs={{0,8},{4,20},{8,0},{12,28},{16,24},{20,4},{24,16},{28,12},{1,9},{5... | collective-permute-start | bytes 1351688 | tf_op jit(solution)/shard_map/ppermute | solution.py:291
  75.8 9.7 %collective-permute-start.22 = (bf16[352,640]{1,0:T(8,128)(2,1)S(1)}, bf16[352,640]{1,0:T(8,128)(2,1)S(1)}, u32[]{:S(2)}, u32[]{:S(2)}) collective-permute-start(bf16[352,640]{1,0:T(8,128)(2,1)S(1)} %get-tuple-element.74), channel_id=1, source_target_pairs={{0,8},{4,20},{8,0},{12,28},{16,24},{20,4},{24,16},{28,12},{1,9},{5... | collective-permute-start | bytes 1351688 | tf_op jit(solution)/shard_map/ppermute | solution.py:291
  80.7 11.9 %collective-permute-start.29 = (bf16[352,640]{1,0:T(8,128)(2,1)S(1)}, bf16[352,640]{1,0:T(8,128)(2,1)S(1)}, u32[]{:S(2)}, u32[]{:S(2)}) collective-permute-start(bf16[352,640]{1,0:T(8,128)(2,1)S(1)} %collective-permute-done.18.refs_3_), channel_id=1, source_target_pairs={{0,4},{4,0},{8,12},{12,8},{16,20},{20,16},{24,28},{28,24},{1,5},{5... | collective-permute-start | bytes 1351688 | tf_op jit(solution)/shard_map/ppermute | solution.py:66
  80.7 11.9 %collective-permute-start.30 = (bf16[336,640]{1,0:T(8,128)(2,1)S(1)}, bf16[336,640]{1,0:T(8,128)(2,1)S(1)}, u32[]{:S(2)}, u32[]{:S(2)}) collective-permute-start(bf16[336,640]{1,0:T(8,128)(2,1)S(1)} %get-tuple-element.79), channel_id=1, source_target_pairs={{0,8},{4,20},{8,0},{12,28},{16,24},{20,4},{24,16},{28,12},{1,9},{5... | collective-permute-start | bytes 1290248 | tf_op jit(solution)/shard_map/ppermute | solution.py:291
  85.5 8.8 %collective-permute-start.23 = (bf16[352,640]{1,0:T(8,128)(2,1)S(1)}, bf16[352,640]{1,0:T(8,128)(2,1)S(1)}, u32[]{:S(2)}, u32[]{:S(2)}) collective-permute-start(bf16[352,640]{1,0:T(8,128)(2,1)S(1)} %get-tuple-element.73), channel_id=1, source_target_pairs={{0,16},{4,12},{8,24},{12,4},{16,0},{20,28},{24,8},{28,20},{1,17},{... | collective-permute-start | bytes 1351688 | tf_op jit(solution)/shard_map/ppermute | solution.py:291
  93.7 36.9 %collective-permute-start.19 = (bf16[1728,640]{1,0:T(8,128)(2,1)S(1)}, bf16[1728,640]{1,0:T(8,128)(2,1)S(1)}, u32[]{:S(2)}, u32[]{:S(2)}) collective-permute-start(bf16[1728,640]{1,0:T(8,128)(2,1)S(1)} %get-tuple-element.69.refs_0_.refs_1_), channel_id=1, source_target_pairs={{0,4},{4,0},{8,12},{12,8},{16,20},{20,16},{24,28},{28,24},{1,5},{5... | collective-permute-start | bytes 6635528 | tf_op jit(solution)/shard_map/ppermute | solution.py:66
  94.3 11.5 %collective-permute-start.26 = (bf16[352,640]{1,0:T(8,128)(2,1)S(1)}, bf16[352,640]{1,0:T(8,128)(2,1)S(1)}, u32[]{:S(2)}, u32[]{:S(2)}) collective-permute-start(bf16[352,640]{1,0:T(8,128)(2,1)S(1)} %get-tuple-element.74), channel_id=1, source_target_pairs={{0,16},{4,12},{8,24},{12,4},{16,0},{20,28},{24,8},{28,20},{1,17},{... | collective-permute-start | bytes 1351688 | tf_op jit(solution)/shard_map/ppermute | solution.py:291
  95.1 10.7 %collective-permute-start.24 = (bf16[352,640]{1,0:T(8,128)(2,1)S(1)}, bf16[352,640]{1,0:T(8,128)(2,1)S(1)}, u32[]{:S(2)}, u32[]{:S(2)}) collective-permute-start(bf16[352,640]{1,0:T(8,128)(2,1)S(1)} %collective-permute-done.23.refs_4_), channel_id=1, source_target_pairs={{0,4},{4,0},{8,12},{12,8},{16,20},{20,16},{24,28},{28,24},{1,5},{5... | collective-permute-start | bytes 1351688 | tf_op jit(solution)/shard_map/ppermute | solution.py:66
  100.9 9.4 %collective-permute-start.32 = (bf16[352,640]{1,0:T(8,128)(2,1)S(1)}, bf16[352,640]{1,0:T(8,128)(2,1)S(1)}, u32[]{:S(2)}, u32[]{:S(2)}) collective-permute-start(bf16[352,640]{1,0:T(8,128)(2,1)S(1)} %collective-permute-done.31.refs_5_), channel_id=1, source_target_pairs={{0,4},{4,0},{8,12},{12,8},{16,20},{20,16},{24,28},{28,24},{1,5},{5... | collective-permute-start | bytes 1351688 | tf_op jit(solution)/shard_map/ppermute | solution.py:66
  100.9 9.4 %collective-permute-start.34 = (bf16[336,640]{1,0:T(8,128)(2,1)S(1)}, bf16[336,640]{1,0:T(8,128)(2,1)S(1)}, u32[]{:S(2)}, u32[]{:S(2)}) collective-permute-start(bf16[336,640]{1,0:T(8,128)(2,1)S(1)} %get-tuple-element.79), channel_id=1, source_target_pairs={{0,16},{4,12},{8,24},{12,4},{16,0},{20,28},{24,8},{28,20},{1,17},{... | collective-permute-start | bytes 1290248 | tf_op jit(solution)/shard_map/ppermute | solution.py:291
  105.8 9.4 %collective-permute-start.27 = (bf16[352,640]{1,0:T(8,128)(2,1)S(1)}, bf16[352,640]{1,0:T(8,128)(2,1)S(1)}, u32[]{:S(2)}, u32[]{:S(2)}) collective-permute-start(bf16[352,640]{1,0:T(8,128)(2,1)S(1)} %collective-permute-done.20.refs_2_), channel_id=1, source_target_pairs={{0,16},{4,12},{8,24},{12,4},{16,0},{20,28},{24,8},{28,20},{1,17},{... | collective-permute-start | bytes 1351688 | tf_op jit(solution)/shard_map/ppermute | solution.py:291
  110.4 9.7 %collective-permute-start.35 = (bf16[352,640]{1,0:T(8,128)(2,1)S(1)}, bf16[352,640]{1,0:T(8,128)(2,1)S(1)}, u32[]{:S(2)}, u32[]{:S(2)}) collective-permute-start(bf16[352,640]{1,0:T(8,128)(2,1)S(1)} %collective-permute-done.18.refs_3_), channel_id=1, source_target_pairs={{0,16},{4,12},{8,24},{12,4},{16,0},{20,28},{24,8},{28,20},{1,17},{... | collective-permute-start | bytes 1351688 | tf_op jit(solution)/shard_map/ppermute | solution.py:291
  111.5 8.5 %collective-permute-start.40 = (bf16[336,640]{1,0:T(8,128)(2,1)S(1)}, bf16[336,640]{1,0:T(8,128)(2,1)S(1)}, u32[]{:S(2)}, u32[]{:S(2)}) collective-permute-start(bf16[336,640]{1,0:T(8,128)(2,1)S(1)} %collective-permute-done.34.refs_5_), channel_id=1, source_target_pairs={{0,4},{4,0},{8,12},{12,8},{16,20},{20,16},{24,28},{28,24},{1,5},{5... | collective-permute-start | bytes 1290248 | tf_op jit(solution)/shard_map/ppermute | solution.py:66
  115.2 9.7 %collective-permute-start.38 = (bf16[352,640]{1,0:T(8,128)(2,1)S(1)}, bf16[352,640]{1,0:T(8,128)(2,1)S(1)}, u32[]{:S(2)}, u32[]{:S(2)}) collective-permute-start(bf16[352,640]{1,0:T(8,128)(2,1)S(1)} %collective-permute-done.22.refs_3_), channel_id=1, source_target_pairs={{0,16},{4,12},{8,24},{12,4},{16,0},{20,28},{24,8},{28,20},{1,17},{... | collective-permute-start | bytes 1351688 | tf_op jit(solution)/shard_map/ppermute | solution.py:291
  116.4 8.9 %collective-permute-start.28 = (bf16[352,640]{1,0:T(8,128)(2,1)S(1)}, bf16[352,640]{1,0:T(8,128)(2,1)S(1)}, u32[]{:S(2)}, u32[]{:S(2)}) collective-permute-start(bf16[352,640]{1,0:T(8,128)(2,1)S(1)} %collective-permute-done.27.refs_6_), channel_id=1, source_target_pairs={{0,4},{4,0},{8,12},{12,8},{16,20},{20,16},{24,28},{28,24},{1,5},{5... | collective-permute-start | bytes 1351688 | tf_op jit(solution)/shard_map/ppermute | solution.py:66
  120.0 9.4 %collective-permute-start.36 = (bf16[352,640]{1,0:T(8,128)(2,1)S(1)}, bf16[352,640]{1,0:T(8,128)(2,1)S(1)}, u32[]{:S(2)}, u32[]{:S(2)}) collective-permute-start(bf16[352,640]{1,0:T(8,128)(2,1)S(1)} %collective-permute-done.35.refs_7_), channel_id=1, source_target_pairs={{0,4},{4,0},{8,12},{12,8},{16,20},{20,16},{24,28},{28,24},{1,5},{5... | collective-permute-start | bytes 1351688 | tf_op jit(solution)/shard_map/ppermute | solution.py:66
  120.0 9.4 %collective-permute-start.41 = (bf16[336,640]{1,0:T(8,128)(2,1)S(1)}, bf16[336,640]{1,0:T(8,128)(2,1)S(1)}, u32[]{:S(2)}, u32[]{:S(2)}) collective-permute-start(bf16[336,640]{1,0:T(8,128)(2,1)S(1)} %collective-permute-done.30.refs_3_), channel_id=1, source_target_pairs={{0,16},{4,12},{8,24},{12,4},{16,0},{20,28},{24,8},{28,20},{1,17},{... | collective-permute-start | bytes 1290248 | tf_op jit(solution)/shard_map/ppermute | solution.py:291
  124.9 10.1 %collective-permute-start.39 = (bf16[352,640]{1,0:T(8,128)(2,1)S(1)}, bf16[352,640]{1,0:T(8,128)(2,1)S(1)}, u32[]{:S(2)}, u32[]{:S(2)}) collective-permute-start(bf16[352,640]{1,0:T(8,128)(2,1)S(1)} %collective-permute-done.38.refs_7_), channel_id=1, source_target_pairs={{0,4},{4,0},{8,12},{12,8},{16,20},{20,16},{24,28},{28,24},{1,5},{5... | collective-permute-start | bytes 1351688 | tf_op jit(solution)/shard_map/ppermute | solution.py:66
  125.3 11.6 %collective-permute-start.44 = (bf16[336,640]{1,0:T(8,128)(2,1)S(1)}, bf16[336,640]{1,0:T(8,128)(2,1)S(1)}, u32[]{:S(2)}, u32[]{:S(2)}) collective-permute-start(bf16[336,640]{1,0:T(8,128)(2,1)S(1)} %get-tuple-element.84), channel_id=1, source_target_pairs={{0,16},{4,12},{8,24},{12,4},{16,0},{20,28},{24,8},{28,20},{1,17},{... | collective-permute-start | bytes 1290248 | tf_op jit(solution)/shard_map/ppermute | solution.py:291
  129.5 9.4 %collective-permute-start.46 = (bf16[336,640]{1,0:T(8,128)(2,1)S(1)}, bf16[336,640]{1,0:T(8,128)(2,1)S(1)}, u32[]{:S(2)}, u32[]{:S(2)}) collective-permute-start(bf16[336,640]{1,0:T(8,128)(2,1)S(1)} %shard_map.103.refs_3_), channel_id=1, source_target_pairs={{0,16},{4,12},{8,24},{12,4},{16,0},{20,28},{24,8},{28,20},{1,17},{... | collective-permute-start | bytes 1290248 | tf_op jit(solution)/shard_map/ppermute | solution.py:291
  130.6 8.8 %collective-permute-start.43 = (bf16[336,640]{1,0:T(8,128)(2,1)S(1)}, bf16[336,640]{1,0:T(8,128)(2,1)S(1)}, u32[]{:S(2)}, u32[]{:S(2)}) collective-permute-start(bf16[336,640]{1,0:T(8,128)(2,1)S(1)} %shard_map.103.refs_3_), channel_id=1, source_target_pairs={{0,4},{4,0},{8,12},{12,8},{16,20},{20,16},{24,28},{28,24},{1,5},{5... | collective-permute-start | bytes 1290248 | tf_op jit(solution)/shard_map/ppermute | solution.py:66
  (30 other events, 304.8 us)

commit v11 on v7

--- a/solution.py
+++ b/solution.py
@@ -233,46 +233,38 @@
     )(projection, master_t, tall)
 
 
-def lay_kernel(*refs, first, count, block, fresh):
+def lay_kernel(*refs, first, count, kinds, fresh):
     refs = refs if fresh else refs[1:]
-    pieces, out, (held, sems) = refs[:-3], refs[-3], refs[-2:]
-    copies = [None] * held.shape[0]
+    pieces, out, sems = refs[:-2], refs[-2], refs[-1]
     me = lax.axis_index("dp")
-    for at in range(0, count, block):
-        slot = at // block % len(copies)
-        size = min(block, count - at)
-        if copies[slot] is not None:
-            copies[slot].wait()
-        for masks, piece in zip(OWNER_MASKS, pieces):
-            width = piece.shape[1]
-            column = pl.multiple_of(other(me, masks) * width, 128)
-            origin = at if piece.shape[0] == count else first + at
-            held[slot, pl.ds(0, size), pl.ds(column, width)] = piece[pl.ds(origin, size), :]
-        copies[slot] = pltpu.make_async_copy(
-            held.at[slot, pl.ds(0, size), :], out.at[pl.ds(first + at, size), :], sems.at[slot]
-        )
-        copies[slot].start()
+    copies = []
+    for at, (kind, piece) in enumerate(zip(kinds, pieces)):
+        width = piece.shape[1]
+        column = pl.multiple_of(other(me, OWNER_MASKS[kind]) * width, 128)
+        part = piece if piece.shape[0] == count else piece.at[pl.ds(first, count), :]
+        target = out.at[pl.ds(first, count), pl.ds(column, width)]
+        copies.append(pltpu.make_async_copy(part, target, sems.at[at]))
     for copy in copies:
-        if copy is not None:
-            copy.wait()
-
-
-def lay(out, shape, span, pieces, block=96):
+        copy.start()
+    for copy in copies:
+        copy.wait()
+
+
+def lay(out, shape, span, kinds, pieces):
     fresh = out is None
     held = [] if fresh else [out]
     first, count = span
     return pl.pallas_call(
-        functools.partial(lay_kernel, first=first, count=count, block=block, fresh=fresh),
+        functools.partial(lay_kernel, first=first, count=count, kinds=kinds, fresh=fresh),
         out_shape=jax.ShapeDtypeStruct(shape, jnp.bfloat16),
         in_specs=[ANY] * len(held) + [VMEM] * len(pieces),
         out_specs=ANY,
-        scratch_shapes=[
-            pltpu.VMEM((4, block, shape[1]), jnp.bfloat16),
-            pltpu.SemaphoreType.DMA((4,)),
-        ],
+        scratch_shapes=[pltpu.SemaphoreType.DMA((len(pieces),))],
         input_output_aliases={} if fresh else {0: 0},
         compiler_params=pltpu.CompilerParams(vmem_limit_bytes=20 * 2**20),
-        cost_estimate=pl.CostEstimate(flops=0, bytes_accessed=4 * count * shape[1], transcendentals=0),
+        cost_estimate=pl.CostEstimate(
+            flops=0, bytes_accessed=4 * count * pieces[0].shape[1] * len(pieces), transcendentals=0
+        ),
     )(*held, *pieces)
 
 
@@ -358,7 +350,13 @@
             pieces = [whole, whole_c]
             for which in range(3):
                 pieces += [got[(which, at)], over[(which, at)]]
-            outs.append(lay(outs[-1], (cols, n_dp * slab_rows), spans[at], pieces))
+            kinds = tuple(range(len(pieces)))
+            shape = (cols, n_dp * slab_rows)
+            if step < len(steps) - 1:
+                outs.append(lay(outs[-1], shape, spans[at], kinds, pieces))
+            else:
+                outs.append(lay(outs[-1], shape, spans[at], kinds[:-1], pieces[:-1]))
+                outs.append(lay(outs[-1], shape, spans[at], kinds[-1:], pieces[-1:]))
     return (moment_one_new, moment_two_new, master_new.T, outs[-1].T)
 
 

time: 118 us -> 122 us (1.034)
  waiting for transfers between devices: 58.8 us -> 63.1 us
    ppermute x22, waiting for transfers between devices: 46 us -> 50.5 us  [turn(): lax.ppermute(value, 'dp', [(i, i ^ masks[i & 1]) for i in range(n_dp)])]
    pallas_call x5 -> x6, Pallas kernels: 9.53 us -> 9.91 us  [lay(): pl.pallas_call(functools.partial(lay_kernel, first=first, count=count, ki...]
  transfers between devices with their start and end apart: 48 -> 48, of which waited for: 24 -> 26; matrix products, arithmetic and copies ran while one was open for 0% -> 0% of each run, Pallas kernels for 12% -> 13%
where the time goes in v11:
time: 122 us
  waiting for transfers between devices  63.1 us (52%)
  starting transfers between devices  36.5 us (30%)
  Pallas kernels  20.5 us (17%)
    ppermute x22, waiting for transfers between devices, turn(): lax.ppermute(value, 'dp', [(i, i ^ masks[i & 1]) for i in range(n_dp)])  50.5 us
    ppermute x22, starting transfers between devices, turn(): lax.ppermute(value, 'dp', [(i, i ^ masks[i & 1]) for i in range(n_dp)])  26.3 us
    ppermute x26, waiting for transfers between devices, send(): return lax.ppermute(value, axis, [(i, i ^ mask) for i in range(size)])  12.6 us
    ppermute x26, starting transfers between devices, send(): return lax.ppermute(value, axis, [(i, i ^ mask) for i in range(size)])  10.3 us
    pallas_call x6, Pallas kernels, lay(): pl.pallas_call(functools.partial(lay_kernel, first=first, count=count, ki...  9.91 us
    pallas_call x1, Pallas kernels, new_master(): pl.pallas_call(master_kernel, out_shape=jax.ShapeDtypeStruct((cols, slab_...  3.12 us
    pallas_call x2, Pallas kernels, weights(): pl.pallas_call(functools.partial(weight_kernel, n_in=len(pieces), spans=s...  3.03 us
  transfers between devices with their start and end apart: 48, of which 26 were waited for; matrix products, arithmetic and copies ran while one was open for 0% of the time, Pallas kernels for 13%

profile of v11, /device:TPU:0, one launch (start us, length us, event | category | flops | bytes accessed | tf_op | source)
XLA Modules:
  0.0 121.5 jit_solution(1941904372335448104)
XLA Ops:
  0.7 2.4 %shard_map.93 = f32[336,640]{1,0:T(8,128)} custom-call(f32[1728,640]{1,0:T(8,128)} %bitcast.6), custom_call_target="tpu_custom_call" | custom-call | tf_op jit(solution)/shard_map/pallas_call | solution.py:86
  3.1 3.0 %collective-permute-start.3 = (f32[336,640]{1,0:T(8,128)}, f32[336,640]{1,0:T(8,128)S(1)}, u32[]{:S(2)}, u32[]{:S(2)}) collective-permute-start(f32[336,640]{1,0:T(8,128)} %shard_map.93), channel_id=1, source_target_pairs={{0,8},{4,20},{8,0},{12,28},{16,24},{20,4},{24,16},{28,12},{1,9},{5... | collective-permute-start | bytes 2580488 | tf_op jit(solution)/shard_map/ppermute | solution.py:283
  8.2 2.6 %collective-permute-start.1 = (bf16[128,256]{1,0:T(8,128)(2,1)S(1)}, bf16[128,256]{1,0:T(8,128)(2,1)S(1)}, u32[]{:S(2)}, u32[]{:S(2)}) collective-permute-start(bf16[128,256]{1,0:T(8,128)(2,1)S(1)} %convolution_convert_fusion.refs_0_), channel_id=1, source_target_pairs={{0,2},{1,3},{2,0},{3,1},{4,6},{5,7},{6,4},{7,5},{8,10},{9,11},{10,... | collective-permute-start | bytes 196616 | tf_op jit(solution)/shard_map/ppermute | solution.py:66
  11.0 4.2 %collective-permute-done.1.refs_2_ = bf16[128,256]{1,0:T(8,128)(2,1)S(1)} collective-permute-done((bf16[128,256]{1,0:T(8,128)(2,1)S(1)}, bf16[128,256]{1,0:T(8,128)(2,1)S(1)}, u32[]{:S(2)}, u32[]{:S(2)}) %collective-permute-start.1) | collective-permute-done | bytes 65568 | tf_op jit(solution)/shard_map/ppermute | solution.py:66
  21.3 2.5 %collective-permute-start.8 = (bf16[32,1728]{1,0:T(8,128)(2,1)S(1)}, bf16[32,1728]{1,0:T(8,128)(2,1)S(1)}, u32[]{:S(2)}, u32[]{:S(2)}) collective-permute-start(bf16[32,1728]{1,0:T(8,128)(2,1)S(1)} %get-tuple-element.60), channel_id=1, source_target_pairs={{0,20},{4,8},{8,28},{12,0},{16,4},{20,24},{24,12},{28,16},{1,21},{... | collective-permute-start | bytes 331784 | tf_op jit(solution)/shard_map/ppermute | solution.py:283
  27.6 2.5 %collective-permute-done.8.refs_5_ = bf16[32,1728]{1,0:T(8,128)(2,1)S(1)} collective-permute-done((bf16[32,1728]{1,0:T(8,128)(2,1)S(1)}, bf16[32,1728]{1,0:T(8,128)(2,1)S(1)}, u32[]{:S(2)}, u32[]{:S(2)}) %collective-permute-start.8) | collective-permute-done | bytes 110624 | tf_op jit(solution)/shard_map/ppermute | solution.py:283
  35.6 2.5 %collective-permute-done.12.refs_2_ = bf16[32,1792]{1,0:T(8,128)(2,1)S(1)} collective-permute-done((bf16[32,1792]{1,0:T(8,128)(2,1)S(1)}, bf16[32,1792]{1,0:T(8,128)(2,1)S(1)}, u32[]{:S(2)}, u32[]{:S(2)}) %collective-permute-start.12) | collective-permute-done | bytes 114720 | tf_op jit(solution)/shard_map/ppermute | solution.py:66
  38.1 2.0 %collective-permute-done.14.refs_4_ = bf16[32,1792]{1,0:T(8,128)(2,1)S(1)} collective-permute-done((bf16[32,1792]{1,0:T(8,128)(2,1)S(1)}, bf16[32,1792]{1,0:T(8,128)(2,1)S(1)}, u32[]{:S(2)}, u32[]{:S(2)}) %collective-permute-start.14) | collective-permute-done | bytes 114720 | tf_op jit(solution)/shard_map/ppermute | solution.py:66
  44.5 3.1 %shard_map.97 = f32[1728,640]{1,0:T(8,128)} custom-call(bf16[5120,256]{1,0:T(8,128)(2,1)S(1)} %copy-done.2, f32[1728,640]{1,0:T(8,128)S(1)} %bitcast.8, bf16[1792,256]{1,0:T(8,128)(2,1)S(1)} %get-tuple-element.66.tall.refs_0_), custom_call_target="tpu_custom_call" | custom-call | flops 566231040 | bytes 8847360 | tf_op jit(solution)/shard_map/pallas_call | solution.py:219
  47.6 2.2 %shard_map.98 = (bf16[352,640]{1,0:T(8,128)(2,1)S(1)}, bf16[336,640]{1,0:T(8,128)(2,1)S(1)}, bf16[336,640]{1,0:T(8,128)(2,1)S(1)}, bf16[1728,640]{1,0:T(8,128)(2,1)S(1)}) custom-call(bf16[5120,256]{1,0:T(8,128)(2,1)S(1)} %copy-done.2, f32[1728,640]{1,0:T(8,128)S(1)} %bitcast.9, bf16[1792,256]{1,0:T(8,128)(2,1)S(1)} %get-tuple-element.66.tall.refs_0_), custom_call_target="tpu_custom_call" | custom-call | flops 901775360 | bytes 7045120 | tf_op jit(solution)/shard_map/pallas_call | solution.py:167
  52.2 3.4 %collective-permute-done.18.refs_3_ = bf16[352,640]{1,0:T(8,128)(2,1)S(1)} collective-permute-done((bf16[352,640]{1,0:T(8,128)(2,1)S(1)}, bf16[352,640]{1,0:T(8,128)(2,1)S(1)}, u32[]{:S(2)}, u32[]{:S(2)}) %collective-permute-start.18) | collective-permute-done | bytes 450592 | tf_op jit(solution)/shard_map/ppermute | solution.py:283
  57.1 3.4 %collective-permute-done.22.refs_3_ = bf16[352,640]{1,0:T(8,128)(2,1)S(1)} collective-permute-done((bf16[352,640]{1,0:T(8,128)(2,1)S(1)}, bf16[352,640]{1,0:T(8,128)(2,1)S(1)}, u32[]{:S(2)}, u32[]{:S(2)}) %collective-permute-start.22) | collective-permute-done | bytes 450592 | tf_op jit(solution)/shard_map/ppermute | solution.py:283
  61.4 6.1 %collective-permute-done.30.refs_3_ = bf16[336,640]{1,0:T(8,128)(2,1)S(1)} collective-permute-done((bf16[336,640]{1,0:T(8,128)(2,1)S(1)}, bf16[336,640]{1,0:T(8,128)(2,1)S(1)}, u32[]{:S(2)}, u32[]{:S(2)}) %collective-permute-start.30) | collective-permute-done | bytes 430112 | tf_op jit(solution)/shard_map/ppermute | solution.py:283
  70.9 5.1 %collective-permute-done.31.refs_5_ = bf16[352,640]{1,0:T(8,128)(2,1)S(1)} collective-permute-done((bf16[352,640]{1,0:T(8,128)(2,1)S(1)}, bf16[352,640]{1,0:T(8,128)(2,1)S(1)}, u32[]{:S(2)}, u32[]{:S(2)}) %collective-permute-start.31) | collective-permute-done | bytes 450592 | tf_op jit(solution)/shard_map/ppermute | solution.py:283
  77.1 3.7 %collective-permute-done.26.refs_5_ = bf16[352,640]{1,0:T(8,128)(2,1)S(1)} collective-permute-done((bf16[352,640]{1,0:T(8,128)(2,1)S(1)}, bf16[352,640]{1,0:T(8,128)(2,1)S(1)}, u32[]{:S(2)}, u32[]{:S(2)}) %collective-permute-start.26) | collective-permute-done | bytes 450592 | tf_op jit(solution)/shard_map/ppermute | solution.py:283
  81.9 3.5 %collective-permute-done.34.refs_5_ = bf16[336,640]{1,0:T(8,128)(2,1)S(1)} collective-permute-done((bf16[336,640]{1,0:T(8,128)(2,1)S(1)}, bf16[336,640]{1,0:T(8,128)(2,1)S(1)}, u32[]{:S(2)}, u32[]{:S(2)}) %collective-permute-start.34) | collective-permute-done | bytes 430112 | tf_op jit(solution)/shard_map/ppermute | solution.py:283
  86.5 3.7 %collective-permute-done.27.refs_6_ = bf16[352,640]{1,0:T(8,128)(2,1)S(1)} collective-permute-done((bf16[352,640]{1,0:T(8,128)(2,1)S(1)}, bf16[352,640]{1,0:T(8,128)(2,1)S(1)}, u32[]{:S(2)}, u32[]{:S(2)}) %collective-permute-start.27) | collective-permute-done | bytes 450592 | tf_op jit(solution)/shard_map/ppermute | solution.py:283
  91.4 3.7 %collective-permute-done.35.refs_7_ = bf16[352,640]{1,0:T(8,128)(2,1)S(1)} collective-permute-done((bf16[352,640]{1,0:T(8,128)(2,1)S(1)}, bf16[352,640]{1,0:T(8,128)(2,1)S(1)}, u32[]{:S(2)}, u32[]{:S(2)}) %collective-permute-start.35) | collective-permute-done | bytes 450592 | tf_op jit(solution)/shard_map/ppermute | solution.py:283
  96.2 3.7 %collective-permute-done.38.refs_7_ = bf16[352,640]{1,0:T(8,128)(2,1)S(1)} collective-permute-done((bf16[352,640]{1,0:T(8,128)(2,1)S(1)}, bf16[352,640]{1,0:T(8,128)(2,1)S(1)}, u32[]{:S(2)}, u32[]{:S(2)}) %collective-permute-start.38) | collective-permute-done | bytes 450592 | tf_op jit(solution)/shard_map/ppermute | solution.py:283
  100.3 4.2 %collective-permute-done.41.refs_7_ = bf16[336,640]{1,0:T(8,128)(2,1)S(1)} collective-permute-done((bf16[336,640]{1,0:T(8,128)(2,1)S(1)}, bf16[336,640]{1,0:T(8,128)(2,1)S(1)}, u32[]{:S(2)}, u32[]{:S(2)}) %collective-permute-start.41) | collective-permute-done | bytes 430112 | tf_op jit(solution)/shard_map/ppermute | solution.py:283
  106.5 1.9 %shard_map.99.refs_0_ = bf16[1728,5120]{1,0:T(8,128)(2,1)} custom-call(bf16[1728,640]{1,0:T(8,128)(2,1)S(1)} %get-tuple-element.69.refs_0_.refs_1_, bf16[1728,640]{1,0:T(8,128)(2,1)S(1)} %collective-permute-done.19.refs_1_.refs_2_, bf16[352,640]{1,0:T(8,128)(2,1)S(1)} %collective-permute-done.20.refs_2_, ...), custom_call_target="tpu_custom_call" | custom-call | bytes 7208960 | tf_op jit(solution)/shard_map/pallas_call | solution.py:257
  108.4 1.9 %shard_map.100.refs_0_ = bf16[1728,5120]{1,0:T(8,128)(2,1)} custom-call(bf16[1728,5120]{1,0:T(8,128)(2,1)} %shard_map.99.refs_0_, bf16[1728,640]{1,0:T(8,128)(2,1)S(1)} %get-tuple-element.69.refs_0_.refs_1_, bf16[1728,640]{1,0:T(8,128)(2,1)S(1)} %collective-permute-done.19.refs_1_.refs_2_, ...), custom_call_target="tpu_custom_call", output_to_operand_aliasing={{}: (0, {})} | custom-call | bytes 7208960 | tf_op jit(solution)/shard_map/pallas_call | solution.py:257
  110.3 1.9 %shard_map.101.refs_0_ = bf16[1728,5120]{1,0:T(8,128)(2,1)} custom-call(bf16[1728,5120]{1,0:T(8,128)(2,1)} %shard_map.100.refs_0_, bf16[1728,640]{1,0:T(8,128)(2,1)S(1)} %get-tuple-element.69.refs_0_.refs_1_, bf16[1728,640]{1,0:T(8,128)(2,1)S(1)} %collective-permute-done.19.refs_1_.refs_2_, ...), custom_call_target="tpu_custom_call", output_to_operand_aliasing={{}: (0, {})} | custom-call | bytes 7208960 | tf_op jit(solution)/shard_map/pallas_call | solution.py:257
  114.5 2.8 %collective-permute-done.46.refs_7_ = bf16[336,640]{1,0:T(8,128)(2,1)S(1)} collective-permute-done((bf16[336,640]{1,0:T(8,128)(2,1)S(1)}, bf16[336,640]{1,0:T(8,128)(2,1)S(1)}, u32[]{:S(2)}, u32[]{:S(2)}) %collective-permute-start.46) | collective-permute-done | bytes 430112 | tf_op jit(solution)/shard_map/ppermute | solution.py:283
  (98 shorter events, 44.7 us)
Async XLA Ops:
  3.1 14.6 %collective-permute-start.3 = (f32[336,640]{1,0:T(8,128)}, f32[336,640]{1,0:T(8,128)S(1)}, u32[]{:S(2)}, u32[]{:S(2)}) collective-permute-start(f32[336,640]{1,0:T(8,128)} %shard_map.93), channel_id=1, source_target_pairs={{0,8},{4,20},{8,0},{12,28},{16,24},{20,4},{24,16},{28,12},{1,9},{5... | collective-permute-start | bytes 2580488 | tf_op jit(solution)/shard_map/ppermute | solution.py:283
  21.3 8.9 %collective-permute-start.8 = (bf16[32,1728]{1,0:T(8,128)(2,1)S(1)}, bf16[32,1728]{1,0:T(8,128)(2,1)S(1)}, u32[]{:S(2)}, u32[]{:S(2)}) collective-permute-start(bf16[32,1728]{1,0:T(8,128)(2,1)S(1)} %get-tuple-element.60), channel_id=1, source_target_pairs={{0,20},{4,8},{8,28},{12,0},{16,4},{20,24},{24,12},{28,16},{1,21},{... | collective-permute-start | bytes 331784 | tf_op jit(solution)/shard_map/ppermute | solution.py:283
  42.4 8.5 %collective-permute-start.20 = (bf16[352,640]{1,0:T(8,128)(2,1)S(1)}, bf16[352,640]{1,0:T(8,128)(2,1)S(1)}, u32[]{:S(2)}, u32[]{:S(2)}) collective-permute-start(bf16[352,640]{1,0:T(8,128)(2,1)S(1)} %get-tuple-element.73), channel_id=1, source_target_pairs={{0,8},{4,20},{8,0},{12,28},{16,24},{20,4},{24,16},{28,12},{1,9},{5... | collective-permute-start | bytes 1351688 | tf_op jit(solution)/shard_map/ppermute | solution.py:283
  43.8 11.8 %collective-permute-start.18 = (bf16[352,640]{1,0:T(8,128)(2,1)S(1)}, bf16[352,640]{1,0:T(8,128)(2,1)S(1)}, u32[]{:S(2)}, u32[]{:S(2)}) collective-permute-start(bf16[352,640]{1,0:T(8,128)(2,1)S(1)} %get-tuple-element.78), channel_id=1, source_target_pairs={{0,8},{4,20},{8,0},{12,28},{16,24},{20,4},{24,16},{28,12},{1,9},{5... | collective-permute-start | bytes 1351688 | tf_op jit(solution)/shard_map/ppermute | solution.py:283
  50.9 9.7 %collective-permute-start.22 = (bf16[352,640]{1,0:T(8,128)(2,1)S(1)}, bf16[352,640]{1,0:T(8,128)(2,1)S(1)}, u32[]{:S(2)}, u32[]{:S(2)}) collective-permute-start(bf16[352,640]{1,0:T(8,128)(2,1)S(1)} %get-tuple-element.74), channel_id=1, source_target_pairs={{0,8},{4,20},{8,0},{12,28},{16,24},{20,4},{24,16},{28,12},{1,9},{5... | collective-permute-start | bytes 1351688 | tf_op jit(solution)/shard_map/ppermute | solution.py:283
  55.7 11.9 %collective-permute-start.29 = (bf16[352,640]{1,0:T(8,128)(2,1)S(1)}, bf16[352,640]{1,0:T(8,128)(2,1)S(1)}, u32[]{:S(2)}, u32[]{:S(2)}) collective-permute-start(bf16[352,640]{1,0:T(8,128)(2,1)S(1)} %collective-permute-done.18.refs_3_), channel_id=1, source_target_pairs={{0,4},{4,0},{8,12},{12,8},{16,20},{20,16},{24,28},{28,24},{1,5},{5... | collective-permute-start | bytes 1351688 | tf_op jit(solution)/shard_map/ppermute | solution.py:66
  55.7 11.9 %collective-permute-start.30 = (bf16[336,640]{1,0:T(8,128)(2,1)S(1)}, bf16[336,640]{1,0:T(8,128)(2,1)S(1)}, u32[]{:S(2)}, u32[]{:S(2)}) collective-permute-start(bf16[336,640]{1,0:T(8,128)(2,1)S(1)} %get-tuple-element.79), channel_id=1, source_target_pairs={{0,8},{4,20},{8,0},{12,28},{16,24},{20,4},{24,16},{28,12},{1,9},{5... | collective-permute-start | bytes 1290248 | tf_op jit(solution)/shard_map/ppermute | solution.py:283
  60.5 8.8 %collective-permute-start.23 = (bf16[352,640]{1,0:T(8,128)(2,1)S(1)}, bf16[352,640]{1,0:T(8,128)(2,1)S(1)}, u32[]{:S(2)}, u32[]{:S(2)}) collective-permute-start(bf16[352,640]{1,0:T(8,128)(2,1)S(1)} %get-tuple-element.73), channel_id=1, source_target_pairs={{0,16},{4,12},{8,24},{12,4},{16,0},{20,28},{24,8},{28,20},{1,17},{... | collective-permute-start | bytes 1351688 | tf_op jit(solution)/shard_map/ppermute | solution.py:283
  67.6 8.4 %collective-permute-start.31 = (bf16[352,640]{1,0:T(8,128)(2,1)S(1)}, bf16[352,640]{1,0:T(8,128)(2,1)S(1)}, u32[]{:S(2)}, u32[]{:S(2)}) collective-permute-start(bf16[352,640]{1,0:T(8,128)(2,1)S(1)} %get-tuple-element.78), channel_id=1, source_target_pairs={{0,16},{4,12},{8,24},{12,4},{16,0},{20,28},{24,8},{28,20},{1,17},{... | collective-permute-start | bytes 1351688 | tf_op jit(solution)/shard_map/ppermute | solution.py:283
  68.7 37.8 %collective-permute-start.19 = (bf16[1728,640]{1,0:T(8,128)(2,1)S(1)}, bf16[1728,640]{1,0:T(8,128)(2,1)S(1)}, u32[]{:S(2)}, u32[]{:S(2)}) collective-permute-start(bf16[1728,640]{1,0:T(8,128)(2,1)S(1)} %get-tuple-element.69.refs_0_.refs_1_), channel_id=1, source_target_pairs={{0,4},{4,0},{8,12},{12,8},{16,20},{20,16},{24,28},{28,24},{1,5},{5... | collective-permute-start | bytes 6635528 | tf_op jit(solution)/shard_map/ppermute | solution.py:66
  69.3 11.5 %collective-permute-start.26 = (bf16[352,640]{1,0:T(8,128)(2,1)S(1)}, bf16[352,640]{1,0:T(8,128)(2,1)S(1)}, u32[]{:S(2)}, u32[]{:S(2)}) collective-permute-start(bf16[352,640]{1,0:T(8,128)(2,1)S(1)} %get-tuple-element.74), channel_id=1, source_target_pairs={{0,16},{4,12},{8,24},{12,4},{16,0},{20,28},{24,8},{28,20},{1,17},{... | collective-permute-start | bytes 1351688 | tf_op jit(solution)/shard_map/ppermute | solution.py:283
  70.1 10.7 %collective-permute-start.24 = (bf16[352,640]{1,0:T(8,128)(2,1)S(1)}, bf16[352,640]{1,0:T(8,128)(2,1)S(1)}, u32[]{:S(2)}, u32[]{:S(2)}) collective-permute-start(bf16[352,640]{1,0:T(8,128)(2,1)S(1)} %collective-permute-done.23.refs_4_), channel_id=1, source_target_pairs={{0,4},{4,0},{8,12},{12,8},{16,20},{20,16},{24,28},{28,24},{1,5},{5... | collective-permute-start | bytes 1351688 | tf_op jit(solution)/shard_map/ppermute | solution.py:66
  76.0 9.4 %collective-permute-start.32 = (bf16[352,640]{1,0:T(8,128)(2,1)S(1)}, bf16[352,640]{1,0:T(8,128)(2,1)S(1)}, u32[]{:S(2)}, u32[]{:S(2)}) collective-permute-start(bf16[352,640]{1,0:T(8,128)(2,1)S(1)} %collective-permute-done.31.refs_5_), channel_id=1, source_target_pairs={{0,4},{4,0},{8,12},{12,8},{16,20},{20,16},{24,28},{28,24},{1,5},{5... | collective-permute-start | bytes 1351688 | tf_op jit(solution)/shard_map/ppermute | solution.py:66
  76.0 9.4 %collective-permute-start.34 = (bf16[336,640]{1,0:T(8,128)(2,1)S(1)}, bf16[336,640]{1,0:T(8,128)(2,1)S(1)}, u32[]{:S(2)}, u32[]{:S(2)}) collective-permute-start(bf16[336,640]{1,0:T(8,128)(2,1)S(1)} %get-tuple-element.79), channel_id=1, source_target_pairs={{0,16},{4,12},{8,24},{12,4},{16,0},{20,28},{24,8},{28,20},{1,17},{... | collective-permute-start | bytes 1290248 | tf_op jit(solution)/shard_map/ppermute | solution.py:283
  80.8 9.4 %collective-permute-start.27 = (bf16[352,640]{1,0:T(8,128)(2,1)S(1)}, bf16[352,640]{1,0:T(8,128)(2,1)S(1)}, u32[]{:S(2)}, u32[]{:S(2)}) collective-permute-start(bf16[352,640]{1,0:T(8,128)(2,1)S(1)} %collective-permute-done.20.refs_2_), channel_id=1, source_target_pairs={{0,16},{4,12},{8,24},{12,4},{16,0},{20,28},{24,8},{28,20},{1,17},{... | collective-permute-start | bytes 1351688 | tf_op jit(solution)/shard_map/ppermute | solution.py:283
  85.4 9.7 %collective-permute-start.35 = (bf16[352,640]{1,0:T(8,128)(2,1)S(1)}, bf16[352,640]{1,0:T(8,128)(2,1)S(1)}, u32[]{:S(2)}, u32[]{:S(2)}) collective-permute-start(bf16[352,640]{1,0:T(8,128)(2,1)S(1)} %collective-permute-done.18.refs_3_), channel_id=1, source_target_pairs={{0,16},{4,12},{8,24},{12,4},{16,0},{20,28},{24,8},{28,20},{1,17},{... | collective-permute-start | bytes 1351688 | tf_op jit(solution)/shard_map/ppermute | solution.py:283
  86.5 8.5 %collective-permute-start.40 = (bf16[336,640]{1,0:T(8,128)(2,1)S(1)}, bf16[336,640]{1,0:T(8,128)(2,1)S(1)}, u32[]{:S(2)}, u32[]{:S(2)}) collective-permute-start(bf16[336,640]{1,0:T(8,128)(2,1)S(1)} %collective-permute-done.34.refs_5_), channel_id=1, source_target_pairs={{0,4},{4,0},{8,12},{12,8},{16,20},{20,16},{24,28},{28,24},{1,5},{5... | collective-permute-start | bytes 1290248 | tf_op jit(solution)/shard_map/ppermute | solution.py:66
  90.2 9.7 %collective-permute-start.38 = (bf16[352,640]{1,0:T(8,128)(2,1)S(1)}, bf16[352,640]{1,0:T(8,128)(2,1)S(1)}, u32[]{:S(2)}, u32[]{:S(2)}) collective-permute-start(bf16[352,640]{1,0:T(8,128)(2,1)S(1)} %collective-permute-done.22.refs_3_), channel_id=1, source_target_pairs={{0,16},{4,12},{8,24},{12,4},{16,0},{20,28},{24,8},{28,20},{1,17},{... | collective-permute-start | bytes 1351688 | tf_op jit(solution)/shard_map/ppermute | solution.py:283
  91.4 13.1 %collective-permute-start.28 = (bf16[352,640]{1,0:T(8,128)(2,1)S(1)}, bf16[352,640]{1,0:T(8,128)(2,1)S(1)}, u32[]{:S(2)}, u32[]{:S(2)}) collective-permute-start(bf16[352,640]{1,0:T(8,128)(2,1)S(1)} %collective-permute-done.27.refs_6_), channel_id=1, source_target_pairs={{0,4},{4,0},{8,12},{12,8},{16,20},{20,16},{24,28},{28,24},{1,5},{5... | collective-permute-start | bytes 1351688 | tf_op jit(solution)/shard_map/ppermute | solution.py:66
  95.0 10.6 %collective-permute-start.36 = (bf16[352,640]{1,0:T(8,128)(2,1)S(1)}, bf16[352,640]{1,0:T(8,128)(2,1)S(1)}, u32[]{:S(2)}, u32[]{:S(2)}) collective-permute-start(bf16[352,640]{1,0:T(8,128)(2,1)S(1)} %collective-permute-done.35.refs_7_), channel_id=1, source_target_pairs={{0,4},{4,0},{8,12},{12,8},{16,20},{20,16},{24,28},{28,24},{1,5},{5... | collective-permute-start | bytes 1351688 | tf_op jit(solution)/shard_map/ppermute | solution.py:66
  95.1 9.4 %collective-permute-start.41 = (bf16[336,640]{1,0:T(8,128)(2,1)S(1)}, bf16[336,640]{1,0:T(8,128)(2,1)S(1)}, u32[]{:S(2)}, u32[]{:S(2)}) collective-permute-start(bf16[336,640]{1,0:T(8,128)(2,1)S(1)} %collective-permute-done.30.refs_3_), channel_id=1, source_target_pairs={{0,16},{4,12},{8,24},{12,4},{16,0},{20,28},{24,8},{28,20},{1,17},{... | collective-permute-start | bytes 1290248 | tf_op jit(solution)/shard_map/ppermute | solution.py:283
  99.9 10.4 %collective-permute-start.39 = (bf16[352,640]{1,0:T(8,128)(2,1)S(1)}, bf16[352,640]{1,0:T(8,128)(2,1)S(1)}, u32[]{:S(2)}, u32[]{:S(2)}) collective-permute-start(bf16[352,640]{1,0:T(8,128)(2,1)S(1)} %collective-permute-done.38.refs_7_), channel_id=1, source_target_pairs={{0,4},{4,0},{8,12},{12,8},{16,20},{20,16},{24,28},{28,24},{1,5},{5... | collective-permute-start | bytes 1351688 | tf_op jit(solution)/shard_map/ppermute | solution.py:66
  105.6 11.7 %collective-permute-start.46 = (bf16[336,640]{1,0:T(8,128)(2,1)S(1)}, bf16[336,640]{1,0:T(8,128)(2,1)S(1)}, u32[]{:S(2)}, u32[]{:S(2)}) collective-permute-start(bf16[336,640]{1,0:T(8,128)(2,1)S(1)} %shard_map.103.refs_3_), channel_id=1, source_target_pairs={{0,16},{4,12},{8,24},{12,4},{16,0},{20,28},{24,8},{28,20},{1,17},{... | collective-permute-start | bytes 1290248 | tf_op jit(solution)/shard_map/ppermute | solution.py:283
  106.5 11.3 %collective-permute-start.43 = (bf16[336,640]{1,0:T(8,128)(2,1)S(1)}, bf16[336,640]{1,0:T(8,128)(2,1)S(1)}, u32[]{:S(2)}, u32[]{:S(2)}) collective-permute-start(bf16[336,640]{1,0:T(8,128)(2,1)S(1)} %shard_map.103.refs_3_), channel_id=1, source_target_pairs={{0,4},{4,0},{8,12},{12,8},{16,20},{20,16},{24,28},{28,24},{1,5},{5... | collective-permute-start | bytes 1290248 | tf_op jit(solution)/shard_map/ppermute | solution.py:66
  (30 other events, 256.0 us)

commit v12 on v11

--- a/solution.py
+++ b/solution.py
@@ -233,12 +233,13 @@
     )(projection, master_t, tall)
 
 
-def lay_kernel(*refs, first, count, kinds, fresh):
+def lay_kernel(*refs, places, fresh):
     refs = refs if fresh else refs[1:]
     pieces, out, sems = refs[:-2], refs[-2], refs[-1]
     me = lax.axis_index("dp")
     copies = []
-    for at, (kind, piece) in enumerate(zip(kinds, pieces)):
+    for at, (index, first, count, kind) in enumerate(places):
+        piece = pieces[index]
         width = piece.shape[1]
         column = pl.multiple_of(other(me, OWNER_MASKS[kind]) * width, 128)
         part = piece if piece.shape[0] == count else piece.at[pl.ds(first, count), :]
@@ -250,21 +251,26 @@
         copy.wait()
 
 
-def lay(out, shape, span, kinds, pieces):
+def lay(out, shape, parts):
     fresh = out is None
     held = [] if fresh else [out]
-    first, count = span
-    return pl.pallas_call(
-        functools.partial(lay_kernel, first=first, count=count, kinds=kinds, fresh=fresh),
+    pieces = []
+    places = []
+    for first, count, kind, piece in parts:
+        known = [at for at, other_piece in enumerate(pieces) if other_piece is piece]
+        if not known:
+            pieces.append(piece)
+        places.append((known[0] if known else len(pieces) - 1, first, count, kind))
+    size = sum(count for _, _, count, _ in places) * pieces[0].shape[1]
+    return pl.pallas_call(
+        functools.partial(lay_kernel, places=tuple(places), fresh=fresh),
         out_shape=jax.ShapeDtypeStruct(shape, jnp.bfloat16),
         in_specs=[ANY] * len(held) + [VMEM] * len(pieces),
         out_specs=ANY,
-        scratch_shapes=[pltpu.SemaphoreType.DMA((len(pieces),))],
+        scratch_shapes=[pltpu.SemaphoreType.DMA((len(places),))],
         input_output_aliases={} if fresh else {0: 0},
         compiler_params=pltpu.CompilerParams(vmem_limit_bytes=20 * 2**20),
-        cost_estimate=pl.CostEstimate(
-            flops=0, bytes_accessed=4 * count * pieces[0].shape[1] * len(pieces), transcendentals=0
-        ),
+        cost_estimate=pl.CostEstimate(flops=0, bytes_accessed=4 * size, transcendentals=0),
     )(*held, *pieces)
 
 
@@ -335,6 +341,14 @@
     later = range(1, len(counts))
     steps = [(phase, at) for phase in range(3) for at in later] + [(1, 0), (2, 0)]
     outs = [None]
+    shape = (cols, n_dp * slab_rows)
+
+    def parts_of(at):
+        pieces = [whole, whole_c]
+        for which in range(3):
+            pieces += [got[(which, at)], over[(which, at)]]
+        return [(*spans[at], kind, piece) for kind, piece in enumerate(pieces)]
+
     for step, (phase, at) in enumerate(steps):
         value = got[(0, at)] if phase == 2 else own[at]
         earlier = [got[steps[step - 2]]] if step >= 2 else []
@@ -342,21 +356,15 @@
         if step == 2:
             earlier.append(master_new)
         got[(phase, at)] = turn(after(value, earlier), TURN_MASKS[min(phase, 1)])
-        held = [outs[len(counts) + step - len(steps)]] if step >= len(steps) - 2 else []
+        held = [outs[step - len(steps) + 3]] if step >= len(steps) - 2 else []
         over[(phase, at)] = hop(after(got[(phase, at)], held), 1)
         if step == 1:
             whole_c = hop(after(whole, [got[steps[1]]]), 1)
-        if phase == 2:
-            pieces = [whole, whole_c]
-            for which in range(3):
-                pieces += [got[(which, at)], over[(which, at)]]
-            kinds = tuple(range(len(pieces)))
-            shape = (cols, n_dp * slab_rows)
-            if step < len(steps) - 1:
-                outs.append(lay(outs[-1], shape, spans[at], kinds, pieces))
-            else:
-                outs.append(lay(outs[-1], shape, spans[at], kinds[:-1], pieces[:-1]))
-                outs.append(lay(outs[-1], shape, spans[at], kinds[-1:], pieces[-1:]))
+        if phase == 2 and at in (2, 4):
+            outs.append(lay(outs[-1], shape, parts_of(at - 1) + parts_of(at)))
+    parts = parts_of(0)
+    outs.append(lay(outs[-1], shape, parts[:-1]))
+    outs.append(lay(outs[-1], shape, parts[-1:]))
     return (moment_one_new, moment_two_new, master_new.T, outs[-1].T)
 
 

time: 122 us -> 116 us (0.951)
  waiting for transfers between devices: 63.1 us -> 58.9 us
  Pallas kernels: 20.5 us -> 19.2 us
    ppermute x22, waiting for transfers between devices: 50.5 us -> 47.5 us  [turn(): lax.ppermute(value, 'dp', [(i, i ^ masks[i & 1]) for i in range(n_dp)])]
    pallas_call x6 -> x4, Pallas kernels: 9.91 us -> 8.54 us  [lay(): pl.pallas_call(functools.partial(lay_kernel, places=tuple(places), fresh=...]
  transfers between devices with their start and end apart: 48 -> 48, of which waited for: 26 -> 25; matrix products, arithmetic and copies ran while one was open for 0% -> 0% of each run, Pallas kernels for 13% -> 12%
where the time goes in v12:
time: 116 us
  waiting for transfers between devices  58.9 us (51%)
  starting transfers between devices  36.8 us (32%)
  Pallas kernels  19.2 us (17%)
    ppermute x22, waiting for transfers between devices, turn(): lax.ppermute(value, 'dp', [(i, i ^ masks[i & 1]) for i in range(n_dp)])  47.5 us
    ppermute x22, starting transfers between devices, turn(): lax.ppermute(value, 'dp', [(i, i ^ masks[i & 1]) for i in range(n_dp)])  26.5 us
    ppermute x26, waiting for transfers between devices, send(): return lax.ppermute(value, axis, [(i, i ^ mask) for i in range(size)])  11.4 us
    ppermute x26, starting transfers between devices, send(): return lax.ppermute(value, axis, [(i, i ^ mask) for i in range(size)])  10.3 us
    pallas_call x4, Pallas kernels, lay(): pl.pallas_call(functools.partial(lay_kernel, places=tuple(places), fresh=...  8.54 us
    pallas_call x1, Pallas kernels, new_master(): pl.pallas_call(master_kernel, out_shape=jax.ShapeDtypeStruct((cols, slab_...  3.12 us
    pallas_call x2, Pallas kernels, weights(): pl.pallas_call(functools.partial(weight_kernel, n_in=len(pieces), spans=s...  3.03 us
    pallas_call x1, Pallas kernels, take(): pl.pallas_call(functools.partial(take_kernel, first=first), out_shape=jax...  2.36 us
  transfers between devices with their start and end apart: 48, of which 25 were waited for; matrix products, arithmetic and copies ran while one was open for 0% of the time, Pallas kernels for 12%

profile of v12, /device:TPU:0, one launch (start us, length us, event | category | flops | bytes accessed | tf_op | source)
XLA Modules:
  0.0 116.2 jit_solution(18148551544978733385)
XLA Ops:
  0.7 2.4 %shard_map.93 = f32[336,640]{1,0:T(8,128)} custom-call(f32[1728,640]{1,0:T(8,128)} %bitcast.6), custom_call_target="tpu_custom_call" | custom-call | tf_op jit(solution)/shard_map/pallas_call | solution.py:86
  3.1 3.0 %collective-permute-start.3 = (f32[336,640]{1,0:T(8,128)}, f32[336,640]{1,0:T(8,128)S(1)}, u32[]{:S(2)}, u32[]{:S(2)}) collective-permute-start(f32[336,640]{1,0:T(8,128)} %shard_map.93), channel_id=1, source_target_pairs={{0,8},{4,20},{8,0},{12,28},{16,24},{20,4},{24,16},{28,12},{1,9},{5... | collective-permute-start | bytes 2580488 | tf_op jit(solution)/shard_map/ppermute | solution.py:289
  8.2 2.6 %collective-permute-start.1 = (bf16[128,256]{1,0:T(8,128)(2,1)S(1)}, bf16[128,256]{1,0:T(8,128)(2,1)S(1)}, u32[]{:S(2)}, u32[]{:S(2)}) collective-permute-start(bf16[128,256]{1,0:T(8,128)(2,1)S(1)} %convolution_convert_fusion.refs_0_), channel_id=1, source_target_pairs={{0,2},{1,3},{2,0},{3,1},{4,6},{5,7},{6,4},{7,5},{8,10},{9,11},{10,... | collective-permute-start | bytes 196616 | tf_op jit(solution)/shard_map/ppermute | solution.py:66
  11.0 4.2 %collective-permute-done.1.refs_2_ = bf16[128,256]{1,0:T(8,128)(2,1)S(1)} collective-permute-done((bf16[128,256]{1,0:T(8,128)(2,1)S(1)}, bf16[128,256]{1,0:T(8,128)(2,1)S(1)}, u32[]{:S(2)}, u32[]{:S(2)}) %collective-permute-start.1) | collective-permute-done | bytes 65568 | tf_op jit(solution)/shard_map/ppermute | solution.py:66
  21.3 2.5 %collective-permute-start.8 = (bf16[32,1728]{1,0:T(8,128)(2,1)S(1)}, bf16[32,1728]{1,0:T(8,128)(2,1)S(1)}, u32[]{:S(2)}, u32[]{:S(2)}) collective-permute-start(bf16[32,1728]{1,0:T(8,128)(2,1)S(1)} %get-tuple-element.60), channel_id=1, source_target_pairs={{0,20},{4,8},{8,28},{12,0},{16,4},{20,24},{24,12},{28,16},{1,21},{... | collective-permute-start | bytes 331784 | tf_op jit(solution)/shard_map/ppermute | solution.py:289
  25.7 1.8 %collective-permute-done.6.refs_3_ = bf16[32,1728]{1,0:T(8,128)(2,1)S(1)} collective-permute-done((bf16[32,1728]{1,0:T(8,128)(2,1)S(1)}, bf16[32,1728]{1,0:T(8,128)(2,1)S(1)}, u32[]{:S(2)}, u32[]{:S(2)}) %collective-permute-start.6) | collective-permute-done | bytes 110624 | tf_op jit(solution)/shard_map/ppermute | solution.py:289
  27.6 2.5 %collective-permute-done.8.refs_5_ = bf16[32,1728]{1,0:T(8,128)(2,1)S(1)} collective-permute-done((bf16[32,1728]{1,0:T(8,128)(2,1)S(1)}, bf16[32,1728]{1,0:T(8,128)(2,1)S(1)}, u32[]{:S(2)}, u32[]{:S(2)}) %collective-permute-start.8) | collective-permute-done | bytes 110624 | tf_op jit(solution)/shard_map/ppermute | solution.py:289
  33.9 1.7 %collective-permute-start.16 = (bf16[32,1792]{1,0:T(8,128)(2,1)S(1)}, bf16[32,1792]{1,0:T(8,128)(2,1)S(1)}, u32[]{:S(2)}, u32[]{:S(2)}) collective-permute-start(bf16[32,1792]{1,0:T(8,128)(2,1)S(1)} %get-tuple-element.65.refs_0_), channel_id=1, source_target_pairs={{0,24},{4,28},{8,16},{12,20},{16,8},{20,12},{24,0},{28,4},{1,25},{... | collective-permute-start | bytes 344072 | tf_op jit(solution)/shard_map/ppermute | solution.py:66
  35.6 2.5 %collective-permute-done.12.refs_2_ = bf16[32,1792]{1,0:T(8,128)(2,1)S(1)} collective-permute-done((bf16[32,1792]{1,0:T(8,128)(2,1)S(1)}, bf16[32,1792]{1,0:T(8,128)(2,1)S(1)}, u32[]{:S(2)}, u32[]{:S(2)}) %collective-permute-start.12) | collective-permute-done | bytes 114720 | tf_op jit(solution)/shard_map/ppermute | solution.py:66
  38.1 2.0 %collective-permute-done.14.refs_4_ = bf16[32,1792]{1,0:T(8,128)(2,1)S(1)} collective-permute-done((bf16[32,1792]{1,0:T(8,128)(2,1)S(1)}, bf16[32,1792]{1,0:T(8,128)(2,1)S(1)}, u32[]{:S(2)}, u32[]{:S(2)}) %collective-permute-start.14) | collective-permute-done | bytes 114720 | tf_op jit(solution)/shard_map/ppermute | solution.py:66
  44.5 3.1 %shard_map.97 = f32[1728,640]{1,0:T(8,128)} custom-call(bf16[5120,256]{1,0:T(8,128)(2,1)S(1)} %copy-done.2, f32[1728,640]{1,0:T(8,128)S(1)} %bitcast.8, bf16[1792,256]{1,0:T(8,128)(2,1)S(1)} %get-tuple-element.66.tall.refs_0_), custom_call_target="tpu_custom_call" | custom-call | flops 566231040 | bytes 8847360 | tf_op jit(solution)/shard_map/pallas_call | solution.py:219
  47.6 2.2 %shard_map.98 = (bf16[352,640]{1,0:T(8,128)(2,1)S(1)}, bf16[336,640]{1,0:T(8,128)(2,1)S(1)}, bf16[336,640]{1,0:T(8,128)(2,1)S(1)}, bf16[1728,640]{1,0:T(8,128)(2,1)S(1)}) custom-call(bf16[5120,256]{1,0:T(8,128)(2,1)S(1)} %copy-done.2, f32[1728,640]{1,0:T(8,128)S(1)} %bitcast.9, bf16[1792,256]{1,0:T(8,128)(2,1)S(1)} %get-tuple-element.66.tall.refs_0_), custom_call_target="tpu_custom_call" | custom-call | flops 901775360 | bytes 7045120 | tf_op jit(solution)/shard_map/pallas_call | solution.py:167
  52.2 3.4 %collective-permute-done.18.refs_8_ = bf16[352,640]{1,0:T(8,128)(2,1)S(1)} collective-permute-done((bf16[352,640]{1,0:T(8,128)(2,1)S(1)}, bf16[352,640]{1,0:T(8,128)(2,1)S(1)}, u32[]{:S(2)}, u32[]{:S(2)}) %collective-permute-start.18) | collective-permute-done | bytes 450592 | tf_op jit(solution)/shard_map/ppermute | solution.py:289
  57.1 3.4 %collective-permute-done.22.refs_3_ = bf16[352,640]{1,0:T(8,128)(2,1)S(1)} collective-permute-done((bf16[352,640]{1,0:T(8,128)(2,1)S(1)}, bf16[352,640]{1,0:T(8,128)(2,1)S(1)}, u32[]{:S(2)}, u32[]{:S(2)}) %collective-permute-start.22) | collective-permute-done | bytes 450592 | tf_op jit(solution)/shard_map/ppermute | solution.py:289
  61.4 6.1 %collective-permute-done.30.refs_9_ = bf16[336,640]{1,0:T(8,128)(2,1)S(1)} collective-permute-done((bf16[336,640]{1,0:T(8,128)(2,1)S(1)}, bf16[336,640]{1,0:T(8,128)(2,1)S(1)}, u32[]{:S(2)}, u32[]{:S(2)}) %collective-permute-start.30) | collective-permute-done | bytes 430112 | tf_op jit(solution)/shard_map/ppermute | solution.py:289
  70.9 5.1 %collective-permute-done.31.refs_10_ = bf16[352,640]{1,0:T(8,128)(2,1)S(1)} collective-permute-done((bf16[352,640]{1,0:T(8,128)(2,1)S(1)}, bf16[352,640]{1,0:T(8,128)(2,1)S(1)}, u32[]{:S(2)}, u32[]{:S(2)}) %collective-permute-start.31) | collective-permute-done | bytes 450592 | tf_op jit(solution)/shard_map/ppermute | solution.py:289
  77.1 3.7 %collective-permute-done.26.refs_5_ = bf16[352,640]{1,0:T(8,128)(2,1)S(1)} collective-permute-done((bf16[352,640]{1,0:T(8,128)(2,1)S(1)}, bf16[352,640]{1,0:T(8,128)(2,1)S(1)}, u32[]{:S(2)}, u32[]{:S(2)}) %collective-permute-start.26) | collective-permute-done | bytes 450592 | tf_op jit(solution)/shard_map/ppermute | solution.py:289
  81.9 3.5 %collective-permute-done.34.refs_11_ = bf16[336,640]{1,0:T(8,128)(2,1)S(1)} collective-permute-done((bf16[336,640]{1,0:T(8,128)(2,1)S(1)}, bf16[336,640]{1,0:T(8,128)(2,1)S(1)}, u32[]{:S(2)}, u32[]{:S(2)}) %collective-permute-start.34) | collective-permute-done | bytes 430112 | tf_op jit(solution)/shard_map/ppermute | solution.py:289
  86.5 3.7 %collective-permute-done.27.refs_6_ = bf16[352,640]{1,0:T(8,128)(2,1)S(1)} collective-permute-done((bf16[352,640]{1,0:T(8,128)(2,1)S(1)}, bf16[352,640]{1,0:T(8,128)(2,1)S(1)}, u32[]{:S(2)}, u32[]{:S(2)}) %collective-permute-start.27) | collective-permute-done | bytes 450592 | tf_op jit(solution)/shard_map/ppermute | solution.py:289
  91.4 3.7 %collective-permute-done.35.refs_12_ = bf16[352,640]{1,0:T(8,128)(2,1)S(1)} collective-permute-done((bf16[352,640]{1,0:T(8,128)(2,1)S(1)}, bf16[352,640]{1,0:T(8,128)(2,1)S(1)}, u32[]{:S(2)}, u32[]{:S(2)}) %collective-permute-start.35) | collective-permute-done | bytes 450592 | tf_op jit(solution)/shard_map/ppermute | solution.py:289
  96.2 3.7 %collective-permute-done.38.refs_7_ = bf16[352,640]{1,0:T(8,128)(2,1)S(1)} collective-permute-done((bf16[352,640]{1,0:T(8,128)(2,1)S(1)}, bf16[352,640]{1,0:T(8,128)(2,1)S(1)}, u32[]{:S(2)}, u32[]{:S(2)}) %collective-permute-start.38) | collective-permute-done | bytes 450592 | tf_op jit(solution)/shard_map/ppermute | solution.py:289
  101.4 3.0 %collective-permute-done.41.refs_13_ = bf16[336,640]{1,0:T(8,128)(2,1)S(1)} collective-permute-done((bf16[336,640]{1,0:T(8,128)(2,1)S(1)}, bf16[336,640]{1,0:T(8,128)(2,1)S(1)}, u32[]{:S(2)}, u32[]{:S(2)}) %collective-permute-start.41) | collective-permute-done | bytes 430112 | tf_op jit(solution)/shard_map/ppermute | solution.py:289
  106.1 3.1 %shard_map.99.refs_0_ = bf16[1728,5120]{1,0:T(8,128)(2,1)} custom-call(bf16[1728,640]{1,0:T(8,128)(2,1)S(1)} %get-tuple-element.69.refs_0_.refs_1_, bf16[1728,640]{1,0:T(8,128)(2,1)S(1)} %collective-permute-done.19.refs_1_.refs_2_, bf16[352,640]{1,0:T(8,128)(2,1)S(1)} %collective-permute-done.20.refs_2_, ...), custom_call_target="tpu_custom_call" | custom-call | bytes 14417920 | tf_op jit(solution)/shard_map/pallas_call | solution.py:265
  109.3 3.0 %shard_map.100.refs_0_ = bf16[1728,5120]{1,0:T(8,128)(2,1)} custom-call(bf16[1728,5120]{1,0:T(8,128)(2,1)} %shard_map.99.refs_0_, bf16[1728,640]{1,0:T(8,128)(2,1)S(1)} %get-tuple-element.69.refs_0_.refs_1_, bf16[1728,640]{1,0:T(8,128)(2,1)S(1)} %collective-permute-done.19.refs_1_.refs_2_, ...), custom_call_target="tpu_custom_call", output_to_operand_aliasing={{}: (0, {})} | custom-call | bytes 14090240 | tf_op jit(solution)/shard_map/pallas_call | solution.py:265
  (96 shorter events, 39.4 us)
Async XLA Ops:
  3.1 14.6 %collective-permute-start.3 = (f32[336,640]{1,0:T(8,128)}, f32[336,640]{1,0:T(8,128)S(1)}, u32[]{:S(2)}, u32[]{:S(2)}) collective-permute-start(f32[336,640]{1,0:T(8,128)} %shard_map.93), channel_id=1, source_target_pairs={{0,8},{4,20},{8,0},{12,28},{16,24},{20,4},{24,16},{28,12},{1,9},{5... | collective-permute-start | bytes 2580488 | tf_op jit(solution)/shard_map/ppermute | solution.py:289
  21.3 8.9 %collective-permute-start.8 = (bf16[32,1728]{1,0:T(8,128)(2,1)S(1)}, bf16[32,1728]{1,0:T(8,128)(2,1)S(1)}, u32[]{:S(2)}, u32[]{:S(2)}) collective-permute-start(bf16[32,1728]{1,0:T(8,128)(2,1)S(1)} %get-tuple-element.60), channel_id=1, source_target_pairs={{0,20},{4,8},{8,28},{12,0},{16,4},{20,24},{24,12},{28,16},{1,21},{... | collective-permute-start | bytes 331784 | tf_op jit(solution)/shard_map/ppermute | solution.py:289
  42.4 8.5 %collective-permute-start.20 = (bf16[352,640]{1,0:T(8,128)(2,1)S(1)}, bf16[352,640]{1,0:T(8,128)(2,1)S(1)}, u32[]{:S(2)}, u32[]{:S(2)}) collective-permute-start(bf16[352,640]{1,0:T(8,128)(2,1)S(1)} %get-tuple-element.73), channel_id=1, source_target_pairs={{0,8},{4,20},{8,0},{12,28},{16,24},{20,4},{24,16},{28,12},{1,9},{5... | collective-permute-start | bytes 1351688 | tf_op jit(solution)/shard_map/ppermute | solution.py:289
  43.8 11.8 %collective-permute-start.18 = (bf16[352,640]{1,0:T(8,128)(2,1)S(1)}, bf16[352,640]{1,0:T(8,128)(2,1)S(1)}, u32[]{:S(2)}, u32[]{:S(2)}) collective-permute-start(bf16[352,640]{1,0:T(8,128)(2,1)S(1)} %get-tuple-element.78), channel_id=1, source_target_pairs={{0,8},{4,20},{8,0},{12,28},{16,24},{20,4},{24,16},{28,12},{1,9},{5... | collective-permute-start | bytes 1351688 | tf_op jit(solution)/shard_map/ppermute | solution.py:289
  50.9 9.7 %collective-permute-start.22 = (bf16[352,640]{1,0:T(8,128)(2,1)S(1)}, bf16[352,640]{1,0:T(8,128)(2,1)S(1)}, u32[]{:S(2)}, u32[]{:S(2)}) collective-permute-start(bf16[352,640]{1,0:T(8,128)(2,1)S(1)} %get-tuple-element.74), channel_id=1, source_target_pairs={{0,8},{4,20},{8,0},{12,28},{16,24},{20,4},{24,16},{28,12},{1,9},{5... | collective-permute-start | bytes 1351688 | tf_op jit(solution)/shard_map/ppermute | solution.py:289
  55.7 11.9 %collective-permute-start.29 = (bf16[352,640]{1,0:T(8,128)(2,1)S(1)}, bf16[352,640]{1,0:T(8,128)(2,1)S(1)}, u32[]{:S(2)}, u32[]{:S(2)}) collective-permute-start(bf16[352,640]{1,0:T(8,128)(2,1)S(1)} %collective-permute-done.18.refs_8_), channel_id=1, source_target_pairs={{0,4},{4,0},{8,12},{12,8},{16,20},{20,16},{24,28},{28,24},{1,5},{5... | collective-permute-start | bytes 1351688 | tf_op jit(solution)/shard_map/ppermute | solution.py:66
  55.7 11.9 %collective-permute-start.30 = (bf16[336,640]{1,0:T(8,128)(2,1)S(1)}, bf16[336,640]{1,0:T(8,128)(2,1)S(1)}, u32[]{:S(2)}, u32[]{:S(2)}) collective-permute-start(bf16[336,640]{1,0:T(8,128)(2,1)S(1)} %get-tuple-element.79), channel_id=1, source_target_pairs={{0,8},{4,20},{8,0},{12,28},{16,24},{20,4},{24,16},{28,12},{1,9},{5... | collective-permute-start | bytes 1290248 | tf_op jit(solution)/shard_map/ppermute | solution.py:289
  60.5 8.8 %collective-permute-start.23 = (bf16[352,640]{1,0:T(8,128)(2,1)S(1)}, bf16[352,640]{1,0:T(8,128)(2,1)S(1)}, u32[]{:S(2)}, u32[]{:S(2)}) collective-permute-start(bf16[352,640]{1,0:T(8,128)(2,1)S(1)} %get-tuple-element.73), channel_id=1, source_target_pairs={{0,16},{4,12},{8,24},{12,4},{16,0},{20,28},{24,8},{28,20},{1,17},{... | collective-permute-start | bytes 1351688 | tf_op jit(solution)/shard_map/ppermute | solution.py:289
  67.6 8.4 %collective-permute-start.31 = (bf16[352,640]{1,0:T(8,128)(2,1)S(1)}, bf16[352,640]{1,0:T(8,128)(2,1)S(1)}, u32[]{:S(2)}, u32[]{:S(2)}) collective-permute-start(bf16[352,640]{1,0:T(8,128)(2,1)S(1)} %get-tuple-element.78), channel_id=1, source_target_pairs={{0,16},{4,12},{8,24},{12,4},{16,0},{20,28},{24,8},{28,20},{1,17},{... | collective-permute-start | bytes 1351688 | tf_op jit(solution)/shard_map/ppermute | solution.py:289
  68.7 36.9 %collective-permute-start.19 = (bf16[1728,640]{1,0:T(8,128)(2,1)S(1)}, bf16[1728,640]{1,0:T(8,128)(2,1)S(1)}, u32[]{:S(2)}, u32[]{:S(2)}) collective-permute-start(bf16[1728,640]{1,0:T(8,128)(2,1)S(1)} %get-tuple-element.69.refs_0_.refs_1_), channel_id=1, source_target_pairs={{0,4},{4,0},{8,12},{12,8},{16,20},{20,16},{24,28},{28,24},{1,5},{5... | collective-permute-start | bytes 6635528 | tf_op jit(solution)/shard_map/ppermute | solution.py:66
  69.3 11.5 %collective-permute-start.26 = (bf16[352,640]{1,0:T(8,128)(2,1)S(1)}, bf16[352,640]{1,0:T(8,128)(2,1)S(1)}, u32[]{:S(2)}, u32[]{:S(2)}) collective-permute-start(bf16[352,640]{1,0:T(8,128)(2,1)S(1)} %get-tuple-element.74), channel_id=1, source_target_pairs={{0,16},{4,12},{8,24},{12,4},{16,0},{20,28},{24,8},{28,20},{1,17},{... | collective-permute-start | bytes 1351688 | tf_op jit(solution)/shard_map/ppermute | solution.py:289
  70.1 10.7 %collective-permute-start.24 = (bf16[352,640]{1,0:T(8,128)(2,1)S(1)}, bf16[352,640]{1,0:T(8,128)(2,1)S(1)}, u32[]{:S(2)}, u32[]{:S(2)}) collective-permute-start(bf16[352,640]{1,0:T(8,128)(2,1)S(1)} %collective-permute-done.23.refs_4_), channel_id=1, source_target_pairs={{0,4},{4,0},{8,12},{12,8},{16,20},{20,16},{24,28},{28,24},{1,5},{5... | collective-permute-start | bytes 1351688 | tf_op jit(solution)/shard_map/ppermute | solution.py:66
  76.0 9.4 %collective-permute-start.32 = (bf16[352,640]{1,0:T(8,128)(2,1)S(1)}, bf16[352,640]{1,0:T(8,128)(2,1)S(1)}, u32[]{:S(2)}, u32[]{:S(2)}) collective-permute-start(bf16[352,640]{1,0:T(8,128)(2,1)S(1)} %collective-permute-done.31.refs_10_), channel_id=1, source_target_pairs={{0,4},{4,0},{8,12},{12,8},{16,20},{20,16},{24,28},{28,24},{1,5},{5... | collective-permute-start | bytes 1351688 | tf_op jit(solution)/shard_map/ppermute | solution.py:66
  76.0 9.4 %collective-permute-start.34 = (bf16[336,640]{1,0:T(8,128)(2,1)S(1)}, bf16[336,640]{1,0:T(8,128)(2,1)S(1)}, u32[]{:S(2)}, u32[]{:S(2)}) collective-permute-start(bf16[336,640]{1,0:T(8,128)(2,1)S(1)} %get-tuple-element.79), channel_id=1, source_target_pairs={{0,16},{4,12},{8,24},{12,4},{16,0},{20,28},{24,8},{28,20},{1,17},{... | collective-permute-start | bytes 1290248 | tf_op jit(solution)/shard_map/ppermute | solution.py:289
  80.8 9.4 %collective-permute-start.27 = (bf16[352,640]{1,0:T(8,128)(2,1)S(1)}, bf16[352,640]{1,0:T(8,128)(2,1)S(1)}, u32[]{:S(2)}, u32[]{:S(2)}) collective-permute-start(bf16[352,640]{1,0:T(8,128)(2,1)S(1)} %collective-permute-done.20.refs_2_), channel_id=1, source_target_pairs={{0,16},{4,12},{8,24},{12,4},{16,0},{20,28},{24,8},{28,20},{1,17},{... | collective-permute-start | bytes 1351688 | tf_op jit(solution)/shard_map/ppermute | solution.py:289
  85.4 9.7 %collective-permute-start.35 = (bf16[352,640]{1,0:T(8,128)(2,1)S(1)}, bf16[352,640]{1,0:T(8,128)(2,1)S(1)}, u32[]{:S(2)}, u32[]{:S(2)}) collective-permute-start(bf16[352,640]{1,0:T(8,128)(2,1)S(1)} %collective-permute-done.18.refs_8_), channel_id=1, source_target_pairs={{0,16},{4,12},{8,24},{12,4},{16,0},{20,28},{24,8},{28,20},{1,17},{... | collective-permute-start | bytes 1351688 | tf_op jit(solution)/shard_map/ppermute | solution.py:289
  86.5 8.5 %collective-permute-start.40 = (bf16[336,640]{1,0:T(8,128)(2,1)S(1)}, bf16[336,640]{1,0:T(8,128)(2,1)S(1)}, u32[]{:S(2)}, u32[]{:S(2)}) collective-permute-start(bf16[336,640]{1,0:T(8,128)(2,1)S(1)} %collective-permute-done.34.refs_11_), channel_id=1, source_target_pairs={{0,4},{4,0},{8,12},{12,8},{16,20},{20,16},{24,28},{28,24},{1,5},{5... | collective-permute-start | bytes 1290248 | tf_op jit(solution)/shard_map/ppermute | solution.py:66
  90.2 9.7 %collective-permute-start.38 = (bf16[352,640]{1,0:T(8,128)(2,1)S(1)}, bf16[352,640]{1,0:T(8,128)(2,1)S(1)}, u32[]{:S(2)}, u32[]{:S(2)}) collective-permute-start(bf16[352,640]{1,0:T(8,128)(2,1)S(1)} %collective-permute-done.22.refs_3_), channel_id=1, source_target_pairs={{0,16},{4,12},{8,24},{12,4},{16,0},{20,28},{24,8},{28,20},{1,17},{... | collective-permute-start | bytes 1351688 | tf_op jit(solution)/shard_map/ppermute | solution.py:289
  91.4 8.5 %collective-permute-start.28 = (bf16[352,640]{1,0:T(8,128)(2,1)S(1)}, bf16[352,640]{1,0:T(8,128)(2,1)S(1)}, u32[]{:S(2)}, u32[]{:S(2)}) collective-permute-start(bf16[352,640]{1,0:T(8,128)(2,1)S(1)} %collective-permute-done.27.refs_6_), channel_id=1, source_target_pairs={{0,4},{4,0},{8,12},{12,8},{16,20},{20,16},{24,28},{28,24},{1,5},{5... | collective-permute-start | bytes 1351688 | tf_op jit(solution)/shard_map/ppermute | solution.py:66
  95.0 9.4 %collective-permute-start.36 = (bf16[352,640]{1,0:T(8,128)(2,1)S(1)}, bf16[352,640]{1,0:T(8,128)(2,1)S(1)}, u32[]{:S(2)}, u32[]{:S(2)}) collective-permute-start(bf16[352,640]{1,0:T(8,128)(2,1)S(1)} %collective-permute-done.35.refs_12_), channel_id=1, source_target_pairs={{0,4},{4,0},{8,12},{12,8},{16,20},{20,16},{24,28},{28,24},{1,5},{5... | collective-permute-start | bytes 1351688 | tf_op jit(solution)/shard_map/ppermute | solution.py:66
  95.1 9.4 %collective-permute-start.41 = (bf16[336,640]{1,0:T(8,128)(2,1)S(1)}, bf16[336,640]{1,0:T(8,128)(2,1)S(1)}, u32[]{:S(2)}, u32[]{:S(2)}) collective-permute-start(bf16[336,640]{1,0:T(8,128)(2,1)S(1)} %collective-permute-done.30.refs_9_), channel_id=1, source_target_pairs={{0,16},{4,12},{8,24},{12,4},{16,0},{20,28},{24,8},{28,20},{1,17},{... | collective-permute-start | bytes 1290248 | tf_op jit(solution)/shard_map/ppermute | solution.py:289
  99.9 9.4 %collective-permute-start.39 = (bf16[352,640]{1,0:T(8,128)(2,1)S(1)}, bf16[352,640]{1,0:T(8,128)(2,1)S(1)}, u32[]{:S(2)}, u32[]{:S(2)}) collective-permute-start(bf16[352,640]{1,0:T(8,128)(2,1)S(1)} %collective-permute-done.38.refs_7_), channel_id=1, source_target_pairs={{0,4},{4,0},{8,12},{12,8},{16,20},{20,16},{24,28},{28,24},{1,5},{5... | collective-permute-start | bytes 1351688 | tf_op jit(solution)/shard_map/ppermute | solution.py:66
  99.9 9.3 %collective-permute-start.44 = (bf16[336,640]{1,0:T(8,128)(2,1)S(1)}, bf16[336,640]{1,0:T(8,128)(2,1)S(1)}, u32[]{:S(2)}, u32[]{:S(2)}) collective-permute-start(bf16[336,640]{1,0:T(8,128)(2,1)S(1)} %get-tuple-element.84), channel_id=1, source_target_pairs={{0,16},{4,12},{8,24},{12,4},{16,0},{20,28},{24,8},{28,20},{1,17},{... | collective-permute-start | bytes 1290248 | tf_op jit(solution)/shard_map/ppermute | solution.py:289
  104.5 9.2 %collective-permute-start.46 = (bf16[336,640]{1,0:T(8,128)(2,1)S(1)}, bf16[336,640]{1,0:T(8,128)(2,1)S(1)}, u32[]{:S(2)}, u32[]{:S(2)}) collective-permute-start(bf16[336,640]{1,0:T(8,128)(2,1)S(1)} %shard_map.101.refs_3_), channel_id=1, source_target_pairs={{0,16},{4,12},{8,24},{12,4},{16,0},{20,28},{24,8},{28,20},{1,17},{... | collective-permute-start | bytes 1290248 | tf_op jit(solution)/shard_map/ppermute | solution.py:289
  (30 other events, 253.6 us)

commit v13 on v12

--- a/solution.py
+++ b/solution.py
@@ -70,25 +70,35 @@
     return me ^ jnp.where((me & 1) == 0, masks[0], masks[1])
 
 
-def take_kernel(source, out, sems, *, first):
-    count = out.shape[0] // sems.shape[0]
-    copies = []
-    for at in range(sems.shape[0]):
-        part = source.at[pl.ds(first + at * count, count), :]
-        copies.append(pltpu.make_async_copy(part, out.at[pl.ds(at * count, count), :], sems.at[at]))
-    for copy in copies:
-        copy.start()
-    for copy in copies:
-        copy.wait()
-
-
-def take(array, first, count):
+def take_kernel(source, out, held, sems):
+    count = held.shape[1]
+    ways = []
+    for at in range(held.shape[0]):
+        rows = pl.ds(at * count, count)
+        ways.append((
+            pltpu.make_async_copy(source.at[rows, :], held.at[at], sems.at[0, at]),
+            pltpu.make_async_copy(held.at[at], out.at[rows, :], sems.at[1, at]),
+        ))
+    for into, _ in ways:
+        into.start()
+    for into, back in ways:
+        into.wait()
+        back.start()
+    for _, back in ways:
+        back.wait()
+
+
+def take(array, count):
+    parts = count // 48 if count % 48 == 0 else 1
     return pl.pallas_call(
-        functools.partial(take_kernel, first=first),
+        take_kernel,
         out_shape=jax.ShapeDtypeStruct((count, array.shape[1]), array.dtype),
         in_specs=[ANY],
-        out_specs=VMEM,
-        scratch_shapes=[pltpu.SemaphoreType.DMA((count // 16,))],
+        out_specs=ANY,
+        scratch_shapes=[
+            pltpu.VMEM((parts, count // parts, array.shape[1]), array.dtype),
+            pltpu.SemaphoreType.DMA((2, parts)),
+        ],
         compiler_params=pltpu.CompilerParams(vmem_limit_bytes=60 * 2**20),
     )(array)
 
@@ -293,7 +303,7 @@
 
     early, counts = chunk_sizes(cols)
     spans = [(sum(counts[:at]), count) for at, count in enumerate(counts)]
-    taken = take(master_t, 0, early[0])
+    taken = take(master_t, early[0])
     ahead = [turn(taken, TURN_MASKS[0])]
     acts = after(acts, [taken])
 
@@ -346,7 +356,7 @@
     def parts_of(at):
         pieces = [whole, whole_c]
         for which in range(3):
-            pieces += [got[(which, at)], over[(which, at)]]
+            pieces += [table[(which, at)] for table in (got, over) if (which, at) in table]
         return [(*spans[at], kind, piece) for kind, piece in enumerate(pieces)]
 
     for step, (phase, at) in enumerate(steps):
@@ -361,9 +371,9 @@
         if step == 1:
             whole_c = hop(after(whole, [got[steps[1]]]), 1)
         if phase == 2 and at in (2, 4):
-            outs.append(lay(outs[-1], shape, parts_of(at - 1) + parts_of(at)))
+            outs.append(lay(outs[-1], shape, parts_of(at - 1) + parts_of(at) + parts_of(0)[at - 2 : at]))
     parts = parts_of(0)
-    outs.append(lay(outs[-1], shape, parts[:-1]))
+    outs.append(lay(outs[-1], shape, parts[4:-1]))
     outs.append(lay(outs[-1], shape, parts[-1:]))
     return (moment_one_new, moment_two_new, master_new.T, outs[-1].T)
 

time: 116 us -> 116 us (level)
  no operation moved by 1% of the time
where the time goes in v13:
time: 116 us
  waiting for transfers between devices  59.4 us (51%)
  starting transfers between devices  36.4 us (31%)
  Pallas kernels  18.9 us (16%)
    ppermute x22, waiting for transfers between devices, turn(): lax.ppermute(value, 'dp', [(i, i ^ masks[i & 1]) for i in range(n_dp)])  47.4 us
    ppermute x22, starting transfers between devices, turn(): lax.ppermute(value, 'dp', [(i, i ^ masks[i & 1]) for i in range(n_dp)])  26.5 us
    ppermute x26, waiting for transfers between devices, send(): return lax.ppermute(value, axis, [(i, i ^ mask) for i in range(size)])  12.1 us
    ppermute x26, starting transfers between devices, send(): return lax.ppermute(value, axis, [(i, i ^ mask) for i in range(size)])  9.92 us
    pallas_call x4, Pallas kernels, lay(): pl.pallas_call(functools.partial(lay_kernel, places=tuple(places), fresh=...  8.48 us
    pallas_call x1, Pallas kernels, new_master(): pl.pallas_call(master_kernel, out_shape=jax.ShapeDtypeStruct((cols, slab_...  3.12 us
    pallas_call x2, Pallas kernels, weights(): pl.pallas_call(functools.partial(weight_kernel, n_in=len(pieces), spans=s...  3.04 us
  transfers between devices with their start and end apart: 48, of which 25 were waited for; matrix products, arithmetic and copies ran while one was open for 0% of the time, Pallas kernels for 12%

profile of v13, /device:TPU:0, one launch (start us, length us, event | category | flops | bytes accessed | tf_op | source)
XLA Modules:
  0.0 116.0 jit_solution(17209039877353238869)
XLA Ops:
  0.7 2.2 %shard_map.93 = f32[336,640]{1,0:T(8,128)} custom-call(f32[1728,640]{1,0:T(8,128)} %bitcast.6), custom_call_target="tpu_custom_call" | custom-call | tf_op jit(solution)/shard_map/pallas_call | solution.py:93
  2.9 3.0 %collective-permute-start.3 = (f32[336,640]{1,0:T(8,128)}, f32[336,640]{1,0:T(8,128)S(1)}, u32[]{:S(2)}, u32[]{:S(2)}) collective-permute-start(f32[336,640]{1,0:T(8,128)} %shard_map.93), channel_id=1, source_target_pairs={{0,8},{4,20},{8,0},{12,28},{16,24},{20,4},{24,16},{28,12},{1,9},{5... | collective-permute-start | bytes 2580488 | tf_op jit(solution)/shard_map/ppermute | solution.py:299
  8.0 2.6 %collective-permute-start.1 = (bf16[128,256]{1,0:T(8,128)(2,1)S(1)}, bf16[128,256]{1,0:T(8,128)(2,1)S(1)}, u32[]{:S(2)}, u32[]{:S(2)}) collective-permute-start(bf16[128,256]{1,0:T(8,128)(2,1)S(1)} %convolution_convert_fusion.refs_0_), channel_id=1, source_target_pairs={{0,2},{1,3},{2,0},{3,1},{4,6},{5,7},{6,4},{7,5},{8,10},{9,11},{10,... | collective-permute-start | bytes 196616 | tf_op jit(solution)/shard_map/ppermute | solution.py:66
  10.8 4.2 %collective-permute-done.1.refs_2_ = bf16[128,256]{1,0:T(8,128)(2,1)S(1)} collective-permute-done((bf16[128,256]{1,0:T(8,128)(2,1)S(1)}, bf16[128,256]{1,0:T(8,128)(2,1)S(1)}, u32[]{:S(2)}, u32[]{:S(2)}) %collective-permute-start.1) | collective-permute-done | bytes 65568 | tf_op jit(solution)/shard_map/ppermute | solution.py:66
  21.1 2.5 %collective-permute-start.8 = (bf16[32,1728]{1,0:T(8,128)(2,1)S(1)}, bf16[32,1728]{1,0:T(8,128)(2,1)S(1)}, u32[]{:S(2)}, u32[]{:S(2)}) collective-permute-start(bf16[32,1728]{1,0:T(8,128)(2,1)S(1)} %get-tuple-element.60), channel_id=1, source_target_pairs={{0,20},{4,8},{8,28},{12,0},{16,4},{20,24},{24,12},{28,16},{1,21},{... | collective-permute-start | bytes 331784 | tf_op jit(solution)/shard_map/ppermute | solution.py:299
  25.5 1.8 %collective-permute-done.6.refs_3_ = bf16[32,1728]{1,0:T(8,128)(2,1)S(1)} collective-permute-done((bf16[32,1728]{1,0:T(8,128)(2,1)S(1)}, bf16[32,1728]{1,0:T(8,128)(2,1)S(1)}, u32[]{:S(2)}, u32[]{:S(2)}) %collective-permute-start.6) | collective-permute-done | bytes 110624 | tf_op jit(solution)/shard_map/ppermute | solution.py:299
  27.4 2.5 %collective-permute-done.8.refs_5_ = bf16[32,1728]{1,0:T(8,128)(2,1)S(1)} collective-permute-done((bf16[32,1728]{1,0:T(8,128)(2,1)S(1)}, bf16[32,1728]{1,0:T(8,128)(2,1)S(1)}, u32[]{:S(2)}, u32[]{:S(2)}) %collective-permute-start.8) | collective-permute-done | bytes 110624 | tf_op jit(solution)/shard_map/ppermute | solution.py:299
  33.7 1.7 %collective-permute-start.16 = (bf16[32,1792]{1,0:T(8,128)(2,1)S(1)}, bf16[32,1792]{1,0:T(8,128)(2,1)S(1)}, u32[]{:S(2)}, u32[]{:S(2)}) collective-permute-start(bf16[32,1792]{1,0:T(8,128)(2,1)S(1)} %get-tuple-element.65.refs_0_), channel_id=1, source_target_pairs={{0,24},{4,28},{8,16},{12,20},{16,8},{20,12},{24,0},{28,4},{1,25},{... | collective-permute-start | bytes 344072 | tf_op jit(solution)/shard_map/ppermute | solution.py:66
  35.4 2.5 %collective-permute-done.12.refs_2_ = bf16[32,1792]{1,0:T(8,128)(2,1)S(1)} collective-permute-done((bf16[32,1792]{1,0:T(8,128)(2,1)S(1)}, bf16[32,1792]{1,0:T(8,128)(2,1)S(1)}, u32[]{:S(2)}, u32[]{:S(2)}) %collective-permute-start.12) | collective-permute-done | bytes 114720 | tf_op jit(solution)/shard_map/ppermute | solution.py:66
  37.9 2.0 %collective-permute-done.14.refs_4_ = bf16[32,1792]{1,0:T(8,128)(2,1)S(1)} collective-permute-done((bf16[32,1792]{1,0:T(8,128)(2,1)S(1)}, bf16[32,1792]{1,0:T(8,128)(2,1)S(1)}, u32[]{:S(2)}, u32[]{:S(2)}) %collective-permute-start.14) | collective-permute-done | bytes 114720 | tf_op jit(solution)/shard_map/ppermute | solution.py:66
  44.3 3.1 %shard_map.97 = f32[1728,640]{1,0:T(8,128)} custom-call(bf16[5120,256]{1,0:T(8,128)(2,1)S(1)} %copy-done.2, f32[1728,640]{1,0:T(8,128)S(1)} %bitcast.8, bf16[1792,256]{1,0:T(8,128)(2,1)S(1)} %get-tuple-element.66.tall.refs_0_), custom_call_target="tpu_custom_call" | custom-call | flops 566231040 | bytes 8847360 | tf_op jit(solution)/shard_map/pallas_call | solution.py:229
  47.4 2.2 %shard_map.98 = (bf16[352,640]{1,0:T(8,128)(2,1)S(1)}, bf16[336,640]{1,0:T(8,128)(2,1)S(1)}, bf16[336,640]{1,0:T(8,128)(2,1)S(1)}, bf16[1728,640]{1,0:T(8,128)(2,1)S(1)}) custom-call(bf16[5120,256]{1,0:T(8,128)(2,1)S(1)} %copy-done.2, f32[1728,640]{1,0:T(8,128)S(1)} %bitcast.9, bf16[1792,256]{1,0:T(8,128)(2,1)S(1)} %get-tuple-element.66.tall.refs_0_), custom_call_target="tpu_custom_call" | custom-call | flops 901775360 | bytes 7045120 | tf_op jit(solution)/shard_map/pallas_call | solution.py:177
  52.0 3.4 %collective-permute-done.18.refs_8_ = bf16[352,640]{1,0:T(8,128)(2,1)S(1)} collective-permute-done((bf16[352,640]{1,0:T(8,128)(2,1)S(1)}, bf16[352,640]{1,0:T(8,128)(2,1)S(1)}, u32[]{:S(2)}, u32[]{:S(2)}) %collective-permute-start.18) | collective-permute-done | bytes 450592 | tf_op jit(solution)/shard_map/ppermute | solution.py:299
  56.9 3.4 %collective-permute-done.22.refs_3_ = bf16[352,640]{1,0:T(8,128)(2,1)S(1)} collective-permute-done((bf16[352,640]{1,0:T(8,128)(2,1)S(1)}, bf16[352,640]{1,0:T(8,128)(2,1)S(1)}, u32[]{:S(2)}, u32[]{:S(2)}) %collective-permute-start.22) | collective-permute-done | bytes 450592 | tf_op jit(solution)/shard_map/ppermute | solution.py:299
  61.2 6.1 %collective-permute-done.30.refs_9_ = bf16[336,640]{1,0:T(8,128)(2,1)S(1)} collective-permute-done((bf16[336,640]{1,0:T(8,128)(2,1)S(1)}, bf16[336,640]{1,0:T(8,128)(2,1)S(1)}, u32[]{:S(2)}, u32[]{:S(2)}) %collective-permute-start.30) | collective-permute-done | bytes 430112 | tf_op jit(solution)/shard_map/ppermute | solution.py:299
  70.7 5.1 %collective-permute-done.31.refs_10_ = bf16[352,640]{1,0:T(8,128)(2,1)S(1)} collective-permute-done((bf16[352,640]{1,0:T(8,128)(2,1)S(1)}, bf16[352,640]{1,0:T(8,128)(2,1)S(1)}, u32[]{:S(2)}, u32[]{:S(2)}) %collective-permute-start.31) | collective-permute-done | bytes 450592 | tf_op jit(solution)/shard_map/ppermute | solution.py:299
  76.9 3.7 %collective-permute-done.26.refs_5_ = bf16[352,640]{1,0:T(8,128)(2,1)S(1)} collective-permute-done((bf16[352,640]{1,0:T(8,128)(2,1)S(1)}, bf16[352,640]{1,0:T(8,128)(2,1)S(1)}, u32[]{:S(2)}, u32[]{:S(2)}) %collective-permute-start.26) | collective-permute-done | bytes 450592 | tf_op jit(solution)/shard_map/ppermute | solution.py:299
  81.7 3.5 %collective-permute-done.34.refs_11_ = bf16[336,640]{1,0:T(8,128)(2,1)S(1)} collective-permute-done((bf16[336,640]{1,0:T(8,128)(2,1)S(1)}, bf16[336,640]{1,0:T(8,128)(2,1)S(1)}, u32[]{:S(2)}, u32[]{:S(2)}) %collective-permute-start.34) | collective-permute-done | bytes 430112 | tf_op jit(solution)/shard_map/ppermute | solution.py:299
  86.3 3.7 %collective-permute-done.27.refs_6_ = bf16[352,640]{1,0:T(8,128)(2,1)S(1)} collective-permute-done((bf16[352,640]{1,0:T(8,128)(2,1)S(1)}, bf16[352,640]{1,0:T(8,128)(2,1)S(1)}, u32[]{:S(2)}, u32[]{:S(2)}) %collective-permute-start.27) | collective-permute-done | bytes 450592 | tf_op jit(solution)/shard_map/ppermute | solution.py:299
  91.1 3.7 %collective-permute-done.35.refs_12_ = bf16[352,640]{1,0:T(8,128)(2,1)S(1)} collective-permute-done((bf16[352,640]{1,0:T(8,128)(2,1)S(1)}, bf16[352,640]{1,0:T(8,128)(2,1)S(1)}, u32[]{:S(2)}, u32[]{:S(2)}) %collective-permute-start.35) | collective-permute-done | bytes 450592 | tf_op jit(solution)/shard_map/ppermute | solution.py:299
  96.0 3.7 %collective-permute-done.38.refs_7_ = bf16[352,640]{1,0:T(8,128)(2,1)S(1)} collective-permute-done((bf16[352,640]{1,0:T(8,128)(2,1)S(1)}, bf16[352,640]{1,0:T(8,128)(2,1)S(1)}, u32[]{:S(2)}, u32[]{:S(2)}) %collective-permute-start.38) | collective-permute-done | bytes 450592 | tf_op jit(solution)/shard_map/ppermute | solution.py:299
  101.3 3.0 %collective-permute-done.41.refs_13_ = bf16[336,640]{1,0:T(8,128)(2,1)S(1)} collective-permute-done((bf16[336,640]{1,0:T(8,128)(2,1)S(1)}, bf16[336,640]{1,0:T(8,128)(2,1)S(1)}, u32[]{:S(2)}, u32[]{:S(2)}) %collective-permute-start.41) | collective-permute-done | bytes 430112 | tf_op jit(solution)/shard_map/ppermute | solution.py:299
  105.9 3.3 %shard_map.99.refs_0_ = bf16[1728,5120]{1,0:T(8,128)(2,1)} custom-call(bf16[1728,640]{1,0:T(8,128)(2,1)S(1)} %get-tuple-element.69.refs_0_.refs_1_, bf16[1728,640]{1,0:T(8,128)(2,1)S(1)} %collective-permute-done.19.refs_1_.refs_2_, bf16[352,640]{1,0:T(8,128)(2,1)S(1)} %collective-permute-done.20.refs_2_, ...), custom_call_target="tpu_custom_call" | custom-call | bytes 16138240 | tf_op jit(solution)/shard_map/pallas_call | solution.py:275
  109.4 3.3 %shard_map.101.refs_0_ = bf16[1728,5120]{1,0:T(8,128)(2,1)} custom-call(bf16[1728,5120]{1,0:T(8,128)(2,1)} %shard_map.99.refs_0_, bf16[1728,640]{1,0:T(8,128)(2,1)S(1)} %get-tuple-element.69.refs_0_.refs_1_, bf16[1728,640]{1,0:T(8,128)(2,1)S(1)} %collective-permute-done.19.refs_1_.refs_2_, ...), custom_call_target="tpu_custom_call", output_to_operand_aliasing={{}: (0, {})} | custom-call | bytes 15810560 | tf_op jit(solution)/shard_map/pallas_call | solution.py:275
  (96 shorter events, 39.0 us)
Async XLA Ops:
  2.9 14.6 %collective-permute-start.3 = (f32[336,640]{1,0:T(8,128)}, f32[336,640]{1,0:T(8,128)S(1)}, u32[]{:S(2)}, u32[]{:S(2)}) collective-permute-start(f32[336,640]{1,0:T(8,128)} %shard_map.93), channel_id=1, source_target_pairs={{0,8},{4,20},{8,0},{12,28},{16,24},{20,4},{24,16},{28,12},{1,9},{5... | collective-permute-start | bytes 2580488 | tf_op jit(solution)/shard_map/ppermute | solution.py:299
  21.1 8.9 %collective-permute-start.8 = (bf16[32,1728]{1,0:T(8,128)(2,1)S(1)}, bf16[32,1728]{1,0:T(8,128)(2,1)S(1)}, u32[]{:S(2)}, u32[]{:S(2)}) collective-permute-start(bf16[32,1728]{1,0:T(8,128)(2,1)S(1)} %get-tuple-element.60), channel_id=1, source_target_pairs={{0,20},{4,8},{8,28},{12,0},{16,4},{20,24},{24,12},{28,16},{1,21},{... | collective-permute-start | bytes 331784 | tf_op jit(solution)/shard_map/ppermute | solution.py:299
  42.2 8.5 %collective-permute-start.20 = (bf16[352,640]{1,0:T(8,128)(2,1)S(1)}, bf16[352,640]{1,0:T(8,128)(2,1)S(1)}, u32[]{:S(2)}, u32[]{:S(2)}) collective-permute-start(bf16[352,640]{1,0:T(8,128)(2,1)S(1)} %get-tuple-element.73), channel_id=1, source_target_pairs={{0,8},{4,20},{8,0},{12,28},{16,24},{20,4},{24,16},{28,12},{1,9},{5... | collective-permute-start | bytes 1351688 | tf_op jit(solution)/shard_map/ppermute | solution.py:299
  43.6 11.8 %collective-permute-start.18 = (bf16[352,640]{1,0:T(8,128)(2,1)S(1)}, bf16[352,640]{1,0:T(8,128)(2,1)S(1)}, u32[]{:S(2)}, u32[]{:S(2)}) collective-permute-start(bf16[352,640]{1,0:T(8,128)(2,1)S(1)} %get-tuple-element.78), channel_id=1, source_target_pairs={{0,8},{4,20},{8,0},{12,28},{16,24},{20,4},{24,16},{28,12},{1,9},{5... | collective-permute-start | bytes 1351688 | tf_op jit(solution)/shard_map/ppermute | solution.py:299
  50.6 9.7 %collective-permute-start.22 = (bf16[352,640]{1,0:T(8,128)(2,1)S(1)}, bf16[352,640]{1,0:T(8,128)(2,1)S(1)}, u32[]{:S(2)}, u32[]{:S(2)}) collective-permute-start(bf16[352,640]{1,0:T(8,128)(2,1)S(1)} %get-tuple-element.74), channel_id=1, source_target_pairs={{0,8},{4,20},{8,0},{12,28},{16,24},{20,4},{24,16},{28,12},{1,9},{5... | collective-permute-start | bytes 1351688 | tf_op jit(solution)/shard_map/ppermute | solution.py:299
  55.5 11.9 %collective-permute-start.29 = (bf16[352,640]{1,0:T(8,128)(2,1)S(1)}, bf16[352,640]{1,0:T(8,128)(2,1)S(1)}, u32[]{:S(2)}, u32[]{:S(2)}) collective-permute-start(bf16[352,640]{1,0:T(8,128)(2,1)S(1)} %collective-permute-done.18.refs_8_), channel_id=1, source_target_pairs={{0,4},{4,0},{8,12},{12,8},{16,20},{20,16},{24,28},{28,24},{1,5},{5... | collective-permute-start | bytes 1351688 | tf_op jit(solution)/shard_map/ppermute | solution.py:66
  55.5 11.9 %collective-permute-start.30 = (bf16[336,640]{1,0:T(8,128)(2,1)S(1)}, bf16[336,640]{1,0:T(8,128)(2,1)S(1)}, u32[]{:S(2)}, u32[]{:S(2)}) collective-permute-start(bf16[336,640]{1,0:T(8,128)(2,1)S(1)} %get-tuple-element.79), channel_id=1, source_target_pairs={{0,8},{4,20},{8,0},{12,28},{16,24},{20,4},{24,16},{28,12},{1,9},{5... | collective-permute-start | bytes 1290248 | tf_op jit(solution)/shard_map/ppermute | solution.py:299
  56.9 47.9 %collective-permute-start.19 = (bf16[1728,640]{1,0:T(8,128)(2,1)S(1)}, bf16[1728,640]{1,0:T(8,128)(2,1)S(1)}, u32[]{:S(2)}, u32[]{:S(2)}) collective-permute-start(bf16[1728,640]{1,0:T(8,128)(2,1)S(1)} %get-tuple-element.69.refs_0_.refs_1_), channel_id=1, source_target_pairs={{0,4},{4,0},{8,12},{12,8},{16,20},{20,16},{24,28},{28,24},{1,5},{5... | collective-permute-start | bytes 6635528 | tf_op jit(solution)/shard_map/ppermute | solution.py:66
  60.3 8.8 %collective-permute-start.23 = (bf16[352,640]{1,0:T(8,128)(2,1)S(1)}, bf16[352,640]{1,0:T(8,128)(2,1)S(1)}, u32[]{:S(2)}, u32[]{:S(2)}) collective-permute-start(bf16[352,640]{1,0:T(8,128)(2,1)S(1)} %get-tuple-element.73), channel_id=1, source_target_pairs={{0,16},{4,12},{8,24},{12,4},{16,0},{20,28},{24,8},{28,20},{1,17},{... | collective-permute-start | bytes 1351688 | tf_op jit(solution)/shard_map/ppermute | solution.py:299
  67.4 8.4 %collective-permute-start.31 = (bf16[352,640]{1,0:T(8,128)(2,1)S(1)}, bf16[352,640]{1,0:T(8,128)(2,1)S(1)}, u32[]{:S(2)}, u32[]{:S(2)}) collective-permute-start(bf16[352,640]{1,0:T(8,128)(2,1)S(1)} %get-tuple-element.78), channel_id=1, source_target_pairs={{0,16},{4,12},{8,24},{12,4},{16,0},{20,28},{24,8},{28,20},{1,17},{... | collective-permute-start | bytes 1351688 | tf_op jit(solution)/shard_map/ppermute | solution.py:299
  69.1 11.5 %collective-permute-start.26 = (bf16[352,640]{1,0:T(8,128)(2,1)S(1)}, bf16[352,640]{1,0:T(8,128)(2,1)S(1)}, u32[]{:S(2)}, u32[]{:S(2)}) collective-permute-start(bf16[352,640]{1,0:T(8,128)(2,1)S(1)} %get-tuple-element.74), channel_id=1, source_target_pairs={{0,16},{4,12},{8,24},{12,4},{16,0},{20,28},{24,8},{28,20},{1,17},{... | collective-permute-start | bytes 1351688 | tf_op jit(solution)/shard_map/ppermute | solution.py:299
  69.9 10.7 %collective-permute-start.24 = (bf16[352,640]{1,0:T(8,128)(2,1)S(1)}, bf16[352,640]{1,0:T(8,128)(2,1)S(1)}, u32[]{:S(2)}, u32[]{:S(2)}) collective-permute-start(bf16[352,640]{1,0:T(8,128)(2,1)S(1)} %collective-permute-done.23.refs_4_), channel_id=1, source_target_pairs={{0,4},{4,0},{8,12},{12,8},{16,20},{20,16},{24,28},{28,24},{1,5},{5... | collective-permute-start | bytes 1351688 | tf_op jit(solution)/shard_map/ppermute | solution.py:66
  75.8 9.4 %collective-permute-start.32 = (bf16[352,640]{1,0:T(8,128)(2,1)S(1)}, bf16[352,640]{1,0:T(8,128)(2,1)S(1)}, u32[]{:S(2)}, u32[]{:S(2)}) collective-permute-start(bf16[352,640]{1,0:T(8,128)(2,1)S(1)} %collective-permute-done.31.refs_10_), channel_id=1, source_target_pairs={{0,4},{4,0},{8,12},{12,8},{16,20},{20,16},{24,28},{28,24},{1,5},{5... | collective-permute-start | bytes 1351688 | tf_op jit(solution)/shard_map/ppermute | solution.py:66
  75.8 9.4 %collective-permute-start.34 = (bf16[336,640]{1,0:T(8,128)(2,1)S(1)}, bf16[336,640]{1,0:T(8,128)(2,1)S(1)}, u32[]{:S(2)}, u32[]{:S(2)}) collective-permute-start(bf16[336,640]{1,0:T(8,128)(2,1)S(1)} %get-tuple-element.79), channel_id=1, source_target_pairs={{0,16},{4,12},{8,24},{12,4},{16,0},{20,28},{24,8},{28,20},{1,17},{... | collective-permute-start | bytes 1290248 | tf_op jit(solution)/shard_map/ppermute | solution.py:299
  80.6 9.4 %collective-permute-start.27 = (bf16[352,640]{1,0:T(8,128)(2,1)S(1)}, bf16[352,640]{1,0:T(8,128)(2,1)S(1)}, u32[]{:S(2)}, u32[]{:S(2)}) collective-permute-start(bf16[352,640]{1,0:T(8,128)(2,1)S(1)} %collective-permute-done.20.refs_2_), channel_id=1, source_target_pairs={{0,16},{4,12},{8,24},{12,4},{16,0},{20,28},{24,8},{28,20},{1,17},{... | collective-permute-start | bytes 1351688 | tf_op jit(solution)/shard_map/ppermute | solution.py:299
  85.2 9.7 %collective-permute-start.35 = (bf16[352,640]{1,0:T(8,128)(2,1)S(1)}, bf16[352,640]{1,0:T(8,128)(2,1)S(1)}, u32[]{:S(2)}, u32[]{:S(2)}) collective-permute-start(bf16[352,640]{1,0:T(8,128)(2,1)S(1)} %collective-permute-done.18.refs_8_), channel_id=1, source_target_pairs={{0,16},{4,12},{8,24},{12,4},{16,0},{20,28},{24,8},{28,20},{1,17},{... | collective-permute-start | bytes 1351688 | tf_op jit(solution)/shard_map/ppermute | solution.py:299
  86.3 8.5 %collective-permute-start.40 = (bf16[336,640]{1,0:T(8,128)(2,1)S(1)}, bf16[336,640]{1,0:T(8,128)(2,1)S(1)}, u32[]{:S(2)}, u32[]{:S(2)}) collective-permute-start(bf16[336,640]{1,0:T(8,128)(2,1)S(1)} %collective-permute-done.34.refs_11_), channel_id=1, source_target_pairs={{0,4},{4,0},{8,12},{12,8},{16,20},{20,16},{24,28},{28,24},{1,5},{5... | collective-permute-start | bytes 1290248 | tf_op jit(solution)/shard_map/ppermute | solution.py:66
  90.0 9.7 %collective-permute-start.38 = (bf16[352,640]{1,0:T(8,128)(2,1)S(1)}, bf16[352,640]{1,0:T(8,128)(2,1)S(1)}, u32[]{:S(2)}, u32[]{:S(2)}) collective-permute-start(bf16[352,640]{1,0:T(8,128)(2,1)S(1)} %collective-permute-done.22.refs_3_), channel_id=1, source_target_pairs={{0,16},{4,12},{8,24},{12,4},{16,0},{20,28},{24,8},{28,20},{1,17},{... | collective-permute-start | bytes 1351688 | tf_op jit(solution)/shard_map/ppermute | solution.py:299
  91.1 9.0 %collective-permute-start.28 = (bf16[352,640]{1,0:T(8,128)(2,1)S(1)}, bf16[352,640]{1,0:T(8,128)(2,1)S(1)}, u32[]{:S(2)}, u32[]{:S(2)}) collective-permute-start(bf16[352,640]{1,0:T(8,128)(2,1)S(1)} %collective-permute-done.27.refs_6_), channel_id=1, source_target_pairs={{0,4},{4,0},{8,12},{12,8},{16,20},{20,16},{24,28},{28,24},{1,5},{5... | collective-permute-start | bytes 1351688 | tf_op jit(solution)/shard_map/ppermute | solution.py:66
  94.8 9.4 %collective-permute-start.36 = (bf16[352,640]{1,0:T(8,128)(2,1)S(1)}, bf16[352,640]{1,0:T(8,128)(2,1)S(1)}, u32[]{:S(2)}, u32[]{:S(2)}) collective-permute-start(bf16[352,640]{1,0:T(8,128)(2,1)S(1)} %collective-permute-done.35.refs_12_), channel_id=1, source_target_pairs={{0,4},{4,0},{8,12},{12,8},{16,20},{20,16},{24,28},{28,24},{1,5},{5... | collective-permute-start | bytes 1351688 | tf_op jit(solution)/shard_map/ppermute | solution.py:66
  94.9 9.4 %collective-permute-start.41 = (bf16[336,640]{1,0:T(8,128)(2,1)S(1)}, bf16[336,640]{1,0:T(8,128)(2,1)S(1)}, u32[]{:S(2)}, u32[]{:S(2)}) collective-permute-start(bf16[336,640]{1,0:T(8,128)(2,1)S(1)} %collective-permute-done.30.refs_9_), channel_id=1, source_target_pairs={{0,16},{4,12},{8,24},{12,4},{16,0},{20,28},{24,8},{28,20},{1,17},{... | collective-permute-start | bytes 1290248 | tf_op jit(solution)/shard_map/ppermute | solution.py:299
  99.7 9.7 %collective-permute-start.39 = (bf16[352,640]{1,0:T(8,128)(2,1)S(1)}, bf16[352,640]{1,0:T(8,128)(2,1)S(1)}, u32[]{:S(2)}, u32[]{:S(2)}) collective-permute-start(bf16[352,640]{1,0:T(8,128)(2,1)S(1)} %collective-permute-done.38.refs_7_), channel_id=1, source_target_pairs={{0,4},{4,0},{8,12},{12,8},{16,20},{20,16},{24,28},{28,24},{1,5},{5... | collective-permute-start | bytes 1351688 | tf_op jit(solution)/shard_map/ppermute | solution.py:66
  100.1 9.1 %collective-permute-start.44 = (bf16[336,640]{1,0:T(8,128)(2,1)S(1)}, bf16[336,640]{1,0:T(8,128)(2,1)S(1)}, u32[]{:S(2)}, u32[]{:S(2)}) collective-permute-start(bf16[336,640]{1,0:T(8,128)(2,1)S(1)} %get-tuple-element.84), channel_id=1, source_target_pairs={{0,16},{4,12},{8,24},{12,4},{16,0},{20,28},{24,8},{28,20},{1,17},{... | collective-permute-start | bytes 1290248 | tf_op jit(solution)/shard_map/ppermute | solution.py:299
  104.8 8.7 %collective-permute-start.46 = (bf16[336,640]{1,0:T(8,128)(2,1)S(1)}, bf16[336,640]{1,0:T(8,128)(2,1)S(1)}, u32[]{:S(2)}, u32[]{:S(2)}) collective-permute-start(bf16[336,640]{1,0:T(8,128)(2,1)S(1)} %shard_map.100.refs_15_), channel_id=1, source_target_pairs={{0,16},{4,12},{8,24},{12,4},{16,0},{20,28},{24,8},{28,20},{1,17},{... | collective-permute-start | bytes 1290248 | tf_op jit(solution)/shard_map/ppermute | solution.py:299
  (30 other events, 250.2 us)

commit v14 on v13

--- a/solution.py
+++ b/solution.py
@@ -23,7 +23,7 @@
 
 TURN_MASKS = ((2, 4), (4, 2))
 UPDATE_MASKS = tuple((k, k) for k in range(8))
-SWAP_MASKS = ((0, 0), (4, 2), (2, 4), (6, 6), (7, 7), (5, 3), (3, 5), (1, 1))
+SWAP_MASKS = ((0, 0), (6, 6), (7, 7), (4, 2), (2, 4), (5, 3), (3, 5), (1, 1))
 OWNER_MASKS = ((0, 0), (1, 1), (2, 4), (5, 3), (4, 2), (3, 5), (6, 6), (7, 7))
 
 
@@ -122,17 +122,28 @@
         out[...] = result[k * rows : (k + 1) * rows, :]
 
 
-def adam_kernel(moment_one, moment_two, *refs):
-    parts, (one_new, two_new, update) = refs[:-3], refs[-3:]
+def adam_kernel(moment_one, moment_two, *refs, outs):
+    parts, outs = refs[:-outs], refs[-outs:]
     grad = parts[0][...].astype(jnp.float32)
     for part in parts[1:]:
         grad = grad + part[...].astype(jnp.float32)
     one, two, value = adam(grad, moment_one[...], moment_two[...])
-    one_new[...] = one
-    two_new[...] = two
-    cols = value.shape[1]
-    update[...] = jnp.zeros_like(update)
-    update[:, :cols] = value
+    if len(outs) == 2:
+        outs[0][...] = one
+        outs[1][...] = two
+    else:
+        outs[0][:, outs[0].shape[1] - 128 :] = jnp.zeros((value.shape[0], 128), value.dtype)
+        outs[0][:, : value.shape[1]] = value
+
+
+def adam_call(moment_one, moment_two, parts, out_shape):
+    return pl.pallas_call(
+        functools.partial(adam_kernel, outs=len(out_shape)),
+        out_shape=out_shape,
+        in_specs=[VMEM] * (2 + len(parts)),
+        out_specs=[VMEM] * len(out_shape),
+        compiler_params=pltpu.CompilerParams(vmem_limit_bytes=16 * 2**20),
+    )(moment_one, moment_two, *parts)
 
 
 def expand(tall, slab, first, count):
@@ -322,18 +333,9 @@
     )(grad_out.T, *tokens)
     parts = lax.optimization_barrier((*parts, *ahead))[:n_dp]
     parts = [part if masks == (0, 0) else turn(part, masks) for part, masks in zip(parts, SWAP_MASKS)]
-    moment_one_new, moment_two_new, update = pl.pallas_call(
-        adam_kernel,
-        out_shape=[
-            jax.ShapeDtypeStruct(moment_one.shape, jnp.float32),
-            jax.ShapeDtypeStruct(moment_two.shape, jnp.float32),
-            jax.ShapeDtypeStruct((rows, wide), jnp.bfloat16),
-        ],
-        in_specs=[VMEM] * (2 + n_dp),
-        out_specs=[VMEM] * 3,
-        compiler_params=pltpu.CompilerParams(vmem_limit_bytes=16 * 2**20),
-    )(moment_one, moment_two, *parts)
-
+    (update,) = adam_call(
+        moment_one, moment_two, parts, [jax.ShapeDtypeStruct((rows, wide), jnp.bfloat16)]
+    )
     updates = {0: update}
     for k in (6, 2, 4, 1):
         updates[k] = hop(update, k)
@@ -347,6 +349,10 @@
     got = {(0, 0): ahead_weights(projection, tall, ahead)}
     over = {(0, 0): hop(got[(0, 0)], 1)}
     master_new = new_master(projection, master_t, tall, cols // 4)
+    moment_one_new, moment_two_new = adam_call(
+        moment_one, moment_two, [after(parts[0], [tall])] + parts[1:],
+        [jax.ShapeDtypeStruct(moment_one.shape, jnp.float32)] * 2,
+    )
 
     later = range(1, len(counts))
     steps = [(phase, at) for phase in range(3) for at in later] + [(1, 0), (2, 0)]
@@ -364,7 +370,7 @@
         earlier = [got[steps[step - 2]]] if step >= 2 else []
         earlier += [over[steps[step - 4]]] if step >= 4 else []
         if step == 2:
-            earlier.append(master_new)
+            earlier += [master_new, moment_one_new]
         got[(phase, at)] = turn(after(value, earlier), TURN_MASKS[min(phase, 1)])
         held = [outs[step - len(steps) + 3]] if step >= len(steps) - 2 else []
         over[(phase, at)] = hop(after(got[(phase, at)], held), 1)

time: 116 us -> 116 us (level)
    ppermute x22, waiting for transfers between devices: 47.4 us -> 45.6 us  [turn(): lax.ppermute(value, 'dp', [(i, i ^ masks[i & 1]) for i in range(n_dp)])]
  transfers between devices with their start and end apart: 48 -> 48, of which waited for: 25 -> 26; matrix products, arithmetic and copies ran while one was open for 0% -> 0% of each run, Pallas kernels for 12% -> 13%
where the time goes in v14:
time: 116 us
  waiting for transfers between devices  58.3 us (50%)
  starting transfers between devices  36.9 us (32%)
  Pallas kernels  19.2 us (17%)
    ppermute x22, waiting for transfers between devices, turn(): lax.ppermute(value, 'dp', [(i, i ^ masks[i & 1]) for i in range(n_dp)])  45.6 us
    ppermute x22, starting transfers between devices, turn(): lax.ppermute(value, 'dp', [(i, i ^ masks[i & 1]) for i in range(n_dp)])  27 us
    ppermute x26, waiting for transfers between devices, send(): return lax.ppermute(value, axis, [(i, i ^ mask) for i in range(size)])  12.6 us
    ppermute x26, starting transfers between devices, send(): return lax.ppermute(value, axis, [(i, i ^ mask) for i in range(size)])  9.88 us
    pallas_call x4, Pallas kernels, lay(): pl.pallas_call(functools.partial(lay_kernel, places=tuple(places), fresh=...  8.48 us
    pallas_call x1, Pallas kernels, new_master(): pl.pallas_call(master_kernel, out_shape=jax.ShapeDtypeStruct((cols, slab_...  3.12 us
    pallas_call x2, Pallas kernels, weights(): pl.pallas_call(functools.partial(weight_kernel, n_in=len(pieces), spans=s...  3.03 us
  transfers between devices with their start and end apart: 48, of which 26 were waited for; matrix products, arithmetic and copies ran while one was open for 0% of the time, Pallas kernels for 13%

profile of v14, /device:TPU:0, one launch (start us, length us, event | category | flops | bytes accessed | tf_op | source)
XLA Modules:
  0.0 115.8 jit_solution(25195762559394492)
XLA Ops:
  0.7 2.2 %shard_map.93 = f32[336,640]{1,0:T(8,128)} custom-call(f32[1728,640]{1,0:T(8,128)} %bitcast.6), custom_call_target="tpu_custom_call" | custom-call | tf_op jit(solution)/shard_map/pallas_call | solution.py:93
  2.9 3.0 %collective-permute-start.3 = (f32[336,640]{1,0:T(8,128)}, f32[336,640]{1,0:T(8,128)S(1)}, u32[]{:S(2)}, u32[]{:S(2)}) collective-permute-start(f32[336,640]{1,0:T(8,128)} %shard_map.93), channel_id=1, source_target_pairs={{0,8},{4,20},{8,0},{12,28},{16,24},{20,4},{24,16},{28,12},{1,9},{5... | collective-permute-start | bytes 2580488 | tf_op jit(solution)/shard_map/ppermute | solution.py:310
  8.0 2.6 %collective-permute-start.1 = (bf16[128,256]{1,0:T(8,128)(2,1)S(1)}, bf16[128,256]{1,0:T(8,128)(2,1)S(1)}, u32[]{:S(2)}, u32[]{:S(2)}) collective-permute-start(bf16[128,256]{1,0:T(8,128)(2,1)S(1)} %convolution_convert_fusion.refs_0_), channel_id=1, source_target_pairs={{0,2},{1,3},{2,0},{3,1},{4,6},{5,7},{6,4},{7,5},{8,10},{9,11},{10,... | collective-permute-start | bytes 196616 | tf_op jit(solution)/shard_map/ppermute | solution.py:66
  10.8 4.2 %collective-permute-done.1.refs_2_ = bf16[128,256]{1,0:T(8,128)(2,1)S(1)} collective-permute-done((bf16[128,256]{1,0:T(8,128)(2,1)S(1)}, bf16[128,256]{1,0:T(8,128)(2,1)S(1)}, u32[]{:S(2)}, u32[]{:S(2)}) %collective-permute-start.1) | collective-permute-done | bytes 65568 | tf_op jit(solution)/shard_map/ppermute | solution.py:66
  15.0 1.6 %collective-permute-done.2.refs_3_ = bf16[128,256]{1,0:T(8,128)(2,1)S(1)} collective-permute-done((bf16[128,256]{1,0:T(8,128)(2,1)S(1)}, bf16[128,256]{1,0:T(8,128)(2,1)S(1)}, u32[]{:S(2)}, u32[]{:S(2)}) %collective-permute-start.2) | collective-permute-done | bytes 65568 | tf_op jit(solution)/shard_map/ppermute | solution.py:66
  17.5 2.3 %collective-permute-start.4 = (bf16[32,1728]{1,0:T(8,128)(2,1)S(1)}, bf16[32,1728]{1,0:T(8,128)(2,1)S(1)}, u32[]{:S(2)}, u32[]{:S(2)}) collective-permute-start(bf16[32,1728]{1,0:T(8,128)(2,1)S(1)} %get-tuple-element.56), channel_id=1, source_target_pairs={{0,24},{4,28},{8,16},{12,20},{16,8},{20,12},{24,0},{28,4},{1,25},{... | collective-permute-start | bytes 331784 | tf_op jit(solution)/shard_map/ppermute | solution.py:310
  23.4 2.9 %collective-permute-done.5.refs_2_ = bf16[32,1728]{1,0:T(8,128)(2,1)S(1)} collective-permute-done((bf16[32,1728]{1,0:T(8,128)(2,1)S(1)}, bf16[32,1728]{1,0:T(8,128)(2,1)S(1)}, u32[]{:S(2)}, u32[]{:S(2)}) %collective-permute-start.5) | collective-permute-done | bytes 110624 | tf_op jit(solution)/shard_map/ppermute | solution.py:310
  26.3 1.8 %collective-permute-done.6.refs_3_ = bf16[32,1728]{1,0:T(8,128)(2,1)S(1)} collective-permute-done((bf16[32,1728]{1,0:T(8,128)(2,1)S(1)}, bf16[32,1728]{1,0:T(8,128)(2,1)S(1)}, u32[]{:S(2)}, u32[]{:S(2)}) %collective-permute-start.6) | collective-permute-done | bytes 110624 | tf_op jit(solution)/shard_map/ppermute | solution.py:310
  34.5 1.9 %collective-permute-done.12.refs_2_ = bf16[32,1792]{1,0:T(8,128)(2,1)S(1)} collective-permute-done((bf16[32,1792]{1,0:T(8,128)(2,1)S(1)}, bf16[32,1792]{1,0:T(8,128)(2,1)S(1)}, u32[]{:S(2)}, u32[]{:S(2)}) %collective-permute-start.12) | collective-permute-done | bytes 114720 | tf_op jit(solution)/shard_map/ppermute | solution.py:66
  36.3 3.3 %collective-permute-done.14.refs_4_ = bf16[32,1792]{1,0:T(8,128)(2,1)S(1)} collective-permute-done((bf16[32,1792]{1,0:T(8,128)(2,1)S(1)}, bf16[32,1792]{1,0:T(8,128)(2,1)S(1)}, u32[]{:S(2)}, u32[]{:S(2)}) %collective-permute-start.14) | collective-permute-done | bytes 114720 | tf_op jit(solution)/shard_map/ppermute | solution.py:66
  44.9 3.1 %shard_map.98 = f32[1728,640]{1,0:T(8,128)} custom-call(bf16[5120,256]{1,0:T(8,128)(2,1)S(1)} %copy-done.2, f32[1728,640]{1,0:T(8,128)S(1)} %bitcast.8, bf16[1792,256]{1,0:T(8,128)(2,1)S(1)} %get-tuple-element.63.tall.refs_0_), custom_call_target="tpu_custom_call" | custom-call | flops 566231040 | bytes 8847360 | tf_op jit(solution)/shard_map/pallas_call | solution.py:240
  48.0 2.2 %shard_map.99 = (bf16[352,640]{1,0:T(8,128)(2,1)S(1)}, bf16[336,640]{1,0:T(8,128)(2,1)S(1)}, bf16[336,640]{1,0:T(8,128)(2,1)S(1)}, bf16[1728,640]{1,0:T(8,128)(2,1)S(1)}) custom-call(bf16[5120,256]{1,0:T(8,128)(2,1)S(1)} %copy-done.2, f32[1728,640]{1,0:T(8,128)S(1)} %bitcast.9, bf16[1792,256]{1,0:T(8,128)(2,1)S(1)} %get-tuple-element.63.tall.refs_0_), custom_call_target="tpu_custom_call" | custom-call | flops 901775360 | bytes 7045120 | tf_op jit(solution)/shard_map/pallas_call | solution.py:188
  51.4 3.8 %collective-permute-done.18.refs_8_ = bf16[352,640]{1,0:T(8,128)(2,1)S(1)} collective-permute-done((bf16[352,640]{1,0:T(8,128)(2,1)S(1)}, bf16[352,640]{1,0:T(8,128)(2,1)S(1)}, u32[]{:S(2)}, u32[]{:S(2)}) %collective-permute-start.18) | collective-permute-done | bytes 450592 | tf_op jit(solution)/shard_map/ppermute | solution.py:310
  56.9 3.2 %collective-permute-done.22.refs_3_ = bf16[352,640]{1,0:T(8,128)(2,1)S(1)} collective-permute-done((bf16[352,640]{1,0:T(8,128)(2,1)S(1)}, bf16[352,640]{1,0:T(8,128)(2,1)S(1)}, u32[]{:S(2)}, u32[]{:S(2)}) %collective-permute-start.22) | collective-permute-done | bytes 450592 | tf_op jit(solution)/shard_map/ppermute | solution.py:310
  61.5 5.6 %collective-permute-done.30.refs_9_ = bf16[336,640]{1,0:T(8,128)(2,1)S(1)} collective-permute-done((bf16[336,640]{1,0:T(8,128)(2,1)S(1)}, bf16[336,640]{1,0:T(8,128)(2,1)S(1)}, u32[]{:S(2)}, u32[]{:S(2)}) %collective-permute-start.30) | collective-permute-done | bytes 430112 | tf_op jit(solution)/shard_map/ppermute | solution.py:310
  70.3 5.2 %collective-permute-done.31.refs_10_ = bf16[352,640]{1,0:T(8,128)(2,1)S(1)} collective-permute-done((bf16[352,640]{1,0:T(8,128)(2,1)S(1)}, bf16[352,640]{1,0:T(8,128)(2,1)S(1)}, u32[]{:S(2)}, u32[]{:S(2)}) %collective-permute-start.31) | collective-permute-done | bytes 450592 | tf_op jit(solution)/shard_map/ppermute | solution.py:310
  76.9 3.4 %collective-permute-done.26.refs_5_ = bf16[352,640]{1,0:T(8,128)(2,1)S(1)} collective-permute-done((bf16[352,640]{1,0:T(8,128)(2,1)S(1)}, bf16[352,640]{1,0:T(8,128)(2,1)S(1)}, u32[]{:S(2)}, u32[]{:S(2)}) %collective-permute-start.26) | collective-permute-done | bytes 450592 | tf_op jit(solution)/shard_map/ppermute | solution.py:310
  81.7 3.2 %collective-permute-done.34.refs_11_ = bf16[336,640]{1,0:T(8,128)(2,1)S(1)} collective-permute-done((bf16[336,640]{1,0:T(8,128)(2,1)S(1)}, bf16[336,640]{1,0:T(8,128)(2,1)S(1)}, u32[]{:S(2)}, u32[]{:S(2)}) %collective-permute-start.34) | collective-permute-done | bytes 430112 | tf_op jit(solution)/shard_map/ppermute | solution.py:310
  86.3 3.4 %collective-permute-done.27.refs_6_ = bf16[352,640]{1,0:T(8,128)(2,1)S(1)} collective-permute-done((bf16[352,640]{1,0:T(8,128)(2,1)S(1)}, bf16[352,640]{1,0:T(8,128)(2,1)S(1)}, u32[]{:S(2)}, u32[]{:S(2)}) %collective-permute-start.27) | collective-permute-done | bytes 450592 | tf_op jit(solution)/shard_map/ppermute | solution.py:310
  91.2 3.4 %collective-permute-done.35.refs_12_ = bf16[352,640]{1,0:T(8,128)(2,1)S(1)} collective-permute-done((bf16[352,640]{1,0:T(8,128)(2,1)S(1)}, bf16[352,640]{1,0:T(8,128)(2,1)S(1)}, u32[]{:S(2)}, u32[]{:S(2)}) %collective-permute-start.35) | collective-permute-done | bytes 450592 | tf_op jit(solution)/shard_map/ppermute | solution.py:310
  96.0 3.4 %collective-permute-done.38.refs_7_ = bf16[352,640]{1,0:T(8,128)(2,1)S(1)} collective-permute-done((bf16[352,640]{1,0:T(8,128)(2,1)S(1)}, bf16[352,640]{1,0:T(8,128)(2,1)S(1)}, u32[]{:S(2)}, u32[]{:S(2)}) %collective-permute-start.38) | collective-permute-done | bytes 450592 | tf_op jit(solution)/shard_map/ppermute | solution.py:310
  101.3 2.7 %collective-permute-done.41.refs_13_ = bf16[336,640]{1,0:T(8,128)(2,1)S(1)} collective-permute-done((bf16[336,640]{1,0:T(8,128)(2,1)S(1)}, bf16[336,640]{1,0:T(8,128)(2,1)S(1)}, u32[]{:S(2)}, u32[]{:S(2)}) %collective-permute-start.41) | collective-permute-done | bytes 430112 | tf_op jit(solution)/shard_map/ppermute | solution.py:310
  105.9 3.3 %shard_map.100.refs_0_ = bf16[1728,5120]{1,0:T(8,128)(2,1)} custom-call(bf16[1728,640]{1,0:T(8,128)(2,1)S(1)} %get-tuple-element.69.refs_0_.refs_1_, bf16[1728,640]{1,0:T(8,128)(2,1)S(1)} %collective-permute-done.19.refs_1_.refs_2_, bf16[352,640]{1,0:T(8,128)(2,1)S(1)} %collective-permute-done.20.refs_2_, ...), custom_call_target="tpu_custom_call" | custom-call | bytes 16138240 | tf_op jit(solution)/shard_map/pallas_call | solution.py:286
  109.4 3.3 %shard_map.102.refs_0_ = bf16[1728,5120]{1,0:T(8,128)(2,1)} custom-call(bf16[1728,5120]{1,0:T(8,128)(2,1)} %shard_map.100.refs_0_, bf16[1728,640]{1,0:T(8,128)(2,1)S(1)} %get-tuple-element.69.refs_0_.refs_1_, bf16[1728,640]{1,0:T(8,128)(2,1)S(1)} %collective-permute-done.19.refs_1_.refs_2_, ...), custom_call_target="tpu_custom_call", output_to_operand_aliasing={{}: (0, {})} | custom-call | bytes 15810560 | tf_op jit(solution)/shard_map/pallas_call | solution.py:286
  (97 shorter events, 39.9 us)
Async XLA Ops:
  2.9 14.6 %collective-permute-start.3 = (f32[336,640]{1,0:T(8,128)}, f32[336,640]{1,0:T(8,128)S(1)}, u32[]{:S(2)}, u32[]{:S(2)}) collective-permute-start(f32[336,640]{1,0:T(8,128)} %shard_map.93), channel_id=1, source_target_pairs={{0,8},{4,20},{8,0},{12,28},{16,24},{20,4},{24,16},{28,12},{1,9},{5... | collective-permute-start | bytes 2580488 | tf_op jit(solution)/shard_map/ppermute | solution.py:310
  20.3 8.5 %collective-permute-start.7 = (bf16[32,1728]{1,0:T(8,128)(2,1)S(1)}, bf16[32,1728]{1,0:T(8,128)(2,1)S(1)}, u32[]{:S(2)}, u32[]{:S(2)}) collective-permute-start(bf16[32,1728]{1,0:T(8,128)(2,1)S(1)} %get-tuple-element.59), channel_id=1, source_target_pairs={{0,8},{4,20},{8,0},{12,28},{16,24},{20,4},{24,16},{28,12},{1,9},{5... | collective-permute-start | bytes 331784 | tf_op jit(solution)/shard_map/ppermute | solution.py:310
  21.6 8.5 %collective-permute-start.8 = (bf16[32,1728]{1,0:T(8,128)(2,1)S(1)}, bf16[32,1728]{1,0:T(8,128)(2,1)S(1)}, u32[]{:S(2)}, u32[]{:S(2)}) collective-permute-start(bf16[32,1728]{1,0:T(8,128)(2,1)S(1)} %get-tuple-element.60), channel_id=1, source_target_pairs={{0,20},{4,8},{8,28},{12,0},{16,4},{20,24},{24,12},{28,16},{1,21},{... | collective-permute-start | bytes 331784 | tf_op jit(solution)/shard_map/ppermute | solution.py:310
  41.9 8.5 %collective-permute-start.20 = (bf16[352,640]{1,0:T(8,128)(2,1)S(1)}, bf16[352,640]{1,0:T(8,128)(2,1)S(1)}, u32[]{:S(2)}, u32[]{:S(2)}) collective-permute-start(bf16[352,640]{1,0:T(8,128)(2,1)S(1)} %get-tuple-element.73), channel_id=1, source_target_pairs={{0,8},{4,20},{8,0},{12,28},{16,24},{20,4},{24,16},{28,12},{1,9},{5... | collective-permute-start | bytes 1351688 | tf_op jit(solution)/shard_map/ppermute | solution.py:310
  43.0 12.2 %collective-permute-start.18 = (bf16[352,640]{1,0:T(8,128)(2,1)S(1)}, bf16[352,640]{1,0:T(8,128)(2,1)S(1)}, u32[]{:S(2)}, u32[]{:S(2)}) collective-permute-start(bf16[352,640]{1,0:T(8,128)(2,1)S(1)} %get-tuple-element.78), channel_id=1, source_target_pairs={{0,8},{4,20},{8,0},{12,28},{16,24},{20,4},{24,16},{28,12},{1,9},{5... | collective-permute-start | bytes 1351688 | tf_op jit(solution)/shard_map/ppermute | solution.py:310
  50.4 9.7 %collective-permute-start.22 = (bf16[352,640]{1,0:T(8,128)(2,1)S(1)}, bf16[352,640]{1,0:T(8,128)(2,1)S(1)}, u32[]{:S(2)}, u32[]{:S(2)}) collective-permute-start(bf16[352,640]{1,0:T(8,128)(2,1)S(1)} %get-tuple-element.74), channel_id=1, source_target_pairs={{0,8},{4,20},{8,0},{12,28},{16,24},{20,4},{24,16},{28,12},{1,9},{5... | collective-permute-start | bytes 1351688 | tf_op jit(solution)/shard_map/ppermute | solution.py:310
  51.3 8.7 %collective-permute-start.21 = (bf16[352,640]{1,0:T(8,128)(2,1)S(1)}, bf16[352,640]{1,0:T(8,128)(2,1)S(1)}, u32[]{:S(2)}, u32[]{:S(2)}) collective-permute-start(bf16[352,640]{1,0:T(8,128)(2,1)S(1)} %collective-permute-done.20.refs_2_), channel_id=1, source_target_pairs={{0,4},{4,0},{8,12},{12,8},{16,20},{20,16},{24,28},{28,24},{1,5},{5... | collective-permute-start | bytes 1351688 | tf_op jit(solution)/shard_map/ppermute | solution.py:66
  55.2 11.9 %collective-permute-start.29 = (bf16[352,640]{1,0:T(8,128)(2,1)S(1)}, bf16[352,640]{1,0:T(8,128)(2,1)S(1)}, u32[]{:S(2)}, u32[]{:S(2)}) collective-permute-start(bf16[352,640]{1,0:T(8,128)(2,1)S(1)} %collective-permute-done.18.refs_8_), channel_id=1, source_target_pairs={{0,4},{4,0},{8,12},{12,8},{16,20},{20,16},{24,28},{28,24},{1,5},{5... | collective-permute-start | bytes 1351688 | tf_op jit(solution)/shard_map/ppermute | solution.py:66
  55.2 11.9 %collective-permute-start.30 = (bf16[336,640]{1,0:T(8,128)(2,1)S(1)}, bf16[336,640]{1,0:T(8,128)(2,1)S(1)}, u32[]{:S(2)}, u32[]{:S(2)}) collective-permute-start(bf16[336,640]{1,0:T(8,128)(2,1)S(1)} %get-tuple-element.79), channel_id=1, source_target_pairs={{0,8},{4,20},{8,0},{12,28},{16,24},{20,4},{24,16},{28,12},{1,9},{5... | collective-permute-start | bytes 1290248 | tf_op jit(solution)/shard_map/ppermute | solution.py:310
  56.2 48.3 %collective-permute-start.19 = (bf16[1728,640]{1,0:T(8,128)(2,1)S(1)}, bf16[1728,640]{1,0:T(8,128)(2,1)S(1)}, u32[]{:S(2)}, u32[]{:S(2)}) collective-permute-start(bf16[1728,640]{1,0:T(8,128)(2,1)S(1)} %get-tuple-element.69.refs_0_.refs_1_), channel_id=1, source_target_pairs={{0,4},{4,0},{8,12},{12,8},{16,20},{20,16},{24,28},{28,24},{1,5},{5... | collective-permute-start | bytes 6635528 | tf_op jit(solution)/shard_map/ppermute | solution.py:66
  60.0 8.8 %collective-permute-start.23 = (bf16[352,640]{1,0:T(8,128)(2,1)S(1)}, bf16[352,640]{1,0:T(8,128)(2,1)S(1)}, u32[]{:S(2)}, u32[]{:S(2)}) collective-permute-start(bf16[352,640]{1,0:T(8,128)(2,1)S(1)} %get-tuple-element.73), channel_id=1, source_target_pairs={{0,16},{4,12},{8,24},{12,4},{16,0},{20,28},{24,8},{28,20},{1,17},{... | collective-permute-start | bytes 1351688 | tf_op jit(solution)/shard_map/ppermute | solution.py:310
  68.8 11.5 %collective-permute-start.26 = (bf16[352,640]{1,0:T(8,128)(2,1)S(1)}, bf16[352,640]{1,0:T(8,128)(2,1)S(1)}, u32[]{:S(2)}, u32[]{:S(2)}) collective-permute-start(bf16[352,640]{1,0:T(8,128)(2,1)S(1)} %get-tuple-element.74), channel_id=1, source_target_pairs={{0,16},{4,12},{8,24},{12,4},{16,0},{20,28},{24,8},{28,20},{1,17},{... | collective-permute-start | bytes 1351688 | tf_op jit(solution)/shard_map/ppermute | solution.py:310
  70.3 10.0 %collective-permute-start.24 = (bf16[352,640]{1,0:T(8,128)(2,1)S(1)}, bf16[352,640]{1,0:T(8,128)(2,1)S(1)}, u32[]{:S(2)}, u32[]{:S(2)}) collective-permute-start(bf16[352,640]{1,0:T(8,128)(2,1)S(1)} %collective-permute-done.23.refs_4_), channel_id=1, source_target_pairs={{0,4},{4,0},{8,12},{12,8},{16,20},{20,16},{24,28},{28,24},{1,5},{5... | collective-permute-start | bytes 1351688 | tf_op jit(solution)/shard_map/ppermute | solution.py:66
  75.5 9.4 %collective-permute-start.32 = (bf16[352,640]{1,0:T(8,128)(2,1)S(1)}, bf16[352,640]{1,0:T(8,128)(2,1)S(1)}, u32[]{:S(2)}, u32[]{:S(2)}) collective-permute-start(bf16[352,640]{1,0:T(8,128)(2,1)S(1)} %collective-permute-done.31.refs_10_), channel_id=1, source_target_pairs={{0,4},{4,0},{8,12},{12,8},{16,20},{20,16},{24,28},{28,24},{1,5},{5... | collective-permute-start | bytes 1351688 | tf_op jit(solution)/shard_map/ppermute | solution.py:66
  75.5 9.4 %collective-permute-start.34 = (bf16[336,640]{1,0:T(8,128)(2,1)S(1)}, bf16[336,640]{1,0:T(8,128)(2,1)S(1)}, u32[]{:S(2)}, u32[]{:S(2)}) collective-permute-start(bf16[336,640]{1,0:T(8,128)(2,1)S(1)} %get-tuple-element.79), channel_id=1, source_target_pairs={{0,16},{4,12},{8,24},{12,4},{16,0},{20,28},{24,8},{28,20},{1,17},{... | collective-permute-start | bytes 1290248 | tf_op jit(solution)/shard_map/ppermute | solution.py:310
  80.3 9.4 %collective-permute-start.27 = (bf16[352,640]{1,0:T(8,128)(2,1)S(1)}, bf16[352,640]{1,0:T(8,128)(2,1)S(1)}, u32[]{:S(2)}, u32[]{:S(2)}) collective-permute-start(bf16[352,640]{1,0:T(8,128)(2,1)S(1)} %collective-permute-done.20.refs_2_), channel_id=1, source_target_pairs={{0,16},{4,12},{8,24},{12,4},{16,0},{20,28},{24,8},{28,20},{1,17},{... | collective-permute-start | bytes 1351688 | tf_op jit(solution)/shard_map/ppermute | solution.py:310
  84.9 9.7 %collective-permute-start.35 = (bf16[352,640]{1,0:T(8,128)(2,1)S(1)}, bf16[352,640]{1,0:T(8,128)(2,1)S(1)}, u32[]{:S(2)}, u32[]{:S(2)}) collective-permute-start(bf16[352,640]{1,0:T(8,128)(2,1)S(1)} %collective-permute-done.18.refs_8_), channel_id=1, source_target_pairs={{0,16},{4,12},{8,24},{12,4},{16,0},{20,28},{24,8},{28,20},{1,17},{... | collective-permute-start | bytes 1351688 | tf_op jit(solution)/shard_map/ppermute | solution.py:310
  89.7 9.7 %collective-permute-start.38 = (bf16[352,640]{1,0:T(8,128)(2,1)S(1)}, bf16[352,640]{1,0:T(8,128)(2,1)S(1)}, u32[]{:S(2)}, u32[]{:S(2)}) collective-permute-start(bf16[352,640]{1,0:T(8,128)(2,1)S(1)} %collective-permute-done.22.refs_3_), channel_id=1, source_target_pairs={{0,16},{4,12},{8,24},{12,4},{16,0},{20,28},{24,8},{28,20},{1,17},{... | collective-permute-start | bytes 1351688 | tf_op jit(solution)/shard_map/ppermute | solution.py:310
  91.2 8.7 %collective-permute-start.28 = (bf16[352,640]{1,0:T(8,128)(2,1)S(1)}, bf16[352,640]{1,0:T(8,128)(2,1)S(1)}, u32[]{:S(2)}, u32[]{:S(2)}) collective-permute-start(bf16[352,640]{1,0:T(8,128)(2,1)S(1)} %collective-permute-done.27.refs_6_), channel_id=1, source_target_pairs={{0,4},{4,0},{8,12},{12,8},{16,20},{20,16},{24,28},{28,24},{1,5},{5... | collective-permute-start | bytes 1351688 | tf_op jit(solution)/shard_map/ppermute | solution.py:66
  94.6 9.4 %collective-permute-start.36 = (bf16[352,640]{1,0:T(8,128)(2,1)S(1)}, bf16[352,640]{1,0:T(8,128)(2,1)S(1)}, u32[]{:S(2)}, u32[]{:S(2)}) collective-permute-start(bf16[352,640]{1,0:T(8,128)(2,1)S(1)} %collective-permute-done.35.refs_12_), channel_id=1, source_target_pairs={{0,4},{4,0},{8,12},{12,8},{16,20},{20,16},{24,28},{28,24},{1,5},{5... | collective-permute-start | bytes 1351688 | tf_op jit(solution)/shard_map/ppermute | solution.py:66
  94.6 9.4 %collective-permute-start.41 = (bf16[336,640]{1,0:T(8,128)(2,1)S(1)}, bf16[336,640]{1,0:T(8,128)(2,1)S(1)}, u32[]{:S(2)}, u32[]{:S(2)}) collective-permute-start(bf16[336,640]{1,0:T(8,128)(2,1)S(1)} %collective-permute-done.30.refs_9_), channel_id=1, source_target_pairs={{0,16},{4,12},{8,24},{12,4},{16,0},{20,28},{24,8},{28,20},{1,17},{... | collective-permute-start | bytes 1290248 | tf_op jit(solution)/shard_map/ppermute | solution.py:310
  99.4 10.0 %collective-permute-start.39 = (bf16[352,640]{1,0:T(8,128)(2,1)S(1)}, bf16[352,640]{1,0:T(8,128)(2,1)S(1)}, u32[]{:S(2)}, u32[]{:S(2)}) collective-permute-start(bf16[352,640]{1,0:T(8,128)(2,1)S(1)} %collective-permute-done.38.refs_7_), channel_id=1, source_target_pairs={{0,4},{4,0},{8,12},{12,8},{16,20},{20,16},{24,28},{28,24},{1,5},{5... | collective-permute-start | bytes 1351688 | tf_op jit(solution)/shard_map/ppermute | solution.py:66
  99.8 9.5 %collective-permute-start.44 = (bf16[336,640]{1,0:T(8,128)(2,1)S(1)}, bf16[336,640]{1,0:T(8,128)(2,1)S(1)}, u32[]{:S(2)}, u32[]{:S(2)}) collective-permute-start(bf16[336,640]{1,0:T(8,128)(2,1)S(1)} %get-tuple-element.84), channel_id=1, source_target_pairs={{0,16},{4,12},{8,24},{12,4},{16,0},{20,28},{24,8},{28,20},{1,17},{... | collective-permute-start | bytes 1290248 | tf_op jit(solution)/shard_map/ppermute | solution.py:310
  104.5 8.7 %collective-permute-start.46 = (bf16[336,640]{1,0:T(8,128)(2,1)S(1)}, bf16[336,640]{1,0:T(8,128)(2,1)S(1)}, u32[]{:S(2)}, u32[]{:S(2)}) collective-permute-start(bf16[336,640]{1,0:T(8,128)(2,1)S(1)} %shard_map.101.refs_15_), channel_id=1, source_target_pairs={{0,16},{4,12},{8,24},{12,4},{16,0},{20,28},{24,8},{28,20},{1,17},{... | collective-permute-start | bytes 1290248 | tf_op jit(solution)/shard_map/ppermute | solution.py:310
  (30 other events, 251.2 us)

commit v15 on v14

--- a/solution.py
+++ b/solution.py
@@ -23,14 +23,14 @@
 
 TURN_MASKS = ((2, 4), (4, 2))
 UPDATE_MASKS = tuple((k, k) for k in range(8))
-SWAP_MASKS = ((0, 0), (6, 6), (7, 7), (4, 2), (2, 4), (5, 3), (3, 5), (1, 1))
+SWAP_MASKS = ((0, 0), (4, 2), (2, 4), (6, 6), (7, 7), (5, 3), (3, 5), (1, 1))
 OWNER_MASKS = ((0, 0), (1, 1), (2, 4), (5, 3), (4, 2), (3, 5), (6, 6), (7, 7))
 
 
 def chunk_sizes(cols):
     small = cols // 80 * 16
     part = -(-(cols - 2 * small) // 48) * 16
-    return (small,), (small, part, part, cols - 2 * part - 2 * small, small)
+    return (small, part, part, cols - 2 * part - 2 * small, small)
 
 
 def adam(grad, moment_one, moment_two):
@@ -312,10 +312,10 @@
     def after(value, earlier):
         return lax.optimization_barrier((value, *earlier))[0] if earlier else value
 
-    early, counts = chunk_sizes(cols)
+    counts = chunk_sizes(cols)
     spans = [(sum(counts[:at]), count) for at, count in enumerate(counts)]
-    taken = take(master_t, early[0])
-    ahead = [turn(taken, TURN_MASKS[0])]
+    taken = take(master_t, counts[0])
+    ahead = turn(taken, TURN_MASKS[0])
     acts = after(acts, [taken])
 
     projected = jnp.dot(acts, projection, preferred_element_type=jnp.float32).astype(jnp.bfloat16)
@@ -331,7 +331,7 @@
         ],
         compiler_params=pltpu.CompilerParams(vmem_limit_bytes=16 * 2**20),
     )(grad_out.T, *tokens)
-    parts = lax.optimization_barrier((*parts, *ahead))[:n_dp]
+    parts = lax.optimization_barrier((*parts, ahead))[:n_dp]
     parts = [part if masks == (0, 0) else turn(part, masks) for part, masks in zip(parts, SWAP_MASKS)]
     (update,) = adam_call(
         moment_one, moment_two, parts, [jax.ShapeDtypeStruct((rows, wide), jnp.bfloat16)]
@@ -343,10 +343,11 @@
         updates[k ^ 1] = hop(updates[k], 1)
     updates = [updates[k] for k in range(n_dp)]
 
-    tall, *own = weights(projection, master_t, updates, spans[1:3])
+    tall, *own = weights(projection, master_t, updates, spans[1:2])
+    own += weights(projection, master_t, [tall], spans[2:3])
     *late, own_first, whole = weights(projection, master_t, [tall], spans[3:] + spans[:1] + [(0, cols)])
     own = [own_first] + own + late
-    got = {(0, 0): ahead_weights(projection, tall, ahead)}
+    got = {(0, 0): ahead_weights(projection, tall, [ahead])}
     over = {(0, 0): hop(got[(0, 0)], 1)}
     master_new = new_master(projection, master_t, tall, cols // 4)
     moment_one_new, moment_two_new = adam_call(

time: 116 us -> 115 us (level)
    pallas_call x2 -> x3, Pallas kernels: 3.03 us -> 3.18 us  [weights(): pl.pallas_call(functools.partial(weight_kernel, n_in=len(pieces), spans=s...]
  transfers between devices with their start and end apart: 48 -> 48, of which waited for: 26 -> 24; matrix products, arithmetic and copies ran while one was open for 0% -> 0% of each run, Pallas kernels for 13% -> 14%
where the time goes in v15:
time: 115 us
  waiting for transfers between devices  57.9 us (50%)
  starting transfers between devices  36.6 us (32%)
  Pallas kernels  19.3 us (17%)
    ppermute x22, waiting for transfers between devices, turn(): lax.ppermute(value, 'dp', [(i, i ^ masks[i & 1]) for i in range(n_dp)])  45.8 us
    ppermute x22, starting transfers between devices, turn(): lax.ppermute(value, 'dp', [(i, i ^ masks[i & 1]) for i in range(n_dp)])  26.7 us
    ppermute x26, waiting for transfers between devices, send(): return lax.ppermute(value, axis, [(i, i ^ mask) for i in range(size)])  12.1 us
    ppermute x26, starting transfers between devices, send(): return lax.ppermute(value, axis, [(i, i ^ mask) for i in range(size)])  9.98 us
    pallas_call x4, Pallas kernels, lay(): pl.pallas_call(functools.partial(lay_kernel, places=tuple(places), fresh=...  8.48 us
    pallas_call x3, Pallas kernels, weights(): pl.pallas_call(functools.partial(weight_kernel, n_in=len(pieces), spans=s...  3.18 us
    pallas_call x1, Pallas kernels, new_master(): pl.pallas_call(master_kernel, out_shape=jax.ShapeDtypeStruct((cols, slab_...  3.12 us
  transfers between devices with their start and end apart: 48, of which 24 were waited for; matrix products, arithmetic and copies ran while one was open for 0% of the time, Pallas kernels for 14%

profile of v15, /device:TPU:0, one launch (start us, length us, event | category | flops | bytes accessed | tf_op | source)
XLA Modules:
  0.0 115.2 jit_solution(6457878844864001581)
XLA Ops:
  0.7 2.2 %shard_map.93 = f32[336,640]{1,0:T(8,128)} custom-call(f32[1728,640]{1,0:T(8,128)} %bitcast.6), custom_call_target="tpu_custom_call" | custom-call | tf_op jit(solution)/shard_map/pallas_call | solution.py:93
  2.9 3.0 %collective-permute-start.3 = (f32[336,640]{1,0:T(8,128)}, f32[336,640]{1,0:T(8,128)S(1)}, u32[]{:S(2)}, u32[]{:S(2)}) collective-permute-start(f32[336,640]{1,0:T(8,128)} %shard_map.93), channel_id=1, source_target_pairs={{0,8},{4,20},{8,0},{12,28},{16,24},{20,4},{24,16},{28,12},{1,9},{5... | collective-permute-start | bytes 2580488 | tf_op jit(solution)/shard_map/ppermute | solution.py:310
  8.0 2.6 %collective-permute-start.1 = (bf16[128,256]{1,0:T(8,128)(2,1)S(1)}, bf16[128,256]{1,0:T(8,128)(2,1)S(1)}, u32[]{:S(2)}, u32[]{:S(2)}) collective-permute-start(bf16[128,256]{1,0:T(8,128)(2,1)S(1)} %convolution_convert_fusion.refs_0_), channel_id=1, source_target_pairs={{0,2},{1,3},{2,0},{3,1},{4,6},{5,7},{6,4},{7,5},{8,10},{9,11},{10,... | collective-permute-start | bytes 196616 | tf_op jit(solution)/shard_map/ppermute | solution.py:66
  10.8 4.2 %collective-permute-done.1.refs_2_ = bf16[128,256]{1,0:T(8,128)(2,1)S(1)} collective-permute-done((bf16[128,256]{1,0:T(8,128)(2,1)S(1)}, bf16[128,256]{1,0:T(8,128)(2,1)S(1)}, u32[]{:S(2)}, u32[]{:S(2)}) %collective-permute-start.1) | collective-permute-done | bytes 65568 | tf_op jit(solution)/shard_map/ppermute | solution.py:66
  21.1 2.5 %collective-permute-start.8 = (bf16[32,1728]{1,0:T(8,128)(2,1)S(1)}, bf16[32,1728]{1,0:T(8,128)(2,1)S(1)}, u32[]{:S(2)}, u32[]{:S(2)}) collective-permute-start(bf16[32,1728]{1,0:T(8,128)(2,1)S(1)} %get-tuple-element.59), channel_id=1, source_target_pairs={{0,20},{4,8},{8,28},{12,0},{16,4},{20,24},{24,12},{28,16},{1,21},{... | collective-permute-start | bytes 331784 | tf_op jit(solution)/shard_map/ppermute | solution.py:310
  25.5 1.8 %collective-permute-done.6.refs_3_ = bf16[32,1728]{1,0:T(8,128)(2,1)S(1)} collective-permute-done((bf16[32,1728]{1,0:T(8,128)(2,1)S(1)}, bf16[32,1728]{1,0:T(8,128)(2,1)S(1)}, u32[]{:S(2)}, u32[]{:S(2)}) %collective-permute-start.6) | collective-permute-done | bytes 110624 | tf_op jit(solution)/shard_map/ppermute | solution.py:310
  27.4 2.5 %collective-permute-done.8.refs_5_ = bf16[32,1728]{1,0:T(8,128)(2,1)S(1)} collective-permute-done((bf16[32,1728]{1,0:T(8,128)(2,1)S(1)}, bf16[32,1728]{1,0:T(8,128)(2,1)S(1)}, u32[]{:S(2)}, u32[]{:S(2)}) %collective-permute-start.8) | collective-permute-done | bytes 110624 | tf_op jit(solution)/shard_map/ppermute | solution.py:310
  33.1 1.7 %collective-permute-start.16 = (bf16[32,1792]{1,0:T(8,128)(2,1)S(1)}, bf16[32,1792]{1,0:T(8,128)(2,1)S(1)}, u32[]{:S(2)}, u32[]{:S(2)}) collective-permute-start(bf16[32,1792]{1,0:T(8,128)(2,1)S(1)} %shard_map.95.refs_0_), channel_id=1, source_target_pairs={{0,24},{4,28},{8,16},{12,20},{16,8},{20,12},{24,0},{28,4},{1,25},{... | collective-permute-start | bytes 344072 | tf_op jit(solution)/shard_map/ppermute | solution.py:66
  34.8 2.5 %collective-permute-done.12.refs_2_ = bf16[32,1792]{1,0:T(8,128)(2,1)S(1)} collective-permute-done((bf16[32,1792]{1,0:T(8,128)(2,1)S(1)}, bf16[32,1792]{1,0:T(8,128)(2,1)S(1)}, u32[]{:S(2)}, u32[]{:S(2)}) %collective-permute-start.12) | collective-permute-done | bytes 114720 | tf_op jit(solution)/shard_map/ppermute | solution.py:66
  37.3 2.0 %collective-permute-done.14.refs_4_ = bf16[32,1792]{1,0:T(8,128)(2,1)S(1)} collective-permute-done((bf16[32,1792]{1,0:T(8,128)(2,1)S(1)}, bf16[32,1792]{1,0:T(8,128)(2,1)S(1)}, u32[]{:S(2)}, u32[]{:S(2)}) %collective-permute-start.14) | collective-permute-done | bytes 114720 | tf_op jit(solution)/shard_map/ppermute | solution.py:66
  44.8 3.1 %shard_map.98 = f32[1728,640]{1,0:T(8,128)} custom-call(bf16[5120,256]{1,0:T(8,128)(2,1)S(1)} %copy-done.2, f32[1728,640]{1,0:T(8,128)S(1)} %bitcast.9, bf16[1792,256]{1,0:T(8,128)(2,1)S(1)} %get-tuple-element.62.tall.refs_0_), custom_call_target="tpu_custom_call" | custom-call | flops 566231040 | bytes 8847360 | tf_op jit(solution)/shard_map/pallas_call | solution.py:240
  48.0 2.2 %shard_map.99 = (bf16[352,640]{1,0:T(8,128)(2,1)S(1)}, bf16[336,640]{1,0:T(8,128)(2,1)S(1)}, bf16[336,640]{1,0:T(8,128)(2,1)S(1)}, bf16[1728,640]{1,0:T(8,128)(2,1)S(1)}) custom-call(bf16[5120,256]{1,0:T(8,128)(2,1)S(1)} %copy-done.2, f32[1728,640]{1,0:T(8,128)S(1)} %bitcast.10, bf16[1792,256]{1,0:T(8,128)(2,1)S(1)} %get-tuple-element.62.tall.refs_0_), custom_call_target="tpu_custom_call" | custom-call | flops 901775360 | bytes 7045120 | tf_op jit(solution)/shard_map/pallas_call | solution.py:188
  51.7 3.0 %collective-permute-done.18.refs_8_ = bf16[352,640]{1,0:T(8,128)(2,1)S(1)} collective-permute-done((bf16[352,640]{1,0:T(8,128)(2,1)S(1)}, bf16[352,640]{1,0:T(8,128)(2,1)S(1)}, u32[]{:S(2)}, u32[]{:S(2)}) %collective-permute-start.18) | collective-permute-done | bytes 450592 | tf_op jit(solution)/shard_map/ppermute | solution.py:310
  56.0 3.4 %collective-permute-done.22.refs_3_ = bf16[352,640]{1,0:T(8,128)(2,1)S(1)} collective-permute-done((bf16[352,640]{1,0:T(8,128)(2,1)S(1)}, bf16[352,640]{1,0:T(8,128)(2,1)S(1)}, u32[]{:S(2)}, u32[]{:S(2)}) %collective-permute-start.22) | collective-permute-done | bytes 450592 | tf_op jit(solution)/shard_map/ppermute | solution.py:310
  60.4 6.1 %collective-permute-done.30.refs_9_ = bf16[336,640]{1,0:T(8,128)(2,1)S(1)} collective-permute-done((bf16[336,640]{1,0:T(8,128)(2,1)S(1)}, bf16[336,640]{1,0:T(8,128)(2,1)S(1)}, u32[]{:S(2)}, u32[]{:S(2)}) %collective-permute-start.30) | collective-permute-done | bytes 430112 | tf_op jit(solution)/shard_map/ppermute | solution.py:310
  69.8 5.1 %collective-permute-done.31.refs_10_ = bf16[352,640]{1,0:T(8,128)(2,1)S(1)} collective-permute-done((bf16[352,640]{1,0:T(8,128)(2,1)S(1)}, bf16[352,640]{1,0:T(8,128)(2,1)S(1)}, u32[]{:S(2)}, u32[]{:S(2)}) %collective-permute-start.31) | collective-permute-done | bytes 450592 | tf_op jit(solution)/shard_map/ppermute | solution.py:310
  76.0 3.7 %collective-permute-done.26.refs_5_ = bf16[352,640]{1,0:T(8,128)(2,1)S(1)} collective-permute-done((bf16[352,640]{1,0:T(8,128)(2,1)S(1)}, bf16[352,640]{1,0:T(8,128)(2,1)S(1)}, u32[]{:S(2)}, u32[]{:S(2)}) %collective-permute-start.26) | collective-permute-done | bytes 450592 | tf_op jit(solution)/shard_map/ppermute | solution.py:310
  80.9 3.5 %collective-permute-done.34.refs_11_ = bf16[336,640]{1,0:T(8,128)(2,1)S(1)} collective-permute-done((bf16[336,640]{1,0:T(8,128)(2,1)S(1)}, bf16[336,640]{1,0:T(8,128)(2,1)S(1)}, u32[]{:S(2)}, u32[]{:S(2)}) %collective-permute-start.34) | collective-permute-done | bytes 430112 | tf_op jit(solution)/shard_map/ppermute | solution.py:310
  85.5 3.7 %collective-permute-done.27.refs_6_ = bf16[352,640]{1,0:T(8,128)(2,1)S(1)} collective-permute-done((bf16[352,640]{1,0:T(8,128)(2,1)S(1)}, bf16[352,640]{1,0:T(8,128)(2,1)S(1)}, u32[]{:S(2)}, u32[]{:S(2)}) %collective-permute-start.27) | collective-permute-done | bytes 450592 | tf_op jit(solution)/shard_map/ppermute | solution.py:310
  90.3 3.7 %collective-permute-done.35.refs_12_ = bf16[352,640]{1,0:T(8,128)(2,1)S(1)} collective-permute-done((bf16[352,640]{1,0:T(8,128)(2,1)S(1)}, bf16[352,640]{1,0:T(8,128)(2,1)S(1)}, u32[]{:S(2)}, u32[]{:S(2)}) %collective-permute-start.35) | collective-permute-done | bytes 450592 | tf_op jit(solution)/shard_map/ppermute | solution.py:310
  95.1 3.7 %collective-permute-done.38.refs_7_ = bf16[352,640]{1,0:T(8,128)(2,1)S(1)} collective-permute-done((bf16[352,640]{1,0:T(8,128)(2,1)S(1)}, bf16[352,640]{1,0:T(8,128)(2,1)S(1)}, u32[]{:S(2)}, u32[]{:S(2)}) %collective-permute-start.38) | collective-permute-done | bytes 450592 | tf_op jit(solution)/shard_map/ppermute | solution.py:310
  100.5 3.0 %collective-permute-done.41.refs_13_ = bf16[336,640]{1,0:T(8,128)(2,1)S(1)} collective-permute-done((bf16[336,640]{1,0:T(8,128)(2,1)S(1)}, bf16[336,640]{1,0:T(8,128)(2,1)S(1)}, u32[]{:S(2)}, u32[]{:S(2)}) %collective-permute-start.41) | collective-permute-done | bytes 430112 | tf_op jit(solution)/shard_map/ppermute | solution.py:310
  105.1 3.3 %shard_map.101.refs_0_ = bf16[1728,5120]{1,0:T(8,128)(2,1)} custom-call(bf16[1728,640]{1,0:T(8,128)(2,1)S(1)} %get-tuple-element.67.refs_0_.refs_1_, bf16[1728,640]{1,0:T(8,128)(2,1)S(1)} %collective-permute-done.19.refs_1_.refs_2_, bf16[352,640]{1,0:T(8,128)(2,1)S(1)} %collective-permute-done.20.refs_2_, ...), custom_call_target="tpu_custom_call" | custom-call | bytes 16138240 | tf_op jit(solution)/shard_map/pallas_call | solution.py:286
  108.5 3.3 %shard_map.103.refs_0_ = bf16[1728,5120]{1,0:T(8,128)(2,1)} custom-call(bf16[1728,5120]{1,0:T(8,128)(2,1)} %shard_map.101.refs_0_, bf16[1728,640]{1,0:T(8,128)(2,1)S(1)} %get-tuple-element.67.refs_0_.refs_1_, bf16[1728,640]{1,0:T(8,128)(2,1)S(1)} %collective-permute-done.19.refs_1_.refs_2_, ...), custom_call_target="tpu_custom_call", output_to_operand_aliasing={{}: (0, {})} | custom-call | bytes 15810560 | tf_op jit(solution)/shard_map/pallas_call | solution.py:286
  (98 shorter events, 38.6 us)
Async XLA Ops:
  2.9 14.6 %collective-permute-start.3 = (f32[336,640]{1,0:T(8,128)}, f32[336,640]{1,0:T(8,128)S(1)}, u32[]{:S(2)}, u32[]{:S(2)}) collective-permute-start(f32[336,640]{1,0:T(8,128)} %shard_map.93), channel_id=1, source_target_pairs={{0,8},{4,20},{8,0},{12,28},{16,24},{20,4},{24,16},{28,12},{1,9},{5... | collective-permute-start | bytes 2580488 | tf_op jit(solution)/shard_map/ppermute | solution.py:310
  21.1 8.9 %collective-permute-start.8 = (bf16[32,1728]{1,0:T(8,128)(2,1)S(1)}, bf16[32,1728]{1,0:T(8,128)(2,1)S(1)}, u32[]{:S(2)}, u32[]{:S(2)}) collective-permute-start(bf16[32,1728]{1,0:T(8,128)(2,1)S(1)} %get-tuple-element.59), channel_id=1, source_target_pairs={{0,20},{4,8},{8,28},{12,0},{16,4},{20,24},{24,12},{28,16},{1,21},{... | collective-permute-start | bytes 331784 | tf_op jit(solution)/shard_map/ppermute | solution.py:310
  41.3 8.9 %collective-permute-start.20 = (bf16[352,640]{1,0:T(8,128)(2,1)S(1)}, bf16[352,640]{1,0:T(8,128)(2,1)S(1)}, u32[]{:S(2)}, u32[]{:S(2)}) collective-permute-start(bf16[352,640]{1,0:T(8,128)(2,1)S(1)} %get-tuple-element.71), channel_id=1, source_target_pairs={{0,8},{4,20},{8,0},{12,28},{16,24},{20,4},{24,16},{28,12},{1,9},{5... | collective-permute-start | bytes 1351688 | tf_op jit(solution)/shard_map/ppermute | solution.py:310
  43.2 11.4 %collective-permute-start.18 = (bf16[352,640]{1,0:T(8,128)(2,1)S(1)}, bf16[352,640]{1,0:T(8,128)(2,1)S(1)}, u32[]{:S(2)}, u32[]{:S(2)}) collective-permute-start(bf16[352,640]{1,0:T(8,128)(2,1)S(1)} %shard_map.100), channel_id=1, source_target_pairs={{0,8},{4,20},{8,0},{12,28},{16,24},{20,4},{24,16},{28,12},{1,9},{5... | collective-permute-start | bytes 1351688 | tf_op jit(solution)/shard_map/ppermute | solution.py:310
  50.2 9.2 %collective-permute-start.22 = (bf16[352,640]{1,0:T(8,128)(2,1)S(1)}, bf16[352,640]{1,0:T(8,128)(2,1)S(1)}, u32[]{:S(2)}, u32[]{:S(2)}) collective-permute-start(bf16[352,640]{1,0:T(8,128)(2,1)S(1)} %get-tuple-element.72), channel_id=1, source_target_pairs={{0,8},{4,20},{8,0},{12,28},{16,24},{20,4},{24,16},{28,12},{1,9},{5... | collective-permute-start | bytes 1351688 | tf_op jit(solution)/shard_map/ppermute | solution.py:310
  54.6 11.9 %collective-permute-start.29 = (bf16[352,640]{1,0:T(8,128)(2,1)S(1)}, bf16[352,640]{1,0:T(8,128)(2,1)S(1)}, u32[]{:S(2)}, u32[]{:S(2)}) collective-permute-start(bf16[352,640]{1,0:T(8,128)(2,1)S(1)} %collective-permute-done.18.refs_8_), channel_id=1, source_target_pairs={{0,4},{4,0},{8,12},{12,8},{16,20},{20,16},{24,28},{28,24},{1,5},{5... | collective-permute-start | bytes 1351688 | tf_op jit(solution)/shard_map/ppermute | solution.py:66
  54.6 11.9 %collective-permute-start.30 = (bf16[336,640]{1,0:T(8,128)(2,1)S(1)}, bf16[336,640]{1,0:T(8,128)(2,1)S(1)}, u32[]{:S(2)}, u32[]{:S(2)}) collective-permute-start(bf16[336,640]{1,0:T(8,128)(2,1)S(1)} %get-tuple-element.77), channel_id=1, source_target_pairs={{0,8},{4,20},{8,0},{12,28},{16,24},{20,4},{24,16},{28,12},{1,9},{5... | collective-permute-start | bytes 1290248 | tf_op jit(solution)/shard_map/ppermute | solution.py:310
  56.0 47.9 %collective-permute-start.19 = (bf16[1728,640]{1,0:T(8,128)(2,1)S(1)}, bf16[1728,640]{1,0:T(8,128)(2,1)S(1)}, u32[]{:S(2)}, u32[]{:S(2)}) collective-permute-start(bf16[1728,640]{1,0:T(8,128)(2,1)S(1)} %get-tuple-element.67.refs_0_.refs_1_), channel_id=1, source_target_pairs={{0,4},{4,0},{8,12},{12,8},{16,20},{20,16},{24,28},{28,24},{1,5},{5... | collective-permute-start | bytes 6635528 | tf_op jit(solution)/shard_map/ppermute | solution.py:66
  59.5 8.8 %collective-permute-start.23 = (bf16[352,640]{1,0:T(8,128)(2,1)S(1)}, bf16[352,640]{1,0:T(8,128)(2,1)S(1)}, u32[]{:S(2)}, u32[]{:S(2)}) collective-permute-start(bf16[352,640]{1,0:T(8,128)(2,1)S(1)} %get-tuple-element.71), channel_id=1, source_target_pairs={{0,16},{4,12},{8,24},{12,4},{16,0},{20,28},{24,8},{28,20},{1,17},{... | collective-permute-start | bytes 1351688 | tf_op jit(solution)/shard_map/ppermute | solution.py:310
  66.5 8.4 %collective-permute-start.31 = (bf16[352,640]{1,0:T(8,128)(2,1)S(1)}, bf16[352,640]{1,0:T(8,128)(2,1)S(1)}, u32[]{:S(2)}, u32[]{:S(2)}) collective-permute-start(bf16[352,640]{1,0:T(8,128)(2,1)S(1)} %shard_map.100), channel_id=1, source_target_pairs={{0,16},{4,12},{8,24},{12,4},{16,0},{20,28},{24,8},{28,20},{1,17},{... | collective-permute-start | bytes 1351688 | tf_op jit(solution)/shard_map/ppermute | solution.py:310
  68.3 11.5 %collective-permute-start.26 = (bf16[352,640]{1,0:T(8,128)(2,1)S(1)}, bf16[352,640]{1,0:T(8,128)(2,1)S(1)}, u32[]{:S(2)}, u32[]{:S(2)}) collective-permute-start(bf16[352,640]{1,0:T(8,128)(2,1)S(1)} %get-tuple-element.72), channel_id=1, source_target_pairs={{0,16},{4,12},{8,24},{12,4},{16,0},{20,28},{24,8},{28,20},{1,17},{... | collective-permute-start | bytes 1351688 | tf_op jit(solution)/shard_map/ppermute | solution.py:310
  69.0 10.7 %collective-permute-start.24 = (bf16[352,640]{1,0:T(8,128)(2,1)S(1)}, bf16[352,640]{1,0:T(8,128)(2,1)S(1)}, u32[]{:S(2)}, u32[]{:S(2)}) collective-permute-start(bf16[352,640]{1,0:T(8,128)(2,1)S(1)} %collective-permute-done.23.refs_4_), channel_id=1, source_target_pairs={{0,4},{4,0},{8,12},{12,8},{16,20},{20,16},{24,28},{28,24},{1,5},{5... | collective-permute-start | bytes 1351688 | tf_op jit(solution)/shard_map/ppermute | solution.py:66
  74.9 9.4 %collective-permute-start.32 = (bf16[352,640]{1,0:T(8,128)(2,1)S(1)}, bf16[352,640]{1,0:T(8,128)(2,1)S(1)}, u32[]{:S(2)}, u32[]{:S(2)}) collective-permute-start(bf16[352,640]{1,0:T(8,128)(2,1)S(1)} %collective-permute-done.31.refs_10_), channel_id=1, source_target_pairs={{0,4},{4,0},{8,12},{12,8},{16,20},{20,16},{24,28},{28,24},{1,5},{5... | collective-permute-start | bytes 1351688 | tf_op jit(solution)/shard_map/ppermute | solution.py:66
  74.9 9.4 %collective-permute-start.34 = (bf16[336,640]{1,0:T(8,128)(2,1)S(1)}, bf16[336,640]{1,0:T(8,128)(2,1)S(1)}, u32[]{:S(2)}, u32[]{:S(2)}) collective-permute-start(bf16[336,640]{1,0:T(8,128)(2,1)S(1)} %get-tuple-element.77), channel_id=1, source_target_pairs={{0,16},{4,12},{8,24},{12,4},{16,0},{20,28},{24,8},{28,20},{1,17},{... | collective-permute-start | bytes 1290248 | tf_op jit(solution)/shard_map/ppermute | solution.py:310
  79.7 9.4 %collective-permute-start.27 = (bf16[352,640]{1,0:T(8,128)(2,1)S(1)}, bf16[352,640]{1,0:T(8,128)(2,1)S(1)}, u32[]{:S(2)}, u32[]{:S(2)}) collective-permute-start(bf16[352,640]{1,0:T(8,128)(2,1)S(1)} %collective-permute-done.20.refs_2_), channel_id=1, source_target_pairs={{0,16},{4,12},{8,24},{12,4},{16,0},{20,28},{24,8},{28,20},{1,17},{... | collective-permute-start | bytes 1351688 | tf_op jit(solution)/shard_map/ppermute | solution.py:310
  84.3 9.7 %collective-permute-start.35 = (bf16[352,640]{1,0:T(8,128)(2,1)S(1)}, bf16[352,640]{1,0:T(8,128)(2,1)S(1)}, u32[]{:S(2)}, u32[]{:S(2)}) collective-permute-start(bf16[352,640]{1,0:T(8,128)(2,1)S(1)} %collective-permute-done.18.refs_8_), channel_id=1, source_target_pairs={{0,16},{4,12},{8,24},{12,4},{16,0},{20,28},{24,8},{28,20},{1,17},{... | collective-permute-start | bytes 1351688 | tf_op jit(solution)/shard_map/ppermute | solution.py:310
  85.5 8.5 %collective-permute-start.40 = (bf16[336,640]{1,0:T(8,128)(2,1)S(1)}, bf16[336,640]{1,0:T(8,128)(2,1)S(1)}, u32[]{:S(2)}, u32[]{:S(2)}) collective-permute-start(bf16[336,640]{1,0:T(8,128)(2,1)S(1)} %collective-permute-done.34.refs_11_), channel_id=1, source_target_pairs={{0,4},{4,0},{8,12},{12,8},{16,20},{20,16},{24,28},{28,24},{1,5},{5... | collective-permute-start | bytes 1290248 | tf_op jit(solution)/shard_map/ppermute | solution.py:66
  89.2 9.7 %collective-permute-start.38 = (bf16[352,640]{1,0:T(8,128)(2,1)S(1)}, bf16[352,640]{1,0:T(8,128)(2,1)S(1)}, u32[]{:S(2)}, u32[]{:S(2)}) collective-permute-start(bf16[352,640]{1,0:T(8,128)(2,1)S(1)} %collective-permute-done.22.refs_3_), channel_id=1, source_target_pairs={{0,16},{4,12},{8,24},{12,4},{16,0},{20,28},{24,8},{28,20},{1,17},{... | collective-permute-start | bytes 1351688 | tf_op jit(solution)/shard_map/ppermute | solution.py:310
  90.3 9.0 %collective-permute-start.28 = (bf16[352,640]{1,0:T(8,128)(2,1)S(1)}, bf16[352,640]{1,0:T(8,128)(2,1)S(1)}, u32[]{:S(2)}, u32[]{:S(2)}) collective-permute-start(bf16[352,640]{1,0:T(8,128)(2,1)S(1)} %collective-permute-done.27.refs_6_), channel_id=1, source_target_pairs={{0,4},{4,0},{8,12},{12,8},{16,20},{20,16},{24,28},{28,24},{1,5},{5... | collective-permute-start | bytes 1351688 | tf_op jit(solution)/shard_map/ppermute | solution.py:66
  94.0 9.4 %collective-permute-start.36 = (bf16[352,640]{1,0:T(8,128)(2,1)S(1)}, bf16[352,640]{1,0:T(8,128)(2,1)S(1)}, u32[]{:S(2)}, u32[]{:S(2)}) collective-permute-start(bf16[352,640]{1,0:T(8,128)(2,1)S(1)} %collective-permute-done.35.refs_12_), channel_id=1, source_target_pairs={{0,4},{4,0},{8,12},{12,8},{16,20},{20,16},{24,28},{28,24},{1,5},{5... | collective-permute-start | bytes 1351688 | tf_op jit(solution)/shard_map/ppermute | solution.py:66
  94.0 9.4 %collective-permute-start.41 = (bf16[336,640]{1,0:T(8,128)(2,1)S(1)}, bf16[336,640]{1,0:T(8,128)(2,1)S(1)}, u32[]{:S(2)}, u32[]{:S(2)}) collective-permute-start(bf16[336,640]{1,0:T(8,128)(2,1)S(1)} %collective-permute-done.30.refs_9_), channel_id=1, source_target_pairs={{0,16},{4,12},{8,24},{12,4},{16,0},{20,28},{24,8},{28,20},{1,17},{... | collective-permute-start | bytes 1290248 | tf_op jit(solution)/shard_map/ppermute | solution.py:310
  98.8 9.7 %collective-permute-start.39 = (bf16[352,640]{1,0:T(8,128)(2,1)S(1)}, bf16[352,640]{1,0:T(8,128)(2,1)S(1)}, u32[]{:S(2)}, u32[]{:S(2)}) collective-permute-start(bf16[352,640]{1,0:T(8,128)(2,1)S(1)} %collective-permute-done.38.refs_7_), channel_id=1, source_target_pairs={{0,4},{4,0},{8,12},{12,8},{16,20},{20,16},{24,28},{28,24},{1,5},{5... | collective-permute-start | bytes 1351688 | tf_op jit(solution)/shard_map/ppermute | solution.py:66
  99.3 9.2 %collective-permute-start.44 = (bf16[336,640]{1,0:T(8,128)(2,1)S(1)}, bf16[336,640]{1,0:T(8,128)(2,1)S(1)}, u32[]{:S(2)}, u32[]{:S(2)}) collective-permute-start(bf16[336,640]{1,0:T(8,128)(2,1)S(1)} %get-tuple-element.82), channel_id=1, source_target_pairs={{0,16},{4,12},{8,24},{12,4},{16,0},{20,28},{24,8},{28,20},{1,17},{... | collective-permute-start | bytes 1290248 | tf_op jit(solution)/shard_map/ppermute | solution.py:310
  103.9 8.7 %collective-permute-start.46 = (bf16[336,640]{1,0:T(8,128)(2,1)S(1)}, bf16[336,640]{1,0:T(8,128)(2,1)S(1)}, u32[]{:S(2)}, u32[]{:S(2)}) collective-permute-start(bf16[336,640]{1,0:T(8,128)(2,1)S(1)} %shard_map.102.refs_15_), channel_id=1, source_target_pairs={{0,16},{4,12},{8,24},{12,4},{16,0},{20,28},{24,8},{28,20},{1,17},{... | collective-permute-start | bytes 1290248 | tf_op jit(solution)/shard_map/ppermute | solution.py:310
  (30 other events, 249.2 us)

commit v16 on v15

--- a/solution.py
+++ b/solution.py
@@ -331,10 +331,9 @@
         ],
         compiler_params=pltpu.CompilerParams(vmem_limit_bytes=16 * 2**20),
     )(grad_out.T, *tokens)
-    parts = lax.optimization_barrier((*parts, ahead))[:n_dp]
     parts = [part if masks == (0, 0) else turn(part, masks) for part, masks in zip(parts, SWAP_MASKS)]
     (update,) = adam_call(
-        moment_one, moment_two, parts, [jax.ShapeDtypeStruct((rows, wide), jnp.bfloat16)]
+        after(moment_one, [ahead]), moment_two, parts, [jax.ShapeDtypeStruct((rows, wide), jnp.bfloat16)]
     )
     updates = {0: update}
     for k in (6, 2, 4, 1):

time: 115 us -> 115 us (level)
  starting transfers between devices: 36.6 us -> 25.9 us
  waiting for transfers between devices: 57.9 us -> 68.6 us
    ppermute x22, starting transfers between devices: 26.7 us -> 16.4 us  [turn(): lax.ppermute(value, 'dp', [(i, i ^ masks[i & 1]) for i in range(n_dp)])]
    ppermute x22, waiting for transfers between devices: 45.8 us -> 55.8 us  [turn(): lax.ppermute(value, 'dp', [(i, i ^ masks[i & 1]) for i in range(n_dp)])]
  transfers between devices with their start and end apart: 48 -> 48, of which waited for: 24 -> 26; matrix products, arithmetic and copies ran while one was open for 0% -> 0% of each run, Pallas kernels for 14% -> 14%
where the time goes in v16:
time: 115 us
  waiting for transfers between devices  68.6 us (60%)
  starting transfers between devices  25.9 us (23%)
  Pallas kernels  19.3 us (17%)
    ppermute x22, waiting for transfers between devices, turn(): lax.ppermute(value, 'dp', [(i, i ^ masks[i & 1]) for i in range(n_dp)])  55.8 us
    ppermute x22, starting transfers between devices, turn(): lax.ppermute(value, 'dp', [(i, i ^ masks[i & 1]) for i in range(n_dp)])  16.4 us
    ppermute x26, waiting for transfers between devices, send(): return lax.ppermute(value, axis, [(i, i ^ mask) for i in range(size)])  12.8 us
    ppermute x26, starting transfers between devices, send(): return lax.ppermute(value, axis, [(i, i ^ mask) for i in range(size)])  9.45 us
    pallas_call x4, Pallas kernels, lay(): pl.pallas_call(functools.partial(lay_kernel, places=tuple(places), fresh=...  8.48 us
    pallas_call x3, Pallas kernels, weights(): pl.pallas_call(functools.partial(weight_kernel, n_in=len(pieces), spans=s...  3.18 us
    pallas_call x1, Pallas kernels, new_master(): pl.pallas_call(master_kernel, out_shape=jax.ShapeDtypeStruct((cols, slab_...  3.12 us
  transfers between devices with their start and end apart: 48, of which 26 were waited for; matrix products, arithmetic and copies ran while one was open for 0% of the time, Pallas kernels for 14%

profile of v16, /device:TPU:0, one launch (start us, length us, event | category | flops | bytes accessed | tf_op | source)
XLA Modules:
  0.0 115.2 jit_solution(2089408776033910177)
XLA Ops:
  0.7 2.2 %shard_map.93 = f32[336,640]{1,0:T(8,128)} custom-call(f32[1728,640]{1,0:T(8,128)} %bitcast.6), custom_call_target="tpu_custom_call" | custom-call | tf_op jit(solution)/shard_map/pallas_call | solution.py:93
  2.9 3.0 %collective-permute-start.3 = (f32[336,640]{1,0:T(8,128)}, f32[336,640]{1,0:T(8,128)S(1)}, u32[]{:S(2)}, u32[]{:S(2)}) collective-permute-start(f32[336,640]{1,0:T(8,128)} %shard_map.93), channel_id=1, source_target_pairs={{0,8},{4,20},{8,0},{12,28},{16,24},{20,4},{24,16},{28,12},{1,9},{5... | collective-permute-start | bytes 2580488 | tf_op jit(solution)/shard_map/ppermute | solution.py:310
  6.4 1.6 %collective-permute-start = (bf16[128,256]{1,0:T(8,128)(2,1)S(1)}, bf16[128,256]{1,0:T(8,128)(2,1)S(1)}, u32[]{:S(2)}, u32[]{:S(2)}) collective-permute-start(bf16[128,256]{1,0:T(8,128)(2,1)S(1)} %convolution_convert_fusion.refs_0_), channel_id=1, source_target_pairs={{0,1},{1,0},{2,3},{3,2},{4,5},{5,4},{6,7},{7,6},{8,9},{9,8},{10,11... | collective-permute-start | bytes 196616 | tf_op jit(solution)/shard_map/ppermute | solution.py:66
  8.0 2.6 %collective-permute-start.1 = (bf16[128,256]{1,0:T(8,128)(2,1)S(1)}, bf16[128,256]{1,0:T(8,128)(2,1)S(1)}, u32[]{:S(2)}, u32[]{:S(2)}) collective-permute-start(bf16[128,256]{1,0:T(8,128)(2,1)S(1)} %convolution_convert_fusion.refs_0_), channel_id=1, source_target_pairs={{0,2},{1,3},{2,0},{3,1},{4,6},{5,7},{6,4},{7,5},{8,10},{9,11},{10,... | collective-permute-start | bytes 196616 | tf_op jit(solution)/shard_map/ppermute | solution.py:66
  10.8 4.2 %collective-permute-done.1.refs_2_ = bf16[128,256]{1,0:T(8,128)(2,1)S(1)} collective-permute-done((bf16[128,256]{1,0:T(8,128)(2,1)S(1)}, bf16[128,256]{1,0:T(8,128)(2,1)S(1)}, u32[]{:S(2)}, u32[]{:S(2)}) %collective-permute-start.1) | collective-permute-done | bytes 65568 | tf_op jit(solution)/shard_map/ppermute | solution.py:66
  15.0 1.6 %collective-permute-done.2.refs_3_ = bf16[128,256]{1,0:T(8,128)(2,1)S(1)} collective-permute-done((bf16[128,256]{1,0:T(8,128)(2,1)S(1)}, bf16[128,256]{1,0:T(8,128)(2,1)S(1)}, u32[]{:S(2)}, u32[]{:S(2)}) %collective-permute-start.2) | collective-permute-done | bytes 65568 | tf_op jit(solution)/shard_map/ppermute | solution.py:66
  21.0 2.2 %collective-permute-done.4.refs_1_ = bf16[32,1728]{1,0:T(8,128)(2,1)S(1)} collective-permute-done((bf16[32,1728]{1,0:T(8,128)(2,1)S(1)}, bf16[32,1728]{1,0:T(8,128)(2,1)S(1)}, u32[]{:S(2)}, u32[]{:S(2)}) %collective-permute-start.4) | collective-permute-done | bytes 110624 | tf_op jit(solution)/shard_map/ppermute | solution.py:310
  25.7 1.8 %collective-permute-done.7.refs_4_ = bf16[32,1728]{1,0:T(8,128)(2,1)S(1)} collective-permute-done((bf16[32,1728]{1,0:T(8,128)(2,1)S(1)}, bf16[32,1728]{1,0:T(8,128)(2,1)S(1)}, u32[]{:S(2)}, u32[]{:S(2)}) %collective-permute-start.7) | collective-permute-done | bytes 110624 | tf_op jit(solution)/shard_map/ppermute | solution.py:310
  27.4 2.5 %collective-permute-done.8.refs_5_ = bf16[32,1728]{1,0:T(8,128)(2,1)S(1)} collective-permute-done((bf16[32,1728]{1,0:T(8,128)(2,1)S(1)}, bf16[32,1728]{1,0:T(8,128)(2,1)S(1)}, u32[]{:S(2)}, u32[]{:S(2)}) %collective-permute-start.8) | collective-permute-done | bytes 110624 | tf_op jit(solution)/shard_map/ppermute | solution.py:310
  35.6 3.7 %collective-permute-done.14.refs_4_ = bf16[32,1792]{1,0:T(8,128)(2,1)S(1)} collective-permute-done((bf16[32,1792]{1,0:T(8,128)(2,1)S(1)}, bf16[32,1792]{1,0:T(8,128)(2,1)S(1)}, u32[]{:S(2)}, u32[]{:S(2)}) %collective-permute-start.14) | collective-permute-done | bytes 114720 | tf_op jit(solution)/shard_map/ppermute | solution.py:66
  44.8 3.1 %shard_map.98 = f32[1728,640]{1,0:T(8,128)} custom-call(bf16[5120,256]{1,0:T(8,128)(2,1)S(1)} %copy-done.2, f32[1728,640]{1,0:T(8,128)S(1)} %bitcast.9, bf16[1792,256]{1,0:T(8,128)(2,1)S(1)} %get-tuple-element.48.tall.refs_0_), custom_call_target="tpu_custom_call" | custom-call | flops 566231040 | bytes 8847360 | tf_op jit(solution)/shard_map/pallas_call | solution.py:240
  48.0 2.2 %shard_map.99 = (bf16[352,640]{1,0:T(8,128)(2,1)S(1)}, bf16[336,640]{1,0:T(8,128)(2,1)S(1)}, bf16[336,640]{1,0:T(8,128)(2,1)S(1)}, bf16[1728,640]{1,0:T(8,128)(2,1)S(1)}) custom-call(bf16[5120,256]{1,0:T(8,128)(2,1)S(1)} %copy-done.2, f32[1728,640]{1,0:T(8,128)S(1)} %bitcast.10, bf16[1792,256]{1,0:T(8,128)(2,1)S(1)} %get-tuple-element.48.tall.refs_0_), custom_call_target="tpu_custom_call" | custom-call | flops 901775360 | bytes 7045120 | tf_op jit(solution)/shard_map/pallas_call | solution.py:188
  50.8 3.8 %collective-permute-done.18.refs_8_ = bf16[352,640]{1,0:T(8,128)(2,1)S(1)} collective-permute-done((bf16[352,640]{1,0:T(8,128)(2,1)S(1)}, bf16[352,640]{1,0:T(8,128)(2,1)S(1)}, u32[]{:S(2)}, u32[]{:S(2)}) %collective-permute-start.18) | collective-permute-done | bytes 450592 | tf_op jit(solution)/shard_map/ppermute | solution.py:310
  55.4 4.1 %collective-permute-done.22.refs_3_ = bf16[352,640]{1,0:T(8,128)(2,1)S(1)} collective-permute-done((bf16[352,640]{1,0:T(8,128)(2,1)S(1)}, bf16[352,640]{1,0:T(8,128)(2,1)S(1)}, u32[]{:S(2)}, u32[]{:S(2)}) %collective-permute-start.22) | collective-permute-done | bytes 450592 | tf_op jit(solution)/shard_map/ppermute | solution.py:310
  60.0 6.5 %collective-permute-done.30.refs_9_ = bf16[336,640]{1,0:T(8,128)(2,1)S(1)} collective-permute-done((bf16[336,640]{1,0:T(8,128)(2,1)S(1)}, bf16[336,640]{1,0:T(8,128)(2,1)S(1)}, u32[]{:S(2)}, u32[]{:S(2)}) %collective-permute-start.30) | collective-permute-done | bytes 430112 | tf_op jit(solution)/shard_map/ppermute | solution.py:310
  68.9 6.0 %collective-permute-done.31.refs_10_ = bf16[352,640]{1,0:T(8,128)(2,1)S(1)} collective-permute-done((bf16[352,640]{1,0:T(8,128)(2,1)S(1)}, bf16[352,640]{1,0:T(8,128)(2,1)S(1)}, u32[]{:S(2)}, u32[]{:S(2)}) %collective-permute-start.31) | collective-permute-done | bytes 450592 | tf_op jit(solution)/shard_map/ppermute | solution.py:310
  75.5 4.3 %collective-permute-done.26.refs_5_ = bf16[352,640]{1,0:T(8,128)(2,1)S(1)} collective-permute-done((bf16[352,640]{1,0:T(8,128)(2,1)S(1)}, bf16[352,640]{1,0:T(8,128)(2,1)S(1)}, u32[]{:S(2)}, u32[]{:S(2)}) %collective-permute-start.26) | collective-permute-done | bytes 450592 | tf_op jit(solution)/shard_map/ppermute | solution.py:310
  80.3 4.1 %collective-permute-done.34.refs_11_ = bf16[336,640]{1,0:T(8,128)(2,1)S(1)} collective-permute-done((bf16[336,640]{1,0:T(8,128)(2,1)S(1)}, bf16[336,640]{1,0:T(8,128)(2,1)S(1)}, u32[]{:S(2)}, u32[]{:S(2)}) %collective-permute-start.34) | collective-permute-done | bytes 430112 | tf_op jit(solution)/shard_map/ppermute | solution.py:310
  84.9 4.3 %collective-permute-done.27.refs_6_ = bf16[352,640]{1,0:T(8,128)(2,1)S(1)} collective-permute-done((bf16[352,640]{1,0:T(8,128)(2,1)S(1)}, bf16[352,640]{1,0:T(8,128)(2,1)S(1)}, u32[]{:S(2)}, u32[]{:S(2)}) %collective-permute-start.27) | collective-permute-done | bytes 450592 | tf_op jit(solution)/shard_map/ppermute | solution.py:310
  89.7 4.3 %collective-permute-done.35.refs_12_ = bf16[352,640]{1,0:T(8,128)(2,1)S(1)} collective-permute-done((bf16[352,640]{1,0:T(8,128)(2,1)S(1)}, bf16[352,640]{1,0:T(8,128)(2,1)S(1)}, u32[]{:S(2)}, u32[]{:S(2)}) %collective-permute-start.35) | collective-permute-done | bytes 450592 | tf_op jit(solution)/shard_map/ppermute | solution.py:310
  94.5 4.3 %collective-permute-done.38.refs_7_ = bf16[352,640]{1,0:T(8,128)(2,1)S(1)} collective-permute-done((bf16[352,640]{1,0:T(8,128)(2,1)S(1)}, bf16[352,640]{1,0:T(8,128)(2,1)S(1)}, u32[]{:S(2)}, u32[]{:S(2)}) %collective-permute-start.38) | collective-permute-done | bytes 450592 | tf_op jit(solution)/shard_map/ppermute | solution.py:310
  99.9 3.6 %collective-permute-done.41.refs_13_ = bf16[336,640]{1,0:T(8,128)(2,1)S(1)} collective-permute-done((bf16[336,640]{1,0:T(8,128)(2,1)S(1)}, bf16[336,640]{1,0:T(8,128)(2,1)S(1)}, u32[]{:S(2)}, u32[]{:S(2)}) %collective-permute-start.41) | collective-permute-done | bytes 430112 | tf_op jit(solution)/shard_map/ppermute | solution.py:310
  104.5 3.3 %shard_map.101.refs_0_ = bf16[1728,5120]{1,0:T(8,128)(2,1)} custom-call(bf16[1728,640]{1,0:T(8,128)(2,1)S(1)} %get-tuple-element.53.refs_0_.refs_1_, bf16[1728,640]{1,0:T(8,128)(2,1)S(1)} %collective-permute-done.19.refs_1_.refs_2_, bf16[352,640]{1,0:T(8,128)(2,1)S(1)} %collective-permute-done.20.refs_2_, ...), custom_call_target="tpu_custom_call" | custom-call | bytes 16138240 | tf_op jit(solution)/shard_map/pallas_call | solution.py:286
  108.1 3.3 %shard_map.103.refs_0_ = bf16[1728,5120]{1,0:T(8,128)(2,1)} custom-call(bf16[1728,5120]{1,0:T(8,128)(2,1)} %shard_map.101.refs_0_, bf16[1728,640]{1,0:T(8,128)(2,1)S(1)} %get-tuple-element.53.refs_0_.refs_1_, bf16[1728,640]{1,0:T(8,128)(2,1)S(1)} %collective-permute-done.19.refs_1_.refs_2_, ...), custom_call_target="tpu_custom_call", output_to_operand_aliasing={{}: (0, {})} | custom-call | bytes 15810560 | tf_op jit(solution)/shard_map/pallas_call | solution.py:286
  (98 shorter events, 31.9 us)
Async XLA Ops:
  2.9 22.1 %collective-permute-start.3 = (f32[336,640]{1,0:T(8,128)}, f32[336,640]{1,0:T(8,128)S(1)}, u32[]{:S(2)}, u32[]{:S(2)}) collective-permute-start(f32[336,640]{1,0:T(8,128)} %shard_map.93), channel_id=1, source_target_pairs={{0,8},{4,20},{8,0},{12,28},{16,24},{20,4},{24,16},{28,12},{1,9},{5... | collective-permute-start | bytes 2580488 | tf_op jit(solution)/shard_map/ppermute | solution.py:310
  41.3 8.9 %collective-permute-start.20 = (bf16[352,640]{1,0:T(8,128)(2,1)S(1)}, bf16[352,640]{1,0:T(8,128)(2,1)S(1)}, u32[]{:S(2)}, u32[]{:S(2)}) collective-permute-start(bf16[352,640]{1,0:T(8,128)(2,1)S(1)} %get-tuple-element.57), channel_id=1, source_target_pairs={{0,8},{4,20},{8,0},{12,28},{16,24},{20,4},{24,16},{28,12},{1,9},{5... | collective-permute-start | bytes 1351688 | tf_op jit(solution)/shard_map/ppermute | solution.py:310
  42.3 12.3 %collective-permute-start.18 = (bf16[352,640]{1,0:T(8,128)(2,1)S(1)}, bf16[352,640]{1,0:T(8,128)(2,1)S(1)}, u32[]{:S(2)}, u32[]{:S(2)}) collective-permute-start(bf16[352,640]{1,0:T(8,128)(2,1)S(1)} %shard_map.100), channel_id=1, source_target_pairs={{0,8},{4,20},{8,0},{12,28},{16,24},{20,4},{24,16},{28,12},{1,9},{5... | collective-permute-start | bytes 1351688 | tf_op jit(solution)/shard_map/ppermute | solution.py:310
  50.2 9.2 %collective-permute-start.22 = (bf16[352,640]{1,0:T(8,128)(2,1)S(1)}, bf16[352,640]{1,0:T(8,128)(2,1)S(1)}, u32[]{:S(2)}, u32[]{:S(2)}) collective-permute-start(bf16[352,640]{1,0:T(8,128)(2,1)S(1)} %get-tuple-element.58), channel_id=1, source_target_pairs={{0,8},{4,20},{8,0},{12,28},{16,24},{20,4},{24,16},{28,12},{1,9},{5... | collective-permute-start | bytes 1351688 | tf_op jit(solution)/shard_map/ppermute | solution.py:310
  50.8 8.7 %collective-permute-start.21 = (bf16[352,640]{1,0:T(8,128)(2,1)S(1)}, bf16[352,640]{1,0:T(8,128)(2,1)S(1)}, u32[]{:S(2)}, u32[]{:S(2)}) collective-permute-start(bf16[352,640]{1,0:T(8,128)(2,1)S(1)} %collective-permute-done.20.refs_2_), channel_id=1, source_target_pairs={{0,4},{4,0},{8,12},{12,8},{16,20},{20,16},{24,28},{28,24},{1,5},{5... | collective-permute-start | bytes 1351688 | tf_op jit(solution)/shard_map/ppermute | solution.py:66
  54.6 11.9 %collective-permute-start.29 = (bf16[352,640]{1,0:T(8,128)(2,1)S(1)}, bf16[352,640]{1,0:T(8,128)(2,1)S(1)}, u32[]{:S(2)}, u32[]{:S(2)}) collective-permute-start(bf16[352,640]{1,0:T(8,128)(2,1)S(1)} %collective-permute-done.18.refs_8_), channel_id=1, source_target_pairs={{0,4},{4,0},{8,12},{12,8},{16,20},{20,16},{24,28},{28,24},{1,5},{5... | collective-permute-start | bytes 1351688 | tf_op jit(solution)/shard_map/ppermute | solution.py:66
  54.6 11.9 %collective-permute-start.30 = (bf16[336,640]{1,0:T(8,128)(2,1)S(1)}, bf16[336,640]{1,0:T(8,128)(2,1)S(1)}, u32[]{:S(2)}, u32[]{:S(2)}) collective-permute-start(bf16[336,640]{1,0:T(8,128)(2,1)S(1)} %get-tuple-element.63), channel_id=1, source_target_pairs={{0,8},{4,20},{8,0},{12,28},{16,24},{20,4},{24,16},{28,12},{1,9},{5... | collective-permute-start | bytes 1290248 | tf_op jit(solution)/shard_map/ppermute | solution.py:310
  55.1 48.8 %collective-permute-start.19 = (bf16[1728,640]{1,0:T(8,128)(2,1)S(1)}, bf16[1728,640]{1,0:T(8,128)(2,1)S(1)}, u32[]{:S(2)}, u32[]{:S(2)}) collective-permute-start(bf16[1728,640]{1,0:T(8,128)(2,1)S(1)} %get-tuple-element.53.refs_0_.refs_1_), channel_id=1, source_target_pairs={{0,4},{4,0},{8,12},{12,8},{16,20},{20,16},{24,28},{28,24},{1,5},{5... | collective-permute-start | bytes 6635528 | tf_op jit(solution)/shard_map/ppermute | solution.py:66
  59.4 8.8 %collective-permute-start.23 = (bf16[352,640]{1,0:T(8,128)(2,1)S(1)}, bf16[352,640]{1,0:T(8,128)(2,1)S(1)}, u32[]{:S(2)}, u32[]{:S(2)}) collective-permute-start(bf16[352,640]{1,0:T(8,128)(2,1)S(1)} %get-tuple-element.57), channel_id=1, source_target_pairs={{0,16},{4,12},{8,24},{12,4},{16,0},{20,28},{24,8},{28,20},{1,17},{... | collective-permute-start | bytes 1351688 | tf_op jit(solution)/shard_map/ppermute | solution.py:310
  68.3 11.5 %collective-permute-start.26 = (bf16[352,640]{1,0:T(8,128)(2,1)S(1)}, bf16[352,640]{1,0:T(8,128)(2,1)S(1)}, u32[]{:S(2)}, u32[]{:S(2)}) collective-permute-start(bf16[352,640]{1,0:T(8,128)(2,1)S(1)} %get-tuple-element.58), channel_id=1, source_target_pairs={{0,16},{4,12},{8,24},{12,4},{16,0},{20,28},{24,8},{28,20},{1,17},{... | collective-permute-start | bytes 1351688 | tf_op jit(solution)/shard_map/ppermute | solution.py:310
  68.8 10.9 %collective-permute-start.24 = (bf16[352,640]{1,0:T(8,128)(2,1)S(1)}, bf16[352,640]{1,0:T(8,128)(2,1)S(1)}, u32[]{:S(2)}, u32[]{:S(2)}) collective-permute-start(bf16[352,640]{1,0:T(8,128)(2,1)S(1)} %collective-permute-done.23.refs_4_), channel_id=1, source_target_pairs={{0,4},{4,0},{8,12},{12,8},{16,20},{20,16},{24,28},{28,24},{1,5},{5... | collective-permute-start | bytes 1351688 | tf_op jit(solution)/shard_map/ppermute | solution.py:66
  74.9 9.4 %collective-permute-start.32 = (bf16[352,640]{1,0:T(8,128)(2,1)S(1)}, bf16[352,640]{1,0:T(8,128)(2,1)S(1)}, u32[]{:S(2)}, u32[]{:S(2)}) collective-permute-start(bf16[352,640]{1,0:T(8,128)(2,1)S(1)} %collective-permute-done.31.refs_10_), channel_id=1, source_target_pairs={{0,4},{4,0},{8,12},{12,8},{16,20},{20,16},{24,28},{28,24},{1,5},{5... | collective-permute-start | bytes 1351688 | tf_op jit(solution)/shard_map/ppermute | solution.py:66
  74.9 9.4 %collective-permute-start.34 = (bf16[336,640]{1,0:T(8,128)(2,1)S(1)}, bf16[336,640]{1,0:T(8,128)(2,1)S(1)}, u32[]{:S(2)}, u32[]{:S(2)}) collective-permute-start(bf16[336,640]{1,0:T(8,128)(2,1)S(1)} %get-tuple-element.63), channel_id=1, source_target_pairs={{0,16},{4,12},{8,24},{12,4},{16,0},{20,28},{24,8},{28,20},{1,17},{... | collective-permute-start | bytes 1290248 | tf_op jit(solution)/shard_map/ppermute | solution.py:310
  79.7 9.4 %collective-permute-start.27 = (bf16[352,640]{1,0:T(8,128)(2,1)S(1)}, bf16[352,640]{1,0:T(8,128)(2,1)S(1)}, u32[]{:S(2)}, u32[]{:S(2)}) collective-permute-start(bf16[352,640]{1,0:T(8,128)(2,1)S(1)} %collective-permute-done.20.refs_2_), channel_id=1, source_target_pairs={{0,16},{4,12},{8,24},{12,4},{16,0},{20,28},{24,8},{28,20},{1,17},{... | collective-permute-start | bytes 1351688 | tf_op jit(solution)/shard_map/ppermute | solution.py:310
  80.3 8.9 %collective-permute-start.37 = (bf16[352,640]{1,0:T(8,128)(2,1)S(1)}, bf16[352,640]{1,0:T(8,128)(2,1)S(1)}, u32[]{:S(2)}, u32[]{:S(2)}) collective-permute-start(bf16[352,640]{1,0:T(8,128)(2,1)S(1)} %collective-permute-done.26.refs_5_), channel_id=1, source_target_pairs={{0,4},{4,0},{8,12},{12,8},{16,20},{20,16},{24,28},{28,24},{1,5},{5... | collective-permute-start | bytes 1351688 | tf_op jit(solution)/shard_map/ppermute | solution.py:66
  84.3 9.7 %collective-permute-start.35 = (bf16[352,640]{1,0:T(8,128)(2,1)S(1)}, bf16[352,640]{1,0:T(8,128)(2,1)S(1)}, u32[]{:S(2)}, u32[]{:S(2)}) collective-permute-start(bf16[352,640]{1,0:T(8,128)(2,1)S(1)} %collective-permute-done.18.refs_8_), channel_id=1, source_target_pairs={{0,16},{4,12},{8,24},{12,4},{16,0},{20,28},{24,8},{28,20},{1,17},{... | collective-permute-start | bytes 1351688 | tf_op jit(solution)/shard_map/ppermute | solution.py:310
  84.9 9.1 %collective-permute-start.40 = (bf16[336,640]{1,0:T(8,128)(2,1)S(1)}, bf16[336,640]{1,0:T(8,128)(2,1)S(1)}, u32[]{:S(2)}, u32[]{:S(2)}) collective-permute-start(bf16[336,640]{1,0:T(8,128)(2,1)S(1)} %collective-permute-done.34.refs_11_), channel_id=1, source_target_pairs={{0,4},{4,0},{8,12},{12,8},{16,20},{20,16},{24,28},{28,24},{1,5},{5... | collective-permute-start | bytes 1290248 | tf_op jit(solution)/shard_map/ppermute | solution.py:66
  89.2 9.7 %collective-permute-start.38 = (bf16[352,640]{1,0:T(8,128)(2,1)S(1)}, bf16[352,640]{1,0:T(8,128)(2,1)S(1)}, u32[]{:S(2)}, u32[]{:S(2)}) collective-permute-start(bf16[352,640]{1,0:T(8,128)(2,1)S(1)} %collective-permute-done.22.refs_3_), channel_id=1, source_target_pairs={{0,16},{4,12},{8,24},{12,4},{16,0},{20,28},{24,8},{28,20},{1,17},{... | collective-permute-start | bytes 1351688 | tf_op jit(solution)/shard_map/ppermute | solution.py:310
  89.7 9.5 %collective-permute-start.28 = (bf16[352,640]{1,0:T(8,128)(2,1)S(1)}, bf16[352,640]{1,0:T(8,128)(2,1)S(1)}, u32[]{:S(2)}, u32[]{:S(2)}) collective-permute-start(bf16[352,640]{1,0:T(8,128)(2,1)S(1)} %collective-permute-done.27.refs_6_), channel_id=1, source_target_pairs={{0,4},{4,0},{8,12},{12,8},{16,20},{20,16},{24,28},{28,24},{1,5},{5... | collective-permute-start | bytes 1351688 | tf_op jit(solution)/shard_map/ppermute | solution.py:66
  94.0 9.4 %collective-permute-start.36 = (bf16[352,640]{1,0:T(8,128)(2,1)S(1)}, bf16[352,640]{1,0:T(8,128)(2,1)S(1)}, u32[]{:S(2)}, u32[]{:S(2)}) collective-permute-start(bf16[352,640]{1,0:T(8,128)(2,1)S(1)} %collective-permute-done.35.refs_12_), channel_id=1, source_target_pairs={{0,4},{4,0},{8,12},{12,8},{16,20},{20,16},{24,28},{28,24},{1,5},{5... | collective-permute-start | bytes 1351688 | tf_op jit(solution)/shard_map/ppermute | solution.py:66
  94.0 9.4 %collective-permute-start.41 = (bf16[336,640]{1,0:T(8,128)(2,1)S(1)}, bf16[336,640]{1,0:T(8,128)(2,1)S(1)}, u32[]{:S(2)}, u32[]{:S(2)}) collective-permute-start(bf16[336,640]{1,0:T(8,128)(2,1)S(1)} %collective-permute-done.30.refs_9_), channel_id=1, source_target_pairs={{0,16},{4,12},{8,24},{12,4},{16,0},{20,28},{24,8},{28,20},{1,17},{... | collective-permute-start | bytes 1290248 | tf_op jit(solution)/shard_map/ppermute | solution.py:310
  98.8 9.2 %collective-permute-start.39 = (bf16[352,640]{1,0:T(8,128)(2,1)S(1)}, bf16[352,640]{1,0:T(8,128)(2,1)S(1)}, u32[]{:S(2)}, u32[]{:S(2)}) collective-permute-start(bf16[352,640]{1,0:T(8,128)(2,1)S(1)} %collective-permute-done.38.refs_7_), channel_id=1, source_target_pairs={{0,4},{4,0},{8,12},{12,8},{16,20},{20,16},{24,28},{28,24},{1,5},{5... | collective-permute-start | bytes 1351688 | tf_op jit(solution)/shard_map/ppermute | solution.py:66
  99.3 8.8 %collective-permute-start.44 = (bf16[336,640]{1,0:T(8,128)(2,1)S(1)}, bf16[336,640]{1,0:T(8,128)(2,1)S(1)}, u32[]{:S(2)}, u32[]{:S(2)}) collective-permute-start(bf16[336,640]{1,0:T(8,128)(2,1)S(1)} %get-tuple-element.68), channel_id=1, source_target_pairs={{0,16},{4,12},{8,24},{12,4},{16,0},{20,28},{24,8},{28,20},{1,17},{... | collective-permute-start | bytes 1290248 | tf_op jit(solution)/shard_map/ppermute | solution.py:310
  103.9 8.7 %collective-permute-start.46 = (bf16[336,640]{1,0:T(8,128)(2,1)S(1)}, bf16[336,640]{1,0:T(8,128)(2,1)S(1)}, u32[]{:S(2)}, u32[]{:S(2)}) collective-permute-start(bf16[336,640]{1,0:T(8,128)(2,1)S(1)} %shard_map.102.refs_15_), channel_id=1, source_target_pairs={{0,16},{4,12},{8,24},{12,4},{16,0},{20,28},{24,8},{28,20},{1,17},{... | collective-permute-start | bytes 1290248 | tf_op jit(solution)/shard_map/ppermute | solution.py:310
  (30 other events, 245.2 us)

commit v17 on v16

--- a/solution.py
+++ b/solution.py
@@ -254,7 +254,7 @@
     )(projection, master_t, tall)
 
 
-def lay_kernel(*refs, places, fresh):
+def lay_kernel(*refs, places, ways, fresh):
     refs = refs if fresh else refs[1:]
     pieces, out, sems = refs[:-2], refs[-2], refs[-1]
     me = lax.axis_index("dp")
@@ -263,9 +263,14 @@
         piece = pieces[index]
         width = piece.shape[1]
         column = pl.multiple_of(other(me, OWNER_MASKS[kind]) * width, 128)
-        part = piece if piece.shape[0] == count else piece.at[pl.ds(first, count), :]
-        target = out.at[pl.ds(first, count), pl.ds(column, width)]
-        copies.append(pltpu.make_async_copy(part, target, sems.at[at]))
+        origin = 0 if piece.shape[0] == count else first
+        size = -(-count // (16 * ways)) * 16
+        for way in range(ways):
+            start = way * size
+            rows = min(size, count - start)
+            part = piece.at[pl.ds(origin + start, rows), :]
+            target = out.at[pl.ds(first + start, rows), pl.ds(column, width)]
+            copies.append(pltpu.make_async_copy(part, target, sems.at[at * ways + way]))
     for copy in copies:
         copy.start()
     for copy in copies:
@@ -283,12 +288,13 @@
             pieces.append(piece)
         places.append((known[0] if known else len(pieces) - 1, first, count, kind))
     size = sum(count for _, _, count, _ in places) * pieces[0].shape[1]
-    return pl.pallas_call(
-        functools.partial(lay_kernel, places=tuple(places), fresh=fresh),
+    ways = 1 if len(places) > 4 else 4
+    return pl.pallas_call(
+        functools.partial(lay_kernel, places=tuple(places), ways=ways, fresh=fresh),
         out_shape=jax.ShapeDtypeStruct(shape, jnp.bfloat16),
         in_specs=[ANY] * len(held) + [VMEM] * len(pieces),
         out_specs=ANY,
-        scratch_shapes=[pltpu.SemaphoreType.DMA((len(places),))],
+        scratch_shapes=[pltpu.SemaphoreType.DMA((len(places) * ways,))],
         input_output_aliases={} if fresh else {0: 0},
         compiler_params=pltpu.CompilerParams(vmem_limit_bytes=20 * 2**20),
         cost_estimate=pl.CostEstimate(flops=0, bytes_accessed=4 * size, transcendentals=0),

time: 115 us -> 115 us (level)
  no operation moved by 1% of the time
where the time goes in v17:
time: 115 us
  waiting for transfers between devices  68.6 us (60%)
  starting transfers between devices  25.9 us (23%)
  Pallas kernels  19.4 us (17%)
    ppermute x22, waiting for transfers between devices, turn(): lax.ppermute(value, 'dp', [(i, i ^ masks[i & 1]) for i in range(n_dp)])  55.8 us
    ppermute x22, starting transfers between devices, turn(): lax.ppermute(value, 'dp', [(i, i ^ masks[i & 1]) for i in range(n_dp)])  16.4 us
    ppermute x26, waiting for transfers between devices, send(): return lax.ppermute(value, axis, [(i, i ^ mask) for i in range(size)])  12.8 us
    ppermute x26, starting transfers between devices, send(): return lax.ppermute(value, axis, [(i, i ^ mask) for i in range(size)])  9.45 us
    pallas_call x4, Pallas kernels, lay(): pl.pallas_call(functools.partial(lay_kernel, places=tuple(places), ways=w...  8.55 us
    pallas_call x3, Pallas kernels, weights(): pl.pallas_call(functools.partial(weight_kernel, n_in=len(pieces), spans=s...  3.18 us
    pallas_call x1, Pallas kernels, new_master(): pl.pallas_call(master_kernel, out_shape=jax.ShapeDtypeStruct((cols, slab_...  3.12 us
  transfers between devices with their start and end apart: 48, of which 26 were waited for; matrix products, arithmetic and copies ran while one was open for 0% of the time, Pallas kernels for 14%

profile of v17, /device:TPU:0, one launch (start us, length us, event | category | flops | bytes accessed | tf_op | source)
XLA Modules:
  0.0 115.2 jit_solution(3268392200376643180)
XLA Ops:
  0.7 2.2 %shard_map.93 = f32[336,640]{1,0:T(8,128)} custom-call(f32[1728,640]{1,0:T(8,128)} %bitcast.6), custom_call_target="tpu_custom_call" | custom-call | tf_op jit(solution)/shard_map/pallas_call | solution.py:93
  2.9 3.0 %collective-permute-start.3 = (f32[336,640]{1,0:T(8,128)}, f32[336,640]{1,0:T(8,128)S(1)}, u32[]{:S(2)}, u32[]{:S(2)}) collective-permute-start(f32[336,640]{1,0:T(8,128)} %shard_map.93), channel_id=1, source_target_pairs={{0,8},{4,20},{8,0},{12,28},{16,24},{20,4},{24,16},{28,12},{1,9},{5... | collective-permute-start | bytes 2580488 | tf_op jit(solution)/shard_map/ppermute | solution.py:316
  6.4 1.6 %collective-permute-start = (bf16[128,256]{1,0:T(8,128)(2,1)S(1)}, bf16[128,256]{1,0:T(8,128)(2,1)S(1)}, u32[]{:S(2)}, u32[]{:S(2)}) collective-permute-start(bf16[128,256]{1,0:T(8,128)(2,1)S(1)} %convolution_convert_fusion.refs_0_), channel_id=1, source_target_pairs={{0,1},{1,0},{2,3},{3,2},{4,5},{5,4},{6,7},{7,6},{8,9},{9,8},{10,11... | collective-permute-start | bytes 196616 | tf_op jit(solution)/shard_map/ppermute | solution.py:66
  8.0 2.6 %collective-permute-start.1 = (bf16[128,256]{1,0:T(8,128)(2,1)S(1)}, bf16[128,256]{1,0:T(8,128)(2,1)S(1)}, u32[]{:S(2)}, u32[]{:S(2)}) collective-permute-start(bf16[128,256]{1,0:T(8,128)(2,1)S(1)} %convolution_convert_fusion.refs_0_), channel_id=1, source_target_pairs={{0,2},{1,3},{2,0},{3,1},{4,6},{5,7},{6,4},{7,5},{8,10},{9,11},{10,... | collective-permute-start | bytes 196616 | tf_op jit(solution)/shard_map/ppermute | solution.py:66
  10.8 4.2 %collective-permute-done.1.refs_2_ = bf16[128,256]{1,0:T(8,128)(2,1)S(1)} collective-permute-done((bf16[128,256]{1,0:T(8,128)(2,1)S(1)}, bf16[128,256]{1,0:T(8,128)(2,1)S(1)}, u32[]{:S(2)}, u32[]{:S(2)}) %collective-permute-start.1) | collective-permute-done | bytes 65568 | tf_op jit(solution)/shard_map/ppermute | solution.py:66
  15.0 1.6 %collective-permute-done.2.refs_3_ = bf16[128,256]{1,0:T(8,128)(2,1)S(1)} collective-permute-done((bf16[128,256]{1,0:T(8,128)(2,1)S(1)}, bf16[128,256]{1,0:T(8,128)(2,1)S(1)}, u32[]{:S(2)}, u32[]{:S(2)}) %collective-permute-start.2) | collective-permute-done | bytes 65568 | tf_op jit(solution)/shard_map/ppermute | solution.py:66
  21.0 2.2 %collective-permute-done.4.refs_1_ = bf16[32,1728]{1,0:T(8,128)(2,1)S(1)} collective-permute-done((bf16[32,1728]{1,0:T(8,128)(2,1)S(1)}, bf16[32,1728]{1,0:T(8,128)(2,1)S(1)}, u32[]{:S(2)}, u32[]{:S(2)}) %collective-permute-start.4) | collective-permute-done | bytes 110624 | tf_op jit(solution)/shard_map/ppermute | solution.py:316
  25.7 1.8 %collective-permute-done.7.refs_4_ = bf16[32,1728]{1,0:T(8,128)(2,1)S(1)} collective-permute-done((bf16[32,1728]{1,0:T(8,128)(2,1)S(1)}, bf16[32,1728]{1,0:T(8,128)(2,1)S(1)}, u32[]{:S(2)}, u32[]{:S(2)}) %collective-permute-start.7) | collective-permute-done | bytes 110624 | tf_op jit(solution)/shard_map/ppermute | solution.py:316
  27.4 2.5 %collective-permute-done.8.refs_5_ = bf16[32,1728]{1,0:T(8,128)(2,1)S(1)} collective-permute-done((bf16[32,1728]{1,0:T(8,128)(2,1)S(1)}, bf16[32,1728]{1,0:T(8,128)(2,1)S(1)}, u32[]{:S(2)}, u32[]{:S(2)}) %collective-permute-start.8) | collective-permute-done | bytes 110624 | tf_op jit(solution)/shard_map/ppermute | solution.py:316
  35.6 3.7 %collective-permute-done.14.refs_4_ = bf16[32,1792]{1,0:T(8,128)(2,1)S(1)} collective-permute-done((bf16[32,1792]{1,0:T(8,128)(2,1)S(1)}, bf16[32,1792]{1,0:T(8,128)(2,1)S(1)}, u32[]{:S(2)}, u32[]{:S(2)}) %collective-permute-start.14) | collective-permute-done | bytes 114720 | tf_op jit(solution)/shard_map/ppermute | solution.py:66
  44.8 3.1 %shard_map.98 = f32[1728,640]{1,0:T(8,128)} custom-call(bf16[5120,256]{1,0:T(8,128)(2,1)S(1)} %copy-done.2, f32[1728,640]{1,0:T(8,128)S(1)} %bitcast.9, bf16[1792,256]{1,0:T(8,128)(2,1)S(1)} %get-tuple-element.48.tall.refs_0_), custom_call_target="tpu_custom_call" | custom-call | flops 566231040 | bytes 8847360 | tf_op jit(solution)/shard_map/pallas_call | solution.py:240
  48.0 2.2 %shard_map.99 = (bf16[352,640]{1,0:T(8,128)(2,1)S(1)}, bf16[336,640]{1,0:T(8,128)(2,1)S(1)}, bf16[336,640]{1,0:T(8,128)(2,1)S(1)}, bf16[1728,640]{1,0:T(8,128)(2,1)S(1)}) custom-call(bf16[5120,256]{1,0:T(8,128)(2,1)S(1)} %copy-done.2, f32[1728,640]{1,0:T(8,128)S(1)} %bitcast.10, bf16[1792,256]{1,0:T(8,128)(2,1)S(1)} %get-tuple-element.48.tall.refs_0_), custom_call_target="tpu_custom_call" | custom-call | flops 901775360 | bytes 7045120 | tf_op jit(solution)/shard_map/pallas_call | solution.py:188
  50.8 3.8 %collective-permute-done.18.refs_8_ = bf16[352,640]{1,0:T(8,128)(2,1)S(1)} collective-permute-done((bf16[352,640]{1,0:T(8,128)(2,1)S(1)}, bf16[352,640]{1,0:T(8,128)(2,1)S(1)}, u32[]{:S(2)}, u32[]{:S(2)}) %collective-permute-start.18) | collective-permute-done | bytes 450592 | tf_op jit(solution)/shard_map/ppermute | solution.py:316
  55.4 4.1 %collective-permute-done.22.refs_3_ = bf16[352,640]{1,0:T(8,128)(2,1)S(1)} collective-permute-done((bf16[352,640]{1,0:T(8,128)(2,1)S(1)}, bf16[352,640]{1,0:T(8,128)(2,1)S(1)}, u32[]{:S(2)}, u32[]{:S(2)}) %collective-permute-start.22) | collective-permute-done | bytes 450592 | tf_op jit(solution)/shard_map/ppermute | solution.py:316
  60.0 6.5 %collective-permute-done.30.refs_9_ = bf16[336,640]{1,0:T(8,128)(2,1)S(1)} collective-permute-done((bf16[336,640]{1,0:T(8,128)(2,1)S(1)}, bf16[336,640]{1,0:T(8,128)(2,1)S(1)}, u32[]{:S(2)}, u32[]{:S(2)}) %collective-permute-start.30) | collective-permute-done | bytes 430112 | tf_op jit(solution)/shard_map/ppermute | solution.py:316
  68.9 6.0 %collective-permute-done.31.refs_10_ = bf16[352,640]{1,0:T(8,128)(2,1)S(1)} collective-permute-done((bf16[352,640]{1,0:T(8,128)(2,1)S(1)}, bf16[352,640]{1,0:T(8,128)(2,1)S(1)}, u32[]{:S(2)}, u32[]{:S(2)}) %collective-permute-start.31) | collective-permute-done | bytes 450592 | tf_op jit(solution)/shard_map/ppermute | solution.py:316
  75.5 4.3 %collective-permute-done.26.refs_5_ = bf16[352,640]{1,0:T(8,128)(2,1)S(1)} collective-permute-done((bf16[352,640]{1,0:T(8,128)(2,1)S(1)}, bf16[352,640]{1,0:T(8,128)(2,1)S(1)}, u32[]{:S(2)}, u32[]{:S(2)}) %collective-permute-start.26) | collective-permute-done | bytes 450592 | tf_op jit(solution)/shard_map/ppermute | solution.py:316
  80.3 4.1 %collective-permute-done.34.refs_11_ = bf16[336,640]{1,0:T(8,128)(2,1)S(1)} collective-permute-done((bf16[336,640]{1,0:T(8,128)(2,1)S(1)}, bf16[336,640]{1,0:T(8,128)(2,1)S(1)}, u32[]{:S(2)}, u32[]{:S(2)}) %collective-permute-start.34) | collective-permute-done | bytes 430112 | tf_op jit(solution)/shard_map/ppermute | solution.py:316
  84.9 4.3 %collective-permute-done.27.refs_6_ = bf16[352,640]{1,0:T(8,128)(2,1)S(1)} collective-permute-done((bf16[352,640]{1,0:T(8,128)(2,1)S(1)}, bf16[352,640]{1,0:T(8,128)(2,1)S(1)}, u32[]{:S(2)}, u32[]{:S(2)}) %collective-permute-start.27) | collective-permute-done | bytes 450592 | tf_op jit(solution)/shard_map/ppermute | solution.py:316
  89.7 4.3 %collective-permute-done.35.refs_12_ = bf16[352,640]{1,0:T(8,128)(2,1)S(1)} collective-permute-done((bf16[352,640]{1,0:T(8,128)(2,1)S(1)}, bf16[352,640]{1,0:T(8,128)(2,1)S(1)}, u32[]{:S(2)}, u32[]{:S(2)}) %collective-permute-start.35) | collective-permute-done | bytes 450592 | tf_op jit(solution)/shard_map/ppermute | solution.py:316
  94.5 4.3 %collective-permute-done.38.refs_7_ = bf16[352,640]{1,0:T(8,128)(2,1)S(1)} collective-permute-done((bf16[352,640]{1,0:T(8,128)(2,1)S(1)}, bf16[352,640]{1,0:T(8,128)(2,1)S(1)}, u32[]{:S(2)}, u32[]{:S(2)}) %collective-permute-start.38) | collective-permute-done | bytes 450592 | tf_op jit(solution)/shard_map/ppermute | solution.py:316
  99.9 3.6 %collective-permute-done.41.refs_13_ = bf16[336,640]{1,0:T(8,128)(2,1)S(1)} collective-permute-done((bf16[336,640]{1,0:T(8,128)(2,1)S(1)}, bf16[336,640]{1,0:T(8,128)(2,1)S(1)}, u32[]{:S(2)}, u32[]{:S(2)}) %collective-permute-start.41) | collective-permute-done | bytes 430112 | tf_op jit(solution)/shard_map/ppermute | solution.py:316
  104.5 3.3 %shard_map.101.refs_0_ = bf16[1728,5120]{1,0:T(8,128)(2,1)} custom-call(bf16[1728,640]{1,0:T(8,128)(2,1)S(1)} %get-tuple-element.53.refs_0_.refs_1_, bf16[1728,640]{1,0:T(8,128)(2,1)S(1)} %collective-permute-done.19.refs_1_.refs_2_, bf16[352,640]{1,0:T(8,128)(2,1)S(1)} %collective-permute-done.20.refs_2_, ...), custom_call_target="tpu_custom_call" | custom-call | bytes 16138240 | tf_op jit(solution)/shard_map/pallas_call | solution.py:292
  108.1 3.3 %shard_map.103.refs_0_ = bf16[1728,5120]{1,0:T(8,128)(2,1)} custom-call(bf16[1728,5120]{1,0:T(8,128)(2,1)} %shard_map.101.refs_0_, bf16[1728,640]{1,0:T(8,128)(2,1)S(1)} %get-tuple-element.53.refs_0_.refs_1_, bf16[1728,640]{1,0:T(8,128)(2,1)S(1)} %collective-permute-done.19.refs_1_.refs_2_, ...), custom_call_target="tpu_custom_call", output_to_operand_aliasing={{}: (0, {})} | custom-call | bytes 15810560 | tf_op jit(solution)/shard_map/pallas_call | solution.py:292
  (98 shorter events, 31.9 us)
Async XLA Ops:
  2.9 22.1 %collective-permute-start.3 = (f32[336,640]{1,0:T(8,128)}, f32[336,640]{1,0:T(8,128)S(1)}, u32[]{:S(2)}, u32[]{:S(2)}) collective-permute-start(f32[336,640]{1,0:T(8,128)} %shard_map.93), channel_id=1, source_target_pairs={{0,8},{4,20},{8,0},{12,28},{16,24},{20,4},{24,16},{28,12},{1,9},{5... | collective-permute-start | bytes 2580488 | tf_op jit(solution)/shard_map/ppermute | solution.py:316
  41.3 8.9 %collective-permute-start.20 = (bf16[352,640]{1,0:T(8,128)(2,1)S(1)}, bf16[352,640]{1,0:T(8,128)(2,1)S(1)}, u32[]{:S(2)}, u32[]{:S(2)}) collective-permute-start(bf16[352,640]{1,0:T(8,128)(2,1)S(1)} %get-tuple-element.57), channel_id=1, source_target_pairs={{0,8},{4,20},{8,0},{12,28},{16,24},{20,4},{24,16},{28,12},{1,9},{5... | collective-permute-start | bytes 1351688 | tf_op jit(solution)/shard_map/ppermute | solution.py:316
  42.3 12.3 %collective-permute-start.18 = (bf16[352,640]{1,0:T(8,128)(2,1)S(1)}, bf16[352,640]{1,0:T(8,128)(2,1)S(1)}, u32[]{:S(2)}, u32[]{:S(2)}) collective-permute-start(bf16[352,640]{1,0:T(8,128)(2,1)S(1)} %shard_map.100), channel_id=1, source_target_pairs={{0,8},{4,20},{8,0},{12,28},{16,24},{20,4},{24,16},{28,12},{1,9},{5... | collective-permute-start | bytes 1351688 | tf_op jit(solution)/shard_map/ppermute | solution.py:316
  50.2 9.2 %collective-permute-start.22 = (bf16[352,640]{1,0:T(8,128)(2,1)S(1)}, bf16[352,640]{1,0:T(8,128)(2,1)S(1)}, u32[]{:S(2)}, u32[]{:S(2)}) collective-permute-start(bf16[352,640]{1,0:T(8,128)(2,1)S(1)} %get-tuple-element.58), channel_id=1, source_target_pairs={{0,8},{4,20},{8,0},{12,28},{16,24},{20,4},{24,16},{28,12},{1,9},{5... | collective-permute-start | bytes 1351688 | tf_op jit(solution)/shard_map/ppermute | solution.py:316
  50.8 8.7 %collective-permute-start.21 = (bf16[352,640]{1,0:T(8,128)(2,1)S(1)}, bf16[352,640]{1,0:T(8,128)(2,1)S(1)}, u32[]{:S(2)}, u32[]{:S(2)}) collective-permute-start(bf16[352,640]{1,0:T(8,128)(2,1)S(1)} %collective-permute-done.20.refs_2_), channel_id=1, source_target_pairs={{0,4},{4,0},{8,12},{12,8},{16,20},{20,16},{24,28},{28,24},{1,5},{5... | collective-permute-start | bytes 1351688 | tf_op jit(solution)/shard_map/ppermute | solution.py:66
  54.6 11.9 %collective-permute-start.29 = (bf16[352,640]{1,0:T(8,128)(2,1)S(1)}, bf16[352,640]{1,0:T(8,128)(2,1)S(1)}, u32[]{:S(2)}, u32[]{:S(2)}) collective-permute-start(bf16[352,640]{1,0:T(8,128)(2,1)S(1)} %collective-permute-done.18.refs_8_), channel_id=1, source_target_pairs={{0,4},{4,0},{8,12},{12,8},{16,20},{20,16},{24,28},{28,24},{1,5},{5... | collective-permute-start | bytes 1351688 | tf_op jit(solution)/shard_map/ppermute | solution.py:66
  54.6 11.9 %collective-permute-start.30 = (bf16[336,640]{1,0:T(8,128)(2,1)S(1)}, bf16[336,640]{1,0:T(8,128)(2,1)S(1)}, u32[]{:S(2)}, u32[]{:S(2)}) collective-permute-start(bf16[336,640]{1,0:T(8,128)(2,1)S(1)} %get-tuple-element.63), channel_id=1, source_target_pairs={{0,8},{4,20},{8,0},{12,28},{16,24},{20,4},{24,16},{28,12},{1,9},{5... | collective-permute-start | bytes 1290248 | tf_op jit(solution)/shard_map/ppermute | solution.py:316
  55.1 48.8 %collective-permute-start.19 = (bf16[1728,640]{1,0:T(8,128)(2,1)S(1)}, bf16[1728,640]{1,0:T(8,128)(2,1)S(1)}, u32[]{:S(2)}, u32[]{:S(2)}) collective-permute-start(bf16[1728,640]{1,0:T(8,128)(2,1)S(1)} %get-tuple-element.53.refs_0_.refs_1_), channel_id=1, source_target_pairs={{0,4},{4,0},{8,12},{12,8},{16,20},{20,16},{24,28},{28,24},{1,5},{5... | collective-permute-start | bytes 6635528 | tf_op jit(solution)/shard_map/ppermute | solution.py:66
  59.4 8.8 %collective-permute-start.23 = (bf16[352,640]{1,0:T(8,128)(2,1)S(1)}, bf16[352,640]{1,0:T(8,128)(2,1)S(1)}, u32[]{:S(2)}, u32[]{:S(2)}) collective-permute-start(bf16[352,640]{1,0:T(8,128)(2,1)S(1)} %get-tuple-element.57), channel_id=1, source_target_pairs={{0,16},{4,12},{8,24},{12,4},{16,0},{20,28},{24,8},{28,20},{1,17},{... | collective-permute-start | bytes 1351688 | tf_op jit(solution)/shard_map/ppermute | solution.py:316
  68.3 11.5 %collective-permute-start.26 = (bf16[352,640]{1,0:T(8,128)(2,1)S(1)}, bf16[352,640]{1,0:T(8,128)(2,1)S(1)}, u32[]{:S(2)}, u32[]{:S(2)}) collective-permute-start(bf16[352,640]{1,0:T(8,128)(2,1)S(1)} %get-tuple-element.58), channel_id=1, source_target_pairs={{0,16},{4,12},{8,24},{12,4},{16,0},{20,28},{24,8},{28,20},{1,17},{... | collective-permute-start | bytes 1351688 | tf_op jit(solution)/shard_map/ppermute | solution.py:316
  68.8 10.9 %collective-permute-start.24 = (bf16[352,640]{1,0:T(8,128)(2,1)S(1)}, bf16[352,640]{1,0:T(8,128)(2,1)S(1)}, u32[]{:S(2)}, u32[]{:S(2)}) collective-permute-start(bf16[352,640]{1,0:T(8,128)(2,1)S(1)} %collective-permute-done.23.refs_4_), channel_id=1, source_target_pairs={{0,4},{4,0},{8,12},{12,8},{16,20},{20,16},{24,28},{28,24},{1,5},{5... | collective-permute-start | bytes 1351688 | tf_op jit(solution)/shard_map/ppermute | solution.py:66
  74.9 9.4 %collective-permute-start.32 = (bf16[352,640]{1,0:T(8,128)(2,1)S(1)}, bf16[352,640]{1,0:T(8,128)(2,1)S(1)}, u32[]{:S(2)}, u32[]{:S(2)}) collective-permute-start(bf16[352,640]{1,0:T(8,128)(2,1)S(1)} %collective-permute-done.31.refs_10_), channel_id=1, source_target_pairs={{0,4},{4,0},{8,12},{12,8},{16,20},{20,16},{24,28},{28,24},{1,5},{5... | collective-permute-start | bytes 1351688 | tf_op jit(solution)/shard_map/ppermute | solution.py:66
  74.9 9.4 %collective-permute-start.34 = (bf16[336,640]{1,0:T(8,128)(2,1)S(1)}, bf16[336,640]{1,0:T(8,128)(2,1)S(1)}, u32[]{:S(2)}, u32[]{:S(2)}) collective-permute-start(bf16[336,640]{1,0:T(8,128)(2,1)S(1)} %get-tuple-element.63), channel_id=1, source_target_pairs={{0,16},{4,12},{8,24},{12,4},{16,0},{20,28},{24,8},{28,20},{1,17},{... | collective-permute-start | bytes 1290248 | tf_op jit(solution)/shard_map/ppermute | solution.py:316
  79.7 9.4 %collective-permute-start.27 = (bf16[352,640]{1,0:T(8,128)(2,1)S(1)}, bf16[352,640]{1,0:T(8,128)(2,1)S(1)}, u32[]{:S(2)}, u32[]{:S(2)}) collective-permute-start(bf16[352,640]{1,0:T(8,128)(2,1)S(1)} %collective-permute-done.20.refs_2_), channel_id=1, source_target_pairs={{0,16},{4,12},{8,24},{12,4},{16,0},{20,28},{24,8},{28,20},{1,17},{... | collective-permute-start | bytes 1351688 | tf_op jit(solution)/shard_map/ppermute | solution.py:316
  80.3 8.9 %collective-permute-start.37 = (bf16[352,640]{1,0:T(8,128)(2,1)S(1)}, bf16[352,640]{1,0:T(8,128)(2,1)S(1)}, u32[]{:S(2)}, u32[]{:S(2)}) collective-permute-start(bf16[352,640]{1,0:T(8,128)(2,1)S(1)} %collective-permute-done.26.refs_5_), channel_id=1, source_target_pairs={{0,4},{4,0},{8,12},{12,8},{16,20},{20,16},{24,28},{28,24},{1,5},{5... | collective-permute-start | bytes 1351688 | tf_op jit(solution)/shard_map/ppermute | solution.py:66
  84.3 9.7 %collective-permute-start.35 = (bf16[352,640]{1,0:T(8,128)(2,1)S(1)}, bf16[352,640]{1,0:T(8,128)(2,1)S(1)}, u32[]{:S(2)}, u32[]{:S(2)}) collective-permute-start(bf16[352,640]{1,0:T(8,128)(2,1)S(1)} %collective-permute-done.18.refs_8_), channel_id=1, source_target_pairs={{0,16},{4,12},{8,24},{12,4},{16,0},{20,28},{24,8},{28,20},{1,17},{... | collective-permute-start | bytes 1351688 | tf_op jit(solution)/shard_map/ppermute | solution.py:316
  84.9 9.1 %collective-permute-start.40 = (bf16[336,640]{1,0:T(8,128)(2,1)S(1)}, bf16[336,640]{1,0:T(8,128)(2,1)S(1)}, u32[]{:S(2)}, u32[]{:S(2)}) collective-permute-start(bf16[336,640]{1,0:T(8,128)(2,1)S(1)} %collective-permute-done.34.refs_11_), channel_id=1, source_target_pairs={{0,4},{4,0},{8,12},{12,8},{16,20},{20,16},{24,28},{28,24},{1,5},{5... | collective-permute-start | bytes 1290248 | tf_op jit(solution)/shard_map/ppermute | solution.py:66
  89.2 9.7 %collective-permute-start.38 = (bf16[352,640]{1,0:T(8,128)(2,1)S(1)}, bf16[352,640]{1,0:T(8,128)(2,1)S(1)}, u32[]{:S(2)}, u32[]{:S(2)}) collective-permute-start(bf16[352,640]{1,0:T(8,128)(2,1)S(1)} %collective-permute-done.22.refs_3_), channel_id=1, source_target_pairs={{0,16},{4,12},{8,24},{12,4},{16,0},{20,28},{24,8},{28,20},{1,17},{... | collective-permute-start | bytes 1351688 | tf_op jit(solution)/shard_map/ppermute | solution.py:316
  89.7 9.5 %collective-permute-start.28 = (bf16[352,640]{1,0:T(8,128)(2,1)S(1)}, bf16[352,640]{1,0:T(8,128)(2,1)S(1)}, u32[]{:S(2)}, u32[]{:S(2)}) collective-permute-start(bf16[352,640]{1,0:T(8,128)(2,1)S(1)} %collective-permute-done.27.refs_6_), channel_id=1, source_target_pairs={{0,4},{4,0},{8,12},{12,8},{16,20},{20,16},{24,28},{28,24},{1,5},{5... | collective-permute-start | bytes 1351688 | tf_op jit(solution)/shard_map/ppermute | solution.py:66
  94.0 9.4 %collective-permute-start.36 = (bf16[352,640]{1,0:T(8,128)(2,1)S(1)}, bf16[352,640]{1,0:T(8,128)(2,1)S(1)}, u32[]{:S(2)}, u32[]{:S(2)}) collective-permute-start(bf16[352,640]{1,0:T(8,128)(2,1)S(1)} %collective-permute-done.35.refs_12_), channel_id=1, source_target_pairs={{0,4},{4,0},{8,12},{12,8},{16,20},{20,16},{24,28},{28,24},{1,5},{5... | collective-permute-start | bytes 1351688 | tf_op jit(solution)/shard_map/ppermute | solution.py:66
  94.0 9.4 %collective-permute-start.41 = (bf16[336,640]{1,0:T(8,128)(2,1)S(1)}, bf16[336,640]{1,0:T(8,128)(2,1)S(1)}, u32[]{:S(2)}, u32[]{:S(2)}) collective-permute-start(bf16[336,640]{1,0:T(8,128)(2,1)S(1)} %collective-permute-done.30.refs_9_), channel_id=1, source_target_pairs={{0,16},{4,12},{8,24},{12,4},{16,0},{20,28},{24,8},{28,20},{1,17},{... | collective-permute-start | bytes 1290248 | tf_op jit(solution)/shard_map/ppermute | solution.py:316
  98.8 9.2 %collective-permute-start.39 = (bf16[352,640]{1,0:T(8,128)(2,1)S(1)}, bf16[352,640]{1,0:T(8,128)(2,1)S(1)}, u32[]{:S(2)}, u32[]{:S(2)}) collective-permute-start(bf16[352,640]{1,0:T(8,128)(2,1)S(1)} %collective-permute-done.38.refs_7_), channel_id=1, source_target_pairs={{0,4},{4,0},{8,12},{12,8},{16,20},{20,16},{24,28},{28,24},{1,5},{5... | collective-permute-start | bytes 1351688 | tf_op jit(solution)/shard_map/ppermute | solution.py:66
  99.3 8.8 %collective-permute-start.44 = (bf16[336,640]{1,0:T(8,128)(2,1)S(1)}, bf16[336,640]{1,0:T(8,128)(2,1)S(1)}, u32[]{:S(2)}, u32[]{:S(2)}) collective-permute-start(bf16[336,640]{1,0:T(8,128)(2,1)S(1)} %get-tuple-element.68), channel_id=1, source_target_pairs={{0,16},{4,12},{8,24},{12,4},{16,0},{20,28},{24,8},{28,20},{1,17},{... | collective-permute-start | bytes 1290248 | tf_op jit(solution)/shard_map/ppermute | solution.py:316
  103.9 8.7 %collective-permute-start.46 = (bf16[336,640]{1,0:T(8,128)(2,1)S(1)}, bf16[336,640]{1,0:T(8,128)(2,1)S(1)}, u32[]{:S(2)}, u32[]{:S(2)}) collective-permute-start(bf16[336,640]{1,0:T(8,128)(2,1)S(1)} %shard_map.102.refs_15_), channel_id=1, source_target_pairs={{0,16},{4,12},{8,24},{12,4},{16,0},{20,28},{24,8},{28,20},{1,17},{... | collective-permute-start | bytes 1290248 | tf_op jit(solution)/shard_map/ppermute | solution.py:316
  (30 other events, 245.2 us)

commit v18 on v16

--- a/solution.py
+++ b/solution.py
@@ -370,7 +370,9 @@
         earlier = [got[steps[step - 2]]] if step >= 2 else []
         earlier += [over[steps[step - 4]]] if step >= 4 else []
         if step == 2:
-            earlier += [master_new, moment_one_new]
+            earlier.append(moment_one_new)
+        if step == 3:
+            earlier.append(master_new)
         got[(phase, at)] = turn(after(value, earlier), TURN_MASKS[min(phase, 1)])
         held = [outs[step - len(steps) + 3]] if step >= len(steps) - 2 else []
         over[(phase, at)] = hop(after(got[(phase, at)], held), 1)

time: 115 us -> 119 us (1.035)
  waiting for transfers between devices: 68.6 us -> 75.4 us
  starting transfers between devices: 25.9 us -> 22.9 us
    ppermute x22, waiting for transfers between devices: 55.8 us -> 62.5 us  [turn(): lax.ppermute(value, 'dp', [(i, i ^ masks[i & 1]) for i in range(n_dp)])]
    ppermute x22, starting transfers between devices: 16.4 us -> 13.5 us  [turn(): lax.ppermute(value, 'dp', [(i, i ^ masks[i & 1]) for i in range(n_dp)])]
  transfers between devices with their start and end apart: 48 -> 48, of which waited for: 26 -> 26; matrix products, arithmetic and copies ran while one was open for 0% -> 0% of each run, Pallas kernels for 14% -> 13%
where the time goes in v18:
time: 119 us
  waiting for transfers between devices  75.4 us (63%)
  starting transfers between devices  22.9 us (19%)
  Pallas kernels  19.3 us (16%)
    ppermute x22, waiting for transfers between devices, turn(): lax.ppermute(value, 'dp', [(i, i ^ masks[i & 1]) for i in range(n_dp)])  62.5 us
    ppermute x22, starting transfers between devices, turn(): lax.ppermute(value, 'dp', [(i, i ^ masks[i & 1]) for i in range(n_dp)])  13.5 us
    ppermute x26, waiting for transfers between devices, send(): return lax.ppermute(value, axis, [(i, i ^ mask) for i in range(size)])  12.8 us
    ppermute x26, starting transfers between devices, send(): return lax.ppermute(value, axis, [(i, i ^ mask) for i in range(size)])  9.34 us
    pallas_call x4, Pallas kernels, lay(): pl.pallas_call(functools.partial(lay_kernel, places=tuple(places), fresh=...  8.48 us
    pallas_call x3, Pallas kernels, weights(): pl.pallas_call(functools.partial(weight_kernel, n_in=len(pieces), spans=s...  3.18 us
    pallas_call x1, Pallas kernels, new_master(): pl.pallas_call(master_kernel, out_shape=jax.ShapeDtypeStruct((cols, slab_...  3.13 us
  transfers between devices with their start and end apart: 48, of which 26 were waited for; matrix products, arithmetic and copies ran while one was open for 0% of the time, Pallas kernels for 13%

profile of v18, /device:TPU:0, one launch (start us, length us, event | category | flops | bytes accessed | tf_op | source)
XLA Modules:
  0.0 119.0 jit_solution(13809533729187434598)
XLA Ops:
  0.7 2.2 %shard_map.93 = f32[336,640]{1,0:T(8,128)} custom-call(f32[1728,640]{1,0:T(8,128)} %bitcast.6), custom_call_target="tpu_custom_call" | custom-call | tf_op jit(solution)/shard_map/pallas_call | solution.py:93
  2.9 3.0 %collective-permute-start.3 = (f32[336,640]{1,0:T(8,128)}, f32[336,640]{1,0:T(8,128)S(1)}, u32[]{:S(2)}, u32[]{:S(2)}) collective-permute-start(f32[336,640]{1,0:T(8,128)} %shard_map.93), channel_id=1, source_target_pairs={{0,8},{4,20},{8,0},{12,28},{16,24},{20,4},{24,16},{28,12},{1,9},{5... | collective-permute-start | bytes 2580488 | tf_op jit(solution)/shard_map/ppermute | solution.py:310
  8.0 2.6 %collective-permute-start.1 = (bf16[128,256]{1,0:T(8,128)(2,1)S(1)}, bf16[128,256]{1,0:T(8,128)(2,1)S(1)}, u32[]{:S(2)}, u32[]{:S(2)}) collective-permute-start(bf16[128,256]{1,0:T(8,128)(2,1)S(1)} %convolution_convert_fusion.refs_0_), channel_id=1, source_target_pairs={{0,2},{1,3},{2,0},{3,1},{4,6},{5,7},{6,4},{7,5},{8,10},{9,11},{10,... | collective-permute-start | bytes 196616 | tf_op jit(solution)/shard_map/ppermute | solution.py:66
  10.8 4.2 %collective-permute-done.1.refs_2_ = bf16[128,256]{1,0:T(8,128)(2,1)S(1)} collective-permute-done((bf16[128,256]{1,0:T(8,128)(2,1)S(1)}, bf16[128,256]{1,0:T(8,128)(2,1)S(1)}, u32[]{:S(2)}, u32[]{:S(2)}) %collective-permute-start.1) | collective-permute-done | bytes 65568 | tf_op jit(solution)/shard_map/ppermute | solution.py:66
  15.0 1.6 %collective-permute-done.2.refs_3_ = bf16[128,256]{1,0:T(8,128)(2,1)S(1)} collective-permute-done((bf16[128,256]{1,0:T(8,128)(2,1)S(1)}, bf16[128,256]{1,0:T(8,128)(2,1)S(1)}, u32[]{:S(2)}, u32[]{:S(2)}) %collective-permute-start.2) | collective-permute-done | bytes 65568 | tf_op jit(solution)/shard_map/ppermute | solution.py:66
  21.0 2.2 %collective-permute-done.4.refs_1_ = bf16[32,1728]{1,0:T(8,128)(2,1)S(1)} collective-permute-done((bf16[32,1728]{1,0:T(8,128)(2,1)S(1)}, bf16[32,1728]{1,0:T(8,128)(2,1)S(1)}, u32[]{:S(2)}, u32[]{:S(2)}) %collective-permute-start.4) | collective-permute-done | bytes 110624 | tf_op jit(solution)/shard_map/ppermute | solution.py:310
  25.7 1.8 %collective-permute-done.7.refs_4_ = bf16[32,1728]{1,0:T(8,128)(2,1)S(1)} collective-permute-done((bf16[32,1728]{1,0:T(8,128)(2,1)S(1)}, bf16[32,1728]{1,0:T(8,128)(2,1)S(1)}, u32[]{:S(2)}, u32[]{:S(2)}) %collective-permute-start.7) | collective-permute-done | bytes 110624 | tf_op jit(solution)/shard_map/ppermute | solution.py:310
  27.4 2.5 %collective-permute-done.8.refs_5_ = bf16[32,1728]{1,0:T(8,128)(2,1)S(1)} collective-permute-done((bf16[32,1728]{1,0:T(8,128)(2,1)S(1)}, bf16[32,1728]{1,0:T(8,128)(2,1)S(1)}, u32[]{:S(2)}, u32[]{:S(2)}) %collective-permute-start.8) | collective-permute-done | bytes 110624 | tf_op jit(solution)/shard_map/ppermute | solution.py:310
  35.6 3.7 %collective-permute-done.14.refs_4_ = bf16[32,1792]{1,0:T(8,128)(2,1)S(1)} collective-permute-done((bf16[32,1792]{1,0:T(8,128)(2,1)S(1)}, bf16[32,1792]{1,0:T(8,128)(2,1)S(1)}, u32[]{:S(2)}, u32[]{:S(2)}) %collective-permute-start.14) | collective-permute-done | bytes 114720 | tf_op jit(solution)/shard_map/ppermute | solution.py:66
  44.8 2.2 %shard_map.99 = (bf16[352,640]{1,0:T(8,128)(2,1)S(1)}, bf16[336,640]{1,0:T(8,128)(2,1)S(1)}, bf16[336,640]{1,0:T(8,128)(2,1)S(1)}, bf16[1728,640]{1,0:T(8,128)(2,1)S(1)}) custom-call(bf16[5120,256]{1,0:T(8,128)(2,1)S(1)} %copy-done.2, f32[1728,640]{1,0:T(8,128)S(1)} %bitcast.9, bf16[1792,256]{1,0:T(8,128)(2,1)S(1)} %get-tuple-element.48.tall.refs_0_), custom_call_target="tpu_custom_call" | custom-call | flops 901775360 | bytes 7045120 | tf_op jit(solution)/shard_map/pallas_call | solution.py:188
  47.1 2.7 %collective-permute-done.20.refs_2_ = bf16[352,640]{1,0:T(8,128)(2,1)S(1)} collective-permute-done((bf16[352,640]{1,0:T(8,128)(2,1)S(1)}, bf16[352,640]{1,0:T(8,128)(2,1)S(1)}, u32[]{:S(2)}, u32[]{:S(2)}) %collective-permute-start.20) | collective-permute-done | bytes 450592 | tf_op jit(solution)/shard_map/ppermute | solution.py:310
  50.3 4.3 %collective-permute-done.18.refs_8_ = bf16[352,640]{1,0:T(8,128)(2,1)S(1)} collective-permute-done((bf16[352,640]{1,0:T(8,128)(2,1)S(1)}, bf16[352,640]{1,0:T(8,128)(2,1)S(1)}, u32[]{:S(2)}, u32[]{:S(2)}) %collective-permute-start.18) | collective-permute-done | bytes 450592 | tf_op jit(solution)/shard_map/ppermute | solution.py:310
  54.6 3.1 %shard_map.98 = f32[1728,640]{1,0:T(8,128)} custom-call(bf16[5120,256]{1,0:T(8,128)(2,1)S(1)} %copy-done.2, f32[1728,640]{1,0:T(8,128)S(1)} %bitcast.10, bf16[1792,256]{1,0:T(8,128)(2,1)S(1)} %get-tuple-element.48.tall.refs_0_), custom_call_target="tpu_custom_call" | custom-call | flops 566231040 | bytes 8847360 | tf_op jit(solution)/shard_map/pallas_call | solution.py:240
  60.0 10.3 %collective-permute-done.30.refs_9_ = bf16[336,640]{1,0:T(8,128)(2,1)S(1)} collective-permute-done((bf16[336,640]{1,0:T(8,128)(2,1)S(1)}, bf16[336,640]{1,0:T(8,128)(2,1)S(1)}, u32[]{:S(2)}, u32[]{:S(2)}) %collective-permute-start.30) | collective-permute-done | bytes 430112 | tf_op jit(solution)/shard_map/ppermute | solution.py:310
  70.3 2.1 %collective-permute-start.26 = (bf16[352,640]{1,0:T(8,128)(2,1)S(1)}, bf16[352,640]{1,0:T(8,128)(2,1)S(1)}, u32[]{:S(2)}, u32[]{:S(2)}) collective-permute-start(bf16[352,640]{1,0:T(8,128)(2,1)S(1)} %get-tuple-element.58), channel_id=1, source_target_pairs={{0,16},{4,12},{8,24},{12,4},{16,0},{20,28},{24,8},{28,20},{1,17},{... | collective-permute-start | bytes 1351688 | tf_op jit(solution)/shard_map/ppermute | solution.py:310
  72.4 6.3 %collective-permute-done.31.refs_10_ = bf16[352,640]{1,0:T(8,128)(2,1)S(1)} collective-permute-done((bf16[352,640]{1,0:T(8,128)(2,1)S(1)}, bf16[352,640]{1,0:T(8,128)(2,1)S(1)}, u32[]{:S(2)}, u32[]{:S(2)}) %collective-permute-start.31) | collective-permute-done | bytes 450592 | tf_op jit(solution)/shard_map/ppermute | solution.py:310
  78.7 4.8 %collective-permute-done.26.refs_5_ = bf16[352,640]{1,0:T(8,128)(2,1)S(1)} collective-permute-done((bf16[352,640]{1,0:T(8,128)(2,1)S(1)}, bf16[352,640]{1,0:T(8,128)(2,1)S(1)}, u32[]{:S(2)}, u32[]{:S(2)}) %collective-permute-start.26) | collective-permute-done | bytes 450592 | tf_op jit(solution)/shard_map/ppermute | solution.py:310
  83.5 4.6 %collective-permute-done.34.refs_11_ = bf16[336,640]{1,0:T(8,128)(2,1)S(1)} collective-permute-done((bf16[336,640]{1,0:T(8,128)(2,1)S(1)}, bf16[336,640]{1,0:T(8,128)(2,1)S(1)}, u32[]{:S(2)}, u32[]{:S(2)}) %collective-permute-start.34) | collective-permute-done | bytes 430112 | tf_op jit(solution)/shard_map/ppermute | solution.py:310
  88.1 4.8 %collective-permute-done.27.refs_6_ = bf16[352,640]{1,0:T(8,128)(2,1)S(1)} collective-permute-done((bf16[352,640]{1,0:T(8,128)(2,1)S(1)}, bf16[352,640]{1,0:T(8,128)(2,1)S(1)}, u32[]{:S(2)}, u32[]{:S(2)}) %collective-permute-start.27) | collective-permute-done | bytes 450592 | tf_op jit(solution)/shard_map/ppermute | solution.py:310
  93.0 4.8 %collective-permute-done.35.refs_12_ = bf16[352,640]{1,0:T(8,128)(2,1)S(1)} collective-permute-done((bf16[352,640]{1,0:T(8,128)(2,1)S(1)}, bf16[352,640]{1,0:T(8,128)(2,1)S(1)}, u32[]{:S(2)}, u32[]{:S(2)}) %collective-permute-start.35) | collective-permute-done | bytes 450592 | tf_op jit(solution)/shard_map/ppermute | solution.py:310
  97.8 4.8 %collective-permute-done.38.refs_7_ = bf16[352,640]{1,0:T(8,128)(2,1)S(1)} collective-permute-done((bf16[352,640]{1,0:T(8,128)(2,1)S(1)}, bf16[352,640]{1,0:T(8,128)(2,1)S(1)}, u32[]{:S(2)}, u32[]{:S(2)}) %collective-permute-start.38) | collective-permute-done | bytes 450592 | tf_op jit(solution)/shard_map/ppermute | solution.py:310
  103.1 4.1 %collective-permute-done.41.refs_13_ = bf16[336,640]{1,0:T(8,128)(2,1)S(1)} collective-permute-done((bf16[336,640]{1,0:T(8,128)(2,1)S(1)}, bf16[336,640]{1,0:T(8,128)(2,1)S(1)}, u32[]{:S(2)}, u32[]{:S(2)}) %collective-permute-start.41) | collective-permute-done | bytes 430112 | tf_op jit(solution)/shard_map/ppermute | solution.py:310
  107.7 3.3 %shard_map.101.refs_0_ = bf16[1728,5120]{1,0:T(8,128)(2,1)} custom-call(bf16[1728,640]{1,0:T(8,128)(2,1)S(1)} %get-tuple-element.53.refs_0_.refs_1_, bf16[1728,640]{1,0:T(8,128)(2,1)S(1)} %collective-permute-done.19.refs_1_.refs_2_, bf16[352,640]{1,0:T(8,128)(2,1)S(1)} %collective-permute-done.20.refs_2_, ...), custom_call_target="tpu_custom_call" | custom-call | bytes 16138240 | tf_op jit(solution)/shard_map/pallas_call | solution.py:286
  111.9 3.3 %shard_map.103.refs_0_ = bf16[1728,5120]{1,0:T(8,128)(2,1)} custom-call(bf16[1728,5120]{1,0:T(8,128)(2,1)} %shard_map.101.refs_0_, bf16[1728,640]{1,0:T(8,128)(2,1)S(1)} %get-tuple-element.53.refs_0_.refs_1_, bf16[1728,640]{1,0:T(8,128)(2,1)S(1)} %collective-permute-done.19.refs_1_.refs_2_, ...), custom_call_target="tpu_custom_call", output_to_operand_aliasing={{}: (0, {})} | custom-call | bytes 15810560 | tf_op jit(solution)/shard_map/pallas_call | solution.py:286
  (98 shorter events, 28.8 us)
Async XLA Ops:
  2.9 22.1 %collective-permute-start.3 = (f32[336,640]{1,0:T(8,128)}, f32[336,640]{1,0:T(8,128)S(1)}, u32[]{:S(2)}, u32[]{:S(2)}) collective-permute-start(f32[336,640]{1,0:T(8,128)} %shard_map.93), channel_id=1, source_target_pairs={{0,8},{4,20},{8,0},{12,28},{16,24},{20,4},{24,16},{28,12},{1,9},{5... | collective-permute-start | bytes 2580488 | tf_op jit(solution)/shard_map/ppermute | solution.py:310
  42.3 12.3 %collective-permute-start.18 = (bf16[352,640]{1,0:T(8,128)(2,1)S(1)}, bf16[352,640]{1,0:T(8,128)(2,1)S(1)}, u32[]{:S(2)}, u32[]{:S(2)}) collective-permute-start(bf16[352,640]{1,0:T(8,128)(2,1)S(1)} %shard_map.100), channel_id=1, source_target_pairs={{0,8},{4,20},{8,0},{12,28},{16,24},{20,4},{24,16},{28,12},{1,9},{5... | collective-permute-start | bytes 1351688 | tf_op jit(solution)/shard_map/ppermute | solution.py:310
  49.8 9.7 %collective-permute-start.22 = (bf16[352,640]{1,0:T(8,128)(2,1)S(1)}, bf16[352,640]{1,0:T(8,128)(2,1)S(1)}, u32[]{:S(2)}, u32[]{:S(2)}) collective-permute-start(bf16[352,640]{1,0:T(8,128)(2,1)S(1)} %get-tuple-element.58), channel_id=1, source_target_pairs={{0,8},{4,20},{8,0},{12,28},{16,24},{20,4},{24,16},{28,12},{1,9},{5... | collective-permute-start | bytes 1351688 | tf_op jit(solution)/shard_map/ppermute | solution.py:310
  50.3 9.2 %collective-permute-start.21 = (bf16[352,640]{1,0:T(8,128)(2,1)S(1)}, bf16[352,640]{1,0:T(8,128)(2,1)S(1)}, u32[]{:S(2)}, u32[]{:S(2)}) collective-permute-start(bf16[352,640]{1,0:T(8,128)(2,1)S(1)} %collective-permute-done.20.refs_2_), channel_id=1, source_target_pairs={{0,4},{4,0},{8,12},{12,8},{16,20},{20,16},{24,28},{28,24},{1,5},{5... | collective-permute-start | bytes 1351688 | tf_op jit(solution)/shard_map/ppermute | solution.py:66
  54.6 15.7 %collective-permute-start.29 = (bf16[352,640]{1,0:T(8,128)(2,1)S(1)}, bf16[352,640]{1,0:T(8,128)(2,1)S(1)}, u32[]{:S(2)}, u32[]{:S(2)}) collective-permute-start(bf16[352,640]{1,0:T(8,128)(2,1)S(1)} %collective-permute-done.18.refs_8_), channel_id=1, source_target_pairs={{0,4},{4,0},{8,12},{12,8},{16,20},{20,16},{24,28},{28,24},{1,5},{5... | collective-permute-start | bytes 1351688 | tf_op jit(solution)/shard_map/ppermute | solution.py:66
  57.7 12.5 %collective-permute-start.30 = (bf16[336,640]{1,0:T(8,128)(2,1)S(1)}, bf16[336,640]{1,0:T(8,128)(2,1)S(1)}, u32[]{:S(2)}, u32[]{:S(2)}) collective-permute-start(bf16[336,640]{1,0:T(8,128)(2,1)S(1)} %get-tuple-element.63), channel_id=1, source_target_pairs={{0,8},{4,20},{8,0},{12,28},{16,24},{20,4},{24,16},{28,12},{1,9},{5... | collective-permute-start | bytes 1290248 | tf_op jit(solution)/shard_map/ppermute | solution.py:310
  58.2 49.5 %collective-permute-start.19 = (bf16[1728,640]{1,0:T(8,128)(2,1)S(1)}, bf16[1728,640]{1,0:T(8,128)(2,1)S(1)}, u32[]{:S(2)}, u32[]{:S(2)}) collective-permute-start(bf16[1728,640]{1,0:T(8,128)(2,1)S(1)} %get-tuple-element.53.refs_0_.refs_1_), channel_id=1, source_target_pairs={{0,4},{4,0},{8,12},{12,8},{16,20},{20,16},{24,28},{28,24},{1,5},{5... | collective-permute-start | bytes 6635528 | tf_op jit(solution)/shard_map/ppermute | solution.py:66
  59.4 10.9 %collective-permute-start.23 = (bf16[352,640]{1,0:T(8,128)(2,1)S(1)}, bf16[352,640]{1,0:T(8,128)(2,1)S(1)}, u32[]{:S(2)}, u32[]{:S(2)}) collective-permute-start(bf16[352,640]{1,0:T(8,128)(2,1)S(1)} %get-tuple-element.57), channel_id=1, source_target_pairs={{0,16},{4,12},{8,24},{12,4},{16,0},{20,28},{24,8},{28,20},{1,17},{... | collective-permute-start | bytes 1351688 | tf_op jit(solution)/shard_map/ppermute | solution.py:310
  60.0 10.3 %collective-permute-start.25 = (bf16[352,640]{1,0:T(8,128)(2,1)S(1)}, bf16[352,640]{1,0:T(8,128)(2,1)S(1)}, u32[]{:S(2)}, u32[]{:S(2)}) collective-permute-start(bf16[352,640]{1,0:T(8,128)(2,1)S(1)} %collective-permute-done.22.refs_3_), channel_id=1, source_target_pairs={{0,4},{4,0},{8,12},{12,8},{16,20},{20,16},{24,28},{28,24},{1,5},{5... | collective-permute-start | bytes 1351688 | tf_op jit(solution)/shard_map/ppermute | solution.py:66
  70.3 13.2 %collective-permute-start.26 = (bf16[352,640]{1,0:T(8,128)(2,1)S(1)}, bf16[352,640]{1,0:T(8,128)(2,1)S(1)}, u32[]{:S(2)}, u32[]{:S(2)}) collective-permute-start(bf16[352,640]{1,0:T(8,128)(2,1)S(1)} %get-tuple-element.58), channel_id=1, source_target_pairs={{0,16},{4,12},{8,24},{12,4},{16,0},{20,28},{24,8},{28,20},{1,17},{... | collective-permute-start | bytes 1351688 | tf_op jit(solution)/shard_map/ppermute | solution.py:310
  72.4 11.1 %collective-permute-start.24 = (bf16[352,640]{1,0:T(8,128)(2,1)S(1)}, bf16[352,640]{1,0:T(8,128)(2,1)S(1)}, u32[]{:S(2)}, u32[]{:S(2)}) collective-permute-start(bf16[352,640]{1,0:T(8,128)(2,1)S(1)} %collective-permute-done.23.refs_4_), channel_id=1, source_target_pairs={{0,4},{4,0},{8,12},{12,8},{16,20},{20,16},{24,28},{28,24},{1,5},{5... | collective-permute-start | bytes 1351688 | tf_op jit(solution)/shard_map/ppermute | solution.py:66
  78.7 9.4 %collective-permute-start.32 = (bf16[352,640]{1,0:T(8,128)(2,1)S(1)}, bf16[352,640]{1,0:T(8,128)(2,1)S(1)}, u32[]{:S(2)}, u32[]{:S(2)}) collective-permute-start(bf16[352,640]{1,0:T(8,128)(2,1)S(1)} %collective-permute-done.31.refs_10_), channel_id=1, source_target_pairs={{0,4},{4,0},{8,12},{12,8},{16,20},{20,16},{24,28},{28,24},{1,5},{5... | collective-permute-start | bytes 1351688 | tf_op jit(solution)/shard_map/ppermute | solution.py:66
  78.7 9.4 %collective-permute-start.34 = (bf16[336,640]{1,0:T(8,128)(2,1)S(1)}, bf16[336,640]{1,0:T(8,128)(2,1)S(1)}, u32[]{:S(2)}, u32[]{:S(2)}) collective-permute-start(bf16[336,640]{1,0:T(8,128)(2,1)S(1)} %get-tuple-element.63), channel_id=1, source_target_pairs={{0,16},{4,12},{8,24},{12,4},{16,0},{20,28},{24,8},{28,20},{1,17},{... | collective-permute-start | bytes 1290248 | tf_op jit(solution)/shard_map/ppermute | solution.py:310
  83.5 9.4 %collective-permute-start.27 = (bf16[352,640]{1,0:T(8,128)(2,1)S(1)}, bf16[352,640]{1,0:T(8,128)(2,1)S(1)}, u32[]{:S(2)}, u32[]{:S(2)}) collective-permute-start(bf16[352,640]{1,0:T(8,128)(2,1)S(1)} %collective-permute-done.20.refs_2_), channel_id=1, source_target_pairs={{0,16},{4,12},{8,24},{12,4},{16,0},{20,28},{24,8},{28,20},{1,17},{... | collective-permute-start | bytes 1351688 | tf_op jit(solution)/shard_map/ppermute | solution.py:310
  83.5 9.4 %collective-permute-start.37 = (bf16[352,640]{1,0:T(8,128)(2,1)S(1)}, bf16[352,640]{1,0:T(8,128)(2,1)S(1)}, u32[]{:S(2)}, u32[]{:S(2)}) collective-permute-start(bf16[352,640]{1,0:T(8,128)(2,1)S(1)} %collective-permute-done.26.refs_5_), channel_id=1, source_target_pairs={{0,4},{4,0},{8,12},{12,8},{16,20},{20,16},{24,28},{28,24},{1,5},{5... | collective-permute-start | bytes 1351688 | tf_op jit(solution)/shard_map/ppermute | solution.py:66
  88.1 9.7 %collective-permute-start.35 = (bf16[352,640]{1,0:T(8,128)(2,1)S(1)}, bf16[352,640]{1,0:T(8,128)(2,1)S(1)}, u32[]{:S(2)}, u32[]{:S(2)}) collective-permute-start(bf16[352,640]{1,0:T(8,128)(2,1)S(1)} %collective-permute-done.18.refs_8_), channel_id=1, source_target_pairs={{0,16},{4,12},{8,24},{12,4},{16,0},{20,28},{24,8},{28,20},{1,17},{... | collective-permute-start | bytes 1351688 | tf_op jit(solution)/shard_map/ppermute | solution.py:310
  88.1 9.7 %collective-permute-start.40 = (bf16[336,640]{1,0:T(8,128)(2,1)S(1)}, bf16[336,640]{1,0:T(8,128)(2,1)S(1)}, u32[]{:S(2)}, u32[]{:S(2)}) collective-permute-start(bf16[336,640]{1,0:T(8,128)(2,1)S(1)} %collective-permute-done.34.refs_11_), channel_id=1, source_target_pairs={{0,4},{4,0},{8,12},{12,8},{16,20},{20,16},{24,28},{28,24},{1,5},{5... | collective-permute-start | bytes 1290248 | tf_op jit(solution)/shard_map/ppermute | solution.py:66
  93.0 9.7 %collective-permute-start.38 = (bf16[352,640]{1,0:T(8,128)(2,1)S(1)}, bf16[352,640]{1,0:T(8,128)(2,1)S(1)}, u32[]{:S(2)}, u32[]{:S(2)}) collective-permute-start(bf16[352,640]{1,0:T(8,128)(2,1)S(1)} %collective-permute-done.22.refs_3_), channel_id=1, source_target_pairs={{0,16},{4,12},{8,24},{12,4},{16,0},{20,28},{24,8},{28,20},{1,17},{... | collective-permute-start | bytes 1351688 | tf_op jit(solution)/shard_map/ppermute | solution.py:310
  93.0 10.1 %collective-permute-start.28 = (bf16[352,640]{1,0:T(8,128)(2,1)S(1)}, bf16[352,640]{1,0:T(8,128)(2,1)S(1)}, u32[]{:S(2)}, u32[]{:S(2)}) collective-permute-start(bf16[352,640]{1,0:T(8,128)(2,1)S(1)} %collective-permute-done.27.refs_6_), channel_id=1, source_target_pairs={{0,4},{4,0},{8,12},{12,8},{16,20},{20,16},{24,28},{28,24},{1,5},{5... | collective-permute-start | bytes 1351688 | tf_op jit(solution)/shard_map/ppermute | solution.py:66
  97.8 9.4 %collective-permute-start.36 = (bf16[352,640]{1,0:T(8,128)(2,1)S(1)}, bf16[352,640]{1,0:T(8,128)(2,1)S(1)}, u32[]{:S(2)}, u32[]{:S(2)}) collective-permute-start(bf16[352,640]{1,0:T(8,128)(2,1)S(1)} %collective-permute-done.35.refs_12_), channel_id=1, source_target_pairs={{0,4},{4,0},{8,12},{12,8},{16,20},{20,16},{24,28},{28,24},{1,5},{5... | collective-permute-start | bytes 1351688 | tf_op jit(solution)/shard_map/ppermute | solution.py:66
  97.8 9.4 %collective-permute-start.41 = (bf16[336,640]{1,0:T(8,128)(2,1)S(1)}, bf16[336,640]{1,0:T(8,128)(2,1)S(1)}, u32[]{:S(2)}, u32[]{:S(2)}) collective-permute-start(bf16[336,640]{1,0:T(8,128)(2,1)S(1)} %collective-permute-done.30.refs_9_), channel_id=1, source_target_pairs={{0,16},{4,12},{8,24},{12,4},{16,0},{20,28},{24,8},{28,20},{1,17},{... | collective-permute-start | bytes 1290248 | tf_op jit(solution)/shard_map/ppermute | solution.py:310
  102.6 9.2 %collective-permute-start.39 = (bf16[352,640]{1,0:T(8,128)(2,1)S(1)}, bf16[352,640]{1,0:T(8,128)(2,1)S(1)}, u32[]{:S(2)}, u32[]{:S(2)}) collective-permute-start(bf16[352,640]{1,0:T(8,128)(2,1)S(1)} %collective-permute-done.38.refs_7_), channel_id=1, source_target_pairs={{0,4},{4,0},{8,12},{12,8},{16,20},{20,16},{24,28},{28,24},{1,5},{5... | collective-permute-start | bytes 1351688 | tf_op jit(solution)/shard_map/ppermute | solution.py:66
  103.1 8.8 %collective-permute-start.44 = (bf16[336,640]{1,0:T(8,128)(2,1)S(1)}, bf16[336,640]{1,0:T(8,128)(2,1)S(1)}, u32[]{:S(2)}, u32[]{:S(2)}) collective-permute-start(bf16[336,640]{1,0:T(8,128)(2,1)S(1)} %get-tuple-element.68), channel_id=1, source_target_pairs={{0,16},{4,12},{8,24},{12,4},{16,0},{20,28},{24,8},{28,20},{1,17},{... | collective-permute-start | bytes 1290248 | tf_op jit(solution)/shard_map/ppermute | solution.py:310
  107.7 8.7 %collective-permute-start.46 = (bf16[336,640]{1,0:T(8,128)(2,1)S(1)}, bf16[336,640]{1,0:T(8,128)(2,1)S(1)}, u32[]{:S(2)}, u32[]{:S(2)}) collective-permute-start(bf16[336,640]{1,0:T(8,128)(2,1)S(1)} %shard_map.102.refs_15_), channel_id=1, source_target_pairs={{0,16},{4,12},{8,24},{12,4},{16,0},{20,28},{24,8},{28,20},{1,17},{... | collective-permute-start | bytes 1290248 | tf_op jit(solution)/shard_map/ppermute | solution.py:310
  (30 other events, 245.9 us)
